TPU v7x, 32 devices: a whole 2x2x4 slice. The times are simulated.
32 devices in a mesh: grp: 2 (over y), mk: 4 (over z), pp: 2 (over x), sub: 2 (over core).
Axes of the slice: x: 2, y: 2, z: 4, core: 2. Of those that a mesh axis runs over, the one named last changes fastest.
Arguments:
- genotypes: bfloat16 [4096, 16384], P(('grp', 'pp', 'sub'), 'mk'), parts along dimension 0, may hold values from -6 to 6
- estimate: bfloat16 [512, 16384], P(('grp', 'pp', 'sub'), 'mk'), parts along dimension 0, may hold values from -0.046875 to 0.046875
- phenotypes: bfloat16 [512, 2048], P('grp', ('pp', 'sub')), parts along dimension 0, may hold values from -6 to 6
- prior_logit: float32 [512], P(('grp', 'pp', 'sub')), parts along dimension 0, may hold values from -2 to 1
- slab_var: float32 [512], P(('grp', 'pp', 'sub')), parts along dimension 0, may hold values from 0.5 to 4
- noise_var: float32 [512], P(('grp', 'pp', 'sub')), parts along dimension 0, may hold values from 0.5 to 2
- tile_chrom: int32 [64], P('grp'), parts along dimension 0, may hold values from 0 to 21, as said below
Outputs:
- updated: bfloat16 [512, 16384], P(('grp', 'pp', 'sub'), 'mk'), parts along dimension 0
- loco_out: bfloat16 [44, 256, 2048], P('grp', 'mk', ('pp', 'sub')), parts along dimension 0
There are 2 independent parts, one for each index of `grp`. A program takes and returns all parts, laid end to end along the dimension named above; each array names one. Nothing has to cross between parts.
Inputs may be any that keep to these rules, and one draw needn't show every extreme that they name: `tile_chrom`: never falling along the tiles; every chromosome owns at least one tile; the tiles of one device (aligned blocks of 8 tiles) name at most 6 chromosomes, and some device names exactly 6.
All inputs are finite; a program needn't handle non-finite values.
Results may differ from a plain program's by a relative error of at most 0.0059.
Values may be sent and summed in bfloat16 or wider, within the bound.
No kernel may reach another device: no remote copies, remote signals or barrier semaphores. Data moves between devices by JAX's collectives and lax.ppermute only.
A program may use at most 64 MiB of HBM per device.

v0:
```python
import math

import jax
import jax.numpy as jnp
from jax import lax
from jax.sharding import PartitionSpec as P

CHROMS = 22
TILE = 512
SPAN = 6


def denoise(estimate, scores, prior_logit, slab_var, noise_var, marker_root, people_root):
    observed = marker_root * estimate.astype(jnp.float32) + scores * (1.0 / people_root)
    slab_col = slab_var[:, None]
    noise_col = noise_var[:, None]
    spread = slab_col + noise_col
    log_odds = (
        prior_logit[:, None]
        + 0.5 * jnp.log(noise_col / spread)
        + 0.5 * observed * observed * (1.0 / noise_col - 1.0 / spread)
    )
    posterior = jax.nn.sigmoid(log_odds) * (slab_col / spread) * observed
    return (posterior * (1.0 / marker_root)).astype(jnp.bfloat16)


def per_device(genotypes, estimate, phenotypes, prior_logit, slab_var, noise_var, tile_chrom):
    people_dev, mark_dev = genotypes.shape
    mk_count = lax.axis_size("mk")
    people_count = lax.axis_size(("pp", "sub"))
    traits = phenotypes.shape[0]
    partial_pred = lax.dot_general(
        lax.all_gather(estimate, ("pp", "sub"), axis=0, tiled=True),
        genotypes,
        (((1,), (1,)), ((), ())),
        preferred_element_type=jnp.float32,
    )
    share_rows = traits // mk_count
    offset = lax.axis_index("mk") * share_rows
    phen_share = lax.dynamic_slice_in_dim(phenotypes, offset, share_rows, 0).astype(jnp.float32)
    prediction = lax.psum(partial_pred, "mk")
    residual = (phenotypes.astype(jnp.float32) - prediction).astype(jnp.bfloat16)
    scores = lax.psum_scatter(
        jnp.dot(residual, genotypes, preferred_element_type=jnp.float32),
        ("pp", "sub"),
        scatter_dimension=0,
        tiled=True,
    )
    updated = denoise(
        estimate,
        scores,
        prior_logit,
        slab_var,
        noise_var,
        math.sqrt(mark_dev * mk_count),
        math.sqrt(people_dev * people_count),
    )
    tile_dev = mark_dev // TILE
    own_tiles = lax.dynamic_slice_in_dim(tile_chrom, lax.axis_index("mk") * tile_dev, tile_dev, 0)
    labels = own_tiles[0] + jnp.arange(SPAN, dtype=jnp.int32)
    member = (labels[:, None] == own_tiles[None, :]).astype(jnp.float32)
    geno_tiles = genotypes.reshape(people_dev, tile_dev, TILE)
    shard_rows = lax.all_gather(updated, ("pp", "sub"), axis=0, tiled=True)
    tile_terms = jnp.einsum(
        "kta,pta->tkp",
        shard_rows.reshape(shard_rows.shape[0], tile_dev, TILE),
        geno_tiles,
        preferred_element_type=jnp.float32,
    )
    local_sums = jnp.einsum("st,tkp->skp", member, tile_terms, precision=lax.Precision.HIGHEST)
    received = lax.all_to_all(local_sums, "mk", split_axis=1, concat_axis=0, tiled=True)
    firsts = tile_chrom.reshape(mk_count, tile_dev)[:, 0]
    sources = (firsts[:, None] + jnp.arange(SPAN, dtype=jnp.int32)[None, :]).reshape(-1)
    assign = (jnp.arange(CHROMS, dtype=jnp.int32)[:, None] == sources[None, :]).astype(jnp.float32)
    chrom_sums = jnp.einsum("cj,jkp->ckp", assign, received, precision=lax.Precision.HIGHEST)
    combined = jnp.sum(chrom_sums, axis=0)
    loco_out = (phen_share[None] - combined[None] + chrom_sums).astype(jnp.bfloat16)
    return (updated, loco_out)


def solution(mesh):
    placed = (
        P(("grp", "pp", "sub"), "mk"),
        P(("grp", "pp", "sub"), "mk"),
        P("grp", ("pp", "sub")),
        P(("grp", "pp", "sub")),
        P(("grp", "pp", "sub")),
        P(("grp", "pp", "sub")),
        P("grp"),
    )
    return jax.shard_map(
        per_device,
        mesh=mesh,
        in_specs=placed,
        out_specs=(P(("grp", "pp", "sub"), "mk"), P("grp", "mk", ("pp", "sub"))),
        check_vma=False,
    )
```

profile of v0, /device:TPU:13, one launch (start us, length us, event | category | flops | bytes accessed | tf_op | source)
XLA Modules:
  0.0 274.6 jit_solution(18358932344819804699)
XLA Ops:
  7.2 0.0 all-gather.3.cloned.1.call-start
  7.2 0.7 all-gather.3.cloned.1.call-update
  7.9 0.0 copy-start.1
  7.9 0.0 all-reduce.2.cloned.1.call-start
  8.0 25.7 %all-gather.3.cloned.1.call-done = bf16[256,4096]{1,0:T(8,128)(2,1)} async-done(((bf16[64,4096]{1,0:T(8,128)(2,1)}), bf16[256,4096]{1,0:T(8,128)(2,1)}) %all-gather.3.cloned.1.call-update) | async-done | bytes 2097168 | tf_op jit(solution)/shard_map/all_gather | solution.py:33
  33.7 4.9 %fusion.26 = f32[256,512]{1,0:T(8,128)} fusion(bf16[256,4096]{1,0:T(8,128)(2,1)} %all-gather.3.cloned.1.call-done, bf16[512,4096]{1,0:T(8,128)(2,1)} %param.7), kind=kOutput, calls=%fused_computation.36 | convolution fusion | flops 1073741824 | bytes 6815744 | tf_op jit(solution)/shard_map/dot_general | solution.py:32
  38.6 0.0 all-reduce.2.cloned.1.call-update
  38.6 0.0 reduce-scatter.2.cloned.1.call-start
  38.7 36.7 %all-reduce.2.cloned.1.call-done = f32[256,512]{1,0:T(8,128)} async-done(((f32[256,512]{1,0:T(8,128)}), f32[256,512]{1,0:T(8,128)}) %all-reduce.2.cloned.1.call-update) | async-done | bytes 524304 | tf_op jit(solution)/shard_map/psum | solution.py:41
  75.4 0.0 copy-done.1
  75.4 5.6 %fusion.17 = f32[256,4096]{1,0:T(8,128)} fusion(bf16[512,4096]{1,0:T(8,128)(2,1)} %param.7, f32[256,512]{1,0:T(8,128)} %all-reduce.2.cloned.1.call-done, bf16[256,512]{1,0:T(8,128)(2,1)S(1)} %copy-done.1), kind=kOutput, calls=%fused_computation.20 | convolution fusion | flops 1074135040 | bytes 9175040 | tf_op jit(solution)/shard_map/dot_general | solution.py:44
  81.0 0.0 copy-start.3
  81.0 0.0 copy-start.4
  81.0 0.0 copy-start.5
  81.0 0.0 copy-start
  81.0 0.0 reduce-scatter.2.cloned.1.call-update
  81.0 0.0 all-gather.5.cloned.1.call-start
  81.1 0.6 copy-done.3
  81.6 0.0 copy-done.4
  81.6 0.0 copy-done.5
  81.7 45.3 %reduce-scatter.2.cloned.1.call-done = f32[64,4096]{1,0:T(8,128)} async-done(((f32[256,4096]{1,0:T(8,128)}), f32[64,4096]{1,0:T(8,128)}) %reduce-scatter.2.cloned.1.call-update) | async-done | bytes 1048592 | tf_op jit(solution)/shard_map/reduce_scatter | solution.py:43
  126.9 0.0 copy-done
  126.9 2.6 fusion.16
  129.5 0.0 all-gather.5.cloned.1.call-update
  129.5 0.0 copy-start.2
  129.5 6.5 %copy.17 = bf16[512,4096]{0,1:T(8,128)(2,1)} copy(bf16[512,4096]{1,0:T(8,128)(2,1)} %param.7) | data formatting | bytes 8388608 | tf_op jit(solution)/shard_map/reshape | solution.py:62
  136.0 0.0 copy-done.2
  136.0 0.1 dynamic_slice.7
  136.2 16.6 %all-gather.5.cloned.1.call-done = bf16[256,4096]{1,0:T(8,128)(2,1)} async-done(((bf16[64,4096]{1,0:T(8,128)(2,1)}), bf16[256,4096]{1,0:T(8,128)(2,1)}) %all-gather.5.cloned.1.call-update) | async-done | bytes 2097168 | tf_op jit(solution)/shard_map/all_gather | solution.py:63
  152.7 4.1 %fusion.4 = f32[8,256,512]{2,1,0:T(8,128)S(1)} fusion(bf16[512,8,512]{0,2,1:T(8,128)(2,1)} %bitcast.23, bf16[32,8,8,512]{3,2,1,0:T(8,128)(2,1)} %bitcast.25), kind=kOutput, calls=%fused_computation.5 | convolution fusion | flops 1073741824 | bytes 10485760 | tf_op jit(solution)/shard_map/kta,pta->tkp/dot_general | solution.py:64
  156.8 6.3 %fusion = f32[6,256,512]{2,0,1:T(8,128)} fusion(f32[8,256,512]{2,1,0:T(8,128)S(1)} %fusion.4, s32[8]{0:T(128)S(1)} %dynamic_slice.7, s32[6]{0:T(128)S(1)} %iota_add_fusion.1), kind=kOutput, calls=%fused_computation | convolution fusion | flops 75497520 | bytes 7340088 | tf_op jit(solution)/shard_map/st,tkp->skp/dot_general | solution.py:70
  163.1 5.1 %all-to-all-start = ((f32[6,256,512]{2,0,1:T(8,128)}), f32[6,256,512]{2,0,1:T(8,128)}, u32[]{:S(2)}, u32[]{:S(2)}) async-start(f32[6,256,512]{2,0,1:T(8,128)} %fusion), calls=%async_computation.1 | async-start | bytes 8388608 | tf_op jit(solution)/shard_map/all_to_all | solution.py:71
  168.1 0.1 reshape.46
  168.2 0.1 slice_reduce_fusion
  168.3 0.1 iota_add_fusion
  168.4 0.1 add.83
  168.5 89.6 %all-to-all-done = f32[6,256,512]{2,0,1:T(8,128)} async-done(((f32[6,256,512]{2,0,1:T(8,128)}), f32[6,256,512]{2,0,1:T(8,128)}, u32[]{:S(2)}, u32[]{:S(2)}) %all-to-all-start) | async-done | bytes 3145760 | tf_op jit(solution)/shard_map/all_to_all | solution.py:71
  258.2 4.0 %copy.11 = f32[6,4,64,512]{3,2,0,1:T(8,128)S(1)} copy(f32[6,4,64,512]{3,0,2,1:T(8,128)} %bitcast.4) | data formatting | bytes 6291456 | tf_op jit(solution)/shard_map/all_to_all | solution.py:71
  262.2 3.7 %fusion.25 = (f32[64,512]{1,0:T(8,128)S(1)}, f32[22,64,512]{2,0,1:T(8,128)S(1)}) fusion(f32[24,64,512]{2,1,0:T(8,128)S(1)} %bitcast.24, s32[24]{0:T(128)S(1)} %add.83), kind=kOutput, calls=%fused_computation.35 | convolution fusion | flops 208306704 | bytes 6160480 | tf_op jit(solution)/shard_map/cj,jkp->ckp/dot_general | solution.py:75
  265.9 0.6 add_convert_fusion
  266.5 1.6 copy.13
  (3 shorter events, 0.1 us)
Async XLA Ops:
  7.2 26.5 %all-gather.3.cloned.1.call-start = ((), (), s32[]{:S(2)}) async-start(), calls=%async_computation.2 | async-start | bytes 2621440 | tf_op jit(solution)/shard_map/all_gather | solution.py:33
  7.9 67.5 %copy-start.1 = (bf16[256,512]{1,0:T(8,128)(2,1)S(1)}, bf16[256,512]{1,0:T(8,128)(2,1)}, u32[]{:S(2)}) copy-start(bf16[256,512]{1,0:T(8,128)(2,1)} %param.9) | copy-start | bytes 786436
  7.9 67.5 %all-reduce.2.cloned.1.call-start = ((), (), s32[]{:S(2)}) async-start(), calls=%async_computation.3 | async-start | bytes 1048576 | tf_op jit(solution)/shard_map/psum | solution.py:41
  38.6 88.3 %reduce-scatter.2.cloned.1.call-start = ((), (), s32[]{:S(2)}) async-start(), calls=%async_computation.4 | async-start | bytes 5242880 | tf_op jit(solution)/shard_map/reduce_scatter | solution.py:43
  81.0 0.7 copy-start.3
  81.0 0.7 copy-start.4
  81.0 0.7 copy-start.5
  81.0 46.0 %copy-start = (bf16[64,4096]{1,0:T(8,128)(2,1)S(1)}, bf16[64,4096]{1,0:T(8,128)(2,1)}, u32[]{:S(2)}) copy-start(bf16[64,4096]{1,0:T(8,128)(2,1)} %param.8) | copy-start | bytes 1572868
  81.0 71.7 %all-gather.5.cloned.1.call-start = ((), (), s32[]{:S(2)}) async-start(), calls=%async_computation.5 | async-start | bytes 2621440 | tf_op jit(solution)/shard_map/all_gather | solution.py:63
  129.5 6.5 %copy-start.2 = (s32[32]{0:T(128)S(1)}, s32[32]{0:T(128)}, u32[]{:S(2)}) copy-start(s32[32]{0:T(128)} %param.13) | copy-start | bytes 388
  163.1 95.1 %all-to-all-start = ((f32[6,256,512]{2,0,1:T(8,128)}), f32[6,256,512]{2,0,1:T(8,128)}, u32[]{:S(2)}, u32[]{:S(2)}) async-start(f32[6,256,512]{2,0,1:T(8,128)} %fusion), calls=%async_computation.1 | async-start | bytes 8388608 | tf_op jit(solution)/shard_map/all_to_all | solution.py:71
Sparse Core Ops, SparseCore 0:
  9.6 24.0 all-gather.2
  38.7 36.6 all-reduce.1
  81.1 45.7 reduce-scatter.1
  129.7 23.0 all-gather.4
where the time goes:
time: 280 us; the launch traced here: 275 us
  waiting for transfers between devices  215 us (77%)
  matrix products  24.5 us (9%)
  between operations  13.8 us (5%)
  local copies, waits for them, and re-layouts  13 us (5%)
  starting transfers between devices  5.23 us (2%)
  other arithmetic  3.29 us (1%)
    all_to_all x1, waiting for transfers between devices, per_device(): lax.all_to_all(local_sums, 'mk', split_axis=1, concat_axis=0, tiled=True)  89.6 us
    reduce_scatter x1, waiting for transfers between devices, per_device(): lax.psum_scatter(jnp.dot(residual, genotypes, preferred_element_type=jnp....  45.3 us
    psum x1, waiting for transfers between devices, per_device(): prediction = lax.psum(partial_pred, 'mk')  36.7 us
    all_gather x1, waiting for transfers between devices, per_device(): lax.all_gather(estimate, ('pp', 'sub'), axis=0, tiled=True)  25.7 us
    all_gather x1, waiting for transfers between devices, per_device(): shard_rows = lax.all_gather(updated, ('pp', 'sub'), axis=0, tiled=True)  16.6 us
    reshape x1, local copies, waits for them, and re-layouts, per_device(): geno_tiles = genotypes.reshape(people_dev, tile_dev, TILE)  6.48 us
    dot_general x1, matrix products, per_device(): jnp.einsum('st,tkp->skp', member, tile_terms, precision=lax.Precision.HIG...  6.27 us
  transfers between devices with their start and end apart: 5, of which 5 were waited for; matrix products, arithmetic and copies ran while one was open for 3% of the time, Pallas kernels for 0%

commit v1 on v0

--- a/solution.py
+++ b/solution.py
@@ -1,13 +1,17 @@
+import functools
 import math
 
 import jax
 import jax.numpy as jnp
 from jax import lax
+from jax.experimental import pallas as pl
+from jax.experimental.pallas import tpu as pltpu
 from jax.sharding import PartitionSpec as P
 
 CHROMS = 22
 TILE = 512
 SPAN = 6
+PIECES = 4
 
 
 def denoise(estimate, scores, prior_logit, slab_var, noise_var, marker_root, people_root):
@@ -24,7 +28,7 @@
     return (posterior * (1.0 / marker_root)).astype(jnp.bfloat16)
 
 
-def per_device(genotypes, estimate, phenotypes, prior_logit, slab_var, noise_var, tile_chrom):
+def whole_mesh_steps(genotypes, estimate, phenotypes, prior_logit, slab_var, noise_var, tile_chrom):
     people_dev, mark_dev = genotypes.shape
     mk_count = lax.axis_size("mk")
     people_count = lax.axis_size(("pp", "sub"))
@@ -78,6 +82,186 @@
     return (updated, loco_out)
 
 
+VMEM = pltpu.MemorySpace.VMEM
+NT = (((1,), (1,)), ((), ()))
+
+
+def local_call(body, outs, args, scalars=(), scratch=(), flops=0):
+    in_bytes = sum(a.size * a.dtype.itemsize for a in args)
+    out_bytes = sum(math.prod(s) * jnp.dtype(d).itemsize for s, d in outs)
+    return pl.pallas_call(
+        body,
+        out_shape=[pltpu.VMEM(s, d) for s, d in outs],
+        in_specs=[pl.BlockSpec(memory_space=pltpu.SMEM)] * len(scalars)
+        + [pl.BlockSpec(memory_space=VMEM)] * len(args),
+        out_specs=[pl.BlockSpec(memory_space=VMEM)] * len(outs),
+        scratch_shapes=list(scratch),
+        cost_estimate=pl.CostEstimate(flops=flops, bytes_accessed=in_bytes + out_bytes, transcendentals=0),
+        compiler_params=pltpu.CompilerParams(vmem_limit_bytes=8 * 2**20),
+    )(*scalars, *[pltpu.with_memory_space_constraint(a, VMEM) for a in args])
+
+
+def predict_body(where, own, across, beside, geno, keep, send):
+    odd = where[0]
+    half = 2 * own.shape[0]
+    rows = jnp.concatenate([own[...], across[...], beside[...]], axis=0)
+    product = lax.dot_general(rows, geno[...], NT, preferred_element_type=jnp.float32)
+
+    @pl.when(odd == 0)
+    def _():
+        keep[...] = product[:half]
+        send[...] = product[half:].astype(send.dtype)
+
+    @pl.when(odd == 1)
+    def _():
+        keep[...] = product[half:]
+        send[...] = product[:half].astype(send.dtype)
+
+
+def score_body(where, mine, other, geno, keep, send):
+    even = where[0] == 0
+    half = mine.shape[0]
+    first = jnp.where(even, mine[...], other[...])
+    second = jnp.where(even, other[...], mine[...])
+    rows = jnp.concatenate([first, second], axis=0)
+    width = 512
+    for at in range(0, geno.shape[1], width):
+        product = jnp.dot(rows, geno[:, at : at + width], preferred_element_type=jnp.float32)
+        keep[:, at : at + width] = product[:half]
+        send[:, at : at + width] = product[half:].astype(send.dtype)
+
+
+def chrom_body(where, labels, own, beside, geno, *outs_and_acc):
+    *outs, acc = outs_and_acc
+    height = own.shape[0] // 2
+    tiles = labels.shape[0]
+    for out in outs:
+        out[...] = jnp.zeros_like(out)
+    for tile in range(tiles):
+        columns = slice(tile * TILE, (tile + 1) * TILE)
+        rows = jnp.concatenate([own[:, columns], beside[:, columns]], axis=0)
+        product = lax.dot_general(rows, geno[:, columns], NT, preferred_element_type=jnp.float32)
+        if tile == 0:
+            acc[...] = product
+        else:
+            same = (labels[tile] == labels[tile - 1]).astype(jnp.float32)
+            acc[...] = acc[...] * same + product
+        slot = labels[tile] - labels[0]
+        for to, out in enumerate(outs):
+            start = pl.multiple_of(where[1 + to] * height, height)
+            out[slot] = acc[pl.ds(start, height), :].astype(out.dtype)
+
+
+def loco_body(firsts, phen, *refs):
+    *sums, out, base, acc = refs
+    total = jnp.zeros(base.shape, jnp.float32)
+    for part in sums:
+        for slot in range(SPAN):
+            total = total + part[slot].astype(jnp.float32)
+    base[...] = phen[...].astype(jnp.float32) - total
+
+    def step(chrom, carry):
+        acc[...] = base[...]
+        for at, part in enumerate(sums):
+            slot = chrom - firsts[at]
+
+            @pl.when((slot >= 0) & (slot < SPAN))
+            def _():
+                acc[...] += part[slot].astype(jnp.float32)
+
+        out[chrom] = acc[...].astype(out.dtype)
+        return carry
+
+    lax.fori_loop(0, CHROMS, step, 0)
+
+
+def piece_steps(genotypes, estimate, phenotypes, prior_logit, slab_var, noise_var, tile_chrom):
+    people_dev, mark_dev = genotypes.shape
+    shard = estimate.shape[0]
+    mk_count = lax.axis_size("mk")
+    people_count = lax.axis_size(("pp", "sub"))
+    marker_root = math.sqrt(mark_dev * mk_count)
+    people_root = math.sqrt(people_dev * people_count)
+    tile_dev = mark_dev // TILE
+    me = lax.axis_index("pp") * 2 + lax.axis_index("sub")
+    depth = lax.axis_index("mk")
+    odd = depth % 2
+    swap = [(0, 1), (1, 0)]
+
+    def along(step):
+        return [(i, i ^ step) for i in range(mk_count)]
+
+    def block_for(step):
+        bits = me ^ depth ^ step
+        return (bits % 2) * 2 + bits // 2
+
+    where = jnp.stack([odd] + [block_for(step) for step in range(mk_count)]).astype(jnp.int32)
+    labels = lax.dynamic_slice_in_dim(tile_chrom, depth * tile_dev, tile_dev, 0)
+    all_firsts = tile_chrom.reshape(mk_count, tile_dev)[:, 0]
+    firsts = jnp.stack([all_firsts[depth ^ step] for step in range(mk_count)])
+    phen_one = lax.dynamic_slice_in_dim(phenotypes, (me ^ odd) * shard, shard, 0)
+    phen_two = lax.dynamic_slice_in_dim(phenotypes, (me ^ odd ^ 2) * shard, shard, 0)
+    phen_share = lax.dynamic_slice_in_dim(phenotypes, depth * shard, shard, 0)
+    params = jnp.stack([prior_logit, slab_var, noise_var])
+    params_across = lax.ppermute(params, "pp", swap)
+
+    (geno,) = local_call(
+        lambda source, target: target.__setitem__(..., source[...]),
+        [(genotypes.shape, genotypes.dtype)],
+        [genotypes],
+    )
+    height = shard // PIECES
+    traits = 4 * height
+    updates, locos = [], []
+    for piece in range(PIECES):
+        rows = slice(piece * height, (piece + 1) * height)
+        own = estimate[rows]
+        across = lax.ppermute(own, "pp", swap)
+        pair = jnp.concatenate([own, across], axis=0)
+        beside = lax.ppermute(pair, "sub", swap)
+        matmul = 2 * traits * people_dev * mark_dev
+        half = (2 * height, people_dev)
+        keep, send = local_call(
+            predict_body, [(half, jnp.float32), (half, jnp.bfloat16)], [own, across, beside, geno], [where], flops=matmul
+        )
+        two = (keep + lax.ppermute(send, "mk", along(1)).astype(jnp.float32)).astype(jnp.bfloat16)
+        four = two.astype(jnp.float32) + lax.ppermute(two, "mk", along(2)).astype(jnp.float32)
+        phen = jnp.concatenate([phen_one[rows], phen_two[rows]], axis=0).astype(jnp.float32)
+        residual = (phen - four).astype(jnp.bfloat16)
+        residual_other = lax.ppermute(residual, "mk", along(1))
+        wide = (2 * height, mark_dev)
+        keep, send = local_call(
+            score_body, [(wide, jnp.float32), (wide, jnp.bfloat16)], [residual, residual_other, geno], [where], flops=matmul
+        )
+        chip = keep + lax.ppermute(send, "sub", swap).astype(jnp.float32)
+        chip_across = jnp.concatenate([chip[height:], chip[:height]], axis=0).astype(jnp.bfloat16)
+        scores = chip + lax.ppermute(chip_across, "pp", swap).astype(jnp.float32)
+        pair_params = jnp.concatenate([params[:, rows], params_across[:, rows]], axis=1)
+        updated = denoise(pair, scores, *pair_params, marker_root, people_root)
+        updates.append(updated[:height])
+        updated_beside = lax.ppermute(updated, "sub", swap)
+        block = ((SPAN, height, people_dev), jnp.bfloat16)
+        sums = local_call(
+            chrom_body,
+            [block] * mk_count,
+            [updated, updated_beside, geno],
+            [where, labels],
+            scratch=[pltpu.VMEM((traits, people_dev), jnp.float32)],
+            flops=matmul,
+        )
+        got = [sums[0]] + [lax.ppermute(sums[step], "mk", along(step)) for step in range(1, mk_count)]
+        (loco,) = local_call(
+            loco_body,
+            [((CHROMS, height, people_dev), jnp.bfloat16)],
+            [phen_share[rows], *got],
+            [firsts],
+            scratch=[pltpu.VMEM((height, people_dev), jnp.float32)] * 2,
+            flops=10 * CHROMS * height * people_dev,
+        )
+        locos.append(loco)
+    return (jnp.concatenate(updates, axis=0), jnp.concatenate(locos, axis=1))
+
+
 def solution(mesh):
     placed = (
         P(("grp", "pp", "sub"), "mk"),
@@ -88,8 +272,9 @@
         P(("grp", "pp", "sub")),
         P("grp"),
     )
+    by_pieces = (mesh.shape["pp"], mesh.shape["sub"], mesh.shape["mk"]) == (2, 2, 4)
     return jax.shard_map(
-        per_device,
+        piece_steps if by_pieces else whole_mesh_steps,
         mesh=mesh,
         in_specs=placed,
         out_specs=(P(("grp", "pp", "sub"), "mk"), P("grp", "mk", ("pp", "sub"))),

time: 280 us -> 122 us (0.44); the launches traced: 275 us -> 120 us
  waiting for transfers between devices: 215 us -> 24.4 us
  starting transfers between devices: 5.23 us -> 45.5 us
  Pallas kernels: 0 us -> 27.8 us
  matrix products: 24.5 us -> 0 us
  between operations: 13.8 us -> 1.08 us
  other arithmetic: 3.29 us -> 7.44 us
    all_to_all x1 -> x0, waiting for transfers between devices: 89.6 us -> none  [per_device(): lax.all_to_all(local_sums, 'mk', split_axis=1, concat_axis=0, tiled=True)]
    ppermute x0 -> x45, starting transfers between devices: none -> 45.5 us  [the longest x12 13.6 us: piece_steps(): lax.ppermute(sums[step], 'mk', along(step))]
    reduce_scatter x1 -> x0, waiting for transfers between devices: 45.3 us -> none  [per_device(): lax.psum_scatter(jnp.dot(residual, genotypes, preferred_element_type=jnp....]
    all_gather x2 -> x0, waiting for transfers between devices: 42.3 us -> none  [the longest x1 25.7 us: per_device(): lax.all_gather(estimate, ('pp', 'sub'), axis=0, tiled=True)]
    psum x1 -> x0, waiting for transfers between devices: 36.7 us -> none  [per_device(): prediction = lax.psum(partial_pred, 'mk')]
    pallas_call x0 -> x17, Pallas kernels: none -> 27.8 us  [local_call(): pl.pallas_call(body, out_shape=[pltpu.VMEM(s, d) for s, d in outs], in_sp...]
    dot_general x5 -> x0, matrix products: 24.5 us -> none  [the longest x1 6.27 us: per_device(): jnp.einsum('st,tkp->skp', member, tile_terms, precision=lax.Precision.HIG...]
    ppermute x0 -> x45, waiting for transfers between devices: none -> 24.4 us  [the longest x4 14.9 us: piece_steps(): scores = chip + lax.ppermute(chip_across, 'pp', swap).astype(jnp.float32)]
  transfers between devices with their start and end apart: 5 -> 45, of which waited for: 5 -> 9; matrix products, arithmetic and copies ran while one was open for 3% -> 7% of each run, Pallas kernels for 0% -> 22%
where the time goes in v1:
time: 122 us; the launch traced here: 120 us
  starting transfers between devices  45.5 us (37%)
  Pallas kernels  27.8 us (23%)
  waiting for transfers between devices  24.4 us (20%)
  local copies, waits for them, and re-layouts  13.9 us (11%)
  other arithmetic  7.44 us (6%)
    pallas_call x17, Pallas kernels, local_call(): pl.pallas_call(body, out_shape=[pltpu.VMEM(s, d) for s, d in outs], in_sp...  27.8 us
    ppermute x4, waiting for transfers between devices, piece_steps(): scores = chip + lax.ppermute(chip_across, 'pp', swap).astype(jnp.float32)  14.9 us
    ppermute x12, starting transfers between devices, piece_steps(): lax.ppermute(sums[step], 'mk', along(step))  13.6 us
    unnamed x16, local copies, waits for them, and re-layouts  10.7 us
    ppermute x12, waiting for transfers between devices, piece_steps(): lax.ppermute(sums[step], 'mk', along(step))  8.12 us
    ppermute x4, starting transfers between devices, piece_steps(): updated_beside = lax.ppermute(updated, 'sub', swap)  6.16 us
    ppermute x4, starting transfers between devices, piece_steps(): lax.ppermute(two, 'mk', along(2)).astype(jnp.float32)  4.99 us
    ppermute x4, starting transfers between devices, piece_steps(): chip = keep + lax.ppermute(send, 'sub', swap).astype(jnp.float32)  4.18 us
  transfers between devices with their start and end apart: 45, of which 9 were waited for; matrix products, arithmetic and copies ran while one was open for 7% of the time, Pallas kernels for 22%

profile of v1, /device:TPU:13, one launch (start us, length us, event | category | flops | bytes accessed | tf_op | source)
XLA Modules:
  0.0 120.0 jit_solution(6831389927183471896)
XLA Ops:
  0.6 1.1 fusion.44
  1.8 1.3 %collective-permute-start.22 = (bf16[16,4096]{1,0:T(8,128)(2,1)S(1)}, bf16[16,4096]{1,0:T(8,128)(2,1)S(1)}, u32[]{:S(2)}, u32[]{:S(2)}) collective-permute-start(bf16[16,4096]{1,0:T(8,128)(2,1)S(1)} %get-tuple-element.68.own), channel_id=1, source_target_pairs={{0,2},{2,0},{1,3},{3,1},{4,6},{6,4},{5,7},{7,5},{8,10},{10,8},{9,1... | collective-permute-start | bytes 393224 | tf_op jit(solution)/shard_map/ppermute | solution.py:219
  3.0 0.7 pad_maximum_fusion.10
  4.0 1.2 %collective-permute-start.15 = (bf16[16,4096]{1,0:T(8,128)(2,1)S(1)}, bf16[16,4096]{1,0:T(8,128)(2,1)S(1)}, u32[]{:S(2)}, u32[]{:S(2)}) collective-permute-start(bf16[16,4096]{1,0:T(8,128)(2,1)S(1)} %get-tuple-element.69.own), channel_id=1, source_target_pairs={{0,2},{2,0},{1,3},{3,1},{4,6},{6,4},{5,7},{7,5},{8,10},{10,8},{9,1... | collective-permute-start | bytes 393224 | tf_op jit(solution)/shard_map/ppermute | solution.py:219
  5.5 1.2 %collective-permute-start.1 = (bf16[16,4096]{1,0:T(8,128)(2,1)S(1)}, bf16[16,4096]{1,0:T(8,128)(2,1)S(1)}, u32[]{:S(2)}, u32[]{:S(2)}) collective-permute-start(bf16[16,4096]{1,0:T(8,128)(2,1)S(1)} %get-tuple-element.66.own), channel_id=1, source_target_pairs={{0,2},{2,0},{1,3},{3,1},{4,6},{6,4},{5,7},{7,5},{8,10},{10,8},{9,1... | collective-permute-start | bytes 393224 | tf_op jit(solution)/shard_map/ppermute | solution.py:219
  6.8 0.9 constant_dynamic-slice_fusion.2
  7.7 2.2 %copy-done.6 = bf16[512,4096]{1,0:T(8,128)(2,1)S(1)} copy-done((bf16[512,4096]{1,0:T(8,128)(2,1)S(1)}, bf16[512,4096]{1,0:T(8,128)(2,1)}, u32[]{:S(2)}) %copy-start.6) | copy-done | bytes 4194328
  10.2 2.0 %copy-done = bf16[512,4096]{1,0:T(8,128)(2,1)} copy-done((bf16[512,4096]{1,0:T(8,128)(2,1)}, bf16[512,4096]{1,0:T(8,128)(2,1)S(1)}, u32[]{:S(2)}) %copy-start) | copy-done | bytes 4194328
  12.6 2.1 %collective-permute-start.23 = (bf16[32,4096]{1,0:T(8,128)(2,1)S(1)}, bf16[32,4096]{1,0:T(8,128)(2,1)S(1)}, u32[]{:S(2)}, u32[]{:S(2)}) collective-permute-start(bf16[32,4096]{1,0:T(8,128)(2,1)S(1)} %pad_maximum_fusion.8), channel_id=1, source_target_pairs={{0,1},{1,0},{2,3},{3,2},{4,5},{5,4},{6,7},{7,6},{8,9},{9,8},{10,11... | collective-permute-start | bytes 786440 | tf_op jit(solution)/shard_map/ppermute | solution.py:221
  14.8 0.5 collective-permute-start.9
  15.4 0.9 collective-permute-start.2
  16.3 2.2 %copy-done.1 = bf16[512,4096]{1,0:T(8,128)(2,1)S(1)} copy-done((bf16[512,4096]{1,0:T(8,128)(2,1)S(1)}, bf16[512,4096]{1,0:T(8,128)(2,1)}, u32[]{:S(2)}) %copy-start.1) | copy-done | bytes 4194328
  18.5 1.9 %shard_map.93 = (f32[32,512]{1,0:T(8,128)S(1)}, bf16[32,512]{1,0:T(8,128)(2,1)S(1)}) custom-call(s32[5]{0:T(128)S(1)} %stack.42.where, bf16[16,4096]{1,0:T(8,128)(2,1)S(1)} %get-tuple-element.68.own, bf16[16,4096]{1,0:T(8,128)(2,1)S(1)} %collective-permute-done.22.across, bf16[32,4096]{1,0:T(8,128)(2,1)S(1)} %collective-permute-done.23.beside, ...), custom_call_target="tpu_custom_call" | custom-call | flops 268435456 | bytes 4816896 | tf_op jit(solution)/shard_map/pallas_call | solution.py:92
  20.7 1.9 %shard_map.91 = (f32[32,512]{1,0:T(8,128)S(1)}, bf16[32,512]{1,0:T(8,128)(2,1)S(1)}) custom-call(s32[5]{0:T(128)S(1)} %stack.42.where, bf16[16,4096]{1,0:T(8,128)(2,1)S(1)} %get-tuple-element.69.own, bf16[16,4096]{1,0:T(8,128)(2,1)S(1)} %collective-permute-done.15.across, bf16[32,4096]{1,0:T(8,128)(2,1)S(1)} %collective-permute-done.16.beside, ...), custom_call_target="tpu_custom_call" | custom-call | flops 268435456 | bytes 4816896 | tf_op jit(solution)/shard_map/pallas_call | solution.py:92
  22.6 1.4 %collective-permute-start.17 = (bf16[32,512]{1,0:T(8,128)(2,1)S(1)}, bf16[32,512]{1,0:T(8,128)(2,1)S(1)}, u32[]{:S(2)}, u32[]{:S(2)}) collective-permute-start(bf16[32,512]{1,0:T(8,128)(2,1)S(1)} %get-tuple-element.43), channel_id=1, source_target_pairs={{0,4},{4,0},{8,12},{12,8},{1,5},{5,1},{9,13},{13,9},{2,6},{6,2},{1... | collective-permute-start | bytes 98312 | tf_op jit(solution)/shard_map/ppermute | solution.py:227
  24.0 1.9 %shard_map.89 = (f32[32,512]{1,0:T(8,128)S(1)}, bf16[32,512]{1,0:T(8,128)(2,1)S(1)}) custom-call(s32[5]{0:T(128)S(1)} %stack.42.where, bf16[16,4096]{1,0:T(8,128)(2,1)S(1)} %get-tuple-element.67.own, bf16[16,4096]{1,0:T(8,128)(2,1)S(1)} %collective-permute-done.8.across, bf16[32,4096]{1,0:T(8,128)(2,1)S(1)} %collective-permute-done.9.beside, ...), custom_call_target="tpu_custom_call" | custom-call | flops 268435456 | bytes 4816896 | tf_op jit(solution)/shard_map/pallas_call | solution.py:92
  26.1 2.1 %shard_map.87 = (f32[32,512]{1,0:T(8,128)S(1)}, bf16[32,512]{1,0:T(8,128)(2,1)S(1)}) custom-call(s32[5]{0:T(128)S(1)} %stack.42.where, bf16[16,4096]{1,0:T(8,128)(2,1)S(1)} %get-tuple-element.66.own, bf16[16,4096]{1,0:T(8,128)(2,1)S(1)} %collective-permute-done.1.across, bf16[32,4096]{1,0:T(8,128)(2,1)S(1)} %collective-permute-done.2.beside, ...), custom_call_target="tpu_custom_call" | custom-call | flops 268435456 | bytes 4816896 | tf_op jit(solution)/shard_map/pallas_call | solution.py:92
  28.3 1.4 %collective-permute-start.3 = (bf16[32,512]{1,0:T(8,128)(2,1)S(1)}, bf16[32,512]{1,0:T(8,128)(2,1)S(1)}, u32[]{:S(2)}, u32[]{:S(2)}) collective-permute-start(bf16[32,512]{1,0:T(8,128)(2,1)S(1)} %get-tuple-element.35), channel_id=1, source_target_pairs={{0,4},{4,0},{8,12},{12,8},{1,5},{5,1},{9,13},{13,9},{2,6},{6,2},{1... | collective-permute-start | bytes 98312 | tf_op jit(solution)/shard_map/ppermute | solution.py:227
  29.6 2.4 %collective-permute-start.25 = (bf16[32,512]{1,0:T(8,128)(2,1)S(1)}, bf16[32,512]{1,0:T(8,128)(2,1)S(1)}, u32[]{:S(2)}, u32[]{:S(2)}) collective-permute-start(bf16[32,512]{1,0:T(8,128)(2,1)S(1)} %add_convert_fusion), channel_id=1, source_target_pairs={{0,8},{4,12},{8,0},{12,4},{1,9},{5,13},{9,1},{13,5},{2,10},{6,14},... | collective-permute-start | bytes 98312 | tf_op jit(solution)/shard_map/ppermute | solution.py:228
  32.2 2.4 %collective-permute-start.11 = (bf16[32,512]{1,0:T(8,128)(2,1)S(1)}, bf16[32,512]{1,0:T(8,128)(2,1)S(1)}, u32[]{:S(2)}, u32[]{:S(2)}) collective-permute-start(bf16[32,512]{1,0:T(8,128)(2,1)S(1)} %add_convert_fusion.2), channel_id=1, source_target_pairs={{0,8},{4,12},{8,0},{12,4},{1,9},{5,13},{9,1},{13,5},{2,10},{6,14},... | collective-permute-start | bytes 98312 | tf_op jit(solution)/shard_map/ppermute | solution.py:228
  34.9 0.8 collective-permute-done.18
  35.8 0.6 collective-permute-start.19
  36.4 1.0 collective-permute-start.12
  37.4 0.4 collective-permute-done.26.other
  37.8 1.4 %shard_map.94 = (f32[32,4096]{1,0:T(8,128)S(1)}, bf16[32,4096]{1,0:T(8,128)(2,1)S(1)}) custom-call(s32[5]{0:T(128)S(1)} %stack.42.where, bf16[32,512]{1,0:T(8,128)(2,1)S(1)} %subtract_convert_fusion.mine, bf16[32,512]{1,0:T(8,128)(2,1)S(1)} %collective-permute-done.26.other, bf16[512,4096]{1,0:T(8,128)(2,1)S(1)} %copy-done.2), custom_call_target="tpu_custom_call" | custom-call | flops 268435456 | bytes 5046272 | tf_op jit(solution)/shard_map/pallas_call | solution.py:92
  39.2 3.2 %collective-permute-start.27 = (bf16[32,4096]{1,0:T(8,128)(2,1)S(1)}, bf16[32,4096]{1,0:T(8,128)(2,1)S(1)}, u32[]{:S(2)}, u32[]{:S(2)}) collective-permute-start(bf16[32,4096]{1,0:T(8,128)(2,1)S(1)} %get-tuple-element.49), channel_id=1, source_target_pairs={{0,1},{1,0},{2,3},{3,2},{4,5},{5,4},{6,7},{7,6},{8,9},{9,8},{10,11... | collective-permute-start | bytes 786440 | tf_op jit(solution)/shard_map/ppermute | solution.py:236
  42.8 1.4 %shard_map.92 = (f32[32,4096]{1,0:T(8,128)S(1)}, bf16[32,4096]{1,0:T(8,128)(2,1)S(1)}) custom-call(s32[5]{0:T(128)S(1)} %stack.42.where, bf16[32,512]{1,0:T(8,128)(2,1)S(1)} %subtract_convert_fusion.1.mine, bf16[32,512]{1,0:T(8,128)(2,1)S(1)} %collective-permute-done.19.other, bf16[512,4096]{1,0:T(8,128)(2,1)S(1)} %copy-done.2), custom_call_target="tpu_custom_call" | custom-call | flops 268435456 | bytes 5046272 | tf_op jit(solution)/shard_map/pallas_call | solution.py:92
  44.5 1.4 %shard_map.90 = (f32[32,4096]{1,0:T(8,128)S(1)}, bf16[32,4096]{1,0:T(8,128)(2,1)S(1)}) custom-call(s32[5]{0:T(128)S(1)} %stack.42.where, bf16[32,512]{1,0:T(8,128)(2,1)S(1)} %subtract_convert_fusion.2.mine, bf16[32,512]{1,0:T(8,128)(2,1)S(1)} %collective-permute-done.12.other, bf16[512,4096]{1,0:T(8,128)(2,1)S(1)} %copy-done.2), custom_call_target="tpu_custom_call" | custom-call | flops 268435456 | bytes 5046272 | tf_op jit(solution)/shard_map/pallas_call | solution.py:92
  46.2 1.4 %shard_map.88 = (f32[32,4096]{1,0:T(8,128)S(1)}, bf16[32,4096]{1,0:T(8,128)(2,1)S(1)}) custom-call(s32[5]{0:T(128)S(1)} %stack.42.where, bf16[32,512]{1,0:T(8,128)(2,1)S(1)} %subtract_convert_fusion.3.mine, bf16[32,512]{1,0:T(8,128)(2,1)S(1)} %collective-permute-done.5.other, bf16[512,4096]{1,0:T(8,128)(2,1)S(1)} %copy-done.2), custom_call_target="tpu_custom_call" | custom-call | flops 268435456 | bytes 5046272 | tf_op jit(solution)/shard_map/pallas_call | solution.py:92
  48.1 1.3 %collective-permute-start.28 = (bf16[32,4096]{1,0:T(8,128)(2,1)S(1)}, bf16[32,4096]{1,0:T(8,128)(2,1)S(1)}, u32[]{:S(2)}, u32[]{:S(2)}) collective-permute-start(bf16[32,4096]{1,0:T(8,128)(2,1)S(1)} %pad_maximum_fusion.9), channel_id=1, source_target_pairs={{0,2},{2,0},{1,3},{3,1},{4,6},{6,4},{5,7},{7,5},{8,10},{10,8},{9,1... | collective-permute-start | bytes 786440 | tf_op jit(solution)/shard_map/ppermute | solution.py:238
  49.9 1.3 %collective-permute-start.14 = (bf16[32,4096]{1,0:T(8,128)(2,1)S(1)}, bf16[32,4096]{1,0:T(8,128)(2,1)S(1)}, u32[]{:S(2)}, u32[]{:S(2)}) collective-permute-start(bf16[32,4096]{1,0:T(8,128)(2,1)S(1)} %pad_maximum_fusion.5), channel_id=1, source_target_pairs={{0,2},{2,0},{1,3},{3,1},{4,6},{6,4},{5,7},{7,5},{8,10},{10,8},{9,1... | collective-permute-start | bytes 786440 | tf_op jit(solution)/shard_map/ppermute | solution.py:238
  51.6 4.2 %collective-permute-done.28 = bf16[32,4096]{1,0:T(8,128)(2,1)S(1)} collective-permute-done((bf16[32,4096]{1,0:T(8,128)(2,1)S(1)}, bf16[32,4096]{1,0:T(8,128)(2,1)S(1)}, u32[]{:S(2)}, u32[]{:S(2)}) %collective-permute-start.28) | collective-permute-done | bytes 262176 | tf_op jit(solution)/shard_map/ppermute | solution.py:238
  56.2 1.7 %collective-permute-start.41 = (bf16[32,4096]{1,0:T(8,128)(2,1)S(1)}, bf16[32,4096]{1,0:T(8,128)(2,1)S(1)}, u32[]{:S(2)}, u32[]{:S(2)}) collective-permute-start(bf16[32,4096]{1,0:T(8,128)(2,1)S(1)} %fusion.36.own), channel_id=1, source_target_pairs={{0,1},{1,0},{2,3},{3,2},{4,5},{5,4},{6,7},{7,6},{8,9},{9,8},{10,11... | collective-permute-start | bytes 786440 | tf_op jit(solution)/shard_map/ppermute | solution.py:242
  57.9 3.6 %collective-permute-done.21 = bf16[32,4096]{1,0:T(8,128)(2,1)S(1)} collective-permute-done((bf16[32,4096]{1,0:T(8,128)(2,1)S(1)}, bf16[32,4096]{1,0:T(8,128)(2,1)S(1)}, u32[]{:S(2)}, u32[]{:S(2)}) %collective-permute-start.21) | collective-permute-done | bytes 262176 | tf_op jit(solution)/shard_map/ppermute | solution.py:238
  61.8 1.7 %collective-permute-start.37 = (bf16[32,4096]{1,0:T(8,128)(2,1)S(1)}, bf16[32,4096]{1,0:T(8,128)(2,1)S(1)}, u32[]{:S(2)}, u32[]{:S(2)}) collective-permute-start(bf16[32,4096]{1,0:T(8,128)(2,1)S(1)} %fusion.37.own), channel_id=1, source_target_pairs={{0,1},{1,0},{2,3},{3,2},{4,5},{5,4},{6,7},{7,6},{8,9},{9,8},{10,11... | collective-permute-start | bytes 786440 | tf_op jit(solution)/shard_map/ppermute | solution.py:242
  63.5 3.6 %collective-permute-done.14 = bf16[32,4096]{1,0:T(8,128)(2,1)S(1)} collective-permute-done((bf16[32,4096]{1,0:T(8,128)(2,1)S(1)}, bf16[32,4096]{1,0:T(8,128)(2,1)S(1)}, u32[]{:S(2)}, u32[]{:S(2)}) %collective-permute-start.14) | collective-permute-done | bytes 262176 | tf_op jit(solution)/shard_map/ppermute | solution.py:238
  67.4 1.7 %collective-permute-start.33 = (bf16[32,4096]{1,0:T(8,128)(2,1)S(1)}, bf16[32,4096]{1,0:T(8,128)(2,1)S(1)}, u32[]{:S(2)}, u32[]{:S(2)}) collective-permute-start(bf16[32,4096]{1,0:T(8,128)(2,1)S(1)} %fusion.38.own), channel_id=1, source_target_pairs={{0,1},{1,0},{2,3},{3,2},{4,5},{5,4},{6,7},{7,6},{8,9},{9,8},{10,11... | collective-permute-start | bytes 786440 | tf_op jit(solution)/shard_map/ppermute | solution.py:242
  69.1 3.6 %collective-permute-done.7 = bf16[32,4096]{1,0:T(8,128)(2,1)S(1)} collective-permute-done((bf16[32,4096]{1,0:T(8,128)(2,1)S(1)}, bf16[32,4096]{1,0:T(8,128)(2,1)S(1)}, u32[]{:S(2)}, u32[]{:S(2)}) %collective-permute-start.7) | collective-permute-done | bytes 262176 | tf_op jit(solution)/shard_map/ppermute | solution.py:238
  73.0 1.1 collective-permute-start.29
  74.2 2.2 %copy-done.3 = bf16[512,4096]{1,0:T(8,128)(2,1)S(1)} copy-done((bf16[512,4096]{1,0:T(8,128)(2,1)S(1)}, bf16[512,4096]{1,0:T(8,128)(2,1)}, u32[]{:S(2)}) %copy-start.3) | copy-done | bytes 4194328
  76.4 1.9 %shard_map.101 = (bf16[6,16,512]{2,1,0:T(8,128)(2,1)S(1)}, bf16[6,16,512]{2,1,0:T(8,128)(2,1)S(1)}, bf16[6,16,512]{2,1,0:T(8,128)(2,1)S(1)}, bf16[6,16,512]{2,1,0:T(8,128)(2,1)S(1)}) custom-call(s32[5]{0:T(128)S(1)} %stack.42.where, s32[8]{0:T(128)S(1)} %dynamic_slice.43.labels, bf16[32,4096]{1,0:T(8,128)(2,1)S(1)} %fusion.36.own, ...), custom_call_target="tpu_custom_call" | custom-call | flops 268435456 | bytes 5111808 | tf_op jit(solution)/shard_map/pallas_call | solution.py:92
  78.3 1.2 %collective-permute-start.42 = (bf16[6,16,512]{2,1,0:T(8,128)(2,1)S(1)}, bf16[6,16,512]{2,1,0:T(8,128)(2,1)S(1)}, u32[]{:S(2)}, u32[]{:S(2)}) collective-permute-start(bf16[6,16,512]{2,1,0:T(8,128)(2,1)S(1)} %get-tuple-element.63), channel_id=1, source_target_pairs={{0,4},{4,0},{8,12},{12,8},{1,5},{5,1},{9,13},{13,9},{2,6},{6,2},{1... | collective-permute-start | bytes 294920 | tf_op jit(solution)/shard_map/ppermute | solution.py:252
  79.6 2.4 %collective-permute-start.43 = (bf16[6,16,512]{2,1,0:T(8,128)(2,1)S(1)}, bf16[6,16,512]{2,1,0:T(8,128)(2,1)S(1)}, u32[]{:S(2)}, u32[]{:S(2)}) collective-permute-start(bf16[6,16,512]{2,1,0:T(8,128)(2,1)S(1)} %get-tuple-element.64), channel_id=1, source_target_pairs={{0,8},{4,12},{8,0},{12,4},{1,9},{5,13},{9,1},{13,5},{2,10},{6,14},... | collective-permute-start | bytes 294920 | tf_op jit(solution)/shard_map/ppermute | solution.py:252
  82.1 0.6 constant_dynamic-slice_fusion.13
  82.7 2.2 %copy-done.4 = bf16[512,4096]{1,0:T(8,128)(2,1)S(1)} copy-done((bf16[512,4096]{1,0:T(8,128)(2,1)S(1)}, bf16[512,4096]{1,0:T(8,128)(2,1)}, u32[]{:S(2)}) %copy-start.4) | copy-done | bytes 4194328
  84.9 1.9 %shard_map.99 = (bf16[6,16,512]{2,1,0:T(8,128)(2,1)S(1)}, bf16[6,16,512]{2,1,0:T(8,128)(2,1)S(1)}, bf16[6,16,512]{2,1,0:T(8,128)(2,1)S(1)}, bf16[6,16,512]{2,1,0:T(8,128)(2,1)S(1)}) custom-call(s32[5]{0:T(128)S(1)} %stack.42.where, s32[8]{0:T(128)S(1)} %dynamic_slice.43.labels, bf16[32,4096]{1,0:T(8,128)(2,1)S(1)} %fusion.37.own, ...), custom_call_target="tpu_custom_call" | custom-call | flops 268435456 | bytes 5111808 | tf_op jit(solution)/shard_map/pallas_call | solution.py:92
  86.9 1.2 %collective-permute-start.38 = (bf16[6,16,512]{2,1,0:T(8,128)(2,1)S(1)}, bf16[6,16,512]{2,1,0:T(8,128)(2,1)S(1)}, u32[]{:S(2)}, u32[]{:S(2)}) collective-permute-start(bf16[6,16,512]{2,1,0:T(8,128)(2,1)S(1)} %get-tuple-element.59), channel_id=1, source_target_pairs={{0,4},{4,0},{8,12},{12,8},{1,5},{5,1},{9,13},{13,9},{2,6},{6,2},{1... | collective-permute-start | bytes 294920 | tf_op jit(solution)/shard_map/ppermute | solution.py:252
  88.1 1.9 %shard_map.97 = (bf16[6,16,512]{2,1,0:T(8,128)(2,1)S(1)}, bf16[6,16,512]{2,1,0:T(8,128)(2,1)S(1)}, bf16[6,16,512]{2,1,0:T(8,128)(2,1)S(1)}, bf16[6,16,512]{2,1,0:T(8,128)(2,1)S(1)}) custom-call(s32[5]{0:T(128)S(1)} %stack.42.where, s32[8]{0:T(128)S(1)} %dynamic_slice.43.labels, bf16[32,4096]{1,0:T(8,128)(2,1)S(1)} %fusion.38.own, ...), custom_call_target="tpu_custom_call" | custom-call | flops 268435456 | bytes 5111808 | tf_op jit(solution)/shard_map/pallas_call | solution.py:92
  90.1 1.5 %collective-permute-start.39 = (bf16[6,16,512]{2,1,0:T(8,128)(2,1)S(1)}, bf16[6,16,512]{2,1,0:T(8,128)(2,1)S(1)}, u32[]{:S(2)}, u32[]{:S(2)}) collective-permute-start(bf16[6,16,512]{2,1,0:T(8,128)(2,1)S(1)} %get-tuple-element.60), channel_id=1, source_target_pairs={{0,8},{4,12},{8,0},{12,4},{1,9},{5,13},{9,1},{13,5},{2,10},{6,14},... | collective-permute-start | bytes 294920 | tf_op jit(solution)/shard_map/ppermute | solution.py:252
  91.6 2.1 %collective-permute-start.34 = (bf16[6,16,512]{2,1,0:T(8,128)(2,1)S(1)}, bf16[6,16,512]{2,1,0:T(8,128)(2,1)S(1)}, u32[]{:S(2)}, u32[]{:S(2)}) collective-permute-start(bf16[6,16,512]{2,1,0:T(8,128)(2,1)S(1)} %get-tuple-element.55), channel_id=1, source_target_pairs={{0,4},{4,0},{8,12},{12,8},{1,5},{5,1},{9,13},{13,9},{2,6},{6,2},{1... | collective-permute-start | bytes 294920 | tf_op jit(solution)/shard_map/ppermute | solution.py:252
  93.7 2.6 %pad_add_fusion.firsts = s32[4]{0:T(128)S(1)} fusion(s32[1]{0:T(128)} %bitcast.23, s32[1]{0:T(128)} %bitcast.22, s32[1]{0:T(128)} %bitcast.21, s32[1]{0:T(128)} %bitcast.20), kind=kLoop, calls=%fused_computation.95 | loop fusion | flops 12 | bytes 32 | tf_op jit(solution)/shard_map/stack | solution.py:201
  96.4 1.9 %shard_map.95 = (bf16[6,16,512]{2,1,0:T(8,128)(2,1)S(1)}, bf16[6,16,512]{2,1,0:T(8,128)(2,1)S(1)}, bf16[6,16,512]{2,1,0:T(8,128)(2,1)S(1)}, bf16[6,16,512]{2,1,0:T(8,128)(2,1)S(1)}) custom-call(s32[5]{0:T(128)S(1)} %stack.42.where, s32[8]{0:T(128)S(1)} %dynamic_slice.43.labels, bf16[32,4096]{1,0:T(8,128)(2,1)S(1)} %fusion.39.own, ...), custom_call_target="tpu_custom_call" | custom-call | flops 268435456 | bytes 5111808 | tf_op jit(solution)/shard_map/pallas_call | solution.py:92
  98.3 1.2 collective-permute-start.35
  99.9 2.1 %collective-permute-start.30 = (bf16[6,16,512]{2,1,0:T(8,128)(2,1)S(1)}, bf16[6,16,512]{2,1,0:T(8,128)(2,1)S(1)}, u32[]{:S(2)}, u32[]{:S(2)}) collective-permute-start(bf16[6,16,512]{2,1,0:T(8,128)(2,1)S(1)} %get-tuple-element.51), channel_id=1, source_target_pairs={{0,4},{4,0},{8,12},{12,8},{1,5},{5,1},{9,13},{13,9},{2,6},{6,2},{1... | collective-permute-start | bytes 294920 | tf_op jit(solution)/shard_map/ppermute | solution.py:252
  101.9 1.2 collective-permute-start.31
  103.4 0.8 pad_maximum_fusion.1
  104.3 1.6 %shard_map.102 = bf16[22,16,512]{2,1,0:T(8,128)(2,1)S(1)} custom-call(s32[4]{0:T(128)S(1)} %pad_add_fusion.firsts, bf16[16,512]{1,0:T(8,128)(2,1)S(1)} %get-tuple-element.80.phen, bf16[6,16,512]{2,1,0:T(8,128)(2,1)S(1)} %get-tuple-element.62.refs_0_, bf16[6,16,512]{2,1,0:T(8,128)(2,1)S(1)} %collective-permute-done.42.refs_1_, ...), custom_call_target="tpu_custom_call" | custom-call | flops 1802240 | bytes 770048 | tf_op jit(solution)/shard_map/pallas_call | solution.py:92
  105.9 1.6 %shard_map.100 = bf16[22,16,512]{2,1,0:T(8,128)(2,1)S(1)} custom-call(s32[4]{0:T(128)S(1)} %pad_add_fusion.firsts, bf16[16,512]{1,0:T(8,128)(2,1)S(1)} %get-tuple-element.71.phen, bf16[6,16,512]{2,1,0:T(8,128)(2,1)S(1)} %get-tuple-element.58.refs_0_, bf16[6,16,512]{2,1,0:T(8,128)(2,1)S(1)} %collective-permute-done.38.refs_1_, ...), custom_call_target="tpu_custom_call" | custom-call | flops 1802240 | bytes 770048 | tf_op jit(solution)/shard_map/pallas_call | solution.py:92
  107.5 4.7 %collective-permute-done.36.refs_3_ = bf16[6,16,512]{2,1,0:T(8,128)(2,1)S(1)} collective-permute-done((bf16[6,16,512]{2,1,0:T(8,128)(2,1)S(1)}, bf16[6,16,512]{2,1,0:T(8,128)(2,1)S(1)}, u32[]{:S(2)}, u32[]{:S(2)}) %collective-permute-start.36) | collective-permute-done | bytes 98336 | tf_op jit(solution)/shard_map/ppermute | solution.py:252
  112.2 1.6 %shard_map.98 = bf16[22,16,512]{2,1,0:T(8,128)(2,1)S(1)} custom-call(s32[4]{0:T(128)S(1)} %pad_add_fusion.firsts, bf16[16,512]{1,0:T(8,128)(2,1)S(1)} %get-tuple-element.72.phen, bf16[6,16,512]{2,1,0:T(8,128)(2,1)S(1)} %get-tuple-element.54.refs_0_, bf16[6,16,512]{2,1,0:T(8,128)(2,1)S(1)} %collective-permute-done.34.refs_1_, ...), custom_call_target="tpu_custom_call" | custom-call | flops 1802240 | bytes 770048 | tf_op jit(solution)/shard_map/pallas_call | solution.py:92
  113.8 0.6 collective-permute-done.31.refs_2_
  114.4 2.7 %collective-permute-done.32.refs_3_ = bf16[6,16,512]{2,1,0:T(8,128)(2,1)S(1)} collective-permute-done((bf16[6,16,512]{2,1,0:T(8,128)(2,1)S(1)}, bf16[6,16,512]{2,1,0:T(8,128)(2,1)S(1)}, u32[]{:S(2)}, u32[]{:S(2)}) %collective-permute-start.32) | collective-permute-done | bytes 98336 | tf_op jit(solution)/shard_map/ppermute | solution.py:252
  117.2 1.6 %shard_map.96 = bf16[22,16,512]{2,1,0:T(8,128)(2,1)S(1)} custom-call(s32[4]{0:T(128)S(1)} %pad_add_fusion.firsts, bf16[16,512]{1,0:T(8,128)(2,1)S(1)} %get-tuple-element.70.phen, bf16[6,16,512]{2,1,0:T(8,128)(2,1)S(1)} %get-tuple-element.50.refs_0_, bf16[6,16,512]{2,1,0:T(8,128)(2,1)S(1)} %collective-permute-done.30.refs_1_, ...), custom_call_target="tpu_custom_call" | custom-call | flops 1802240 | bytes 770048 | tf_op jit(solution)/shard_map/pallas_call | solution.py:92
  118.8 1.2 pad_maximum_fusion
  (109 shorter events, 7.3 us)
Async XLA Ops:
  1.8 10.8 %collective-permute-start.22 = (bf16[16,4096]{1,0:T(8,128)(2,1)S(1)}, bf16[16,4096]{1,0:T(8,128)(2,1)S(1)}, u32[]{:S(2)}, u32[]{:S(2)}) collective-permute-start(bf16[16,4096]{1,0:T(8,128)(2,1)S(1)} %get-tuple-element.68.own), channel_id=1, source_target_pairs={{0,2},{2,0},{1,3},{3,1},{4,6},{6,4},{5,7},{7,5},{8,10},{10,8},{9,1... | collective-permute-start | bytes 393224 | tf_op jit(solution)/shard_map/ppermute | solution.py:219
  3.7 8.5 %collective-permute-start = (f32[3,64]{1,0:T(4,128)S(1)}, f32[3,64]{1,0:T(4,128)S(1)}, u32[]{:S(2)}, u32[]{:S(2)}) collective-permute-start(f32[3,64]{1,0:T(4,128)S(1)} %pad_maximum_fusion.10), channel_id=1, source_target_pairs={{0,2},{2,0},{1,3},{3,1},{4,6},{6,4},{5,7},{7,5},{8,10},{10,8},{9,1... | collective-permute-start | bytes 2312 | tf_op jit(solution)/shard_map/ppermute | solution.py:206
  4.0 10.7 %collective-permute-start.15 = (bf16[16,4096]{1,0:T(8,128)(2,1)S(1)}, bf16[16,4096]{1,0:T(8,128)(2,1)S(1)}, u32[]{:S(2)}, u32[]{:S(2)}) collective-permute-start(bf16[16,4096]{1,0:T(8,128)(2,1)S(1)} %get-tuple-element.69.own), channel_id=1, source_target_pairs={{0,2},{2,0},{1,3},{3,1},{4,6},{6,4},{5,7},{7,5},{8,10},{10,8},{9,1... | collective-permute-start | bytes 393224 | tf_op jit(solution)/shard_map/ppermute | solution.py:219
  5.3 9.6 %collective-permute-start.8 = (bf16[16,4096]{1,0:T(8,128)(2,1)S(1)}, bf16[16,4096]{1,0:T(8,128)(2,1)S(1)}, u32[]{:S(2)}, u32[]{:S(2)}) collective-permute-start(bf16[16,4096]{1,0:T(8,128)(2,1)S(1)} %get-tuple-element.67.own), channel_id=1, source_target_pairs={{0,2},{2,0},{1,3},{3,1},{4,6},{6,4},{5,7},{7,5},{8,10},{10,8},{9,1... | collective-permute-start | bytes 393224 | tf_op jit(solution)/shard_map/ppermute | solution.py:219
  5.5 9.9 %collective-permute-start.1 = (bf16[16,4096]{1,0:T(8,128)(2,1)S(1)}, bf16[16,4096]{1,0:T(8,128)(2,1)S(1)}, u32[]{:S(2)}, u32[]{:S(2)}) collective-permute-start(bf16[16,4096]{1,0:T(8,128)(2,1)S(1)} %get-tuple-element.66.own), channel_id=1, source_target_pairs={{0,2},{2,0},{1,3},{3,1},{4,6},{6,4},{5,7},{7,5},{8,10},{10,8},{9,1... | collective-permute-start | bytes 393224 | tf_op jit(solution)/shard_map/ppermute | solution.py:219
  7.7 2.2 %copy-start.6 = (bf16[512,4096]{1,0:T(8,128)(2,1)S(1)}, bf16[512,4096]{1,0:T(8,128)(2,1)}, u32[]{:S(2)}) copy-start(bf16[512,4096]{1,0:T(8,128)(2,1)} %source.1) | copy-start | bytes 12582916
  10.2 2.0 %copy-start = (bf16[512,4096]{1,0:T(8,128)(2,1)}, bf16[512,4096]{1,0:T(8,128)(2,1)S(1)}, u32[]{:S(2)}) copy-start(bf16[512,4096]{1,0:T(8,128)(2,1)S(1)} %shard_map.86.geno) | copy-start | bytes 12582916
  12.6 3.8 %collective-permute-start.23 = (bf16[32,4096]{1,0:T(8,128)(2,1)S(1)}, bf16[32,4096]{1,0:T(8,128)(2,1)S(1)}, u32[]{:S(2)}, u32[]{:S(2)}) collective-permute-start(bf16[32,4096]{1,0:T(8,128)(2,1)S(1)} %pad_maximum_fusion.8), channel_id=1, source_target_pairs={{0,1},{1,0},{2,3},{3,2},{4,5},{5,4},{6,7},{7,6},{8,9},{9,8},{10,11... | collective-permute-start | bytes 786440 | tf_op jit(solution)/shard_map/ppermute | solution.py:221
  14.7 6.0 %collective-permute-start.16 = (bf16[32,4096]{1,0:T(8,128)(2,1)S(1)}, bf16[32,4096]{1,0:T(8,128)(2,1)S(1)}, u32[]{:S(2)}, u32[]{:S(2)}) collective-permute-start(bf16[32,4096]{1,0:T(8,128)(2,1)S(1)} %pad_maximum_fusion.6), channel_id=1, source_target_pairs={{0,1},{1,0},{2,3},{3,2},{4,5},{5,4},{6,7},{7,6},{8,9},{9,8},{10,11... | collective-permute-start | bytes 786440 | tf_op jit(solution)/shard_map/ppermute | solution.py:221
  14.8 9.1 %collective-permute-start.9 = (bf16[32,4096]{1,0:T(8,128)(2,1)S(1)}, bf16[32,4096]{1,0:T(8,128)(2,1)S(1)}, u32[]{:S(2)}, u32[]{:S(2)}) collective-permute-start(bf16[32,4096]{1,0:T(8,128)(2,1)S(1)} %pad_maximum_fusion.4), channel_id=1, source_target_pairs={{0,1},{1,0},{2,3},{3,2},{4,5},{5,4},{6,7},{7,6},{8,9},{9,8},{10,11... | collective-permute-start | bytes 786440 | tf_op jit(solution)/shard_map/ppermute | solution.py:221
  15.4 10.7 %collective-permute-start.2 = (bf16[32,4096]{1,0:T(8,128)(2,1)S(1)}, bf16[32,4096]{1,0:T(8,128)(2,1)S(1)}, u32[]{:S(2)}, u32[]{:S(2)}) collective-permute-start(bf16[32,4096]{1,0:T(8,128)(2,1)S(1)} %pad_maximum_fusion.2), channel_id=1, source_target_pairs={{0,1},{1,0},{2,3},{3,2},{4,5},{5,4},{6,7},{7,6},{8,9},{9,8},{10,11... | collective-permute-start | bytes 786440 | tf_op jit(solution)/shard_map/ppermute | solution.py:221
  16.3 2.2 %copy-start.1 = (bf16[512,4096]{1,0:T(8,128)(2,1)S(1)}, bf16[512,4096]{1,0:T(8,128)(2,1)}, u32[]{:S(2)}) copy-start(bf16[512,4096]{1,0:T(8,128)(2,1)} %copy-done) | copy-start | bytes 12582916
  20.4 9.2 %collective-permute-start.24 = (bf16[32,512]{1,0:T(8,128)(2,1)S(1)}, bf16[32,512]{1,0:T(8,128)(2,1)S(1)}, u32[]{:S(2)}, u32[]{:S(2)}) collective-permute-start(bf16[32,512]{1,0:T(8,128)(2,1)S(1)} %get-tuple-element.47), channel_id=1, source_target_pairs={{0,4},{4,0},{8,12},{12,8},{1,5},{5,1},{9,13},{13,9},{2,6},{6,2},{1... | collective-permute-start | bytes 98312 | tf_op jit(solution)/shard_map/ppermute | solution.py:227
  22.6 9.4 %collective-permute-start.17 = (bf16[32,512]{1,0:T(8,128)(2,1)S(1)}, bf16[32,512]{1,0:T(8,128)(2,1)S(1)}, u32[]{:S(2)}, u32[]{:S(2)}) collective-permute-start(bf16[32,512]{1,0:T(8,128)(2,1)S(1)} %get-tuple-element.43), channel_id=1, source_target_pairs={{0,4},{4,0},{8,12},{12,8},{1,5},{5,1},{9,13},{13,9},{2,6},{6,2},{1... | collective-permute-start | bytes 98312 | tf_op jit(solution)/shard_map/ppermute | solution.py:227
  25.9 11.9 %copy-start.2 = (bf16[512,4096]{1,0:T(8,128)(2,1)S(1)}, bf16[512,4096]{1,0:T(8,128)(2,1)}, u32[]{:S(2)}) copy-start(bf16[512,4096]{1,0:T(8,128)(2,1)} %copy-done) | copy-start | bytes 12582916
  25.9 6.2 %collective-permute-start.10 = (bf16[32,512]{1,0:T(8,128)(2,1)S(1)}, bf16[32,512]{1,0:T(8,128)(2,1)S(1)}, u32[]{:S(2)}, u32[]{:S(2)}) collective-permute-start(bf16[32,512]{1,0:T(8,128)(2,1)S(1)} %get-tuple-element.39), channel_id=1, source_target_pairs={{0,4},{4,0},{8,12},{12,8},{1,5},{5,1},{9,13},{13,9},{2,6},{6,2},{1... | collective-permute-start | bytes 98312 | tf_op jit(solution)/shard_map/ppermute | solution.py:227
  28.3 6.3 %collective-permute-start.3 = (bf16[32,512]{1,0:T(8,128)(2,1)S(1)}, bf16[32,512]{1,0:T(8,128)(2,1)S(1)}, u32[]{:S(2)}, u32[]{:S(2)}) collective-permute-start(bf16[32,512]{1,0:T(8,128)(2,1)S(1)} %get-tuple-element.35), channel_id=1, source_target_pairs={{0,4},{4,0},{8,12},{12,8},{1,5},{5,1},{9,13},{13,9},{2,6},{6,2},{1... | collective-permute-start | bytes 98312 | tf_op jit(solution)/shard_map/ppermute | solution.py:227
  29.6 5.0 %collective-permute-start.25 = (bf16[32,512]{1,0:T(8,128)(2,1)S(1)}, bf16[32,512]{1,0:T(8,128)(2,1)S(1)}, u32[]{:S(2)}, u32[]{:S(2)}) collective-permute-start(bf16[32,512]{1,0:T(8,128)(2,1)S(1)} %add_convert_fusion), channel_id=1, source_target_pairs={{0,8},{4,12},{8,0},{12,4},{1,9},{5,13},{9,1},{13,5},{2,10},{6,14},... | collective-permute-start | bytes 98312 | tf_op jit(solution)/shard_map/ppermute | solution.py:228
  32.0 3.7 %collective-permute-start.18 = (bf16[32,512]{1,0:T(8,128)(2,1)S(1)}, bf16[32,512]{1,0:T(8,128)(2,1)S(1)}, u32[]{:S(2)}, u32[]{:S(2)}) collective-permute-start(bf16[32,512]{1,0:T(8,128)(2,1)S(1)} %add_convert_fusion.1), channel_id=1, source_target_pairs={{0,8},{4,12},{8,0},{12,4},{1,9},{5,13},{9,1},{13,5},{2,10},{6,14},... | collective-permute-start | bytes 98312 | tf_op jit(solution)/shard_map/ppermute | solution.py:228
  32.2 4.2 %collective-permute-start.11 = (bf16[32,512]{1,0:T(8,128)(2,1)S(1)}, bf16[32,512]{1,0:T(8,128)(2,1)S(1)}, u32[]{:S(2)}, u32[]{:S(2)}) collective-permute-start(bf16[32,512]{1,0:T(8,128)(2,1)S(1)} %add_convert_fusion.2), channel_id=1, source_target_pairs={{0,8},{4,12},{8,0},{12,4},{1,9},{5,13},{9,1},{13,5},{2,10},{6,14},... | collective-permute-start | bytes 98312 | tf_op jit(solution)/shard_map/ppermute | solution.py:228
  34.6 7.8 %collective-permute-start.4 = (bf16[32,512]{1,0:T(8,128)(2,1)S(1)}, bf16[32,512]{1,0:T(8,128)(2,1)S(1)}, u32[]{:S(2)}, u32[]{:S(2)}) collective-permute-start(bf16[32,512]{1,0:T(8,128)(2,1)S(1)} %add_convert_fusion.3), channel_id=1, source_target_pairs={{0,8},{4,12},{8,0},{12,4},{1,9},{5,13},{9,1},{13,5},{2,10},{6,14},... | collective-permute-start | bytes 98312 | tf_op jit(solution)/shard_map/ppermute | solution.py:228
  34.7 3.1 %collective-permute-start.26 = (bf16[32,512]{1,0:T(8,128)(2,1)S(1)}, bf16[32,512]{1,0:T(8,128)(2,1)S(1)}, u32[]{:S(2)}, u32[]{:S(2)}) collective-permute-start(bf16[32,512]{1,0:T(8,128)(2,1)S(1)} %subtract_convert_fusion.mine), channel_id=1, source_target_pairs={{0,4},{4,0},{8,12},{12,8},{1,5},{5,1},{9,13},{13,9},{2,6},{6,2},{1... | collective-permute-start | bytes 98312 | tf_op jit(solution)/shard_map/ppermute | solution.py:231
  35.8 7.0 %collective-permute-start.19 = (bf16[32,512]{1,0:T(8,128)(2,1)S(1)}, bf16[32,512]{1,0:T(8,128)(2,1)S(1)}, u32[]{:S(2)}, u32[]{:S(2)}) collective-permute-start(bf16[32,512]{1,0:T(8,128)(2,1)S(1)} %subtract_convert_fusion.1.mine), channel_id=1, source_target_pairs={{0,4},{4,0},{8,12},{12,8},{1,5},{5,1},{9,13},{13,9},{2,6},{6,2},{1... | collective-permute-start | bytes 98312 | tf_op jit(solution)/shard_map/ppermute | solution.py:231
  36.4 8.1 %collective-permute-start.12 = (bf16[32,512]{1,0:T(8,128)(2,1)S(1)}, bf16[32,512]{1,0:T(8,128)(2,1)S(1)}, u32[]{:S(2)}, u32[]{:S(2)}) collective-permute-start(bf16[32,512]{1,0:T(8,128)(2,1)S(1)} %subtract_convert_fusion.2.mine), channel_id=1, source_target_pairs={{0,4},{4,0},{8,12},{12,8},{1,5},{5,1},{9,13},{13,9},{2,6},{6,2},{1... | collective-permute-start | bytes 98312 | tf_op jit(solution)/shard_map/ppermute | solution.py:231
  39.2 8.7 %collective-permute-start.27 = (bf16[32,4096]{1,0:T(8,128)(2,1)S(1)}, bf16[32,4096]{1,0:T(8,128)(2,1)S(1)}, u32[]{:S(2)}, u32[]{:S(2)}) collective-permute-start(bf16[32,4096]{1,0:T(8,128)(2,1)S(1)} %get-tuple-element.49), channel_id=1, source_target_pairs={{0,1},{1,0},{2,3},{3,2},{4,5},{5,4},{6,7},{7,6},{8,9},{9,8},{10,11... | collective-permute-start | bytes 786440 | tf_op jit(solution)/shard_map/ppermute | solution.py:236
  42.4 3.8 %collective-permute-start.5 = (bf16[32,512]{1,0:T(8,128)(2,1)S(1)}, bf16[32,512]{1,0:T(8,128)(2,1)S(1)}, u32[]{:S(2)}, u32[]{:S(2)}) collective-permute-start(bf16[32,512]{1,0:T(8,128)(2,1)S(1)} %subtract_convert_fusion.3.mine), channel_id=1, source_target_pairs={{0,4},{4,0},{8,12},{12,8},{1,5},{5,1},{9,13},{13,9},{2,6},{6,2},{1... | collective-permute-start | bytes 98312 | tf_op jit(solution)/shard_map/ppermute | solution.py:231
  44.1 5.2 %collective-permute-start.20 = (bf16[32,4096]{1,0:T(8,128)(2,1)S(1)}, bf16[32,4096]{1,0:T(8,128)(2,1)S(1)}, u32[]{:S(2)}, u32[]{:S(2)}) collective-permute-start(bf16[32,4096]{1,0:T(8,128)(2,1)S(1)} %get-tuple-element.45), channel_id=1, source_target_pairs={{0,1},{1,0},{2,3},{3,2},{4,5},{5,4},{6,7},{7,6},{8,9},{9,8},{10,11... | collective-permute-start | bytes 786440 | tf_op jit(solution)/shard_map/ppermute | solution.py:236
  45.9 3.9 %collective-permute-start.13 = (bf16[32,4096]{1,0:T(8,128)(2,1)S(1)}, bf16[32,4096]{1,0:T(8,128)(2,1)S(1)}, u32[]{:S(2)}, u32[]{:S(2)}) collective-permute-start(bf16[32,4096]{1,0:T(8,128)(2,1)S(1)} %get-tuple-element.41), channel_id=1, source_target_pairs={{0,1},{1,0},{2,3},{3,2},{4,5},{5,4},{6,7},{7,6},{8,9},{9,8},{10,11... | collective-permute-start | bytes 786440 | tf_op jit(solution)/shard_map/ppermute | solution.py:236
  47.6 3.6 %collective-permute-start.6 = (bf16[32,4096]{1,0:T(8,128)(2,1)S(1)}, bf16[32,4096]{1,0:T(8,128)(2,1)S(1)}, u32[]{:S(2)}, u32[]{:S(2)}) collective-permute-start(bf16[32,4096]{1,0:T(8,128)(2,1)S(1)} %get-tuple-element.37), channel_id=1, source_target_pairs={{0,1},{1,0},{2,3},{3,2},{4,5},{5,4},{6,7},{7,6},{8,9},{9,8},{10,11... | collective-permute-start | bytes 786440 | tf_op jit(solution)/shard_map/ppermute | solution.py:236
  48.1 7.8 %collective-permute-start.28 = (bf16[32,4096]{1,0:T(8,128)(2,1)S(1)}, bf16[32,4096]{1,0:T(8,128)(2,1)S(1)}, u32[]{:S(2)}, u32[]{:S(2)}) collective-permute-start(bf16[32,4096]{1,0:T(8,128)(2,1)S(1)} %pad_maximum_fusion.9), channel_id=1, source_target_pairs={{0,2},{2,0},{1,3},{3,1},{4,6},{6,4},{5,7},{7,5},{8,10},{10,8},{9,1... | collective-permute-start | bytes 786440 | tf_op jit(solution)/shard_map/ppermute | solution.py:238
  49.4 12.0 %collective-permute-start.21 = (bf16[32,4096]{1,0:T(8,128)(2,1)S(1)}, bf16[32,4096]{1,0:T(8,128)(2,1)S(1)}, u32[]{:S(2)}, u32[]{:S(2)}) collective-permute-start(bf16[32,4096]{1,0:T(8,128)(2,1)S(1)} %pad_maximum_fusion.7), channel_id=1, source_target_pairs={{0,2},{2,0},{1,3},{3,1},{4,6},{6,4},{5,7},{7,5},{8,10},{10,8},{9,1... | collective-permute-start | bytes 786440 | tf_op jit(solution)/shard_map/ppermute | solution.py:238
  49.9 17.2 %collective-permute-start.14 = (bf16[32,4096]{1,0:T(8,128)(2,1)S(1)}, bf16[32,4096]{1,0:T(8,128)(2,1)S(1)}, u32[]{:S(2)}, u32[]{:S(2)}) collective-permute-start(bf16[32,4096]{1,0:T(8,128)(2,1)S(1)} %pad_maximum_fusion.5), channel_id=1, source_target_pairs={{0,2},{2,0},{1,3},{3,1},{4,6},{6,4},{5,7},{7,5},{8,10},{10,8},{9,1... | collective-permute-start | bytes 786440 | tf_op jit(solution)/shard_map/ppermute | solution.py:238
  51.3 21.4 %collective-permute-start.7 = (bf16[32,4096]{1,0:T(8,128)(2,1)S(1)}, bf16[32,4096]{1,0:T(8,128)(2,1)S(1)}, u32[]{:S(2)}, u32[]{:S(2)}) collective-permute-start(bf16[32,4096]{1,0:T(8,128)(2,1)S(1)} %pad_maximum_fusion.3), channel_id=1, source_target_pairs={{0,2},{2,0},{1,3},{3,1},{4,6},{6,4},{5,7},{7,5},{8,10},{10,8},{9,1... | collective-permute-start | bytes 786440 | tf_op jit(solution)/shard_map/ppermute | solution.py:238
  55.8 18.3 %copy-start.7 = (s32[32]{0:T(128)S(1)}, s32[32]{0:T(128)}, u32[]{:S(2)}) copy-start(s32[32]{0:T(128)} %param.13) | copy-start | bytes 388
  56.2 18.0 %collective-permute-start.41 = (bf16[32,4096]{1,0:T(8,128)(2,1)S(1)}, bf16[32,4096]{1,0:T(8,128)(2,1)S(1)}, u32[]{:S(2)}, u32[]{:S(2)}) collective-permute-start(bf16[32,4096]{1,0:T(8,128)(2,1)S(1)} %fusion.36.own), channel_id=1, source_target_pairs={{0,1},{1,0},{2,3},{3,2},{4,5},{5,4},{6,7},{7,6},{8,9},{9,8},{10,11... | collective-permute-start | bytes 786440 | tf_op jit(solution)/shard_map/ppermute | solution.py:242
  61.8 20.9 %collective-permute-start.37 = (bf16[32,4096]{1,0:T(8,128)(2,1)S(1)}, bf16[32,4096]{1,0:T(8,128)(2,1)S(1)}, u32[]{:S(2)}, u32[]{:S(2)}) collective-permute-start(bf16[32,4096]{1,0:T(8,128)(2,1)S(1)} %fusion.37.own), channel_id=1, source_target_pairs={{0,1},{1,0},{2,3},{3,2},{4,5},{5,4},{6,7},{7,6},{8,9},{9,8},{10,11... | collective-permute-start | bytes 786440 | tf_op jit(solution)/shard_map/ppermute | solution.py:242
  67.4 19.4 %collective-permute-start.33 = (bf16[32,4096]{1,0:T(8,128)(2,1)S(1)}, bf16[32,4096]{1,0:T(8,128)(2,1)S(1)}, u32[]{:S(2)}, u32[]{:S(2)}) collective-permute-start(bf16[32,4096]{1,0:T(8,128)(2,1)S(1)} %fusion.38.own), channel_id=1, source_target_pairs={{0,1},{1,0},{2,3},{3,2},{4,5},{5,4},{6,7},{7,6},{8,9},{9,8},{10,11... | collective-permute-start | bytes 786440 | tf_op jit(solution)/shard_map/ppermute | solution.py:242
  73.0 17.0 %collective-permute-start.29 = (bf16[32,4096]{1,0:T(8,128)(2,1)S(1)}, bf16[32,4096]{1,0:T(8,128)(2,1)S(1)}, u32[]{:S(2)}, u32[]{:S(2)}) collective-permute-start(bf16[32,4096]{1,0:T(8,128)(2,1)S(1)} %fusion.39.own), channel_id=1, source_target_pairs={{0,1},{1,0},{2,3},{3,2},{4,5},{5,4},{6,7},{7,6},{8,9},{9,8},{10,11... | collective-permute-start | bytes 786440 | tf_op jit(solution)/shard_map/ppermute | solution.py:242
  74.2 2.2 %copy-start.3 = (bf16[512,4096]{1,0:T(8,128)(2,1)S(1)}, bf16[512,4096]{1,0:T(8,128)(2,1)}, u32[]{:S(2)}) copy-start(bf16[512,4096]{1,0:T(8,128)(2,1)} %copy-done) | copy-start | bytes 12582916
  78.3 13.3 %collective-permute-start.42 = (bf16[6,16,512]{2,1,0:T(8,128)(2,1)S(1)}, bf16[6,16,512]{2,1,0:T(8,128)(2,1)S(1)}, u32[]{:S(2)}, u32[]{:S(2)}) collective-permute-start(bf16[6,16,512]{2,1,0:T(8,128)(2,1)S(1)} %get-tuple-element.63), channel_id=1, source_target_pairs={{0,4},{4,0},{8,12},{12,8},{1,5},{5,1},{9,13},{13,9},{2,6},{6,2},{1... | collective-permute-start | bytes 294920 | tf_op jit(solution)/shard_map/ppermute | solution.py:252
  79.6 12.0 %collective-permute-start.43 = (bf16[6,16,512]{2,1,0:T(8,128)(2,1)S(1)}, bf16[6,16,512]{2,1,0:T(8,128)(2,1)S(1)}, u32[]{:S(2)}, u32[]{:S(2)}) collective-permute-start(bf16[6,16,512]{2,1,0:T(8,128)(2,1)S(1)} %get-tuple-element.64), channel_id=1, source_target_pairs={{0,8},{4,12},{8,0},{12,4},{1,9},{5,13},{9,1},{13,5},{2,10},{6,14},... | collective-permute-start | bytes 294920 | tf_op jit(solution)/shard_map/ppermute | solution.py:252
  82.7 15.6 %collective-permute-start.44 = (bf16[6,16,512]{2,1,0:T(8,128)(2,1)S(1)}, bf16[6,16,512]{2,1,0:T(8,128)(2,1)S(1)}, u32[]{:S(2)}, u32[]{:S(2)}) collective-permute-start(bf16[6,16,512]{2,1,0:T(8,128)(2,1)S(1)} %get-tuple-element.65), channel_id=1, source_target_pairs={{0,12},{4,8},{8,4},{12,0},{1,13},{5,9},{9,5},{13,1},{2,14},{6,10},... | collective-permute-start | bytes 294920 | tf_op jit(solution)/shard_map/ppermute | solution.py:252
  82.7 2.2 %copy-start.4 = (bf16[512,4096]{1,0:T(8,128)(2,1)S(1)}, bf16[512,4096]{1,0:T(8,128)(2,1)}, u32[]{:S(2)}) copy-start(bf16[512,4096]{1,0:T(8,128)(2,1)} %copy-done) | copy-start | bytes 12582916
  86.9 9.5 %copy-start.5 = (bf16[512,4096]{1,0:T(8,128)(2,1)S(1)}, bf16[512,4096]{1,0:T(8,128)(2,1)}, u32[]{:S(2)}) copy-start(bf16[512,4096]{1,0:T(8,128)(2,1)} %copy-done) | copy-start | bytes 12582916
  86.9 12.6 %collective-permute-start.38 = (bf16[6,16,512]{2,1,0:T(8,128)(2,1)S(1)}, bf16[6,16,512]{2,1,0:T(8,128)(2,1)S(1)}, u32[]{:S(2)}, u32[]{:S(2)}) collective-permute-start(bf16[6,16,512]{2,1,0:T(8,128)(2,1)S(1)} %get-tuple-element.59), channel_id=1, source_target_pairs={{0,4},{4,0},{8,12},{12,8},{1,5},{5,1},{9,13},{13,9},{2,6},{6,2},{1... | collective-permute-start | bytes 294920 | tf_op jit(solution)/shard_map/ppermute | solution.py:252
  90.1 9.8 %collective-permute-start.39 = (bf16[6,16,512]{2,1,0:T(8,128)(2,1)S(1)}, bf16[6,16,512]{2,1,0:T(8,128)(2,1)S(1)}, u32[]{:S(2)}, u32[]{:S(2)}) collective-permute-start(bf16[6,16,512]{2,1,0:T(8,128)(2,1)S(1)} %get-tuple-element.60), channel_id=1, source_target_pairs={{0,8},{4,12},{8,0},{12,4},{1,9},{5,13},{9,1},{13,5},{2,10},{6,14},... | collective-permute-start | bytes 294920 | tf_op jit(solution)/shard_map/ppermute | solution.py:252
  91.6 10.3 %collective-permute-start.40 = (bf16[6,16,512]{2,1,0:T(8,128)(2,1)S(1)}, bf16[6,16,512]{2,1,0:T(8,128)(2,1)S(1)}, u32[]{:S(2)}, u32[]{:S(2)}) collective-permute-start(bf16[6,16,512]{2,1,0:T(8,128)(2,1)S(1)} %get-tuple-element.61), channel_id=1, source_target_pairs={{0,12},{4,8},{8,4},{12,0},{1,13},{5,9},{9,5},{13,1},{2,14},{6,10},... | collective-permute-start | bytes 294920 | tf_op jit(solution)/shard_map/ppermute | solution.py:252
  91.6 11.5 %collective-permute-start.34 = (bf16[6,16,512]{2,1,0:T(8,128)(2,1)S(1)}, bf16[6,16,512]{2,1,0:T(8,128)(2,1)S(1)}, u32[]{:S(2)}, u32[]{:S(2)}) collective-permute-start(bf16[6,16,512]{2,1,0:T(8,128)(2,1)S(1)} %get-tuple-element.55), channel_id=1, source_target_pairs={{0,4},{4,0},{8,12},{12,8},{1,5},{5,1},{9,13},{13,9},{2,6},{6,2},{1... | collective-permute-start | bytes 294920 | tf_op jit(solution)/shard_map/ppermute | solution.py:252
  98.3 9.1 %collective-permute-start.35 = (bf16[6,16,512]{2,1,0:T(8,128)(2,1)S(1)}, bf16[6,16,512]{2,1,0:T(8,128)(2,1)S(1)}, u32[]{:S(2)}, u32[]{:S(2)}) collective-permute-start(bf16[6,16,512]{2,1,0:T(8,128)(2,1)S(1)} %get-tuple-element.56), channel_id=1, source_target_pairs={{0,8},{4,12},{8,0},{12,4},{1,9},{5,13},{9,1},{13,5},{2,10},{6,14},... | collective-permute-start | bytes 294920 | tf_op jit(solution)/shard_map/ppermute | solution.py:252
  99.5 12.7 %collective-permute-start.36 = (bf16[6,16,512]{2,1,0:T(8,128)(2,1)S(1)}, bf16[6,16,512]{2,1,0:T(8,128)(2,1)S(1)}, u32[]{:S(2)}, u32[]{:S(2)}) collective-permute-start(bf16[6,16,512]{2,1,0:T(8,128)(2,1)S(1)} %get-tuple-element.57), channel_id=1, source_target_pairs={{0,12},{4,8},{8,4},{12,0},{1,13},{5,9},{9,5},{13,1},{2,14},{6,10},... | collective-permute-start | bytes 294920 | tf_op jit(solution)/shard_map/ppermute | solution.py:252
  99.9 13.9 %collective-permute-start.30 = (bf16[6,16,512]{2,1,0:T(8,128)(2,1)S(1)}, bf16[6,16,512]{2,1,0:T(8,128)(2,1)S(1)}, u32[]{:S(2)}, u32[]{:S(2)}) collective-permute-start(bf16[6,16,512]{2,1,0:T(8,128)(2,1)S(1)} %get-tuple-element.51), channel_id=1, source_target_pairs={{0,4},{4,0},{8,12},{12,8},{1,5},{5,1},{9,13},{13,9},{2,6},{6,2},{1... | collective-permute-start | bytes 294920 | tf_op jit(solution)/shard_map/ppermute | solution.py:252
  101.9 12.5 %collective-permute-start.31 = (bf16[6,16,512]{2,1,0:T(8,128)(2,1)S(1)}, bf16[6,16,512]{2,1,0:T(8,128)(2,1)S(1)}, u32[]{:S(2)}, u32[]{:S(2)}) collective-permute-start(bf16[6,16,512]{2,1,0:T(8,128)(2,1)S(1)} %get-tuple-element.52), channel_id=1, source_target_pairs={{0,8},{4,12},{8,0},{12,4},{1,9},{5,13},{9,1},{13,5},{2,10},{6,14},... | collective-permute-start | bytes 294920 | tf_op jit(solution)/shard_map/ppermute | solution.py:252
  103.1 14.0 %collective-permute-start.32 = (bf16[6,16,512]{2,1,0:T(8,128)(2,1)S(1)}, bf16[6,16,512]{2,1,0:T(8,128)(2,1)S(1)}, u32[]{:S(2)}, u32[]{:S(2)}) collective-permute-start(bf16[6,16,512]{2,1,0:T(8,128)(2,1)S(1)} %get-tuple-element.53), channel_id=1, source_target_pairs={{0,12},{4,8},{8,4},{12,0},{1,13},{5,9},{9,5},{13,1},{2,14},{6,10},... | collective-permute-start | bytes 294920 | tf_op jit(solution)/shard_map/ppermute | solution.py:252

commit v2 on v0

--- a/solution.py
+++ b/solution.py
@@ -1,13 +1,22 @@
+import functools
 import math
 
 import jax
 import jax.numpy as jnp
 from jax import lax
+from jax.experimental import pallas as pl
+from jax.experimental.pallas import tpu as pltpu
 from jax.sharding import PartitionSpec as P
 
 CHROMS = 22
 TILE = 512
 SPAN = 6
+LOADS = 2
+SPLIT = 4
+CHAIN = True
+FIRST = (1, 1)
+SECOND = ((0, 0, 1, 1), (1, 0, 1, 1))
+ORDER = (('pred', 0), ('two', 0), ('pred', 1), ('res', 0), ('two', 1), ('score', 0), ('chip', 0), ('res', 1), ('score', 1), ('chip', 1), ('den', 0), ('chrom', 0), ('den', 1), ('chrom', 1), ('leave', 0), ('leave', 1))
 
 
 def denoise(estimate, scores, prior_logit, slab_var, noise_var, marker_root, people_root):
@@ -24,7 +33,7 @@
     return (posterior * (1.0 / marker_root)).astype(jnp.bfloat16)
 
 
-def per_device(genotypes, estimate, phenotypes, prior_logit, slab_var, noise_var, tile_chrom):
+def whole_mesh_steps(genotypes, estimate, phenotypes, prior_logit, slab_var, noise_var, tile_chrom):
     people_dev, mark_dev = genotypes.shape
     mk_count = lax.axis_size("mk")
     people_count = lax.axis_size(("pp", "sub"))
@@ -78,6 +87,351 @@
     return (updated, loco_out)
 
 
+VMEM = pltpu.MemorySpace.VMEM
+NT = (((1,), (1,)), ((), ()))
+
+
+class Steps:
+    def __init__(self, genotypes):
+        self.genotypes = genotypes
+        self.token = jnp.zeros((8, 128), jnp.float32)
+
+    def call(self, body, outs, scalars=(), args=(), streamed=False, scratch=(), after=(), into=None):
+        geno = self.genotypes
+        tiles = geno.shape[1] // TILE
+        after = list(after) + [into] * (into is not None)
+        skip = 1 + len(after)
+        filled = [] if into is None else [jax.ShapeDtypeStruct(into.shape, into.dtype)]
+        count = skip + len(scalars) + len(args)
+
+        def kernel(*refs):
+            ins, rest = list(refs[skip:count]), list(refs[count:])
+            if streamed:
+                source = rest.pop(0)
+                held, arrived = rest[1 + len(outs) : 3 + len(outs)]
+                del rest[1 + len(outs) : 3 + len(outs)]
+                copies = []
+                for part in range(LOADS):
+                    columns = pl.ds(part * geno.shape[1] // LOADS, geno.shape[1] // LOADS)
+                    copies.append(pltpu.make_async_copy(source.at[:, columns], held.at[:, columns], arrived.at[part]))
+                for copy in copies:
+                    copy.start()
+
+                def need(tile):
+                    if tile * LOADS % tiles == 0:
+                        copies[tile * LOADS // tiles].wait()
+
+                ins += [held, need]
+            body(*ins, *rest[1:])
+
+        anywhere = pl.BlockSpec(memory_space=pl.ANY)
+        stream_scratch = [pltpu.VMEM(geno.shape, geno.dtype), pltpu.SemaphoreType.DMA((LOADS,))] if streamed else []
+        token, *results = pl.pallas_call(
+            kernel,
+            out_shape=[jax.ShapeDtypeStruct(self.token.shape, self.token.dtype), *outs, *filled],
+            in_specs=[anywhere] * skip
+            + [pl.BlockSpec(memory_space=pltpu.SMEM)] * len(scalars)
+            + [pl.BlockSpec(memory_space=VMEM)] * len(args)
+            + [anywhere] * streamed,
+            out_specs=[anywhere] + [pl.BlockSpec(memory_space=VMEM)] * len(outs) + [anywhere] * len(filled),
+            scratch_shapes=stream_scratch + list(scratch),
+            input_output_aliases={0: 0} if into is None else {0: 0, skip - 1: 1 + len(outs)},
+            cost_estimate=pl.CostEstimate(flops=1, bytes_accessed=1, transcendentals=0),
+            compiler_params=pltpu.CompilerParams(vmem_limit_bytes=12 * 2**20),
+        )(self.token, *after, *scalars, *[pltpu.with_memory_space_constraint(a, VMEM) for a in args], *[pltpu.with_memory_space_constraint(geno, pltpu.MemorySpace.HBM)] * streamed)
+        if CHAIN:
+            self.token = token
+        return results
+
+
+def columns_of(tile):
+    return slice(tile * TILE, (tile + 1) * TILE)
+
+
+def place():
+    return lax.axis_index("pp") * 2 + lax.axis_index("sub"), lax.axis_index("mk")
+
+
+def row_at(start, height):
+    return pl.ds(pl.multiple_of(start, 16), height)
+
+
+def piece_of(refs, tile):
+    each = refs[0].shape[1] // TILE
+    return refs[tile // each], columns_of(tile % each)
+
+
+def predict_body(own, across, beside, corner, geno, need, keep, send, product):
+    odd = place()[1] % 2
+    half = 2 * own.shape[0]
+    for tile in range(geno.shape[1] // TILE):
+        part = columns_of(tile)
+        rows = jnp.concatenate([own[:, part], across[:, part], beside[:, part], corner[:, part]], axis=0)
+        need(tile)
+        term = lax.dot_general(rows, geno[:, part], NT, preferred_element_type=jnp.float32)
+        product[...] = term if tile == 0 else product[...] + term
+    keep[...] = product[row_at(odd * half, half), :]
+    send[...] = product[row_at(half - odd * half, half), :].astype(send.dtype)
+
+
+def two_body(keep, came, two):
+    two[...] = (keep[...] + came[...].astype(jnp.float32)).astype(two.dtype)
+
+
+def residual_body(shard, low, phen, two, came, residual):
+    me, depth = place()
+    height = two.shape[0] // 2
+    for block in range(2):
+        at = slice(block * height, (block + 1) * height)
+        prediction = two[at, :].astype(jnp.float32) + came[at, :].astype(jnp.float32)
+        start = (me ^ (depth % 2) ^ (2 * block)) * shard + low
+        measured = phen[row_at(start, height), :].astype(jnp.float32)
+        residual[at, :] = (measured - prediction).astype(residual.dtype)
+
+
+def score_body(low, mine, other, geno, need, keep, *sends):
+    even = place()[1] % 2 == 0
+    half = keep.shape[0]
+    height, block = half // 2, mine.shape[0] // 2
+
+    def rows_of(ref):
+        return jnp.concatenate([ref[low : low + height], ref[block + low : block + low + height]], axis=0)
+
+    first = jnp.where(even, rows_of(mine), rows_of(other))
+    second = jnp.where(even, rows_of(other), rows_of(mine))
+    rows = jnp.concatenate([first, second], axis=0)
+    for tile in range(geno.shape[1] // TILE):
+        part = columns_of(tile)
+        need(tile)
+        product = jnp.dot(rows, geno[:, part], preferred_element_type=jnp.float32)
+        keep[:, part] = product[:half]
+        send, inner = piece_of(sends, tile)
+        send[:, inner] = product[half:].astype(send.dtype)
+
+
+def chip_body(keep, *refs):
+    *came, chip, send = refs
+    height = keep.shape[0] // 2
+    for tile in range(keep.shape[1] // TILE):
+        part = columns_of(tile)
+        ref, inner = piece_of(came, tile)
+        total = keep[:, part] + ref[:, inner].astype(jnp.float32)
+        chip[:, part] = total
+        send[:height, part] = total[height:].astype(send.dtype)
+        send[height:, part] = total[:height].astype(send.dtype)
+
+
+def denoise_body(marker_root, people_root, low, first, own, across, chip, came, coefs, coefs_across, *refs):
+    *updated, whole, stored = refs
+    height = updated[0].shape[0] // 2
+    at = slice(low, low + height)
+    coef = jnp.concatenate([coefs[first : first + height], coefs_across[first : first + height]], axis=0)
+    base, curve, gain = coef[:, 0:1], coef[:, 1:2], coef[:, 2:3]
+    for tile in range(own.shape[1] // TILE):
+        part = columns_of(tile)
+        scores = chip[:, part] + came[:, part].astype(jnp.float32)
+        estimate = jnp.concatenate([own[at, part], across[at, part]], axis=0).astype(jnp.float32)
+        observed = marker_root * estimate + scores * (1.0 / people_root)
+        log_odds = base + curve * observed * observed
+        posterior = jax.nn.sigmoid(log_odds) * gain * observed
+        ref, inner = piece_of(updated, tile)
+        ref[:, inner] = (posterior * (1.0 / marker_root)).astype(ref.dtype)
+    copies, width = [], updated[0].shape[1]
+    for at, ref in enumerate(updated):
+        target = whole.at[pl.ds(first, height), pl.ds(at * width, width)]
+        copies.append(pltpu.make_async_copy(ref.at[pl.ds(0, height)], target, stored.at[at]))
+    for copy in copies:
+        copy.start()
+    for copy in copies:
+        copy.wait()
+
+
+def chrom_body(labels, *refs):
+    own, beside, (geno, need, *outs, acc) = refs[:SPLIT], refs[SPLIT : 2 * SPLIT], refs[2 * SPLIT :]
+    me, depth = place()
+    height = own[0].shape[0] // 2
+    base = depth * (geno.shape[1] // TILE)
+    starts = []
+    for to in range(len(outs)):
+        bits = me ^ depth ^ to
+        starts.append(((bits % 2) * 2 + bits // 2) * height)
+    for out in outs:
+        out[...] = jnp.zeros_like(out)
+    for tile in range(geno.shape[1] // TILE):
+        part = columns_of(tile)
+        halves = [ref[:, inner] for ref, inner in (piece_of(own, tile), piece_of(beside, tile))]
+        rows = jnp.concatenate(halves, axis=0)
+        need(tile)
+        product = lax.dot_general(rows, geno[:, part], NT, preferred_element_type=jnp.float32)
+        if tile == 0:
+            acc[...] = product
+        else:
+            same = (labels[base + tile] == labels[base + tile - 1]).astype(jnp.float32)
+            acc[...] = acc[...] * same + product
+        slot = labels[base + tile] - labels[base]
+        for start, out in zip(starts, outs):
+            out[slot] = acc[row_at(start, height), :].astype(out.dtype)
+
+
+def loco_body(row, shard, tiles, labels, phen, *refs):
+    *sums, out, base, acc, stage, done = refs
+    height = base.shape[0]
+    _, depth = place()
+    firsts = [labels[(depth ^ step) * tiles] for step in range(len(sums))]
+    total = jnp.zeros(base.shape, jnp.float32)
+    for part in sums:
+        for slot in range(SPAN):
+            total = total + part[slot].astype(jnp.float32)
+    base[...] = phen[row_at(depth * shard + row, height), :].astype(jnp.float32) - total
+
+    def copy(chrom):
+        return pltpu.make_async_copy(stage.at[chrom], out.at[chrom, pl.ds(row, height)], done.at[chrom])
+
+    def step(chrom, carry):
+        acc[...] = base[...]
+        for first, part in zip(firsts, sums):
+            slot = chrom - first
+
+            @pl.when((slot >= 0) & (slot < SPAN))
+            def _():
+                acc[...] += part[slot].astype(jnp.float32)
+
+        stage[chrom] = acc[...].astype(stage.dtype)
+        copy(chrom).start()
+        return carry
+
+    lax.fori_loop(0, CHROMS, step, 0)
+
+    def finish(chrom, carry):
+        copy(chrom).wait()
+        return carry
+
+    lax.fori_loop(0, CHROMS, finish, 0)
+
+
+def leave_out(loco, token, shape, row, height, tiles, labels, phen, sums):
+    people = phen.shape[1]
+    anywhere = pl.BlockSpec(memory_space=pl.ANY)
+    specs = [anywhere, pl.BlockSpec(memory_space=pltpu.SMEM)] + [pl.BlockSpec(memory_space=VMEM)] * (1 + len(sums))
+    args = [token, labels] + [pltpu.with_memory_space_constraint(a, VMEM) for a in (phen, *sums)]
+    before, aliases = 1, {0: 1}
+    if loco is not None:
+        specs, args, before, aliases = [anywhere] + specs, [loco] + args, 2, {0: 0, 1: 1}
+
+    def body(*refs):
+        ins, (out, _, *scratch) = refs[before : len(args)], refs[len(args) :]
+        loco_body(row, shape[1], tiles, *ins, out, *scratch)
+
+    return pl.pallas_call(
+        body,
+        out_shape=[jax.ShapeDtypeStruct(shape, jnp.bfloat16), jax.ShapeDtypeStruct(token.shape, token.dtype)],
+        in_specs=specs,
+        out_specs=[anywhere, anywhere],
+        scratch_shapes=[pltpu.VMEM((height, people), jnp.float32)] * 2
+        + [pltpu.VMEM((shape[0], height, people), jnp.bfloat16), pltpu.SemaphoreType.DMA((shape[0],))],
+        input_output_aliases=aliases,
+        cost_estimate=pl.CostEstimate(flops=1, bytes_accessed=1, transcendentals=0),
+        compiler_params=pltpu.CompilerParams(vmem_limit_bytes=8 * 2**20),
+    )(*args)
+
+
+def piece_steps(genotypes, estimate, phenotypes, prior_logit, slab_var, noise_var, tile_chrom):
+    people_dev, mark_dev = genotypes.shape
+    shard = estimate.shape[0]
+    mk_count = lax.axis_size("mk")
+    people_count = lax.axis_size(("pp", "sub"))
+    marker_root = math.sqrt(mark_dev * mk_count)
+    people_root = math.sqrt(people_dev * people_count)
+    tile_dev = mark_dev // TILE
+    swap = [(0, 1), (1, 0)]
+
+    def along(step):
+        return [(i, i ^ step) for i in range(mk_count)]
+
+    firsts, row = [], 0
+    for part in FIRST:
+        firsts.append((row, shard * part // sum(FIRST)))
+        row += firsts[-1][1]
+    seconds = [(of, firsts[of][1] * a // n, firsts[of][1] * b // n - firsts[of][1] * a // n) for of, a, b, n in SECOND]
+
+    own = [estimate[row : row + height] for row, height in firsts]
+    across = [lax.ppermute(one, "pp", swap) for one in own]
+    beside = [lax.ppermute(one, "sub", swap) for one in own]
+    corner = [lax.ppermute(one, "sub", swap) for one in across]
+    spread = slab_var + noise_var
+    coefs = jnp.stack(
+        [prior_logit + 0.5 * jnp.log(noise_var / spread), 0.5 * (1.0 / noise_var - 1.0 / spread), slab_var / spread],
+        axis=1,
+    )
+    coefs_across = lax.ppermute(coefs, "pp", swap)
+    steps, whole, loco = Steps(genotypes), jnp.zeros(estimate.shape, estimate.dtype), None
+    before, after = [{} for _ in firsts], [{} for _ in seconds]
+    f32, bf16 = jnp.float32, jnp.bfloat16
+    for stage, at in ORDER:
+        if stage in ("pred", "two", "res"):
+            now, (row, height) = before[at], firsts[at]
+        else:
+            now, (of, low, height) = after[at], seconds[at]
+            row = firsts[of][0] + low
+        half, wide = (2 * height, people_dev), (2 * height, mark_dev)
+        narrow = pltpu.VMEM((2 * height, mark_dev // SPLIT), bf16)
+        if stage == "pred":
+            keep, send = steps.call(
+                predict_body,
+                [pltpu.VMEM(half, f32), pltpu.VMEM(half, bf16)],
+                args=[own[at], across[at], beside[at], corner[at]],
+                streamed=True,
+                scratch=[pltpu.VMEM((4 * height, people_dev), f32)],
+            )
+            now["pred"] = keep, lax.ppermute(send, "mk", along(1))
+        elif stage == "two":
+            (two,) = steps.call(two_body, [pltpu.VMEM(half, bf16)], args=now["pred"])
+            now["two"] = two, lax.ppermute(two, "mk", along(2))
+        elif stage == "res":
+            body = functools.partial(residual_body, shard, row)
+            (residual,) = steps.call(body, [pltpu.VMEM(half, bf16)], args=[phenotypes, *now["two"]])
+            now["res"] = residual, lax.ppermute(residual, "mk", along(1))
+        elif stage == "score":
+            keep, *sends = steps.call(
+                functools.partial(score_body, low),
+                [pltpu.VMEM(wide, f32)] + [narrow] * SPLIT,
+                args=before[of]["res"],
+                streamed=True,
+                after=[coefs_across],
+            )
+            now["score"] = [keep] + [lax.ppermute(send, "sub", swap) for send in sends]
+        elif stage == "chip":
+            chip, send = steps.call(chip_body, [pltpu.VMEM(wide, f32), pltpu.VMEM(wide, bf16)], args=now["score"])
+            now["chip"] = chip, lax.ppermute(send, "pp", swap)
+        elif stage == "den":
+            *updated, whole = steps.call(
+                functools.partial(denoise_body, marker_root, people_root, low, row),
+                [narrow] * SPLIT,
+                args=[own[of], across[of], *now["chip"], coefs, coefs_across],
+                scratch=[pltpu.SemaphoreType.DMA((SPLIT,))],
+                into=whole,
+            )
+            now["den"] = updated + [lax.ppermute(one, "sub", swap) for one in updated]
+        elif stage == "chrom":
+            sums = steps.call(
+                chrom_body,
+                [pltpu.VMEM((SPAN, height, people_dev), bf16)] * mk_count,
+                [tile_chrom],
+                now["den"],
+                streamed=True,
+                scratch=[pltpu.VMEM((4 * height, people_dev), f32)],
+            )
+            now["chrom"] = [sums[0]] + [lax.ppermute(sums[step], "mk", along(step)) for step in range(1, mk_count)]
+        else:
+            shape = (CHROMS, shard, people_dev)
+            loco, token = leave_out(
+                loco, steps.token, shape, row, height, tile_dev, tile_chrom, phenotypes, now["chrom"]
+            )
+            if CHAIN:
+                steps.token = token
+    return (whole, loco)
+
+
 def solution(mesh):
     placed = (
         P(("grp", "pp", "sub"), "mk"),
@@ -88,8 +442,9 @@
         P(("grp", "pp", "sub")),
         P("grp"),
     )
+    by_pieces = (mesh.shape["pp"], mesh.shape["sub"], mesh.shape["mk"]) == (2, 2, 4)
     return jax.shard_map(
-        per_device,
+        piece_steps if by_pieces else whole_mesh_steps,
         mesh=mesh,
         in_specs=placed,
         out_specs=(P(("grp", "pp", "sub"), "mk"), P("grp", "mk", ("pp", "sub"))),

time: 280 us -> 107 us (0.38); the launches traced: 275 us -> 107 us
  waiting for transfers between devices: 215 us -> 43.5 us
  starting transfers between devices: 5.23 us -> 33.6 us
  Pallas kernels: 0 us -> 26.9 us
  matrix products: 24.5 us -> 0 us
  between operations: 13.8 us -> 0.84 us
  local copies, waits for them, and re-layouts: 13 us -> 2.02 us
  other arithmetic: 3.29 us -> 0.02 us
    all_to_all x1 -> x0, waiting for transfers between devices: 89.6 us -> none  [per_device(): lax.all_to_all(local_sums, 'mk', split_axis=1, concat_axis=0, tiled=True)]
    reduce_scatter x1 -> x0, waiting for transfers between devices: 45.3 us -> none  [per_device(): lax.psum_scatter(jnp.dot(residual, genotypes, preferred_element_type=jnp....]
    ppermute x0 -> x37, waiting for transfers between devices: none -> 43.5 us  [the longest x6 25.8 us: piece_steps(): lax.ppermute(sums[step], 'mk', along(step))]
    all_gather x2 -> x0, waiting for transfers between devices: 42.3 us -> none  [the longest x1 25.7 us: per_device(): lax.all_gather(estimate, ('pp', 'sub'), axis=0, tiled=True)]
    psum x1 -> x0, waiting for transfers between devices: 36.7 us -> none  [per_device(): prediction = lax.psum(partial_pred, 'mk')]
    ppermute x0 -> x37, starting transfers between devices: none -> 33.6 us  [the longest x6 6.56 us: piece_steps(): lax.ppermute(sums[step], 'mk', along(step))]
    pallas_call x0 -> x16, Pallas kernels: none -> 26.9 us  [the longest x14 22.3 us: call(): pl.pallas_call(kernel, out_shape=[jax.ShapeDtypeStruct(self.token.shape,...]
    dot_general x5 -> x0, matrix products: 24.5 us -> none  [the longest x1 6.27 us: per_device(): jnp.einsum('st,tkp->skp', member, tile_terms, precision=lax.Precision.HIG...]
  transfers between devices with their start and end apart: 5 -> 37, of which waited for: 5 -> 22; matrix products, arithmetic and copies ran while one was open for 3% -> 1% of each run, Pallas kernels for 0% -> 20%
where the time goes in v2:
time: 107 us
  waiting for transfers between devices  43.5 us (41%)
  starting transfers between devices  33.6 us (31%)
  Pallas kernels  26.9 us (25%)
  local copies, waits for them, and re-layouts  2.02 us (2%)
    ppermute x6, waiting for transfers between devices, piece_steps(): lax.ppermute(sums[step], 'mk', along(step))  25.8 us
    pallas_call x14, Pallas kernels, call(): pl.pallas_call(kernel, out_shape=[jax.ShapeDtypeStruct(self.token.shape,...  22.3 us
    ppermute x2, waiting for transfers between devices, piece_steps(): across = [lax.ppermute(one, 'pp', swap) for one in own]  7.65 us
    ppermute x6, starting transfers between devices, piece_steps(): lax.ppermute(sums[step], 'mk', along(step))  6.56 us
    ppermute x8, starting transfers between devices, piece_steps(): now['score'] = [keep] + [lax.ppermute(send, 'sub', swap) for send in sends]  6.02 us
    ppermute x8, starting transfers between devices, piece_steps(): now['den'] = updated + [lax.ppermute(one, 'sub', swap) for one in updated]  5.78 us
    pallas_call x2, Pallas kernels, leave_out(): pl.pallas_call(body, out_shape=[jax.ShapeDtypeStruct(shape, jnp.bfloat16)...  4.58 us
    ppermute x2, starting transfers between devices, piece_steps(): now['two'] = (two, lax.ppermute(two, 'mk', along(2)))  3.22 us
  transfers between devices with their start and end apart: 37, of which 22 were waited for; matrix products, arithmetic and copies ran while one was open for 1% of the time, Pallas kernels for 20%

profile of v2, /device:TPU:13, one launch (start us, length us, event | category | flops | bytes accessed | tf_op | source)
XLA Modules:
  0.0 106.9 jit_solution(9676211451705922748)
XLA Ops:
  0.6 1.1 fusion
  1.7 1.3 %collective-permute-start = (bf16[32,4096]{1,0:T(8,128)(2,1)S(1)}, bf16[32,4096]{1,0:T(8,128)(2,1)S(1)}, u32[]{:S(2)}, u32[]{:S(2)}) collective-permute-start(bf16[32,4096]{1,0:T(8,128)(2,1)S(1)} %get-tuple-element.117.refs_1_.refs_2_), channel_id=1, source_target_pairs={{0,2},{2,0},{1,3},{3,1},{4,6},{6,4},{5,7},{7,5},{8,10},{10,8},{9,1... | collective-permute-start | bytes 786440 | tf_op jit(solution)/shard_map/ppermute | solution.py:358
  3.0 1.0 collective-permute-start.1
  3.9 5.0 %collective-permute-done.refs_2_.refs_3_ = bf16[32,4096]{1,0:T(8,128)(2,1)S(1)} collective-permute-done((bf16[32,4096]{1,0:T(8,128)(2,1)S(1)}, bf16[32,4096]{1,0:T(8,128)(2,1)S(1)}, u32[]{:S(2)}, u32[]{:S(2)}) %collective-permute-start) | collective-permute-done | bytes 262176 | tf_op jit(solution)/shard_map/ppermute | solution.py:358
  8.9 1.5 %collective-permute-start.2 = (bf16[32,4096]{1,0:T(8,128)(2,1)S(1)}, bf16[32,4096]{1,0:T(8,128)(2,1)S(1)}, u32[]{:S(2)}, u32[]{:S(2)}) collective-permute-start(bf16[32,4096]{1,0:T(8,128)(2,1)S(1)} %collective-permute-done.refs_2_.refs_3_), channel_id=1, source_target_pairs={{0,1},{1,0},{2,3},{3,2},{4,5},{5,4},{6,7},{7,6},{8,9},{9,8},{10,11... | collective-permute-start | bytes 786440 | tf_op jit(solution)/shard_map/ppermute | solution.py:360
  10.5 1.2 %collective-permute-start.4 = (bf16[32,4096]{1,0:T(8,128)(2,1)S(1)}, bf16[32,4096]{1,0:T(8,128)(2,1)S(1)}, u32[]{:S(2)}, u32[]{:S(2)}) collective-permute-start(bf16[32,4096]{1,0:T(8,128)(2,1)S(1)} %get-tuple-element.116.refs_1_.refs_2_), channel_id=1, source_target_pairs={{0,2},{2,0},{1,3},{3,1},{4,6},{6,4},{5,7},{7,5},{8,10},{10,8},{9,1... | collective-permute-start | bytes 786440 | tf_op jit(solution)/shard_map/ppermute | solution.py:358
  11.7 3.2 %shard_map.86 = (f32[8,128]{1,0:T(8,128)S(1)}, f32[64,512]{1,0:T(8,128)S(1)}, bf16[64,512]{1,0:T(8,128)(2,1)S(1)}) custom-call(f32[8,128]{1,0:T(8,128)S(1)} %broadcast_in_dim.6.refs_0_, bf16[32,4096]{1,0:T(8,128)(2,1)S(1)} %get-tuple-element.117.refs_1_.refs_2_, ...), custom_call_target="tpu_custom_call", output_to_operand_aliasing={{0}: (0, {})} | custom-call | flops 1 | bytes 1 | tf_op jit(solution)/shard_map/pallas_call | solution.py:129
  15.0 0.2 collective-permute-start.3
  15.2 0.6 collective-permute-start.5
  15.8 2.6 %collective-permute-done.4.refs_2_.refs_3_ = bf16[32,4096]{1,0:T(8,128)(2,1)S(1)} collective-permute-done((bf16[32,4096]{1,0:T(8,128)(2,1)S(1)}, bf16[32,4096]{1,0:T(8,128)(2,1)S(1)}, u32[]{:S(2)}, u32[]{:S(2)}) %collective-permute-start.4) | collective-permute-done | bytes 262176 | tf_op jit(solution)/shard_map/ppermute | solution.py:358
  18.4 0.8 collective-permute-start.6
  19.2 2.4 %collective-permute-start.7 = (bf16[64,512]{1,0:T(8,128)(2,1)S(1)}, bf16[64,512]{1,0:T(8,128)(2,1)S(1)}, u32[]{:S(2)}, u32[]{:S(2)}) collective-permute-start(bf16[64,512]{1,0:T(8,128)(2,1)S(1)} %get-tuple-element.64.refs_2_), channel_id=1, source_target_pairs={{0,8},{4,12},{8,0},{12,4},{1,9},{5,13},{9,1},{13,5},{2,10},{6,14},... | collective-permute-start | bytes 196616 | tf_op jit(solution)/shard_map/ppermute | solution.py:389
  21.7 3.2 %shard_map.88 = (f32[8,128]{1,0:T(8,128)S(1)}, f32[64,512]{1,0:T(8,128)S(1)}, bf16[64,512]{1,0:T(8,128)(2,1)S(1)}) custom-call(f32[8,128]{1,0:T(8,128)S(1)} %get-tuple-element.62.refs_0_, bf16[32,4096]{1,0:T(8,128)(2,1)S(1)} %get-tuple-element.116.refs_1_.refs_2_, ...), custom_call_target="tpu_custom_call", output_to_operand_aliasing={{0}: (0, {})} | custom-call | flops 1 | bytes 1 | tf_op jit(solution)/shard_map/pallas_call | solution.py:129
  24.9 0.2 collective-permute-start.8
  25.2 1.4 %collective-permute-start.10 = (bf16[64,512]{1,0:T(8,128)(2,1)S(1)}, bf16[64,512]{1,0:T(8,128)(2,1)S(1)}, u32[]{:S(2)}, u32[]{:S(2)}) collective-permute-start(bf16[64,512]{1,0:T(8,128)(2,1)S(1)} %get-tuple-element.69.refs_2_), channel_id=1, source_target_pairs={{0,4},{4,0},{8,12},{12,8},{1,5},{5,1},{9,13},{13,9},{2,6},{6,2},{1... | collective-permute-start | bytes 196616 | tf_op jit(solution)/shard_map/ppermute | solution.py:393
  26.7 1.2 %collective-permute-start.9 = (f32[64,3]{1,0:T(8,128)S(1)}, f32[64,3]{1,0:T(8,128)S(1)}, u32[]{:S(2)}, u32[]{:S(2)}) collective-permute-start(f32[64,3]{1,0:T(8,128)S(1)} %copy.31.refs_6_), channel_id=1, source_target_pairs={{0,2},{2,0},{1,3},{3,1},{4,6},{6,4},{5,7},{7,5},{8,10},{10,8},{9,1... | collective-permute-start | bytes 2312 | tf_op jit(solution)/shard_map/ppermute | solution.py:366
  27.9 0.2 collective-permute-done.8.refs_2_
  28.1 1.6 %collective-permute-done.9.refs_1_.refs_7_ = f32[64,3]{1,0:T(8,128)S(1)} collective-permute-done((f32[64,3]{1,0:T(8,128)S(1)}, f32[64,3]{1,0:T(8,128)S(1)}, u32[]{:S(2)}, u32[]{:S(2)}) %collective-permute-start.9) | collective-permute-done | bytes 800 | tf_op jit(solution)/shard_map/ppermute | solution.py:366
  29.7 2.7 %shard_map.91 = (f32[8,128]{1,0:T(8,128)S(1)}, f32[64,4096]{1,0:T(8,128)S(1)}, bf16[64,1024]{1,0:T(8,128)(2,1)S(1)}, bf16[64,1024]{1,0:T(8,128)(2,1)S(1)}, bf16[...) custom-call(f32[8,128]{1,0:T(8,128)S(1)} %get-tuple-element.68.refs_0_, ...), custom_call_target="tpu_custom_call", output_to_operand_aliasing={{0}: (0, {})} | custom-call | flops 1 | bytes 1 | tf_op jit(solution)/shard_map/pallas_call | solution.py:129
  32.4 2.1 %collective-permute-start.11 = (bf16[64,1024]{1,0:T(8,128)(2,1)S(1)}, bf16[64,1024]{1,0:T(8,128)(2,1)S(1)}, u32[]{:S(2)}, u32[]{:S(2)}) collective-permute-start(bf16[64,1024]{1,0:T(8,128)(2,1)S(1)} %get-tuple-element.72), channel_id=1, source_target_pairs={{0,1},{1,0},{2,3},{3,2},{4,5},{5,4},{6,7},{7,6},{8,9},{9,8},{10,11... | collective-permute-start | bytes 393224 | tf_op jit(solution)/shard_map/ppermute | solution.py:402
  34.7 0.4 collective-permute-start.13
  35.2 0.8 collective-permute-start.15
  36.1 0.3 collective-permute-done.14.refs_5_
  36.4 0.1 shard_map.92
  36.6 2.7 %collective-permute-done.15.refs_3_ = bf16[64,512]{1,0:T(8,128)(2,1)S(1)} collective-permute-done((bf16[64,512]{1,0:T(8,128)(2,1)S(1)}, bf16[64,512]{1,0:T(8,128)(2,1)S(1)}, u32[]{:S(2)}, u32[]{:S(2)}) %collective-permute-start.15) | collective-permute-done | bytes 65568 | tf_op jit(solution)/shard_map/ppermute | solution.py:389
  39.3 0.1 collective-permute-start.16
  39.5 1.2 %collective-permute-start.21 = (bf16[64,4096]{1,0:T(8,128)(2,1)S(1)}, bf16[64,4096]{1,0:T(8,128)(2,1)S(1)}, u32[]{:S(2)}, u32[]{:S(2)}) collective-permute-start(bf16[64,4096]{1,0:T(8,128)(2,1)S(1)} %get-tuple-element.88), channel_id=1, source_target_pairs={{0,2},{2,0},{1,3},{3,1},{4,6},{6,4},{5,7},{7,5},{8,10},{10,8},{9,1... | collective-permute-start | bytes 1572872 | tf_op jit(solution)/shard_map/ppermute | solution.py:405
  40.7 1.8 %collective-permute-done.16.refs_3_ = bf16[64,512]{1,0:T(8,128)(2,1)S(1)} collective-permute-done((bf16[64,512]{1,0:T(8,128)(2,1)S(1)}, bf16[64,512]{1,0:T(8,128)(2,1)S(1)}, u32[]{:S(2)}, u32[]{:S(2)}) %collective-permute-start.16) | collective-permute-done | bytes 65568 | tf_op jit(solution)/shard_map/ppermute | solution.py:393
  42.5 2.7 %shard_map.94 = (f32[8,128]{1,0:T(8,128)S(1)}, f32[64,4096]{1,0:T(8,128)S(1)}, bf16[64,1024]{1,0:T(8,128)(2,1)S(1)}, bf16[64,1024]{1,0:T(8,128)(2,1)S(1)}, bf16[...) custom-call(f32[8,128]{1,0:T(8,128)S(1)} %get-tuple-element.78.refs_0_, ...), custom_call_target="tpu_custom_call", output_to_operand_aliasing={{0}: (0, {})} | custom-call | flops 1 | bytes 1 | tf_op jit(solution)/shard_map/pallas_call | solution.py:129
  45.2 2.7 %collective-permute-start.17 = (bf16[64,1024]{1,0:T(8,128)(2,1)S(1)}, bf16[64,1024]{1,0:T(8,128)(2,1)S(1)}, u32[]{:S(2)}, u32[]{:S(2)}) collective-permute-start(bf16[64,1024]{1,0:T(8,128)(2,1)S(1)} %get-tuple-element.82), channel_id=1, source_target_pairs={{0,1},{1,0},{2,3},{3,2},{4,5},{5,4},{6,7},{7,6},{8,9},{9,8},{10,11... | collective-permute-start | bytes 393224 | tf_op jit(solution)/shard_map/ppermute | solution.py:402
  48.0 0.4 collective-permute-start.19
  48.5 0.4 collective-permute-done.17.refs_2_
  48.9 0.4 collective-permute-done.18.refs_3_
  49.2 0.2 collective-permute-done.19.refs_4_
  49.4 0.3 collective-permute-done.20.refs_5_
  49.8 0.1 shard_map.95
  49.9 1.3 %collective-permute-start.26 = (bf16[64,4096]{1,0:T(8,128)(2,1)S(1)}, bf16[64,4096]{1,0:T(8,128)(2,1)S(1)}, u32[]{:S(2)}, u32[]{:S(2)}) collective-permute-start(bf16[64,4096]{1,0:T(8,128)(2,1)S(1)} %get-tuple-element.97), channel_id=1, source_target_pairs={{0,2},{2,0},{1,3},{3,1},{4,6},{6,4},{5,7},{7,5},{8,10},{10,8},{9,1... | collective-permute-start | bytes 1572872 | tf_op jit(solution)/shard_map/ppermute | solution.py:405
  51.1 0.8 broadcast_in_dim.7.refs_1_
  52.0 1.2 %shard_map.96 = (f32[8,128]{1,0:T(8,128)S(1)}, bf16[64,1024]{1,0:T(8,128)(2,1)S(1)}, bf16[64,1024]{1,0:T(8,128)(2,1)S(1)}, bf16[64,1024]{1,0:T(8,128)(2,1)S(1)},...) custom-call(f32[8,128]{1,0:T(8,128)S(1)} %get-tuple-element.86.refs_0_, ...), custom_call_target="tpu_custom_call", output_to_operand_aliasing={{0}: (0, {}), {5}: (1, {})} | custom-call | flops 1 | bytes 1 | tf_op jit(solution)/shard_map/pallas_call | solution.py:129
  53.2 3.4 %collective-permute-start.22 = (bf16[64,1024]{1,0:T(8,128)(2,1)S(1)}, bf16[64,1024]{1,0:T(8,128)(2,1)S(1)}, u32[]{:S(2)}, u32[]{:S(2)}) collective-permute-start(bf16[64,1024]{1,0:T(8,128)(2,1)S(1)} %get-tuple-element.90.refs_2_), channel_id=1, source_target_pairs={{0,1},{1,0},{2,3},{3,2},{4,5},{5,4},{6,7},{7,6},{8,9},{9,8},{10,11... | collective-permute-start | bytes 393224 | tf_op jit(solution)/shard_map/ppermute | solution.py:414
  56.7 0.4 collective-permute-start.24
  57.2 0.4 collective-permute-done.22.refs_6_
  57.6 0.4 collective-permute-done.23.refs_7_
  58.0 0.2 collective-permute-done.24.refs_8_
  58.2 0.3 collective-permute-done.25.refs_9_
  58.5 3.9 %shard_map.97 = (f32[8,128]{1,0:T(8,128)S(1)}, bf16[6,32,512]{2,1,0:T(8,128)(2,1)S(1)}, bf16[6,32,512]{2,1,0:T(8,128)(2,1)S(1)}, bf16[6,32,512]{2,1,0:T(8,128)(2,1)S(1)}, bf16[6,32,512]{2,1,0:T(8,128)(2,1)S(1)}) custom-call(f32[8,128]{1,0:T(8,128)S(1)} %get-tuple-element.89.refs_0_, s32[32]{0:T(128)S(1)} %copy-done.1, ...), custom_call_target="tpu_custom_call", output_to_operand_aliasing={{0}: (0, {})} | custom-call | flops 1 | bytes 1 | tf_op jit(solution)/shard_map/pallas_call | solution.py:129
  62.4 1.3 %collective-permute-start.31 = (bf16[6,32,512]{2,1,0:T(8,128)(2,1)S(1)}, bf16[6,32,512]{2,1,0:T(8,128)(2,1)S(1)}, u32[]{:S(2)}, u32[]{:S(2)}) collective-permute-start(bf16[6,32,512]{2,1,0:T(8,128)(2,1)S(1)} %get-tuple-element.106), channel_id=1, source_target_pairs={{0,4},{4,0},{8,12},{12,8},{1,5},{5,1},{9,13},{13,9},{2,6},{6,2},{1... | collective-permute-start | bytes 589832 | tf_op jit(solution)/shard_map/ppermute | solution.py:424
  63.7 0.3 collective-permute-done.26.refs_5_
  63.9 1.2 %shard_map.98 = (f32[8,128]{1,0:T(8,128)S(1)}, bf16[64,1024]{1,0:T(8,128)(2,1)S(1)}, bf16[64,1024]{1,0:T(8,128)(2,1)S(1)}, bf16[64,1024]{1,0:T(8,128)(2,1)S(1)},...) custom-call(f32[8,128]{1,0:T(8,128)S(1)} %get-tuple-element.94.refs_0_, ...), custom_call_target="tpu_custom_call", output_to_operand_aliasing={{0}: (0, {}), {5}: (1, {})} | custom-call | flops 1 | bytes 1 | tf_op jit(solution)/shard_map/pallas_call | solution.py:129
  65.2 1.2 %collective-permute-start.27 = (bf16[64,1024]{1,0:T(8,128)(2,1)S(1)}, bf16[64,1024]{1,0:T(8,128)(2,1)S(1)}, u32[]{:S(2)}, u32[]{:S(2)}) collective-permute-start(bf16[64,1024]{1,0:T(8,128)(2,1)S(1)} %get-tuple-element.100.refs_2_), channel_id=1, source_target_pairs={{0,1},{1,0},{2,3},{3,2},{4,5},{5,4},{6,7},{7,6},{8,9},{9,8},{10,11... | collective-permute-start | bytes 393224 | tf_op jit(solution)/shard_map/ppermute | solution.py:414
  66.4 0.4 collective-permute-start.29
  66.9 0.4 collective-permute-done.27.refs_6_
  67.3 2.3 %collective-permute-start.32 = (bf16[6,32,512]{2,1,0:T(8,128)(2,1)S(1)}, bf16[6,32,512]{2,1,0:T(8,128)(2,1)S(1)}, u32[]{:S(2)}, u32[]{:S(2)}) collective-permute-start(bf16[6,32,512]{2,1,0:T(8,128)(2,1)S(1)} %get-tuple-element.107), channel_id=1, source_target_pairs={{0,8},{4,12},{8,0},{12,4},{1,9},{5,13},{9,1},{13,5},{2,10},{6,14},... | collective-permute-start | bytes 589832 | tf_op jit(solution)/shard_map/ppermute | solution.py:424
  69.6 0.3 collective-permute-start.33
  69.9 3.9 %shard_map.99 = (f32[8,128]{1,0:T(8,128)S(1)}, bf16[6,32,512]{2,1,0:T(8,128)(2,1)S(1)}, bf16[6,32,512]{2,1,0:T(8,128)(2,1)S(1)}, bf16[6,32,512]{2,1,0:T(8,128)(2,1)S(1)}, bf16[6,32,512]{2,1,0:T(8,128)(2,1)S(1)}) custom-call(f32[8,128]{1,0:T(8,128)S(1)} %get-tuple-element.99.refs_0_, s32[32]{0:T(128)S(1)} %copy-done.1, ...), custom_call_target="tpu_custom_call", output_to_operand_aliasing={{0}: (0, {})} | custom-call | flops 1 | bytes 1 | tf_op jit(solution)/shard_map/pallas_call | solution.py:129
  73.8 1.3 %collective-permute-start.34 = (bf16[6,32,512]{2,1,0:T(8,128)(2,1)S(1)}, bf16[6,32,512]{2,1,0:T(8,128)(2,1)S(1)}, u32[]{:S(2)}, u32[]{:S(2)}) collective-permute-start(bf16[6,32,512]{2,1,0:T(8,128)(2,1)S(1)} %get-tuple-element.112), channel_id=1, source_target_pairs={{0,4},{4,0},{8,12},{12,8},{1,5},{5,1},{9,13},{13,9},{2,6},{6,2},{1... | collective-permute-start | bytes 589832 | tf_op jit(solution)/shard_map/ppermute | solution.py:424
  75.1 1.1 %collective-permute-start.35 = (bf16[6,32,512]{2,1,0:T(8,128)(2,1)S(1)}, bf16[6,32,512]{2,1,0:T(8,128)(2,1)S(1)}, u32[]{:S(2)}, u32[]{:S(2)}) collective-permute-start(bf16[6,32,512]{2,1,0:T(8,128)(2,1)S(1)} %get-tuple-element.113), channel_id=1, source_target_pairs={{0,8},{4,12},{8,0},{12,4},{1,9},{5,13},{9,1},{13,5},{2,10},{6,14},... | collective-permute-start | bytes 589832 | tf_op jit(solution)/shard_map/ppermute | solution.py:424
  76.2 0.3 collective-permute-start.36
  76.5 6.2 %collective-permute-done.32.refs_5_ = bf16[6,32,512]{2,1,0:T(8,128)(2,1)S(1)} collective-permute-done((bf16[6,32,512]{2,1,0:T(8,128)(2,1)S(1)}, bf16[6,32,512]{2,1,0:T(8,128)(2,1)S(1)}, u32[]{:S(2)}, u32[]{:S(2)}) %collective-permute-start.32) | collective-permute-done | bytes 196640 | tf_op jit(solution)/shard_map/ppermute | solution.py:424
  82.8 13.4 %collective-permute-done.33.refs_6_ = bf16[6,32,512]{2,1,0:T(8,128)(2,1)S(1)} collective-permute-done((bf16[6,32,512]{2,1,0:T(8,128)(2,1)S(1)}, bf16[6,32,512]{2,1,0:T(8,128)(2,1)S(1)}, u32[]{:S(2)}, u32[]{:S(2)}) %collective-permute-start.33) | collective-permute-done | bytes 196640 | tf_op jit(solution)/shard_map/ppermute | solution.py:424
  96.2 2.3 %shard_map.100 = (bf16[22,64,512]{2,1,0:T(8,128)(2,1)}, f32[8,128]{1,0:T(8,128)S(1)}) custom-call(f32[8,128]{1,0:T(8,128)S(1)} %get-tuple-element.104.refs_0_, s32[32]{0:T(128)S(1)} %copy-done.1, bf16[256,512]{1,0:T(8,128)(2,1)S(1)} %copy-done, bf16[6,32,512]{2,1,0:T(8,128)(2,1)S(1)} %get-tuple-element.105.refs_3_, ...), custom_call_target="tpu_custom_call", output_to_operand_aliasing={{1}: (0, {})} | custom-call | flops 1 | bytes 1 | tf_op jit(solution)/shard_map/pallas_call | solution.py:325
  98.5 0.9 collective-permute-done.35.refs_6_
  99.4 5.2 %collective-permute-done.36.refs_7_ = bf16[6,32,512]{2,1,0:T(8,128)(2,1)S(1)} collective-permute-done((bf16[6,32,512]{2,1,0:T(8,128)(2,1)S(1)}, bf16[6,32,512]{2,1,0:T(8,128)(2,1)S(1)}, u32[]{:S(2)}, u32[]{:S(2)}) %collective-permute-start.36) | collective-permute-done | bytes 196640 | tf_op jit(solution)/shard_map/ppermute | solution.py:424
  104.6 2.3 %shard_map.101 = (bf16[22,64,512]{2,1,0:T(8,128)(2,1)}, f32[8,128]{1,0:T(8,128)S(1)}) custom-call(bf16[22,64,512]{2,1,0:T(8,128)(2,1)} %get-tuple-element.109.refs_0_, f32[8,128]{1,0:T(8,128)S(1)} %get-tuple-element.110.refs_1_, s32[32]{0:T(128)S(1)} %copy-done.1, bf16[256,512]{1,0:T(8,128)(2,1)S(1)} %copy-done, ...), custom_call_target="tpu_custom_call", output_to_operand_aliasing={{0}: (0, {}), {1}: (1, {})} | custom-call | flops 1 | bytes 1 | tf_op jit(solution)/shard_map/pallas_call | solution.py:325
  (42 shorter events, 1.0 us)
Async XLA Ops:
  1.7 7.2 %collective-permute-start = (bf16[32,4096]{1,0:T(8,128)(2,1)S(1)}, bf16[32,4096]{1,0:T(8,128)(2,1)S(1)}, u32[]{:S(2)}, u32[]{:S(2)}) collective-permute-start(bf16[32,4096]{1,0:T(8,128)(2,1)S(1)} %get-tuple-element.117.refs_1_.refs_2_), channel_id=1, source_target_pairs={{0,2},{2,0},{1,3},{3,1},{4,6},{6,4},{5,7},{7,5},{8,10},{10,8},{9,1... | collective-permute-start | bytes 786440 | tf_op jit(solution)/shard_map/ppermute | solution.py:358
  3.0 8.7 %collective-permute-start.1 = (bf16[32,4096]{1,0:T(8,128)(2,1)S(1)}, bf16[32,4096]{1,0:T(8,128)(2,1)S(1)}, u32[]{:S(2)}, u32[]{:S(2)}) collective-permute-start(bf16[32,4096]{1,0:T(8,128)(2,1)S(1)} %get-tuple-element.117.refs_1_.refs_2_), channel_id=1, source_target_pairs={{0,1},{1,0},{2,3},{3,2},{4,5},{5,4},{6,7},{7,6},{8,9},{9,8},{10,11... | collective-permute-start | bytes 786440 | tf_op jit(solution)/shard_map/ppermute | solution.py:359
  8.9 2.8 %collective-permute-start.2 = (bf16[32,4096]{1,0:T(8,128)(2,1)S(1)}, bf16[32,4096]{1,0:T(8,128)(2,1)S(1)}, u32[]{:S(2)}, u32[]{:S(2)}) collective-permute-start(bf16[32,4096]{1,0:T(8,128)(2,1)S(1)} %collective-permute-done.refs_2_.refs_3_), channel_id=1, source_target_pairs={{0,1},{1,0},{2,3},{3,2},{4,5},{5,4},{6,7},{7,6},{8,9},{9,8},{10,11... | collective-permute-start | bytes 786440 | tf_op jit(solution)/shard_map/ppermute | solution.py:360
  10.5 7.9 %collective-permute-start.4 = (bf16[32,4096]{1,0:T(8,128)(2,1)S(1)}, bf16[32,4096]{1,0:T(8,128)(2,1)S(1)}, u32[]{:S(2)}, u32[]{:S(2)}) collective-permute-start(bf16[32,4096]{1,0:T(8,128)(2,1)S(1)} %get-tuple-element.116.refs_1_.refs_2_), channel_id=1, source_target_pairs={{0,2},{2,0},{1,3},{3,1},{4,6},{6,4},{5,7},{7,5},{8,10},{10,8},{9,1... | collective-permute-start | bytes 786440 | tf_op jit(solution)/shard_map/ppermute | solution.py:358
  11.7 9.9 %copy-start.2 = (f32[64]{0:T(128)S(1)}, f32[64]{0:T(128)}, u32[]{:S(2)}) copy-start(f32[64]{0:T(128)} %param.10) | copy-start | bytes 772
  11.7 9.9 %copy-start.3 = (f32[64]{0:T(128)S(1)}, f32[64]{0:T(128)}, u32[]{:S(2)}) copy-start(f32[64]{0:T(128)} %param.12) | copy-start | bytes 772
  11.7 9.9 %copy-start.4 = (f32[64]{0:T(128)S(1)}, f32[64]{0:T(128)}, u32[]{:S(2)}) copy-start(f32[64]{0:T(128)} %param.11) | copy-start | bytes 772
  15.0 4.3 %collective-permute-start.3 = (bf16[64,512]{1,0:T(8,128)(2,1)S(1)}, bf16[64,512]{1,0:T(8,128)(2,1)S(1)}, u32[]{:S(2)}, u32[]{:S(2)}) collective-permute-start(bf16[64,512]{1,0:T(8,128)(2,1)S(1)} %get-tuple-element.61), channel_id=1, source_target_pairs={{0,4},{4,0},{8,12},{12,8},{1,5},{5,1},{9,13},{13,9},{2,6},{6,2},{1... | collective-permute-start | bytes 196616 | tf_op jit(solution)/shard_map/ppermute | solution.py:386
  15.2 6.4 %collective-permute-start.5 = (bf16[32,4096]{1,0:T(8,128)(2,1)S(1)}, bf16[32,4096]{1,0:T(8,128)(2,1)S(1)}, u32[]{:S(2)}, u32[]{:S(2)}) collective-permute-start(bf16[32,4096]{1,0:T(8,128)(2,1)S(1)} %get-tuple-element.116.refs_1_.refs_2_), channel_id=1, source_target_pairs={{0,1},{1,0},{2,3},{3,2},{4,5},{5,4},{6,7},{7,6},{8,9},{9,8},{10,11... | collective-permute-start | bytes 786440 | tf_op jit(solution)/shard_map/ppermute | solution.py:359
  18.4 3.2 %collective-permute-start.6 = (bf16[32,4096]{1,0:T(8,128)(2,1)S(1)}, bf16[32,4096]{1,0:T(8,128)(2,1)S(1)}, u32[]{:S(2)}, u32[]{:S(2)}) collective-permute-start(bf16[32,4096]{1,0:T(8,128)(2,1)S(1)} %collective-permute-done.4.refs_2_.refs_3_), channel_id=1, source_target_pairs={{0,1},{1,0},{2,3},{3,2},{4,5},{5,4},{6,7},{7,6},{8,9},{9,8},{10,11... | collective-permute-start | bytes 786440 | tf_op jit(solution)/shard_map/ppermute | solution.py:360
  19.2 5.9 %collective-permute-start.7 = (bf16[64,512]{1,0:T(8,128)(2,1)S(1)}, bf16[64,512]{1,0:T(8,128)(2,1)S(1)}, u32[]{:S(2)}, u32[]{:S(2)}) collective-permute-start(bf16[64,512]{1,0:T(8,128)(2,1)S(1)} %get-tuple-element.64.refs_2_), channel_id=1, source_target_pairs={{0,8},{4,12},{8,0},{12,4},{1,9},{5,13},{9,1},{13,5},{2,10},{6,14},... | collective-permute-start | bytes 196616 | tf_op jit(solution)/shard_map/ppermute | solution.py:389
  21.6 3.5 %copy-start = (bf16[256,512]{1,0:T(8,128)(2,1)S(1)}, bf16[256,512]{1,0:T(8,128)(2,1)}, u32[]{:S(2)}) copy-start(bf16[256,512]{1,0:T(8,128)(2,1)} %refs_3_.1) | copy-start | bytes 786436
  24.9 3.2 %collective-permute-start.8 = (bf16[64,512]{1,0:T(8,128)(2,1)S(1)}, bf16[64,512]{1,0:T(8,128)(2,1)S(1)}, u32[]{:S(2)}, u32[]{:S(2)}) collective-permute-start(bf16[64,512]{1,0:T(8,128)(2,1)S(1)} %get-tuple-element.67), channel_id=1, source_target_pairs={{0,4},{4,0},{8,12},{12,8},{1,5},{5,1},{9,13},{13,9},{2,6},{6,2},{1... | collective-permute-start | bytes 196616 | tf_op jit(solution)/shard_map/ppermute | solution.py:386
  25.2 4.6 %collective-permute-start.10 = (bf16[64,512]{1,0:T(8,128)(2,1)S(1)}, bf16[64,512]{1,0:T(8,128)(2,1)S(1)}, u32[]{:S(2)}, u32[]{:S(2)}) collective-permute-start(bf16[64,512]{1,0:T(8,128)(2,1)S(1)} %get-tuple-element.69.refs_2_), channel_id=1, source_target_pairs={{0,4},{4,0},{8,12},{12,8},{1,5},{5,1},{9,13},{13,9},{2,6},{6,2},{1... | collective-permute-start | bytes 196616 | tf_op jit(solution)/shard_map/ppermute | solution.py:393
  26.7 3.1 %collective-permute-start.9 = (f32[64,3]{1,0:T(8,128)S(1)}, f32[64,3]{1,0:T(8,128)S(1)}, u32[]{:S(2)}, u32[]{:S(2)}) collective-permute-start(f32[64,3]{1,0:T(8,128)S(1)} %copy.31.refs_6_), channel_id=1, source_target_pairs={{0,2},{2,0},{1,3},{3,1},{4,6},{6,4},{5,7},{7,5},{8,10},{10,8},{9,1... | collective-permute-start | bytes 2312 | tf_op jit(solution)/shard_map/ppermute | solution.py:366
  32.4 3.6 %collective-permute-start.11 = (bf16[64,1024]{1,0:T(8,128)(2,1)S(1)}, bf16[64,1024]{1,0:T(8,128)(2,1)S(1)}, u32[]{:S(2)}, u32[]{:S(2)}) collective-permute-start(bf16[64,1024]{1,0:T(8,128)(2,1)S(1)} %get-tuple-element.72), channel_id=1, source_target_pairs={{0,1},{1,0},{2,3},{3,2},{4,5},{5,4},{6,7},{7,6},{8,9},{9,8},{10,11... | collective-permute-start | bytes 393224 | tf_op jit(solution)/shard_map/ppermute | solution.py:402
  34.6 1.4 %collective-permute-start.12 = (bf16[64,1024]{1,0:T(8,128)(2,1)S(1)}, bf16[64,1024]{1,0:T(8,128)(2,1)S(1)}, u32[]{:S(2)}, u32[]{:S(2)}) collective-permute-start(bf16[64,1024]{1,0:T(8,128)(2,1)S(1)} %get-tuple-element.73), channel_id=1, source_target_pairs={{0,1},{1,0},{2,3},{3,2},{4,5},{5,4},{6,7},{7,6},{8,9},{9,8},{10,11... | collective-permute-start | bytes 393224 | tf_op jit(solution)/shard_map/ppermute | solution.py:402
  34.7 1.5 %collective-permute-start.13 = (bf16[64,1024]{1,0:T(8,128)(2,1)S(1)}, bf16[64,1024]{1,0:T(8,128)(2,1)S(1)}, u32[]{:S(2)}, u32[]{:S(2)}) collective-permute-start(bf16[64,1024]{1,0:T(8,128)(2,1)S(1)} %get-tuple-element.74), channel_id=1, source_target_pairs={{0,1},{1,0},{2,3},{3,2},{4,5},{5,4},{6,7},{7,6},{8,9},{9,8},{10,11... | collective-permute-start | bytes 393224 | tf_op jit(solution)/shard_map/ppermute | solution.py:402
  35.1 1.3 %collective-permute-start.14 = (bf16[64,1024]{1,0:T(8,128)(2,1)S(1)}, bf16[64,1024]{1,0:T(8,128)(2,1)S(1)}, u32[]{:S(2)}, u32[]{:S(2)}) collective-permute-start(bf16[64,1024]{1,0:T(8,128)(2,1)S(1)} %get-tuple-element.75), channel_id=1, source_target_pairs={{0,1},{1,0},{2,3},{3,2},{4,5},{5,4},{6,7},{7,6},{8,9},{9,8},{10,11... | collective-permute-start | bytes 393224 | tf_op jit(solution)/shard_map/ppermute | solution.py:402
  35.2 4.1 %collective-permute-start.15 = (bf16[64,512]{1,0:T(8,128)(2,1)S(1)}, bf16[64,512]{1,0:T(8,128)(2,1)S(1)}, u32[]{:S(2)}, u32[]{:S(2)}) collective-permute-start(bf16[64,512]{1,0:T(8,128)(2,1)S(1)} %get-tuple-element.77.refs_2_), channel_id=1, source_target_pairs={{0,8},{4,12},{8,0},{12,4},{1,9},{5,13},{9,1},{13,5},{2,10},{6,14},... | collective-permute-start | bytes 196616 | tf_op jit(solution)/shard_map/ppermute | solution.py:389
  39.3 3.2 %collective-permute-start.16 = (bf16[64,512]{1,0:T(8,128)(2,1)S(1)}, bf16[64,512]{1,0:T(8,128)(2,1)S(1)}, u32[]{:S(2)}, u32[]{:S(2)}) collective-permute-start(bf16[64,512]{1,0:T(8,128)(2,1)S(1)} %get-tuple-element.79.refs_2_), channel_id=1, source_target_pairs={{0,4},{4,0},{8,12},{12,8},{1,5},{5,1},{9,13},{13,9},{2,6},{6,2},{1... | collective-permute-start | bytes 196616 | tf_op jit(solution)/shard_map/ppermute | solution.py:393
  39.5 11.7 %collective-permute-start.21 = (bf16[64,4096]{1,0:T(8,128)(2,1)S(1)}, bf16[64,4096]{1,0:T(8,128)(2,1)S(1)}, u32[]{:S(2)}, u32[]{:S(2)}) collective-permute-start(bf16[64,4096]{1,0:T(8,128)(2,1)S(1)} %get-tuple-element.88), channel_id=1, source_target_pairs={{0,2},{2,0},{1,3},{3,1},{4,6},{6,4},{5,7},{7,5},{8,10},{10,8},{9,1... | collective-permute-start | bytes 1572872 | tf_op jit(solution)/shard_map/ppermute | solution.py:405
  45.2 3.7 %collective-permute-start.17 = (bf16[64,1024]{1,0:T(8,128)(2,1)S(1)}, bf16[64,1024]{1,0:T(8,128)(2,1)S(1)}, u32[]{:S(2)}, u32[]{:S(2)}) collective-permute-start(bf16[64,1024]{1,0:T(8,128)(2,1)S(1)} %get-tuple-element.82), channel_id=1, source_target_pairs={{0,1},{1,0},{2,3},{3,2},{4,5},{5,4},{6,7},{7,6},{8,9},{9,8},{10,11... | collective-permute-start | bytes 393224 | tf_op jit(solution)/shard_map/ppermute | solution.py:402
  47.9 1.3 %collective-permute-start.18 = (bf16[64,1024]{1,0:T(8,128)(2,1)S(1)}, bf16[64,1024]{1,0:T(8,128)(2,1)S(1)}, u32[]{:S(2)}, u32[]{:S(2)}) collective-permute-start(bf16[64,1024]{1,0:T(8,128)(2,1)S(1)} %get-tuple-element.83), channel_id=1, source_target_pairs={{0,1},{1,0},{2,3},{3,2},{4,5},{5,4},{6,7},{7,6},{8,9},{9,8},{10,11... | collective-permute-start | bytes 393224 | tf_op jit(solution)/shard_map/ppermute | solution.py:402
  48.0 1.5 %collective-permute-start.19 = (bf16[64,1024]{1,0:T(8,128)(2,1)S(1)}, bf16[64,1024]{1,0:T(8,128)(2,1)S(1)}, u32[]{:S(2)}, u32[]{:S(2)}) collective-permute-start(bf16[64,1024]{1,0:T(8,128)(2,1)S(1)} %get-tuple-element.84), channel_id=1, source_target_pairs={{0,1},{1,0},{2,3},{3,2},{4,5},{5,4},{6,7},{7,6},{8,9},{9,8},{10,11... | collective-permute-start | bytes 393224 | tf_op jit(solution)/shard_map/ppermute | solution.py:402
  48.4 1.3 %collective-permute-start.20 = (bf16[64,1024]{1,0:T(8,128)(2,1)S(1)}, bf16[64,1024]{1,0:T(8,128)(2,1)S(1)}, u32[]{:S(2)}, u32[]{:S(2)}) collective-permute-start(bf16[64,1024]{1,0:T(8,128)(2,1)S(1)} %get-tuple-element.85), channel_id=1, source_target_pairs={{0,1},{1,0},{2,3},{3,2},{4,5},{5,4},{6,7},{7,6},{8,9},{9,8},{10,11... | collective-permute-start | bytes 393224 | tf_op jit(solution)/shard_map/ppermute | solution.py:402
  49.9 14.1 %collective-permute-start.26 = (bf16[64,4096]{1,0:T(8,128)(2,1)S(1)}, bf16[64,4096]{1,0:T(8,128)(2,1)S(1)}, u32[]{:S(2)}, u32[]{:S(2)}) collective-permute-start(bf16[64,4096]{1,0:T(8,128)(2,1)S(1)} %get-tuple-element.97), channel_id=1, source_target_pairs={{0,2},{2,0},{1,3},{3,1},{4,6},{6,4},{5,7},{7,5},{8,10},{10,8},{9,1... | collective-permute-start | bytes 1572872 | tf_op jit(solution)/shard_map/ppermute | solution.py:405
  52.0 6.5 %copy-start.1 = (s32[32]{0:T(128)S(1)}, s32[32]{0:T(128)}, u32[]{:S(2)}) copy-start(s32[32]{0:T(128)} %refs_2_.3) | copy-start | bytes 388
  53.2 4.4 %collective-permute-start.22 = (bf16[64,1024]{1,0:T(8,128)(2,1)S(1)}, bf16[64,1024]{1,0:T(8,128)(2,1)S(1)}, u32[]{:S(2)}, u32[]{:S(2)}) collective-permute-start(bf16[64,1024]{1,0:T(8,128)(2,1)S(1)} %get-tuple-element.90.refs_2_), channel_id=1, source_target_pairs={{0,1},{1,0},{2,3},{3,2},{4,5},{5,4},{6,7},{7,6},{8,9},{9,8},{10,11... | collective-permute-start | bytes 393224 | tf_op jit(solution)/shard_map/ppermute | solution.py:414
  56.6 1.3 %collective-permute-start.23 = (bf16[64,1024]{1,0:T(8,128)(2,1)S(1)}, bf16[64,1024]{1,0:T(8,128)(2,1)S(1)}, u32[]{:S(2)}, u32[]{:S(2)}) collective-permute-start(bf16[64,1024]{1,0:T(8,128)(2,1)S(1)} %get-tuple-element.91.refs_3_), channel_id=1, source_target_pairs={{0,1},{1,0},{2,3},{3,2},{4,5},{5,4},{6,7},{7,6},{8,9},{9,8},{10,11... | collective-permute-start | bytes 393224 | tf_op jit(solution)/shard_map/ppermute | solution.py:414
  56.7 1.5 %collective-permute-start.24 = (bf16[64,1024]{1,0:T(8,128)(2,1)S(1)}, bf16[64,1024]{1,0:T(8,128)(2,1)S(1)}, u32[]{:S(2)}, u32[]{:S(2)}) collective-permute-start(bf16[64,1024]{1,0:T(8,128)(2,1)S(1)} %get-tuple-element.92.refs_4_), channel_id=1, source_target_pairs={{0,1},{1,0},{2,3},{3,2},{4,5},{5,4},{6,7},{7,6},{8,9},{9,8},{10,11... | collective-permute-start | bytes 393224 | tf_op jit(solution)/shard_map/ppermute | solution.py:414
  57.1 1.3 %collective-permute-start.25 = (bf16[64,1024]{1,0:T(8,128)(2,1)S(1)}, bf16[64,1024]{1,0:T(8,128)(2,1)S(1)}, u32[]{:S(2)}, u32[]{:S(2)}) collective-permute-start(bf16[64,1024]{1,0:T(8,128)(2,1)S(1)} %get-tuple-element.93.refs_5_), channel_id=1, source_target_pairs={{0,1},{1,0},{2,3},{3,2},{4,5},{5,4},{6,7},{7,6},{8,9},{9,8},{10,11... | collective-permute-start | bytes 393224 | tf_op jit(solution)/shard_map/ppermute | solution.py:414
  62.4 13.9 %collective-permute-start.31 = (bf16[6,32,512]{2,1,0:T(8,128)(2,1)S(1)}, bf16[6,32,512]{2,1,0:T(8,128)(2,1)S(1)}, u32[]{:S(2)}, u32[]{:S(2)}) collective-permute-start(bf16[6,32,512]{2,1,0:T(8,128)(2,1)S(1)} %get-tuple-element.106), channel_id=1, source_target_pairs={{0,4},{4,0},{8,12},{12,8},{1,5},{5,1},{9,13},{13,9},{2,6},{6,2},{1... | collective-permute-start | bytes 589832 | tf_op jit(solution)/shard_map/ppermute | solution.py:424
  65.2 2.2 %collective-permute-start.27 = (bf16[64,1024]{1,0:T(8,128)(2,1)S(1)}, bf16[64,1024]{1,0:T(8,128)(2,1)S(1)}, u32[]{:S(2)}, u32[]{:S(2)}) collective-permute-start(bf16[64,1024]{1,0:T(8,128)(2,1)S(1)} %get-tuple-element.100.refs_2_), channel_id=1, source_target_pairs={{0,1},{1,0},{2,3},{3,2},{4,5},{5,4},{6,7},{7,6},{8,9},{9,8},{10,11... | collective-permute-start | bytes 393224 | tf_op jit(solution)/shard_map/ppermute | solution.py:414
  66.3 3.3 %collective-permute-start.28 = (bf16[64,1024]{1,0:T(8,128)(2,1)S(1)}, bf16[64,1024]{1,0:T(8,128)(2,1)S(1)}, u32[]{:S(2)}, u32[]{:S(2)}) collective-permute-start(bf16[64,1024]{1,0:T(8,128)(2,1)S(1)} %get-tuple-element.101.refs_3_), channel_id=1, source_target_pairs={{0,1},{1,0},{2,3},{3,2},{4,5},{5,4},{6,7},{7,6},{8,9},{9,8},{10,11... | collective-permute-start | bytes 393224 | tf_op jit(solution)/shard_map/ppermute | solution.py:414
  66.4 3.5 %collective-permute-start.29 = (bf16[64,1024]{1,0:T(8,128)(2,1)S(1)}, bf16[64,1024]{1,0:T(8,128)(2,1)S(1)}, u32[]{:S(2)}, u32[]{:S(2)}) collective-permute-start(bf16[64,1024]{1,0:T(8,128)(2,1)S(1)} %get-tuple-element.102.refs_4_), channel_id=1, source_target_pairs={{0,1},{1,0},{2,3},{3,2},{4,5},{5,4},{6,7},{7,6},{8,9},{9,8},{10,11... | collective-permute-start | bytes 393224 | tf_op jit(solution)/shard_map/ppermute | solution.py:414
  66.9 3.1 %collective-permute-start.30 = (bf16[64,1024]{1,0:T(8,128)(2,1)S(1)}, bf16[64,1024]{1,0:T(8,128)(2,1)S(1)}, u32[]{:S(2)}, u32[]{:S(2)}) collective-permute-start(bf16[64,1024]{1,0:T(8,128)(2,1)S(1)} %get-tuple-element.103.refs_5_), channel_id=1, source_target_pairs={{0,1},{1,0},{2,3},{3,2},{4,5},{5,4},{6,7},{7,6},{8,9},{9,8},{10,11... | collective-permute-start | bytes 393224 | tf_op jit(solution)/shard_map/ppermute | solution.py:414
  67.3 15.4 %collective-permute-start.32 = (bf16[6,32,512]{2,1,0:T(8,128)(2,1)S(1)}, bf16[6,32,512]{2,1,0:T(8,128)(2,1)S(1)}, u32[]{:S(2)}, u32[]{:S(2)}) collective-permute-start(bf16[6,32,512]{2,1,0:T(8,128)(2,1)S(1)} %get-tuple-element.107), channel_id=1, source_target_pairs={{0,8},{4,12},{8,0},{12,4},{1,9},{5,13},{9,1},{13,5},{2,10},{6,14},... | collective-permute-start | bytes 589832 | tf_op jit(solution)/shard_map/ppermute | solution.py:424
  69.6 26.6 %collective-permute-start.33 = (bf16[6,32,512]{2,1,0:T(8,128)(2,1)S(1)}, bf16[6,32,512]{2,1,0:T(8,128)(2,1)S(1)}, u32[]{:S(2)}, u32[]{:S(2)}) collective-permute-start(bf16[6,32,512]{2,1,0:T(8,128)(2,1)S(1)} %get-tuple-element.108), channel_id=1, source_target_pairs={{0,12},{4,8},{8,4},{12,0},{1,13},{5,9},{9,5},{13,1},{2,14},{6,10},... | collective-permute-start | bytes 589832 | tf_op jit(solution)/shard_map/ppermute | solution.py:424
  73.8 24.7 %collective-permute-start.34 = (bf16[6,32,512]{2,1,0:T(8,128)(2,1)S(1)}, bf16[6,32,512]{2,1,0:T(8,128)(2,1)S(1)}, u32[]{:S(2)}, u32[]{:S(2)}) collective-permute-start(bf16[6,32,512]{2,1,0:T(8,128)(2,1)S(1)} %get-tuple-element.112), channel_id=1, source_target_pairs={{0,4},{4,0},{8,12},{12,8},{1,5},{5,1},{9,13},{13,9},{2,6},{6,2},{1... | collective-permute-start | bytes 589832 | tf_op jit(solution)/shard_map/ppermute | solution.py:424
  75.1 24.3 %collective-permute-start.35 = (bf16[6,32,512]{2,1,0:T(8,128)(2,1)S(1)}, bf16[6,32,512]{2,1,0:T(8,128)(2,1)S(1)}, u32[]{:S(2)}, u32[]{:S(2)}) collective-permute-start(bf16[6,32,512]{2,1,0:T(8,128)(2,1)S(1)} %get-tuple-element.113), channel_id=1, source_target_pairs={{0,8},{4,12},{8,0},{12,4},{1,9},{5,13},{9,1},{13,5},{2,10},{6,14},... | collective-permute-start | bytes 589832 | tf_op jit(solution)/shard_map/ppermute | solution.py:424
  76.2 28.4 %collective-permute-start.36 = (bf16[6,32,512]{2,1,0:T(8,128)(2,1)S(1)}, bf16[6,32,512]{2,1,0:T(8,128)(2,1)S(1)}, u32[]{:S(2)}, u32[]{:S(2)}) collective-permute-start(bf16[6,32,512]{2,1,0:T(8,128)(2,1)S(1)} %get-tuple-element.114), channel_id=1, source_target_pairs={{0,12},{4,8},{8,4},{12,0},{1,13},{5,9},{9,5},{13,1},{2,14},{6,10},... | collective-permute-start | bytes 589832 | tf_op jit(solution)/shard_map/ppermute | solution.py:424

commit v3 on v2

--- a/solution.py
+++ b/solution.py
@@ -13,10 +13,13 @@
 SPAN = 6
 LOADS = 2
 SPLIT = 4
+SCORE_SPLIT = 8
+TOGETHER = ()
 CHAIN = True
+RESIDENT = True
 FIRST = (1, 1)
 SECOND = ((0, 0, 1, 1), (1, 0, 1, 1))
-ORDER = (('pred', 0), ('two', 0), ('pred', 1), ('res', 0), ('two', 1), ('score', 0), ('chip', 0), ('res', 1), ('score', 1), ('chip', 1), ('den', 0), ('chrom', 0), ('den', 1), ('chrom', 1), ('leave', 0), ('leave', 1))
+ORDER = (('pred', 0), ('two', 0), ('pred', 1), ('res', 0), ('two', 1), ('score', 0), ('res', 1), ('chip', 0), ('score', 1), ('chip', 1), ('den', 0), ('chrom', 0), ('den', 1), ('chrom', 1), ('leave', 0), ('leave', 1))
 
 
 def denoise(estimate, scores, prior_logit, slab_var, noise_var, marker_root, people_root):
@@ -96,17 +99,19 @@
         self.genotypes = genotypes
         self.token = jnp.zeros((8, 128), jnp.float32)
 
-    def call(self, body, outs, scalars=(), args=(), streamed=False, scratch=(), after=(), into=None):
+    def call(self, body, outs, scalars=(), args=(), streamed=False, scratch=(), after=(), into=None, fresh=None):
         geno = self.genotypes
         tiles = geno.shape[1] // TILE
         after = list(after) + [into] * (into is not None)
         skip = 1 + len(after)
-        filled = [] if into is None else [jax.ShapeDtypeStruct(into.shape, into.dtype)]
+        filled = [fresh] * (fresh is not None) + [jax.ShapeDtypeStruct(one.shape, one.dtype) for one in [into] * (into is not None)]
         count = skip + len(scalars) + len(args)
 
         def kernel(*refs):
             ins, rest = list(refs[skip:count]), list(refs[count:])
-            if streamed:
+            if streamed and RESIDENT:
+                ins += [rest.pop(0), lambda tile: None]
+            elif streamed:
                 source = rest.pop(0)
                 held, arrived = rest[1 + len(outs) : 3 + len(outs)]
                 del rest[1 + len(outs) : 3 + len(outs)]
@@ -125,20 +130,20 @@
             body(*ins, *rest[1:])
 
         anywhere = pl.BlockSpec(memory_space=pl.ANY)
-        stream_scratch = [pltpu.VMEM(geno.shape, geno.dtype), pltpu.SemaphoreType.DMA((LOADS,))] if streamed else []
+        stream_scratch = [pltpu.VMEM(geno.shape, geno.dtype), pltpu.SemaphoreType.DMA((LOADS,))] if streamed and not RESIDENT else []
         token, *results = pl.pallas_call(
             kernel,
             out_shape=[jax.ShapeDtypeStruct(self.token.shape, self.token.dtype), *outs, *filled],
             in_specs=[anywhere] * skip
             + [pl.BlockSpec(memory_space=pltpu.SMEM)] * len(scalars)
             + [pl.BlockSpec(memory_space=VMEM)] * len(args)
-            + [anywhere] * streamed,
+            + [pl.BlockSpec(memory_space=VMEM) if RESIDENT else anywhere] * streamed,
             out_specs=[anywhere] + [pl.BlockSpec(memory_space=VMEM)] * len(outs) + [anywhere] * len(filled),
             scratch_shapes=stream_scratch + list(scratch),
             input_output_aliases={0: 0} if into is None else {0: 0, skip - 1: 1 + len(outs)},
             cost_estimate=pl.CostEstimate(flops=1, bytes_accessed=1, transcendentals=0),
             compiler_params=pltpu.CompilerParams(vmem_limit_bytes=12 * 2**20),
-        )(self.token, *after, *scalars, *[pltpu.with_memory_space_constraint(a, VMEM) for a in args], *[pltpu.with_memory_space_constraint(geno, pltpu.MemorySpace.HBM)] * streamed)
+        )(self.token, *after, *scalars, *[pltpu.with_memory_space_constraint(a, VMEM) for a in args], *[pltpu.with_memory_space_constraint(geno, VMEM if RESIDENT else pltpu.MemorySpace.HBM)] * streamed)
         if CHAIN:
             self.token = token
         return results
@@ -246,17 +251,19 @@
         copy.wait()
 
 
-def chrom_body(labels, *refs):
+def chrom_body(together, labels, *refs):
     own, beside, (geno, need, *outs, acc) = refs[:SPLIT], refs[SPLIT : 2 * SPLIT], refs[2 * SPLIT :]
+    if together:
+        outs = [outs[0].at[to] for to in range(outs[0].shape[0])]
     me, depth = place()
     height = own[0].shape[0] // 2
     base = depth * (geno.shape[1] // TILE)
     starts = []
     for to in range(len(outs)):
-        bits = me ^ depth ^ to
+        bits = me ^ to if together else me ^ depth ^ to
         starts.append(((bits % 2) * 2 + bits // 2) * height)
     for out in outs:
-        out[...] = jnp.zeros_like(out)
+        out[...] = jnp.zeros(out.shape, out.dtype)
     for tile in range(geno.shape[1] // TILE):
         part = columns_of(tile)
         halves = [ref[:, inner] for ref, inner in (piece_of(own, tile), piece_of(beside, tile))]
@@ -273,11 +280,14 @@
             out[slot] = acc[row_at(start, height), :].astype(out.dtype)
 
 
-def loco_body(row, shard, tiles, labels, phen, *refs):
+def loco_body(row, shard, tiles, count, labels, phen, *refs):
     *sums, out, base, acc, stage, done = refs
     height = base.shape[0]
     _, depth = place()
-    firsts = [labels[(depth ^ step) * tiles] for step in range(len(sums))]
+    if len(sums) == 1:
+        firsts, sums = [labels[step * tiles] for step in range(count)], [sums[0].at[step] for step in range(count)]
+    else:
+        firsts = [labels[(depth ^ step) * tiles] for step in range(count)]
     total = jnp.zeros(base.shape, jnp.float32)
     for part in sums:
         for slot in range(SPAN):
@@ -309,7 +319,7 @@
     lax.fori_loop(0, CHROMS, finish, 0)
 
 
-def leave_out(loco, token, shape, row, height, tiles, labels, phen, sums):
+def leave_out(loco, token, shape, row, height, tiles, count, labels, phen, sums):
     people = phen.shape[1]
     anywhere = pl.BlockSpec(memory_space=pl.ANY)
     specs = [anywhere, pl.BlockSpec(memory_space=pltpu.SMEM)] + [pl.BlockSpec(memory_space=VMEM)] * (1 + len(sums))
@@ -320,7 +330,7 @@
 
     def body(*refs):
         ins, (out, _, *scratch) = refs[before : len(args)], refs[len(args) :]
-        loco_body(row, shape[1], tiles, *ins, out, *scratch)
+        loco_body(row, shape[1], tiles, count, *ins, out, *scratch)
 
     return pl.pallas_call(
         body,
@@ -364,7 +374,7 @@
         axis=1,
     )
     coefs_across = lax.ppermute(coefs, "pp", swap)
-    steps, whole, loco = Steps(genotypes), jnp.zeros(estimate.shape, estimate.dtype), None
+    steps, whole, loco = Steps(genotypes), None, None
     before, after = [{} for _ in firsts], [{} for _ in seconds]
     f32, bf16 = jnp.float32, jnp.bfloat16
     for stage, at in ORDER:
@@ -394,7 +404,7 @@
         elif stage == "score":
             keep, *sends = steps.call(
                 functools.partial(score_body, low),
-                [pltpu.VMEM(wide, f32)] + [narrow] * SPLIT,
+                [pltpu.VMEM(wide, f32)] + [pltpu.VMEM((2 * height, mark_dev // SCORE_SPLIT), bf16)] * SCORE_SPLIT,
                 args=before[of]["res"],
                 streamed=True,
                 after=[coefs_across],
@@ -410,22 +420,27 @@
                 args=[own[of], across[of], *now["chip"], coefs, coefs_across],
                 scratch=[pltpu.SemaphoreType.DMA((SPLIT,))],
                 into=whole,
+                fresh=None if whole is not None else jax.ShapeDtypeStruct(estimate.shape, estimate.dtype),
             )
             now["den"] = updated + [lax.ppermute(one, "sub", swap) for one in updated]
         elif stage == "chrom":
+            block, together = (SPAN, height, people_dev), at in TOGETHER
             sums = steps.call(
-                chrom_body,
-                [pltpu.VMEM((SPAN, height, people_dev), bf16)] * mk_count,
+                functools.partial(chrom_body, together),
+                [pltpu.VMEM((mk_count, *block), bf16)] if together else [pltpu.VMEM(block, bf16)] * mk_count,
                 [tile_chrom],
                 now["den"],
                 streamed=True,
                 scratch=[pltpu.VMEM((4 * height, people_dev), f32)],
             )
-            now["chrom"] = [sums[0]] + [lax.ppermute(sums[step], "mk", along(step)) for step in range(1, mk_count)]
+            if together:
+                now["chrom"] = [lax.all_to_all(sums[0], "mk", 0, 0, tiled=True)]
+            else:
+                now["chrom"] = [sums[0]] + [lax.ppermute(sums[step], "mk", along(step)) for step in range(1, mk_count)]
         else:
             shape = (CHROMS, shard, people_dev)
             loco, token = leave_out(
-                loco, steps.token, shape, row, height, tile_dev, tile_chrom, phenotypes, now["chrom"]
+                loco, steps.token, shape, row, height, tile_dev, mk_count, tile_chrom, phenotypes, now["chrom"]
             )
             if CHAIN:
                 steps.token = token

time: 107 us -> 105 us (0.981)
  Pallas kernels: 26.9 us -> 16 us
  local copies, waits for them, and re-layouts: 2.02 us -> 5.57 us
  waiting for transfers between devices: 43.5 us -> 46.7 us
  starting transfers between devices: 33.6 us -> 35 us
    pallas_call x14, Pallas kernels: 22.3 us -> 11.5 us  [call(): pl.pallas_call(kernel, out_shape=[jax.ShapeDtypeStruct(self.token.shape,...]
    ppermute x2, waiting for transfers between devices: 0.28 us -> 7.93 us  [piece_steps(): now['chip'] = (chip, lax.ppermute(send, 'pp', swap))]
    unnamed x10 -> x18, local copies, waits for them, and re-layouts: 0.03 us -> 4.4 us
    ppermute x2, waiting for transfers between devices: 2.74 us -> 0.01 us  [piece_steps(): now['two'] = (two, lax.ppermute(two, 'mk', along(2)))]
    ppermute x1, waiting for transfers between devices: 1.63 us -> 0.01 us  [piece_steps(): coefs_across = lax.ppermute(coefs, 'pp', swap)]
    ppermute x2, starting transfers between devices: 3.22 us -> 4.77 us  [piece_steps(): now['two'] = (two, lax.ppermute(two, 'mk', along(2)))]
    ppermute x2, starting transfers between devices: 1.49 us -> 3.03 us  [piece_steps(): now['res'] = (residual, lax.ppermute(residual, 'mk', along(1)))]
    ppermute x6, waiting for transfers between devices: 25.8 us -> 26.9 us  [piece_steps(): lax.ppermute(sums[step], 'mk', along(step))]
  transfers between devices with their start and end apart: 37 -> 45, of which waited for: 22 -> 20; matrix products, arithmetic and copies ran while one was open for 1% -> 0% of each run, Pallas kernels for 20% -> 13%
where the time goes in v3:
time: 105 us; the launch traced here: 104 us
  waiting for transfers between devices  46.7 us (44%)
  starting transfers between devices  35 us (33%)
  Pallas kernels  16 us (15%)
  local copies, waits for them, and re-layouts  5.57 us (5%)
    ppermute x6, waiting for transfers between devices, piece_steps(): lax.ppermute(sums[step], 'mk', along(step))  26.9 us
    pallas_call x14, Pallas kernels, call(): pl.pallas_call(kernel, out_shape=[jax.ShapeDtypeStruct(self.token.shape,...  11.5 us
    ppermute x2, waiting for transfers between devices, piece_steps(): now['chip'] = (chip, lax.ppermute(send, 'pp', swap))  7.93 us
    ppermute x2, waiting for transfers between devices, piece_steps(): across = [lax.ppermute(one, 'pp', swap) for one in own]  7.13 us
    ppermute x16, starting transfers between devices, piece_steps(): now['score'] = [keep] + [lax.ppermute(send, 'sub', swap) for send in sends]  6.25 us
    ppermute x6, starting transfers between devices, piece_steps(): lax.ppermute(sums[step], 'mk', along(step))  5.95 us
    ppermute x8, starting transfers between devices, piece_steps(): now['den'] = updated + [lax.ppermute(one, 'sub', swap) for one in updated]  5.17 us
    ppermute x2, starting transfers between devices, piece_steps(): now['two'] = (two, lax.ppermute(two, 'mk', along(2)))  4.77 us
  transfers between devices with their start and end apart: 45, of which 20 were waited for; matrix products, arithmetic and copies ran while one was open for 0% of the time, Pallas kernels for 13%

profile of v3, /device:TPU:13, one launch (start us, length us, event | category | flops | bytes accessed | tf_op | source)
XLA Modules:
  0.0 104.2 jit_solution(14129999975135731839)
XLA Ops:
  0.6 1.1 %fusion = (bf16[32,4096]{1,0:T(8,128)(2,1)S(1)}, bf16[32,4096]{1,0:T(8,128)(2,1)S(1)}) fusion(bf16[64,4096]{1,0:T(8,128)(2,1)} %param.8), kind=kLoop, calls=%fused_computation.5 | loop fusion | bytes 1048576 | tf_op jit(solution)/shard_map/slice | solution.py:367
  1.7 1.3 %collective-permute-start = (bf16[32,4096]{1,0:T(8,128)(2,1)S(1)}, bf16[32,4096]{1,0:T(8,128)(2,1)S(1)}, u32[]{:S(2)}, u32[]{:S(2)}) collective-permute-start(bf16[32,4096]{1,0:T(8,128)(2,1)S(1)} %get-tuple-element.133.refs_1_), channel_id=1, source_target_pairs={{0,2},{2,0},{1,3},{3,1},{4,6},{6,4},{5,7},{7,5},{8,10},{10,8},{9,1... | collective-permute-start | bytes 786440 | tf_op jit(solution)/shard_map/ppermute | solution.py:368
  3.0 1.0 collective-permute-start.1
  3.9 5.0 %collective-permute-done.refs_2_ = bf16[32,4096]{1,0:T(8,128)(2,1)S(1)} collective-permute-done((bf16[32,4096]{1,0:T(8,128)(2,1)S(1)}, bf16[32,4096]{1,0:T(8,128)(2,1)S(1)}, u32[]{:S(2)}, u32[]{:S(2)}) %collective-permute-start) | collective-permute-done | bytes 262176 | tf_op jit(solution)/shard_map/ppermute | solution.py:368
  8.9 1.5 %collective-permute-start.2 = (bf16[32,4096]{1,0:T(8,128)(2,1)S(1)}, bf16[32,4096]{1,0:T(8,128)(2,1)S(1)}, u32[]{:S(2)}, u32[]{:S(2)}) collective-permute-start(bf16[32,4096]{1,0:T(8,128)(2,1)S(1)} %collective-permute-done.refs_2_), channel_id=1, source_target_pairs={{0,1},{1,0},{2,3},{3,2},{4,5},{5,4},{6,7},{7,6},{8,9},{9,8},{10,11... | collective-permute-start | bytes 786440 | tf_op jit(solution)/shard_map/ppermute | solution.py:370
  10.5 1.2 %collective-permute-start.4 = (bf16[32,4096]{1,0:T(8,128)(2,1)S(1)}, bf16[32,4096]{1,0:T(8,128)(2,1)S(1)}, u32[]{:S(2)}, u32[]{:S(2)}) collective-permute-start(bf16[32,4096]{1,0:T(8,128)(2,1)S(1)} %get-tuple-element.132.refs_1_.refs_2_), channel_id=1, source_target_pairs={{0,2},{2,0},{1,3},{3,1},{4,6},{6,4},{5,7},{7,5},{8,10},{10,8},{9,1... | collective-permute-start | bytes 786440 | tf_op jit(solution)/shard_map/ppermute | solution.py:368
  11.7 2.2 %copy-done = bf16[512,4096]{1,0:T(8,128)(2,1)S(1)} copy-done((bf16[512,4096]{1,0:T(8,128)(2,1)S(1)}, bf16[512,4096]{1,0:T(8,128)(2,1)}, u32[]{:S(2)}) %copy-start) | copy-done | bytes 4194328
  13.9 1.6 %shard_map.86 = (f32[8,128]{1,0:T(8,128)S(1)}, f32[64,512]{1,0:T(8,128)S(1)}, bf16[64,512]{1,0:T(8,128)(2,1)S(1)}) custom-call(f32[8,128]{1,0:T(8,128)S(1)} %broadcast_in_dim.3.refs_0_, bf16[32,4096]{1,0:T(8,128)(2,1)S(1)} %get-tuple-element.133.refs_1_, bf16[32,4096]{1,0:T(8,128)(2,1)S(1)} %collective-permute-done.refs_2_, ...), custom_call_target="tpu_custom_call", output_to_operand_aliasing={{0}: (0, {})} | custom-call | flops 1 | bytes 1 | tf_op jit(solution)/shard_map/pallas_call | solution.py:134
  15.5 0.2 collective-permute-start.3
  15.7 0.6 collective-permute-start.5
  16.3 2.1 %collective-permute-done.4.refs_2_.refs_3_ = bf16[32,4096]{1,0:T(8,128)(2,1)S(1)} collective-permute-done((bf16[32,4096]{1,0:T(8,128)(2,1)S(1)}, bf16[32,4096]{1,0:T(8,128)(2,1)S(1)}, u32[]{:S(2)}, u32[]{:S(2)}) %collective-permute-start.4) | collective-permute-done | bytes 262176 | tf_op jit(solution)/shard_map/ppermute | solution.py:368
  18.4 0.8 collective-permute-start.6
  19.2 2.4 %collective-permute-start.7 = (bf16[64,512]{1,0:T(8,128)(2,1)S(1)}, bf16[64,512]{1,0:T(8,128)(2,1)S(1)}, u32[]{:S(2)}, u32[]{:S(2)}) collective-permute-start(bf16[64,512]{1,0:T(8,128)(2,1)S(1)} %get-tuple-element.72.refs_2_), channel_id=1, source_target_pairs={{0,8},{4,12},{8,0},{12,4},{1,9},{5,13},{9,1},{13,5},{2,10},{6,14},... | collective-permute-start | bytes 196616 | tf_op jit(solution)/shard_map/ppermute | solution.py:399
  21.7 1.6 %shard_map.88 = (f32[8,128]{1,0:T(8,128)S(1)}, f32[64,512]{1,0:T(8,128)S(1)}, bf16[64,512]{1,0:T(8,128)(2,1)S(1)}) custom-call(f32[8,128]{1,0:T(8,128)S(1)} %get-tuple-element.70.refs_0_, bf16[32,4096]{1,0:T(8,128)(2,1)S(1)} %get-tuple-element.132.refs_1_.refs_2_, ...), custom_call_target="tpu_custom_call", output_to_operand_aliasing={{0}: (0, {})} | custom-call | flops 1 | bytes 1 | tf_op jit(solution)/shard_map/pallas_call | solution.py:134
  23.2 0.2 collective-permute-start.8
  23.5 1.4 %collective-permute-start.10 = (bf16[64,512]{1,0:T(8,128)(2,1)S(1)}, bf16[64,512]{1,0:T(8,128)(2,1)S(1)}, u32[]{:S(2)}, u32[]{:S(2)}) collective-permute-start(bf16[64,512]{1,0:T(8,128)(2,1)S(1)} %get-tuple-element.77.refs_2_), channel_id=1, source_target_pairs={{0,4},{4,0},{8,12},{12,8},{1,5},{5,1},{9,13},{13,9},{2,6},{6,2},{1... | collective-permute-start | bytes 196616 | tf_op jit(solution)/shard_map/ppermute | solution.py:403
  25.0 1.2 %collective-permute-start.9 = (f32[64,3]{1,0:T(8,128)S(1)}, f32[64,3]{1,0:T(8,128)S(1)}, u32[]{:S(2)}, u32[]{:S(2)}) collective-permute-start(f32[64,3]{1,0:T(8,128)S(1)} %copy.30.refs_5_.refs_6_), channel_id=1, source_target_pairs={{0,2},{2,0},{1,3},{3,1},{4,6},{6,4},{5,7},{7,5},{8,10},{10,8},{9,1... | collective-permute-start | bytes 2312 | tf_op jit(solution)/shard_map/ppermute | solution.py:376
  26.4 2.4 %collective-permute-start.11 = (bf16[64,512]{1,0:T(8,128)(2,1)S(1)}, bf16[64,512]{1,0:T(8,128)(2,1)S(1)}, u32[]{:S(2)}, u32[]{:S(2)}) collective-permute-start(bf16[64,512]{1,0:T(8,128)(2,1)S(1)} %get-tuple-element.79.refs_2_), channel_id=1, source_target_pairs={{0,8},{4,12},{8,0},{12,4},{1,9},{5,13},{9,1},{13,5},{2,10},{6,14},... | collective-permute-start | bytes 196616 | tf_op jit(solution)/shard_map/ppermute | solution.py:399
  28.8 2.2 %copy-done.2 = bf16[512,4096]{1,0:T(8,128)(2,1)S(1)} copy-done((bf16[512,4096]{1,0:T(8,128)(2,1)S(1)}, bf16[512,4096]{1,0:T(8,128)(2,1)}, u32[]{:S(2)}) %copy-start.2) | copy-done | bytes 4194328
  31.0 0.7 shard_map.91
  31.8 1.9 %collective-permute-start.12 = (bf16[64,512]{1,0:T(8,128)(2,1)S(1)}, bf16[64,512]{1,0:T(8,128)(2,1)S(1)}, u32[]{:S(2)}, u32[]{:S(2)}) collective-permute-start(bf16[64,512]{1,0:T(8,128)(2,1)S(1)} %get-tuple-element.82), channel_id=1, source_target_pairs={{0,1},{1,0},{2,3},{3,2},{4,5},{5,4},{6,7},{7,6},{8,9},{9,8},{10,11... | collective-permute-start | bytes 196616 | tf_op jit(solution)/shard_map/ppermute | solution.py:412
  33.7 0.4 collective-permute-start.14
  34.2 0.4 collective-permute-start.16
  34.7 0.2 collective-permute-start.17
  34.9 0.3 collective-permute-start.18
  35.2 0.2 collective-permute-start.19
  35.5 1.7 %collective-permute-start.20 = (bf16[64,512]{1,0:T(8,128)(2,1)S(1)}, bf16[64,512]{1,0:T(8,128)(2,1)S(1)}, u32[]{:S(2)}, u32[]{:S(2)}) collective-permute-start(bf16[64,512]{1,0:T(8,128)(2,1)S(1)} %get-tuple-element.91.refs_2_), channel_id=1, source_target_pairs={{0,4},{4,0},{8,12},{12,8},{1,5},{5,1},{9,13},{13,9},{2,6},{6,2},{1... | collective-permute-start | bytes 196616 | tf_op jit(solution)/shard_map/ppermute | solution.py:403
  37.3 0.6 collective-permute-start.29
  37.8 1.4 %collective-permute-done.20.refs_3_ = bf16[64,512]{1,0:T(8,128)(2,1)S(1)} collective-permute-done((bf16[64,512]{1,0:T(8,128)(2,1)S(1)}, bf16[64,512]{1,0:T(8,128)(2,1)S(1)}, u32[]{:S(2)}, u32[]{:S(2)}) %collective-permute-start.20) | collective-permute-done | bytes 65568 | tf_op jit(solution)/shard_map/ppermute | solution.py:403
  39.2 0.7 shard_map.94
  40.0 1.0 collective-permute-start.21
  41.0 0.4 collective-permute-start.23
  41.6 0.3 collective-permute-done.21.refs_2_
  41.9 0.4 collective-permute-start.25
  42.4 0.4 collective-permute-start.27
  42.9 0.2 collective-permute-done.25.refs_6_
  43.1 0.4 collective-permute-done.26.refs_7_
  43.6 0.4 collective-permute-done.28.refs_9_
  44.1 1.2 %collective-permute-start.34 = (bf16[64,4096]{1,0:T(8,128)(2,1)S(1)}, bf16[64,4096]{1,0:T(8,128)(2,1)S(1)}, u32[]{:S(2)}, u32[]{:S(2)}) collective-permute-start(bf16[64,4096]{1,0:T(8,128)(2,1)S(1)} %get-tuple-element.113), channel_id=1, source_target_pairs={{0,2},{2,0},{1,3},{3,1},{4,6},{6,4},{5,7},{7,5},{8,10},{10,8},{9,1... | collective-permute-start | bytes 1572872 | tf_op jit(solution)/shard_map/ppermute | solution.py:415
  45.3 5.0 %collective-permute-done.29.refs_4_ = bf16[64,4096]{1,0:T(8,128)(2,1)S(1)} collective-permute-done((bf16[64,4096]{1,0:T(8,128)(2,1)S(1)}, bf16[64,4096]{1,0:T(8,128)(2,1)S(1)}, u32[]{:S(2)}, u32[]{:S(2)}) %collective-permute-start.29) | collective-permute-done | bytes 524320 | tf_op jit(solution)/shard_map/ppermute | solution.py:415
  50.2 1.2 %shard_map.96 = (f32[8,128]{1,0:T(8,128)S(1)}, bf16[64,1024]{1,0:T(8,128)(2,1)S(1)}, bf16[64,1024]{1,0:T(8,128)(2,1)S(1)}, bf16[64,1024]{1,0:T(8,128)(2,1)S(1)},...) custom-call(f32[8,128]{1,0:T(8,128)S(1)} %get-tuple-element.102.refs_0_, ...), custom_call_target="tpu_custom_call", output_to_operand_aliasing={{0}: (0, {})} | custom-call | flops 1 | bytes 1 | tf_op jit(solution)/shard_map/pallas_call | solution.py:134
  51.5 2.5 %collective-permute-start.30 = (bf16[64,1024]{1,0:T(8,128)(2,1)S(1)}, bf16[64,1024]{1,0:T(8,128)(2,1)S(1)}, u32[]{:S(2)}, u32[]{:S(2)}) collective-permute-start(bf16[64,1024]{1,0:T(8,128)(2,1)S(1)} %get-tuple-element.106.refs_2_), channel_id=1, source_target_pairs={{0,1},{1,0},{2,3},{3,2},{4,5},{5,4},{6,7},{7,6},{8,9},{9,8},{10,11... | collective-permute-start | bytes 393224 | tf_op jit(solution)/shard_map/ppermute | solution.py:425
  54.1 0.4 collective-permute-start.32
  54.6 0.4 collective-permute-done.30.refs_6_
  55.0 0.4 collective-permute-done.31.refs_7_
  55.5 0.3 collective-permute-done.33.refs_9_
  55.9 2.1 %shard_map.97 = (f32[8,128]{1,0:T(8,128)S(1)}, bf16[6,32,512]{2,1,0:T(8,128)(2,1)S(1)}, bf16[6,32,512]{2,1,0:T(8,128)(2,1)S(1)}, bf16[6,32,512]{2,1,0:T(8,128)(2,1)S(1)}, bf16[6,32,512]{2,1,0:T(8,128)(2,1)S(1)}) custom-call(f32[8,128]{1,0:T(8,128)S(1)} %get-tuple-element.105.refs_0_, s32[32]{0:T(128)S(1)} %copy-done.5, ...), custom_call_target="tpu_custom_call", output_to_operand_aliasing={{0}: (0, {})} | custom-call | flops 1 | bytes 1 | tf_op jit(solution)/shard_map/pallas_call | solution.py:134
  57.9 0.6 collective-permute-start.39
  58.5 3.0 %collective-permute-done.34.refs_5_ = bf16[64,4096]{1,0:T(8,128)(2,1)S(1)} collective-permute-done((bf16[64,4096]{1,0:T(8,128)(2,1)S(1)}, bf16[64,4096]{1,0:T(8,128)(2,1)S(1)}, u32[]{:S(2)}, u32[]{:S(2)}) %collective-permute-start.34) | collective-permute-done | bytes 524320 | tf_op jit(solution)/shard_map/ppermute | solution.py:415
  61.5 1.2 %shard_map.98 = (f32[8,128]{1,0:T(8,128)S(1)}, bf16[64,1024]{1,0:T(8,128)(2,1)S(1)}, bf16[64,1024]{1,0:T(8,128)(2,1)S(1)}, bf16[64,1024]{1,0:T(8,128)(2,1)S(1)},...) custom-call(f32[8,128]{1,0:T(8,128)S(1)} %get-tuple-element.110.refs_0_, ...), custom_call_target="tpu_custom_call", output_to_operand_aliasing={{0}: (0, {}), {5}: (1, {})} | custom-call | flops 1 | bytes 1 | tf_op jit(solution)/shard_map/pallas_call | solution.py:134
  62.7 1.5 %collective-permute-start.35 = (bf16[64,1024]{1,0:T(8,128)(2,1)S(1)}, bf16[64,1024]{1,0:T(8,128)(2,1)S(1)}, u32[]{:S(2)}, u32[]{:S(2)}) collective-permute-start(bf16[64,1024]{1,0:T(8,128)(2,1)S(1)} %get-tuple-element.116.refs_2_), channel_id=1, source_target_pairs={{0,1},{1,0},{2,3},{3,2},{4,5},{5,4},{6,7},{7,6},{8,9},{9,8},{10,11... | collective-permute-start | bytes 393224 | tf_op jit(solution)/shard_map/ppermute | solution.py:425
  64.3 0.4 collective-permute-start.37
  64.8 0.4 collective-permute-done.35.refs_6_
  65.2 2.0 %collective-permute-start.40 = (bf16[6,32,512]{2,1,0:T(8,128)(2,1)S(1)}, bf16[6,32,512]{2,1,0:T(8,128)(2,1)S(1)}, u32[]{:S(2)}, u32[]{:S(2)}) collective-permute-start(bf16[6,32,512]{2,1,0:T(8,128)(2,1)S(1)} %get-tuple-element.123), channel_id=1, source_target_pairs={{0,8},{4,12},{8,0},{12,4},{1,9},{5,13},{9,1},{13,5},{2,10},{6,14},... | collective-permute-start | bytes 589832 | tf_op jit(solution)/shard_map/ppermute | solution.py:439
  67.3 2.1 %shard_map.99 = (f32[8,128]{1,0:T(8,128)S(1)}, bf16[6,32,512]{2,1,0:T(8,128)(2,1)S(1)}, bf16[6,32,512]{2,1,0:T(8,128)(2,1)S(1)}, bf16[6,32,512]{2,1,0:T(8,128)(2,1)S(1)}, bf16[6,32,512]{2,1,0:T(8,128)(2,1)S(1)}) custom-call(f32[8,128]{1,0:T(8,128)S(1)} %get-tuple-element.115.refs_0_, s32[32]{0:T(128)S(1)} %copy-done.5, ...), custom_call_target="tpu_custom_call", output_to_operand_aliasing={{0}: (0, {})} | custom-call | flops 1 | bytes 1 | tf_op jit(solution)/shard_map/pallas_call | solution.py:134
  69.4 1.5 %collective-permute-start.42 = (bf16[6,32,512]{2,1,0:T(8,128)(2,1)S(1)}, bf16[6,32,512]{2,1,0:T(8,128)(2,1)S(1)}, u32[]{:S(2)}, u32[]{:S(2)}) collective-permute-start(bf16[6,32,512]{2,1,0:T(8,128)(2,1)S(1)} %get-tuple-element.128), channel_id=1, source_target_pairs={{0,4},{4,0},{8,12},{12,8},{1,5},{5,1},{9,13},{13,9},{2,6},{6,2},{1... | collective-permute-start | bytes 589832 | tf_op jit(solution)/shard_map/ppermute | solution.py:439
  70.9 1.5 %collective-permute-start.43 = (bf16[6,32,512]{2,1,0:T(8,128)(2,1)S(1)}, bf16[6,32,512]{2,1,0:T(8,128)(2,1)S(1)}, u32[]{:S(2)}, u32[]{:S(2)}) collective-permute-start(bf16[6,32,512]{2,1,0:T(8,128)(2,1)S(1)} %get-tuple-element.129), channel_id=1, source_target_pairs={{0,8},{4,12},{8,0},{12,4},{1,9},{5,13},{9,1},{13,5},{2,10},{6,14},... | collective-permute-start | bytes 589832 | tf_op jit(solution)/shard_map/ppermute | solution.py:439
  72.5 0.2 collective-permute-start.44
  72.7 7.1 %collective-permute-done.40.refs_5_ = bf16[6,32,512]{2,1,0:T(8,128)(2,1)S(1)} collective-permute-done((bf16[6,32,512]{2,1,0:T(8,128)(2,1)S(1)}, bf16[6,32,512]{2,1,0:T(8,128)(2,1)S(1)}, u32[]{:S(2)}, u32[]{:S(2)}) %collective-permute-start.40) | collective-permute-done | bytes 196640 | tf_op jit(solution)/shard_map/ppermute | solution.py:439
  79.8 13.7 %collective-permute-done.41.refs_6_ = bf16[6,32,512]{2,1,0:T(8,128)(2,1)S(1)} collective-permute-done((bf16[6,32,512]{2,1,0:T(8,128)(2,1)S(1)}, bf16[6,32,512]{2,1,0:T(8,128)(2,1)S(1)}, u32[]{:S(2)}, u32[]{:S(2)}) %collective-permute-start.41) | collective-permute-done | bytes 196640 | tf_op jit(solution)/shard_map/ppermute | solution.py:439
  93.5 2.3 %shard_map.100 = (bf16[22,64,512]{2,1,0:T(8,128)(2,1)}, f32[8,128]{1,0:T(8,128)S(1)}) custom-call(f32[8,128]{1,0:T(8,128)S(1)} %get-tuple-element.120.refs_0_, s32[32]{0:T(128)S(1)} %copy-done.5, bf16[256,512]{1,0:T(8,128)(2,1)S(1)} %copy-done.4, bf16[6,32,512]{2,1,0:T(8,128)(2,1)S(1)} %get-tuple-element.121.refs_3_, ...), custom_call_target="tpu_custom_call", output_to_operand_aliasing={{1}: (0, {})} | custom-call | flops 1 | bytes 1 | tf_op jit(solution)/shard_map/pallas_call | solution.py:335
  95.8 0.8 collective-permute-done.43.refs_6_
  96.6 5.3 %collective-permute-done.44.refs_7_ = bf16[6,32,512]{2,1,0:T(8,128)(2,1)S(1)} collective-permute-done((bf16[6,32,512]{2,1,0:T(8,128)(2,1)S(1)}, bf16[6,32,512]{2,1,0:T(8,128)(2,1)S(1)}, u32[]{:S(2)}, u32[]{:S(2)}) %collective-permute-start.44) | collective-permute-done | bytes 196640 | tf_op jit(solution)/shard_map/ppermute | solution.py:439
  101.9 2.3 %shard_map.101 = (bf16[22,64,512]{2,1,0:T(8,128)(2,1)}, f32[8,128]{1,0:T(8,128)S(1)}) custom-call(bf16[22,64,512]{2,1,0:T(8,128)(2,1)} %get-tuple-element.125.refs_0_, f32[8,128]{1,0:T(8,128)S(1)} %get-tuple-element.126.refs_1_, s32[32]{0:T(128)S(1)} %copy-done.5, bf16[256,512]{1,0:T(8,128)(2,1)S(1)} %copy-done.4, ...), custom_call_target="tpu_custom_call", output_to_operand_aliasing={{0}: (0, {}), {1}: (1, {})} | custom-call | flops 1 | bytes 1 | tf_op jit(solution)/shard_map/pallas_call | solution.py:335
  (65 shorter events, 2.1 us)
Async XLA Ops:
  1.7 7.2 %collective-permute-start = (bf16[32,4096]{1,0:T(8,128)(2,1)S(1)}, bf16[32,4096]{1,0:T(8,128)(2,1)S(1)}, u32[]{:S(2)}, u32[]{:S(2)}) collective-permute-start(bf16[32,4096]{1,0:T(8,128)(2,1)S(1)} %get-tuple-element.133.refs_1_), channel_id=1, source_target_pairs={{0,2},{2,0},{1,3},{3,1},{4,6},{6,4},{5,7},{7,5},{8,10},{10,8},{9,1... | collective-permute-start | bytes 786440 | tf_op jit(solution)/shard_map/ppermute | solution.py:368
  3.0 8.7 %collective-permute-start.1 = (bf16[32,4096]{1,0:T(8,128)(2,1)S(1)}, bf16[32,4096]{1,0:T(8,128)(2,1)S(1)}, u32[]{:S(2)}, u32[]{:S(2)}) collective-permute-start(bf16[32,4096]{1,0:T(8,128)(2,1)S(1)} %get-tuple-element.133.refs_1_), channel_id=1, source_target_pairs={{0,1},{1,0},{2,3},{3,2},{4,5},{5,4},{6,7},{7,6},{8,9},{9,8},{10,11... | collective-permute-start | bytes 786440 | tf_op jit(solution)/shard_map/ppermute | solution.py:369
  8.9 2.8 %collective-permute-start.2 = (bf16[32,4096]{1,0:T(8,128)(2,1)S(1)}, bf16[32,4096]{1,0:T(8,128)(2,1)S(1)}, u32[]{:S(2)}, u32[]{:S(2)}) collective-permute-start(bf16[32,4096]{1,0:T(8,128)(2,1)S(1)} %collective-permute-done.refs_2_), channel_id=1, source_target_pairs={{0,1},{1,0},{2,3},{3,2},{4,5},{5,4},{6,7},{7,6},{8,9},{9,8},{10,11... | collective-permute-start | bytes 786440 | tf_op jit(solution)/shard_map/ppermute | solution.py:370
  10.5 7.9 %collective-permute-start.4 = (bf16[32,4096]{1,0:T(8,128)(2,1)S(1)}, bf16[32,4096]{1,0:T(8,128)(2,1)S(1)}, u32[]{:S(2)}, u32[]{:S(2)}) collective-permute-start(bf16[32,4096]{1,0:T(8,128)(2,1)S(1)} %get-tuple-element.132.refs_1_.refs_2_), channel_id=1, source_target_pairs={{0,2},{2,0},{1,3},{3,1},{4,6},{6,4},{5,7},{7,5},{8,10},{10,8},{9,1... | collective-permute-start | bytes 786440 | tf_op jit(solution)/shard_map/ppermute | solution.py:368
  11.7 2.2 %copy-start = (bf16[512,4096]{1,0:T(8,128)(2,1)S(1)}, bf16[512,4096]{1,0:T(8,128)(2,1)}, u32[]{:S(2)}) copy-start(bf16[512,4096]{1,0:T(8,128)(2,1)} %refs_10_.3) | copy-start | bytes 12582916
  13.9 7.7 %copy-start.6 = (f32[64]{0:T(128)S(1)}, f32[64]{0:T(128)}, u32[]{:S(2)}) copy-start(f32[64]{0:T(128)} %param.10) | copy-start | bytes 772
  13.9 7.7 %copy-start.7 = (f32[64]{0:T(128)S(1)}, f32[64]{0:T(128)}, u32[]{:S(2)}) copy-start(f32[64]{0:T(128)} %param.12) | copy-start | bytes 772
  13.9 7.7 %copy-start.8 = (f32[64]{0:T(128)S(1)}, f32[64]{0:T(128)}, u32[]{:S(2)}) copy-start(f32[64]{0:T(128)} %param.11) | copy-start | bytes 772
  13.9 7.7 %copy-start.1 = (bf16[512,4096]{1,0:T(8,128)(2,1)S(1)}, bf16[512,4096]{1,0:T(8,128)(2,1)}, u32[]{:S(2)}) copy-start(bf16[512,4096]{1,0:T(8,128)(2,1)} %refs_10_.3) | copy-start | bytes 12582916
  15.5 3.7 %collective-permute-start.3 = (bf16[64,512]{1,0:T(8,128)(2,1)S(1)}, bf16[64,512]{1,0:T(8,128)(2,1)S(1)}, u32[]{:S(2)}, u32[]{:S(2)}) collective-permute-start(bf16[64,512]{1,0:T(8,128)(2,1)S(1)} %get-tuple-element.69), channel_id=1, source_target_pairs={{0,4},{4,0},{8,12},{12,8},{1,5},{5,1},{9,13},{13,9},{2,6},{6,2},{1... | collective-permute-start | bytes 196616 | tf_op jit(solution)/shard_map/ppermute | solution.py:396
  15.7 5.9 %collective-permute-start.5 = (bf16[32,4096]{1,0:T(8,128)(2,1)S(1)}, bf16[32,4096]{1,0:T(8,128)(2,1)S(1)}, u32[]{:S(2)}, u32[]{:S(2)}) collective-permute-start(bf16[32,4096]{1,0:T(8,128)(2,1)S(1)} %get-tuple-element.132.refs_1_.refs_2_), channel_id=1, source_target_pairs={{0,1},{1,0},{2,3},{3,2},{4,5},{5,4},{6,7},{7,6},{8,9},{9,8},{10,11... | collective-permute-start | bytes 786440 | tf_op jit(solution)/shard_map/ppermute | solution.py:369
  18.4 3.2 %collective-permute-start.6 = (bf16[32,4096]{1,0:T(8,128)(2,1)S(1)}, bf16[32,4096]{1,0:T(8,128)(2,1)S(1)}, u32[]{:S(2)}, u32[]{:S(2)}) collective-permute-start(bf16[32,4096]{1,0:T(8,128)(2,1)S(1)} %collective-permute-done.4.refs_2_.refs_3_), channel_id=1, source_target_pairs={{0,1},{1,0},{2,3},{3,2},{4,5},{5,4},{6,7},{7,6},{8,9},{9,8},{10,11... | collective-permute-start | bytes 786440 | tf_op jit(solution)/shard_map/ppermute | solution.py:370
  19.2 4.2 %collective-permute-start.7 = (bf16[64,512]{1,0:T(8,128)(2,1)S(1)}, bf16[64,512]{1,0:T(8,128)(2,1)S(1)}, u32[]{:S(2)}, u32[]{:S(2)}) collective-permute-start(bf16[64,512]{1,0:T(8,128)(2,1)S(1)} %get-tuple-element.72.refs_2_), channel_id=1, source_target_pairs={{0,8},{4,12},{8,0},{12,4},{1,9},{5,13},{9,1},{13,5},{2,10},{6,14},... | collective-permute-start | bytes 196616 | tf_op jit(solution)/shard_map/ppermute | solution.py:399
  21.7 1.8 %copy-start.4 = (bf16[256,512]{1,0:T(8,128)(2,1)S(1)}, bf16[256,512]{1,0:T(8,128)(2,1)}, u32[]{:S(2)}) copy-start(bf16[256,512]{1,0:T(8,128)(2,1)} %refs_3_.1) | copy-start | bytes 786436
  23.2 3.2 %collective-permute-start.8 = (bf16[64,512]{1,0:T(8,128)(2,1)S(1)}, bf16[64,512]{1,0:T(8,128)(2,1)S(1)}, u32[]{:S(2)}, u32[]{:S(2)}) collective-permute-start(bf16[64,512]{1,0:T(8,128)(2,1)S(1)} %get-tuple-element.75), channel_id=1, source_target_pairs={{0,4},{4,0},{8,12},{12,8},{1,5},{5,1},{9,13},{13,9},{2,6},{6,2},{1... | collective-permute-start | bytes 196616 | tf_op jit(solution)/shard_map/ppermute | solution.py:396
  23.5 5.3 %collective-permute-start.10 = (bf16[64,512]{1,0:T(8,128)(2,1)S(1)}, bf16[64,512]{1,0:T(8,128)(2,1)S(1)}, u32[]{:S(2)}, u32[]{:S(2)}) collective-permute-start(bf16[64,512]{1,0:T(8,128)(2,1)S(1)} %get-tuple-element.77.refs_2_), channel_id=1, source_target_pairs={{0,4},{4,0},{8,12},{12,8},{1,5},{5,1},{9,13},{13,9},{2,6},{6,2},{1... | collective-permute-start | bytes 196616 | tf_op jit(solution)/shard_map/ppermute | solution.py:403
  25.0 3.9 %collective-permute-start.9 = (f32[64,3]{1,0:T(8,128)S(1)}, f32[64,3]{1,0:T(8,128)S(1)}, u32[]{:S(2)}, u32[]{:S(2)}) collective-permute-start(f32[64,3]{1,0:T(8,128)S(1)} %copy.30.refs_5_.refs_6_), channel_id=1, source_target_pairs={{0,2},{2,0},{1,3},{3,1},{4,6},{6,4},{5,7},{7,5},{8,10},{10,8},{9,1... | collective-permute-start | bytes 2312 | tf_op jit(solution)/shard_map/ppermute | solution.py:376
  26.4 7.8 %collective-permute-start.11 = (bf16[64,512]{1,0:T(8,128)(2,1)S(1)}, bf16[64,512]{1,0:T(8,128)(2,1)S(1)}, u32[]{:S(2)}, u32[]{:S(2)}) collective-permute-start(bf16[64,512]{1,0:T(8,128)(2,1)S(1)} %get-tuple-element.79.refs_2_), channel_id=1, source_target_pairs={{0,8},{4,12},{8,0},{12,4},{1,9},{5,13},{9,1},{13,5},{2,10},{6,14},... | collective-permute-start | bytes 196616 | tf_op jit(solution)/shard_map/ppermute | solution.py:399
  28.8 2.2 %copy-start.2 = (bf16[512,4096]{1,0:T(8,128)(2,1)S(1)}, bf16[512,4096]{1,0:T(8,128)(2,1)}, u32[]{:S(2)}) copy-start(bf16[512,4096]{1,0:T(8,128)(2,1)} %refs_10_.3) | copy-start | bytes 12582916
  31.0 8.2 %copy-start.3 = (bf16[512,4096]{1,0:T(8,128)(2,1)S(1)}, bf16[512,4096]{1,0:T(8,128)(2,1)}, u32[]{:S(2)}) copy-start(bf16[512,4096]{1,0:T(8,128)(2,1)} %refs_10_.3) | copy-start | bytes 12582916
  31.8 2.9 %collective-permute-start.12 = (bf16[64,512]{1,0:T(8,128)(2,1)S(1)}, bf16[64,512]{1,0:T(8,128)(2,1)S(1)}, u32[]{:S(2)}, u32[]{:S(2)}) collective-permute-start(bf16[64,512]{1,0:T(8,128)(2,1)S(1)} %get-tuple-element.82), channel_id=1, source_target_pairs={{0,1},{1,0},{2,3},{3,2},{4,5},{5,4},{6,7},{7,6},{8,9},{9,8},{10,11... | collective-permute-start | bytes 196616 | tf_op jit(solution)/shard_map/ppermute | solution.py:412
  33.6 1.3 %collective-permute-start.13 = (bf16[64,512]{1,0:T(8,128)(2,1)S(1)}, bf16[64,512]{1,0:T(8,128)(2,1)S(1)}, u32[]{:S(2)}, u32[]{:S(2)}) collective-permute-start(bf16[64,512]{1,0:T(8,128)(2,1)S(1)} %get-tuple-element.83), channel_id=1, source_target_pairs={{0,1},{1,0},{2,3},{3,2},{4,5},{5,4},{6,7},{7,6},{8,9},{9,8},{10,11... | collective-permute-start | bytes 196616 | tf_op jit(solution)/shard_map/ppermute | solution.py:412
  33.7 1.5 %collective-permute-start.14 = (bf16[64,512]{1,0:T(8,128)(2,1)S(1)}, bf16[64,512]{1,0:T(8,128)(2,1)S(1)}, u32[]{:S(2)}, u32[]{:S(2)}) collective-permute-start(bf16[64,512]{1,0:T(8,128)(2,1)S(1)} %get-tuple-element.84), channel_id=1, source_target_pairs={{0,1},{1,0},{2,3},{3,2},{4,5},{5,4},{6,7},{7,6},{8,9},{9,8},{10,11... | collective-permute-start | bytes 196616 | tf_op jit(solution)/shard_map/ppermute | solution.py:412
  34.1 1.3 %collective-permute-start.15 = (bf16[64,512]{1,0:T(8,128)(2,1)S(1)}, bf16[64,512]{1,0:T(8,128)(2,1)S(1)}, u32[]{:S(2)}, u32[]{:S(2)}) collective-permute-start(bf16[64,512]{1,0:T(8,128)(2,1)S(1)} %get-tuple-element.85), channel_id=1, source_target_pairs={{0,1},{1,0},{2,3},{3,2},{4,5},{5,4},{6,7},{7,6},{8,9},{9,8},{10,11... | collective-permute-start | bytes 196616 | tf_op jit(solution)/shard_map/ppermute | solution.py:412
  34.2 2.9 %collective-permute-start.16 = (bf16[64,512]{1,0:T(8,128)(2,1)S(1)}, bf16[64,512]{1,0:T(8,128)(2,1)S(1)}, u32[]{:S(2)}, u32[]{:S(2)}) collective-permute-start(bf16[64,512]{1,0:T(8,128)(2,1)S(1)} %get-tuple-element.86), channel_id=1, source_target_pairs={{0,1},{1,0},{2,3},{3,2},{4,5},{5,4},{6,7},{7,6},{8,9},{9,8},{10,11... | collective-permute-start | bytes 196616 | tf_op jit(solution)/shard_map/ppermute | solution.py:412
  34.7 2.5 %collective-permute-start.17 = (bf16[64,512]{1,0:T(8,128)(2,1)S(1)}, bf16[64,512]{1,0:T(8,128)(2,1)S(1)}, u32[]{:S(2)}, u32[]{:S(2)}) collective-permute-start(bf16[64,512]{1,0:T(8,128)(2,1)S(1)} %get-tuple-element.87), channel_id=1, source_target_pairs={{0,1},{1,0},{2,3},{3,2},{4,5},{5,4},{6,7},{7,6},{8,9},{9,8},{10,11... | collective-permute-start | bytes 196616 | tf_op jit(solution)/shard_map/ppermute | solution.py:412
  34.9 2.2 %collective-permute-start.18 = (bf16[64,512]{1,0:T(8,128)(2,1)S(1)}, bf16[64,512]{1,0:T(8,128)(2,1)S(1)}, u32[]{:S(2)}, u32[]{:S(2)}) collective-permute-start(bf16[64,512]{1,0:T(8,128)(2,1)S(1)} %get-tuple-element.88), channel_id=1, source_target_pairs={{0,1},{1,0},{2,3},{3,2},{4,5},{5,4},{6,7},{7,6},{8,9},{9,8},{10,11... | collective-permute-start | bytes 196616 | tf_op jit(solution)/shard_map/ppermute | solution.py:412
  35.2 2.0 %collective-permute-start.19 = (bf16[64,512]{1,0:T(8,128)(2,1)S(1)}, bf16[64,512]{1,0:T(8,128)(2,1)S(1)}, u32[]{:S(2)}, u32[]{:S(2)}) collective-permute-start(bf16[64,512]{1,0:T(8,128)(2,1)S(1)} %get-tuple-element.89), channel_id=1, source_target_pairs={{0,1},{1,0},{2,3},{3,2},{4,5},{5,4},{6,7},{7,6},{8,9},{9,8},{10,11... | collective-permute-start | bytes 196616 | tf_op jit(solution)/shard_map/ppermute | solution.py:412
  35.5 3.8 %collective-permute-start.20 = (bf16[64,512]{1,0:T(8,128)(2,1)S(1)}, bf16[64,512]{1,0:T(8,128)(2,1)S(1)}, u32[]{:S(2)}, u32[]{:S(2)}) collective-permute-start(bf16[64,512]{1,0:T(8,128)(2,1)S(1)} %get-tuple-element.91.refs_2_), channel_id=1, source_target_pairs={{0,4},{4,0},{8,12},{12,8},{1,5},{5,1},{9,13},{13,9},{2,6},{6,2},{1... | collective-permute-start | bytes 196616 | tf_op jit(solution)/shard_map/ppermute | solution.py:403
  37.3 13.0 %collective-permute-start.29 = (bf16[64,4096]{1,0:T(8,128)(2,1)S(1)}, bf16[64,4096]{1,0:T(8,128)(2,1)S(1)}, u32[]{:S(2)}, u32[]{:S(2)}) collective-permute-start(bf16[64,4096]{1,0:T(8,128)(2,1)S(1)} %get-tuple-element.104), channel_id=1, source_target_pairs={{0,2},{2,0},{1,3},{3,1},{4,6},{6,4},{5,7},{7,5},{8,10},{10,8},{9,1... | collective-permute-start | bytes 1572872 | tf_op jit(solution)/shard_map/ppermute | solution.py:415
  40.0 1.9 %collective-permute-start.21 = (bf16[64,512]{1,0:T(8,128)(2,1)S(1)}, bf16[64,512]{1,0:T(8,128)(2,1)S(1)}, u32[]{:S(2)}, u32[]{:S(2)}) collective-permute-start(bf16[64,512]{1,0:T(8,128)(2,1)S(1)} %get-tuple-element.94), channel_id=1, source_target_pairs={{0,1},{1,0},{2,3},{3,2},{4,5},{5,4},{6,7},{7,6},{8,9},{9,8},{10,11... | collective-permute-start | bytes 196616 | tf_op jit(solution)/shard_map/ppermute | solution.py:412
  41.0 1.3 %collective-permute-start.22 = (bf16[64,512]{1,0:T(8,128)(2,1)S(1)}, bf16[64,512]{1,0:T(8,128)(2,1)S(1)}, u32[]{:S(2)}, u32[]{:S(2)}) collective-permute-start(bf16[64,512]{1,0:T(8,128)(2,1)S(1)} %get-tuple-element.95), channel_id=1, source_target_pairs={{0,1},{1,0},{2,3},{3,2},{4,5},{5,4},{6,7},{7,6},{8,9},{9,8},{10,11... | collective-permute-start | bytes 196616 | tf_op jit(solution)/shard_map/ppermute | solution.py:412
  41.0 1.3 %collective-permute-start.23 = (bf16[64,512]{1,0:T(8,128)(2,1)S(1)}, bf16[64,512]{1,0:T(8,128)(2,1)S(1)}, u32[]{:S(2)}, u32[]{:S(2)}) collective-permute-start(bf16[64,512]{1,0:T(8,128)(2,1)S(1)} %get-tuple-element.96), channel_id=1, source_target_pairs={{0,1},{1,0},{2,3},{3,2},{4,5},{5,4},{6,7},{7,6},{8,9},{9,8},{10,11... | collective-permute-start | bytes 196616 | tf_op jit(solution)/shard_map/ppermute | solution.py:412
  41.5 1.3 %collective-permute-start.24 = (bf16[64,512]{1,0:T(8,128)(2,1)S(1)}, bf16[64,512]{1,0:T(8,128)(2,1)S(1)}, u32[]{:S(2)}, u32[]{:S(2)}) collective-permute-start(bf16[64,512]{1,0:T(8,128)(2,1)S(1)} %get-tuple-element.97), channel_id=1, source_target_pairs={{0,1},{1,0},{2,3},{3,2},{4,5},{5,4},{6,7},{7,6},{8,9},{9,8},{10,11... | collective-permute-start | bytes 196616 | tf_op jit(solution)/shard_map/ppermute | solution.py:412
  41.9 1.3 %collective-permute-start.25 = (bf16[64,512]{1,0:T(8,128)(2,1)S(1)}, bf16[64,512]{1,0:T(8,128)(2,1)S(1)}, u32[]{:S(2)}, u32[]{:S(2)}) collective-permute-start(bf16[64,512]{1,0:T(8,128)(2,1)S(1)} %get-tuple-element.98), channel_id=1, source_target_pairs={{0,1},{1,0},{2,3},{3,2},{4,5},{5,4},{6,7},{7,6},{8,9},{9,8},{10,11... | collective-permute-start | bytes 196616 | tf_op jit(solution)/shard_map/ppermute | solution.py:412
  42.2 1.3 %collective-permute-start.26 = (bf16[64,512]{1,0:T(8,128)(2,1)S(1)}, bf16[64,512]{1,0:T(8,128)(2,1)S(1)}, u32[]{:S(2)}, u32[]{:S(2)}) collective-permute-start(bf16[64,512]{1,0:T(8,128)(2,1)S(1)} %get-tuple-element.99), channel_id=1, source_target_pairs={{0,1},{1,0},{2,3},{3,2},{4,5},{5,4},{6,7},{7,6},{8,9},{9,8},{10,11... | collective-permute-start | bytes 196616 | tf_op jit(solution)/shard_map/ppermute | solution.py:412
  42.4 1.3 %collective-permute-start.27 = (bf16[64,512]{1,0:T(8,128)(2,1)S(1)}, bf16[64,512]{1,0:T(8,128)(2,1)S(1)}, u32[]{:S(2)}, u32[]{:S(2)}) collective-permute-start(bf16[64,512]{1,0:T(8,128)(2,1)S(1)} %get-tuple-element.100), channel_id=1, source_target_pairs={{0,1},{1,0},{2,3},{3,2},{4,5},{5,4},{6,7},{7,6},{8,9},{9,8},{10,11... | collective-permute-start | bytes 196616 | tf_op jit(solution)/shard_map/ppermute | solution.py:412
  42.7 1.3 %collective-permute-start.28 = (bf16[64,512]{1,0:T(8,128)(2,1)S(1)}, bf16[64,512]{1,0:T(8,128)(2,1)S(1)}, u32[]{:S(2)}, u32[]{:S(2)}) collective-permute-start(bf16[64,512]{1,0:T(8,128)(2,1)S(1)} %get-tuple-element.101), channel_id=1, source_target_pairs={{0,1},{1,0},{2,3},{3,2},{4,5},{5,4},{6,7},{7,6},{8,9},{9,8},{10,11... | collective-permute-start | bytes 196616 | tf_op jit(solution)/shard_map/ppermute | solution.py:412
  44.1 11.7 %copy-start.5 = (s32[32]{0:T(128)S(1)}, s32[32]{0:T(128)}, u32[]{:S(2)}) copy-start(s32[32]{0:T(128)} %refs_2_.3) | copy-start | bytes 388
  44.1 17.4 %collective-permute-start.34 = (bf16[64,4096]{1,0:T(8,128)(2,1)S(1)}, bf16[64,4096]{1,0:T(8,128)(2,1)S(1)}, u32[]{:S(2)}, u32[]{:S(2)}) collective-permute-start(bf16[64,4096]{1,0:T(8,128)(2,1)S(1)} %get-tuple-element.113), channel_id=1, source_target_pairs={{0,2},{2,0},{1,3},{3,1},{4,6},{6,4},{5,7},{7,5},{8,10},{10,8},{9,1... | collective-permute-start | bytes 1572872 | tf_op jit(solution)/shard_map/ppermute | solution.py:415
  51.5 3.5 %collective-permute-start.30 = (bf16[64,1024]{1,0:T(8,128)(2,1)S(1)}, bf16[64,1024]{1,0:T(8,128)(2,1)S(1)}, u32[]{:S(2)}, u32[]{:S(2)}) collective-permute-start(bf16[64,1024]{1,0:T(8,128)(2,1)S(1)} %get-tuple-element.106.refs_2_), channel_id=1, source_target_pairs={{0,1},{1,0},{2,3},{3,2},{4,5},{5,4},{6,7},{7,6},{8,9},{9,8},{10,11... | collective-permute-start | bytes 393224 | tf_op jit(solution)/shard_map/ppermute | solution.py:425
  54.0 1.3 %collective-permute-start.31 = (bf16[64,1024]{1,0:T(8,128)(2,1)S(1)}, bf16[64,1024]{1,0:T(8,128)(2,1)S(1)}, u32[]{:S(2)}, u32[]{:S(2)}) collective-permute-start(bf16[64,1024]{1,0:T(8,128)(2,1)S(1)} %get-tuple-element.107.refs_3_), channel_id=1, source_target_pairs={{0,1},{1,0},{2,3},{3,2},{4,5},{5,4},{6,7},{7,6},{8,9},{9,8},{10,11... | collective-permute-start | bytes 393224 | tf_op jit(solution)/shard_map/ppermute | solution.py:425
  54.1 1.5 %collective-permute-start.32 = (bf16[64,1024]{1,0:T(8,128)(2,1)S(1)}, bf16[64,1024]{1,0:T(8,128)(2,1)S(1)}, u32[]{:S(2)}, u32[]{:S(2)}) collective-permute-start(bf16[64,1024]{1,0:T(8,128)(2,1)S(1)} %get-tuple-element.108.refs_4_), channel_id=1, source_target_pairs={{0,1},{1,0},{2,3},{3,2},{4,5},{5,4},{6,7},{7,6},{8,9},{9,8},{10,11... | collective-permute-start | bytes 393224 | tf_op jit(solution)/shard_map/ppermute | solution.py:425
  54.5 1.3 %collective-permute-start.33 = (bf16[64,1024]{1,0:T(8,128)(2,1)S(1)}, bf16[64,1024]{1,0:T(8,128)(2,1)S(1)}, u32[]{:S(2)}, u32[]{:S(2)}) collective-permute-start(bf16[64,1024]{1,0:T(8,128)(2,1)S(1)} %get-tuple-element.109.refs_5_), channel_id=1, source_target_pairs={{0,1},{1,0},{2,3},{3,2},{4,5},{5,4},{6,7},{7,6},{8,9},{9,8},{10,11... | collective-permute-start | bytes 393224 | tf_op jit(solution)/shard_map/ppermute | solution.py:425
  57.9 14.5 %collective-permute-start.39 = (bf16[6,32,512]{2,1,0:T(8,128)(2,1)S(1)}, bf16[6,32,512]{2,1,0:T(8,128)(2,1)S(1)}, u32[]{:S(2)}, u32[]{:S(2)}) collective-permute-start(bf16[6,32,512]{2,1,0:T(8,128)(2,1)S(1)} %get-tuple-element.122), channel_id=1, source_target_pairs={{0,4},{4,0},{8,12},{12,8},{1,5},{5,1},{9,13},{13,9},{2,6},{6,2},{1... | collective-permute-start | bytes 589832 | tf_op jit(solution)/shard_map/ppermute | solution.py:439
  62.7 2.5 %collective-permute-start.35 = (bf16[64,1024]{1,0:T(8,128)(2,1)S(1)}, bf16[64,1024]{1,0:T(8,128)(2,1)S(1)}, u32[]{:S(2)}, u32[]{:S(2)}) collective-permute-start(bf16[64,1024]{1,0:T(8,128)(2,1)S(1)} %get-tuple-element.116.refs_2_), channel_id=1, source_target_pairs={{0,1},{1,0},{2,3},{3,2},{4,5},{5,4},{6,7},{7,6},{8,9},{9,8},{10,11... | collective-permute-start | bytes 393224 | tf_op jit(solution)/shard_map/ppermute | solution.py:425
  64.2 3.0 %collective-permute-start.36 = (bf16[64,1024]{1,0:T(8,128)(2,1)S(1)}, bf16[64,1024]{1,0:T(8,128)(2,1)S(1)}, u32[]{:S(2)}, u32[]{:S(2)}) collective-permute-start(bf16[64,1024]{1,0:T(8,128)(2,1)S(1)} %get-tuple-element.117.refs_3_), channel_id=1, source_target_pairs={{0,1},{1,0},{2,3},{3,2},{4,5},{5,4},{6,7},{7,6},{8,9},{9,8},{10,11... | collective-permute-start | bytes 393224 | tf_op jit(solution)/shard_map/ppermute | solution.py:425
  64.3 3.0 %collective-permute-start.37 = (bf16[64,1024]{1,0:T(8,128)(2,1)S(1)}, bf16[64,1024]{1,0:T(8,128)(2,1)S(1)}, u32[]{:S(2)}, u32[]{:S(2)}) collective-permute-start(bf16[64,1024]{1,0:T(8,128)(2,1)S(1)} %get-tuple-element.118.refs_4_), channel_id=1, source_target_pairs={{0,1},{1,0},{2,3},{3,2},{4,5},{5,4},{6,7},{7,6},{8,9},{9,8},{10,11... | collective-permute-start | bytes 393224 | tf_op jit(solution)/shard_map/ppermute | solution.py:425
  64.7 2.6 %collective-permute-start.38 = (bf16[64,1024]{1,0:T(8,128)(2,1)S(1)}, bf16[64,1024]{1,0:T(8,128)(2,1)S(1)}, u32[]{:S(2)}, u32[]{:S(2)}) collective-permute-start(bf16[64,1024]{1,0:T(8,128)(2,1)S(1)} %get-tuple-element.119.refs_5_), channel_id=1, source_target_pairs={{0,1},{1,0},{2,3},{3,2},{4,5},{5,4},{6,7},{7,6},{8,9},{9,8},{10,11... | collective-permute-start | bytes 393224 | tf_op jit(solution)/shard_map/ppermute | solution.py:425
  65.2 14.6 %collective-permute-start.40 = (bf16[6,32,512]{2,1,0:T(8,128)(2,1)S(1)}, bf16[6,32,512]{2,1,0:T(8,128)(2,1)S(1)}, u32[]{:S(2)}, u32[]{:S(2)}) collective-permute-start(bf16[6,32,512]{2,1,0:T(8,128)(2,1)S(1)} %get-tuple-element.123), channel_id=1, source_target_pairs={{0,8},{4,12},{8,0},{12,4},{1,9},{5,13},{9,1},{13,5},{2,10},{6,14},... | collective-permute-start | bytes 589832 | tf_op jit(solution)/shard_map/ppermute | solution.py:439
  67.2 26.2 %collective-permute-start.41 = (bf16[6,32,512]{2,1,0:T(8,128)(2,1)S(1)}, bf16[6,32,512]{2,1,0:T(8,128)(2,1)S(1)}, u32[]{:S(2)}, u32[]{:S(2)}) collective-permute-start(bf16[6,32,512]{2,1,0:T(8,128)(2,1)S(1)} %get-tuple-element.124), channel_id=1, source_target_pairs={{0,12},{4,8},{8,4},{12,0},{1,13},{5,9},{9,5},{13,1},{2,14},{6,10},... | collective-permute-start | bytes 589832 | tf_op jit(solution)/shard_map/ppermute | solution.py:439
  69.4 26.4 %collective-permute-start.42 = (bf16[6,32,512]{2,1,0:T(8,128)(2,1)S(1)}, bf16[6,32,512]{2,1,0:T(8,128)(2,1)S(1)}, u32[]{:S(2)}, u32[]{:S(2)}) collective-permute-start(bf16[6,32,512]{2,1,0:T(8,128)(2,1)S(1)} %get-tuple-element.128), channel_id=1, source_target_pairs={{0,4},{4,0},{8,12},{12,8},{1,5},{5,1},{9,13},{13,9},{2,6},{6,2},{1... | collective-permute-start | bytes 589832 | tf_op jit(solution)/shard_map/ppermute | solution.py:439
  70.9 25.7 %collective-permute-start.43 = (bf16[6,32,512]{2,1,0:T(8,128)(2,1)S(1)}, bf16[6,32,512]{2,1,0:T(8,128)(2,1)S(1)}, u32[]{:S(2)}, u32[]{:S(2)}) collective-permute-start(bf16[6,32,512]{2,1,0:T(8,128)(2,1)S(1)} %get-tuple-element.129), channel_id=1, source_target_pairs={{0,8},{4,12},{8,0},{12,4},{1,9},{5,13},{9,1},{13,5},{2,10},{6,14},... | collective-permute-start | bytes 589832 | tf_op jit(solution)/shard_map/ppermute | solution.py:439
  72.5 29.4 %collective-permute-start.44 = (bf16[6,32,512]{2,1,0:T(8,128)(2,1)S(1)}, bf16[6,32,512]{2,1,0:T(8,128)(2,1)S(1)}, u32[]{:S(2)}, u32[]{:S(2)}) collective-permute-start(bf16[6,32,512]{2,1,0:T(8,128)(2,1)S(1)} %get-tuple-element.130), channel_id=1, source_target_pairs={{0,12},{4,8},{8,4},{12,0},{1,13},{5,9},{9,5},{13,1},{2,14},{6,10},... | collective-permute-start | bytes 589832 | tf_op jit(solution)/shard_map/ppermute | solution.py:439

commit v4 on v3

--- a/solution.py
+++ b/solution.py
@@ -17,6 +17,8 @@
 TOGETHER = ()
 CHAIN = True
 RESIDENT = True
+TOUCH = False
+HOLD = True
 FIRST = (1, 1)
 SECOND = ((0, 0, 1, 1), (1, 0, 1, 1))
 ORDER = (('pred', 0), ('two', 0), ('pred', 1), ('res', 0), ('two', 1), ('score', 0), ('res', 1), ('chip', 0), ('score', 1), ('chip', 1), ('den', 0), ('chrom', 0), ('den', 1), ('chrom', 1), ('leave', 0), ('leave', 1))
@@ -102,6 +104,7 @@
     def call(self, body, outs, scalars=(), args=(), streamed=False, scratch=(), after=(), into=None, fresh=None):
         geno = self.genotypes
         tiles = geno.shape[1] // TILE
+        given = streamed or TOUCH
         after = list(after) + [into] * (into is not None)
         skip = 1 + len(after)
         filled = [fresh] * (fresh is not None) + [jax.ShapeDtypeStruct(one.shape, one.dtype) for one in [into] * (into is not None)]
@@ -109,6 +112,8 @@
 
         def kernel(*refs):
             ins, rest = list(refs[skip:count]), list(refs[count:])
+            if given and not streamed:
+                rest.pop(0)
             if streamed and RESIDENT:
                 ins += [rest.pop(0), lambda tile: None]
             elif streamed:
@@ -137,13 +142,13 @@
             in_specs=[anywhere] * skip
             + [pl.BlockSpec(memory_space=pltpu.SMEM)] * len(scalars)
             + [pl.BlockSpec(memory_space=VMEM)] * len(args)
-            + [pl.BlockSpec(memory_space=VMEM) if RESIDENT else anywhere] * streamed,
+            + [pl.BlockSpec(memory_space=VMEM) if RESIDENT else anywhere] * given,
             out_specs=[anywhere] + [pl.BlockSpec(memory_space=VMEM)] * len(outs) + [anywhere] * len(filled),
             scratch_shapes=stream_scratch + list(scratch),
             input_output_aliases={0: 0} if into is None else {0: 0, skip - 1: 1 + len(outs)},
             cost_estimate=pl.CostEstimate(flops=1, bytes_accessed=1, transcendentals=0),
             compiler_params=pltpu.CompilerParams(vmem_limit_bytes=12 * 2**20),
-        )(self.token, *after, *scalars, *[pltpu.with_memory_space_constraint(a, VMEM) for a in args], *[pltpu.with_memory_space_constraint(geno, VMEM if RESIDENT else pltpu.MemorySpace.HBM)] * streamed)
+        )(self.token, *after, *scalars, *[pltpu.with_memory_space_constraint(a, VMEM) for a in args], *[pltpu.with_memory_space_constraint(geno, VMEM if RESIDENT else pltpu.MemorySpace.HBM)] * given)
         if CHAIN:
             self.token = token
         return results
@@ -432,6 +437,7 @@
                 now["den"],
                 streamed=True,
                 scratch=[pltpu.VMEM((4 * height, people_dev), f32)],
+                after=[after[at - 1]["chrom"][2]] if at and HOLD else [],
             )
             if together:
                 now["chrom"] = [lax.all_to_all(sums[0], "mk", 0, 0, tiled=True)]

time: 105 us -> 97.5 us (0.929)
  waiting for transfers between devices: 46.7 us -> 37.5 us
  starting transfers between devices: 35 us -> 36.9 us
    ppermute x6, waiting for transfers between devices: 26.9 us -> 19.2 us  [piece_steps(): lax.ppermute(sums[step], 'mk', along(step))]
    ppermute x6, starting transfers between devices: 5.95 us -> 7.9 us  [piece_steps(): lax.ppermute(sums[step], 'mk', along(step))]
    ppermute x2, waiting for transfers between devices: 7.93 us -> 6.39 us  [piece_steps(): now['chip'] = (chip, lax.ppermute(send, 'pp', swap))]
  transfers between devices with their start and end apart: 45 -> 45, of which waited for: 20 -> 21; matrix products, arithmetic and copies ran while one was open for 0% -> 0% of each run, Pallas kernels for 13% -> 14%
where the time goes in v4:
time: 97.5 us; the launch traced here: 96.9 us
  waiting for transfers between devices  37.5 us (38%)
  starting transfers between devices  36.9 us (38%)
  Pallas kernels  16 us (16%)
  local copies, waits for them, and re-layouts  5.57 us (6%)
    ppermute x6, waiting for transfers between devices, piece_steps(): lax.ppermute(sums[step], 'mk', along(step))  19.2 us
    pallas_call x14, Pallas kernels, call(): pl.pallas_call(kernel, out_shape=[jax.ShapeDtypeStruct(self.token.shape,...  11.4 us
    ppermute x6, starting transfers between devices, piece_steps(): lax.ppermute(sums[step], 'mk', along(step))  7.9 us
    ppermute x2, waiting for transfers between devices, piece_steps(): across = [lax.ppermute(one, 'pp', swap) for one in own]  7.13 us
    ppermute x2, waiting for transfers between devices, piece_steps(): now['chip'] = (chip, lax.ppermute(send, 'pp', swap))  6.39 us
    ppermute x16, starting transfers between devices, piece_steps(): now['score'] = [keep] + [lax.ppermute(send, 'sub', swap) for send in sends]  6.25 us
    ppermute x8, starting transfers between devices, piece_steps(): now['den'] = updated + [lax.ppermute(one, 'sub', swap) for one in updated]  5.17 us
    ppermute x2, starting transfers between devices, piece_steps(): now['two'] = (two, lax.ppermute(two, 'mk', along(2)))  4.77 us
  transfers between devices with their start and end apart: 45, of which 21 were waited for; matrix products, arithmetic and copies ran while one was open for 0% of the time, Pallas kernels for 14%

profile of v4, /device:TPU:13, one launch (start us, length us, event | category | flops | bytes accessed | tf_op | source)
XLA Modules:
  0.0 96.9 jit_solution(5480061838952319396)
XLA Ops:
  0.6 1.1 %fusion = (bf16[32,4096]{1,0:T(8,128)(2,1)S(1)}, bf16[32,4096]{1,0:T(8,128)(2,1)S(1)}) fusion(bf16[64,4096]{1,0:T(8,128)(2,1)} %param.8), kind=kLoop, calls=%fused_computation.5 | loop fusion | bytes 1048576 | tf_op jit(solution)/shard_map/slice | solution.py:372
  1.7 1.3 %collective-permute-start = (bf16[32,4096]{1,0:T(8,128)(2,1)S(1)}, bf16[32,4096]{1,0:T(8,128)(2,1)S(1)}, u32[]{:S(2)}, u32[]{:S(2)}) collective-permute-start(bf16[32,4096]{1,0:T(8,128)(2,1)S(1)} %get-tuple-element.133.refs_1_), channel_id=1, source_target_pairs={{0,2},{2,0},{1,3},{3,1},{4,6},{6,4},{5,7},{7,5},{8,10},{10,8},{9,1... | collective-permute-start | bytes 786440 | tf_op jit(solution)/shard_map/ppermute | solution.py:373
  3.0 1.0 collective-permute-start.1
  3.9 5.0 %collective-permute-done.refs_2_ = bf16[32,4096]{1,0:T(8,128)(2,1)S(1)} collective-permute-done((bf16[32,4096]{1,0:T(8,128)(2,1)S(1)}, bf16[32,4096]{1,0:T(8,128)(2,1)S(1)}, u32[]{:S(2)}, u32[]{:S(2)}) %collective-permute-start) | collective-permute-done | bytes 262176 | tf_op jit(solution)/shard_map/ppermute | solution.py:373
  8.9 1.5 %collective-permute-start.2 = (bf16[32,4096]{1,0:T(8,128)(2,1)S(1)}, bf16[32,4096]{1,0:T(8,128)(2,1)S(1)}, u32[]{:S(2)}, u32[]{:S(2)}) collective-permute-start(bf16[32,4096]{1,0:T(8,128)(2,1)S(1)} %collective-permute-done.refs_2_), channel_id=1, source_target_pairs={{0,1},{1,0},{2,3},{3,2},{4,5},{5,4},{6,7},{7,6},{8,9},{9,8},{10,11... | collective-permute-start | bytes 786440 | tf_op jit(solution)/shard_map/ppermute | solution.py:375
  10.5 1.2 %collective-permute-start.4 = (bf16[32,4096]{1,0:T(8,128)(2,1)S(1)}, bf16[32,4096]{1,0:T(8,128)(2,1)S(1)}, u32[]{:S(2)}, u32[]{:S(2)}) collective-permute-start(bf16[32,4096]{1,0:T(8,128)(2,1)S(1)} %get-tuple-element.132.refs_1_.refs_2_), channel_id=1, source_target_pairs={{0,2},{2,0},{1,3},{3,1},{4,6},{6,4},{5,7},{7,5},{8,10},{10,8},{9,1... | collective-permute-start | bytes 786440 | tf_op jit(solution)/shard_map/ppermute | solution.py:373
  11.7 2.2 %copy-done = bf16[512,4096]{1,0:T(8,128)(2,1)S(1)} copy-done((bf16[512,4096]{1,0:T(8,128)(2,1)S(1)}, bf16[512,4096]{1,0:T(8,128)(2,1)}, u32[]{:S(2)}) %copy-start) | copy-done | bytes 4194328
  13.9 1.6 %shard_map.86 = (f32[8,128]{1,0:T(8,128)S(1)}, f32[64,512]{1,0:T(8,128)S(1)}, bf16[64,512]{1,0:T(8,128)(2,1)S(1)}) custom-call(f32[8,128]{1,0:T(8,128)S(1)} %broadcast_in_dim.3.refs_0_, bf16[32,4096]{1,0:T(8,128)(2,1)S(1)} %get-tuple-element.133.refs_1_, bf16[32,4096]{1,0:T(8,128)(2,1)S(1)} %collective-permute-done.refs_2_, ...), custom_call_target="tpu_custom_call", output_to_operand_aliasing={{0}: (0, {})} | custom-call | flops 1 | bytes 1 | tf_op jit(solution)/shard_map/pallas_call | solution.py:139
  15.5 0.2 collective-permute-start.3
  15.7 0.6 collective-permute-start.5
  16.3 2.1 %collective-permute-done.4.refs_2_.refs_3_ = bf16[32,4096]{1,0:T(8,128)(2,1)S(1)} collective-permute-done((bf16[32,4096]{1,0:T(8,128)(2,1)S(1)}, bf16[32,4096]{1,0:T(8,128)(2,1)S(1)}, u32[]{:S(2)}, u32[]{:S(2)}) %collective-permute-start.4) | collective-permute-done | bytes 262176 | tf_op jit(solution)/shard_map/ppermute | solution.py:373
  18.4 0.8 collective-permute-start.6
  19.2 2.4 %collective-permute-start.7 = (bf16[64,512]{1,0:T(8,128)(2,1)S(1)}, bf16[64,512]{1,0:T(8,128)(2,1)S(1)}, u32[]{:S(2)}, u32[]{:S(2)}) collective-permute-start(bf16[64,512]{1,0:T(8,128)(2,1)S(1)} %get-tuple-element.72.refs_2_), channel_id=1, source_target_pairs={{0,8},{4,12},{8,0},{12,4},{1,9},{5,13},{9,1},{13,5},{2,10},{6,14},... | collective-permute-start | bytes 196616 | tf_op jit(solution)/shard_map/ppermute | solution.py:404
  21.7 1.6 %shard_map.88 = (f32[8,128]{1,0:T(8,128)S(1)}, f32[64,512]{1,0:T(8,128)S(1)}, bf16[64,512]{1,0:T(8,128)(2,1)S(1)}) custom-call(f32[8,128]{1,0:T(8,128)S(1)} %get-tuple-element.70.refs_0_, bf16[32,4096]{1,0:T(8,128)(2,1)S(1)} %get-tuple-element.132.refs_1_.refs_2_, ...), custom_call_target="tpu_custom_call", output_to_operand_aliasing={{0}: (0, {})} | custom-call | flops 1 | bytes 1 | tf_op jit(solution)/shard_map/pallas_call | solution.py:139
  23.2 0.2 collective-permute-start.8
  23.5 1.4 %collective-permute-start.10 = (bf16[64,512]{1,0:T(8,128)(2,1)S(1)}, bf16[64,512]{1,0:T(8,128)(2,1)S(1)}, u32[]{:S(2)}, u32[]{:S(2)}) collective-permute-start(bf16[64,512]{1,0:T(8,128)(2,1)S(1)} %get-tuple-element.77.refs_2_), channel_id=1, source_target_pairs={{0,4},{4,0},{8,12},{12,8},{1,5},{5,1},{9,13},{13,9},{2,6},{6,2},{1... | collective-permute-start | bytes 196616 | tf_op jit(solution)/shard_map/ppermute | solution.py:408
  25.0 1.2 %collective-permute-start.9 = (f32[64,3]{1,0:T(8,128)S(1)}, f32[64,3]{1,0:T(8,128)S(1)}, u32[]{:S(2)}, u32[]{:S(2)}) collective-permute-start(f32[64,3]{1,0:T(8,128)S(1)} %copy.30.refs_5_.refs_6_), channel_id=1, source_target_pairs={{0,2},{2,0},{1,3},{3,1},{4,6},{6,4},{5,7},{7,5},{8,10},{10,8},{9,1... | collective-permute-start | bytes 2312 | tf_op jit(solution)/shard_map/ppermute | solution.py:381
  26.4 2.4 %collective-permute-start.11 = (bf16[64,512]{1,0:T(8,128)(2,1)S(1)}, bf16[64,512]{1,0:T(8,128)(2,1)S(1)}, u32[]{:S(2)}, u32[]{:S(2)}) collective-permute-start(bf16[64,512]{1,0:T(8,128)(2,1)S(1)} %get-tuple-element.79.refs_2_), channel_id=1, source_target_pairs={{0,8},{4,12},{8,0},{12,4},{1,9},{5,13},{9,1},{13,5},{2,10},{6,14},... | collective-permute-start | bytes 196616 | tf_op jit(solution)/shard_map/ppermute | solution.py:404
  28.8 2.2 %copy-done.2 = bf16[512,4096]{1,0:T(8,128)(2,1)S(1)} copy-done((bf16[512,4096]{1,0:T(8,128)(2,1)S(1)}, bf16[512,4096]{1,0:T(8,128)(2,1)}, u32[]{:S(2)}) %copy-start.2) | copy-done | bytes 4194328
  31.0 0.7 shard_map.91
  31.8 1.9 %collective-permute-start.12 = (bf16[64,512]{1,0:T(8,128)(2,1)S(1)}, bf16[64,512]{1,0:T(8,128)(2,1)S(1)}, u32[]{:S(2)}, u32[]{:S(2)}) collective-permute-start(bf16[64,512]{1,0:T(8,128)(2,1)S(1)} %get-tuple-element.82), channel_id=1, source_target_pairs={{0,1},{1,0},{2,3},{3,2},{4,5},{5,4},{6,7},{7,6},{8,9},{9,8},{10,11... | collective-permute-start | bytes 196616 | tf_op jit(solution)/shard_map/ppermute | solution.py:417
  33.7 0.4 collective-permute-start.14
  34.2 0.4 collective-permute-start.16
  34.7 0.2 collective-permute-start.17
  34.9 0.3 collective-permute-start.18
  35.2 0.2 collective-permute-start.19
  35.5 1.7 %collective-permute-start.20 = (bf16[64,512]{1,0:T(8,128)(2,1)S(1)}, bf16[64,512]{1,0:T(8,128)(2,1)S(1)}, u32[]{:S(2)}, u32[]{:S(2)}) collective-permute-start(bf16[64,512]{1,0:T(8,128)(2,1)S(1)} %get-tuple-element.91.refs_2_), channel_id=1, source_target_pairs={{0,4},{4,0},{8,12},{12,8},{1,5},{5,1},{9,13},{13,9},{2,6},{6,2},{1... | collective-permute-start | bytes 196616 | tf_op jit(solution)/shard_map/ppermute | solution.py:408
  37.3 0.6 collective-permute-start.29
  37.8 1.4 %collective-permute-done.20.refs_3_ = bf16[64,512]{1,0:T(8,128)(2,1)S(1)} collective-permute-done((bf16[64,512]{1,0:T(8,128)(2,1)S(1)}, bf16[64,512]{1,0:T(8,128)(2,1)S(1)}, u32[]{:S(2)}, u32[]{:S(2)}) %collective-permute-start.20) | collective-permute-done | bytes 65568 | tf_op jit(solution)/shard_map/ppermute | solution.py:408
  39.2 0.7 shard_map.94
  40.0 1.0 %collective-permute-start.21 = (bf16[64,512]{1,0:T(8,128)(2,1)S(1)}, bf16[64,512]{1,0:T(8,128)(2,1)S(1)}, u32[]{:S(2)}, u32[]{:S(2)}) collective-permute-start(bf16[64,512]{1,0:T(8,128)(2,1)S(1)} %get-tuple-element.94), channel_id=1, source_target_pairs={{0,1},{1,0},{2,3},{3,2},{4,5},{5,4},{6,7},{7,6},{8,9},{9,8},{10,11... | collective-permute-start | bytes 196616 | tf_op jit(solution)/shard_map/ppermute | solution.py:417
  41.0 0.4 collective-permute-start.23
  41.6 0.3 collective-permute-done.21.refs_2_
  41.9 0.4 collective-permute-start.25
  42.4 0.4 collective-permute-start.27
  43.1 0.4 collective-permute-done.26.refs_7_
  43.6 0.4 collective-permute-done.28.refs_9_
  44.1 1.2 %collective-permute-start.34 = (bf16[64,4096]{1,0:T(8,128)(2,1)S(1)}, bf16[64,4096]{1,0:T(8,128)(2,1)S(1)}, u32[]{:S(2)}, u32[]{:S(2)}) collective-permute-start(bf16[64,4096]{1,0:T(8,128)(2,1)S(1)} %get-tuple-element.113), channel_id=1, source_target_pairs={{0,2},{2,0},{1,3},{3,1},{4,6},{6,4},{5,7},{7,5},{8,10},{10,8},{9,1... | collective-permute-start | bytes 1572872 | tf_op jit(solution)/shard_map/ppermute | solution.py:420
  45.3 5.0 %collective-permute-done.29.refs_4_ = bf16[64,4096]{1,0:T(8,128)(2,1)S(1)} collective-permute-done((bf16[64,4096]{1,0:T(8,128)(2,1)S(1)}, bf16[64,4096]{1,0:T(8,128)(2,1)S(1)}, u32[]{:S(2)}, u32[]{:S(2)}) %collective-permute-start.29) | collective-permute-done | bytes 524320 | tf_op jit(solution)/shard_map/ppermute | solution.py:420
  50.2 1.2 %shard_map.96 = (f32[8,128]{1,0:T(8,128)S(1)}, bf16[64,1024]{1,0:T(8,128)(2,1)S(1)}, bf16[64,1024]{1,0:T(8,128)(2,1)S(1)}, bf16[64,1024]{1,0:T(8,128)(2,1)S(1)},...) custom-call(f32[8,128]{1,0:T(8,128)S(1)} %get-tuple-element.102.refs_0_, ...), custom_call_target="tpu_custom_call", output_to_operand_aliasing={{0}: (0, {})} | custom-call | flops 1 | bytes 1 | tf_op jit(solution)/shard_map/pallas_call | solution.py:139
  51.5 2.5 %collective-permute-start.30 = (bf16[64,1024]{1,0:T(8,128)(2,1)S(1)}, bf16[64,1024]{1,0:T(8,128)(2,1)S(1)}, u32[]{:S(2)}, u32[]{:S(2)}) collective-permute-start(bf16[64,1024]{1,0:T(8,128)(2,1)S(1)} %get-tuple-element.106.refs_2_), channel_id=1, source_target_pairs={{0,1},{1,0},{2,3},{3,2},{4,5},{5,4},{6,7},{7,6},{8,9},{9,8},{10,11... | collective-permute-start | bytes 393224 | tf_op jit(solution)/shard_map/ppermute | solution.py:430
  54.1 0.4 collective-permute-start.32
  54.6 0.4 collective-permute-done.30.refs_6_
  55.0 0.4 collective-permute-done.31.refs_7_
  55.5 0.3 collective-permute-done.33.refs_9_
  55.9 2.1 %shard_map.97 = (f32[8,128]{1,0:T(8,128)S(1)}, bf16[6,32,512]{2,1,0:T(8,128)(2,1)S(1)}, bf16[6,32,512]{2,1,0:T(8,128)(2,1)S(1)}, bf16[6,32,512]{2,1,0:T(8,128)(2,1)S(1)}, bf16[6,32,512]{2,1,0:T(8,128)(2,1)S(1)}) custom-call(f32[8,128]{1,0:T(8,128)S(1)} %get-tuple-element.105.refs_0_, s32[32]{0:T(128)S(1)} %copy-done.5, ...), custom_call_target="tpu_custom_call", output_to_operand_aliasing={{0}: (0, {})} | custom-call | flops 1 | bytes 1 | tf_op jit(solution)/shard_map/pallas_call | solution.py:139
  57.9 2.1 %collective-permute-start.35 = (bf16[6,32,512]{2,1,0:T(8,128)(2,1)S(1)}, bf16[6,32,512]{2,1,0:T(8,128)(2,1)S(1)}, u32[]{:S(2)}, u32[]{:S(2)}) collective-permute-start(bf16[6,32,512]{2,1,0:T(8,128)(2,1)S(1)} %get-tuple-element.116), channel_id=1, source_target_pairs={{0,8},{4,12},{8,0},{12,4},{1,9},{5,13},{9,1},{13,5},{2,10},{6,14},... | collective-permute-start | bytes 589832 | tf_op jit(solution)/shard_map/ppermute | solution.py:445
  60.0 1.4 %collective-permute-done.34.refs_5_ = bf16[64,4096]{1,0:T(8,128)(2,1)S(1)} collective-permute-done((bf16[64,4096]{1,0:T(8,128)(2,1)S(1)}, bf16[64,4096]{1,0:T(8,128)(2,1)S(1)}, u32[]{:S(2)}, u32[]{:S(2)}) %collective-permute-start.34) | collective-permute-done | bytes 524320 | tf_op jit(solution)/shard_map/ppermute | solution.py:420
  61.5 1.2 %shard_map.98 = (f32[8,128]{1,0:T(8,128)S(1)}, bf16[64,1024]{1,0:T(8,128)(2,1)S(1)}, bf16[64,1024]{1,0:T(8,128)(2,1)S(1)}, bf16[64,1024]{1,0:T(8,128)(2,1)S(1)},...) custom-call(f32[8,128]{1,0:T(8,128)S(1)} %get-tuple-element.110.refs_0_, ...), custom_call_target="tpu_custom_call", output_to_operand_aliasing={{0}: (0, {}), {5}: (1, {})} | custom-call | flops 1 | bytes 1 | tf_op jit(solution)/shard_map/pallas_call | solution.py:139
  62.7 1.5 %collective-permute-start.36 = (bf16[64,1024]{1,0:T(8,128)(2,1)S(1)}, bf16[64,1024]{1,0:T(8,128)(2,1)S(1)}, u32[]{:S(2)}, u32[]{:S(2)}) collective-permute-start(bf16[64,1024]{1,0:T(8,128)(2,1)S(1)} %get-tuple-element.117.refs_3_), channel_id=1, source_target_pairs={{0,1},{1,0},{2,3},{3,2},{4,5},{5,4},{6,7},{7,6},{8,9},{9,8},{10,11... | collective-permute-start | bytes 393224 | tf_op jit(solution)/shard_map/ppermute | solution.py:430
  64.3 0.4 collective-permute-start.38
  64.8 0.4 collective-permute-done.36.refs_7_
  65.2 0.9 collective-permute-start.40
  66.1 1.4 %collective-permute-start.41 = (bf16[6,32,512]{2,1,0:T(8,128)(2,1)S(1)}, bf16[6,32,512]{2,1,0:T(8,128)(2,1)S(1)}, u32[]{:S(2)}, u32[]{:S(2)}) collective-permute-start(bf16[6,32,512]{2,1,0:T(8,128)(2,1)S(1)} %get-tuple-element.124), channel_id=1, source_target_pairs={{0,12},{4,8},{8,4},{12,0},{1,13},{5,9},{9,5},{13,1},{2,14},{6,10},... | collective-permute-start | bytes 589832 | tf_op jit(solution)/shard_map/ppermute | solution.py:445
  67.5 1.1 %collective-permute-done.35.refs_1_.refs_5_ = bf16[6,32,512]{2,1,0:T(8,128)(2,1)S(1)} collective-permute-done((bf16[6,32,512]{2,1,0:T(8,128)(2,1)S(1)}, bf16[6,32,512]{2,1,0:T(8,128)(2,1)S(1)}, u32[]{:S(2)}, u32[]{:S(2)}) %collective-permute-start.35) | collective-permute-done | bytes 196640 | tf_op jit(solution)/shard_map/ppermute | solution.py:445
  68.7 2.1 %shard_map.99 = (f32[8,128]{1,0:T(8,128)S(1)}, bf16[6,32,512]{2,1,0:T(8,128)(2,1)S(1)}, bf16[6,32,512]{2,1,0:T(8,128)(2,1)S(1)}, bf16[6,32,512]{2,1,0:T(8,128)(2,1)S(1)}, bf16[6,32,512]{2,1,0:T(8,128)(2,1)S(1)}) custom-call(f32[8,128]{1,0:T(8,128)S(1)} %get-tuple-element.115.refs_0_, ...), custom_call_target="tpu_custom_call", output_to_operand_aliasing={{0}: (0, {})} | custom-call | flops 1 | bytes 1 | tf_op jit(solution)/shard_map/pallas_call | solution.py:139
  70.8 1.3 %collective-permute-start.42 = (bf16[6,32,512]{2,1,0:T(8,128)(2,1)S(1)}, bf16[6,32,512]{2,1,0:T(8,128)(2,1)S(1)}, u32[]{:S(2)}, u32[]{:S(2)}) collective-permute-start(bf16[6,32,512]{2,1,0:T(8,128)(2,1)S(1)} %get-tuple-element.128), channel_id=1, source_target_pairs={{0,4},{4,0},{8,12},{12,8},{1,5},{5,1},{9,13},{13,9},{2,6},{6,2},{1... | collective-permute-start | bytes 589832 | tf_op jit(solution)/shard_map/ppermute | solution.py:445
  72.1 1.9 %collective-permute-start.43 = (bf16[6,32,512]{2,1,0:T(8,128)(2,1)S(1)}, bf16[6,32,512]{2,1,0:T(8,128)(2,1)S(1)}, u32[]{:S(2)}, u32[]{:S(2)}) collective-permute-start(bf16[6,32,512]{2,1,0:T(8,128)(2,1)S(1)} %get-tuple-element.129), channel_id=1, source_target_pairs={{0,8},{4,12},{8,0},{12,4},{1,9},{5,13},{9,1},{13,5},{2,10},{6,14},... | collective-permute-start | bytes 589832 | tf_op jit(solution)/shard_map/ppermute | solution.py:445
  74.2 2.9 %collective-permute-done.41.refs_6_ = bf16[6,32,512]{2,1,0:T(8,128)(2,1)S(1)} collective-permute-done((bf16[6,32,512]{2,1,0:T(8,128)(2,1)S(1)}, bf16[6,32,512]{2,1,0:T(8,128)(2,1)S(1)}, u32[]{:S(2)}, u32[]{:S(2)}) %collective-permute-start.41) | collective-permute-done | bytes 196640 | tf_op jit(solution)/shard_map/ppermute | solution.py:445
  77.1 2.3 %shard_map.100 = (bf16[22,64,512]{2,1,0:T(8,128)(2,1)}, f32[8,128]{1,0:T(8,128)S(1)}) custom-call(f32[8,128]{1,0:T(8,128)S(1)} %get-tuple-element.121.refs_0_, s32[32]{0:T(128)S(1)} %copy-done.5, bf16[256,512]{1,0:T(8,128)(2,1)S(1)} %copy-done.4, bf16[6,32,512]{2,1,0:T(8,128)(2,1)S(1)} %get-tuple-element.122.refs_3_, ...), custom_call_target="tpu_custom_call", output_to_operand_aliasing={{1}: (0, {})} | custom-call | flops 1 | bytes 1 | tf_op jit(solution)/shard_map/pallas_call | solution.py:340
  79.4 5.6 %collective-permute-done.42.refs_5_ = bf16[6,32,512]{2,1,0:T(8,128)(2,1)S(1)} collective-permute-done((bf16[6,32,512]{2,1,0:T(8,128)(2,1)S(1)}, bf16[6,32,512]{2,1,0:T(8,128)(2,1)S(1)}, u32[]{:S(2)}, u32[]{:S(2)}) %collective-permute-start.42) | collective-permute-done | bytes 196640 | tf_op jit(solution)/shard_map/ppermute | solution.py:445
  85.0 4.8 %collective-permute-done.43.refs_6_ = bf16[6,32,512]{2,1,0:T(8,128)(2,1)S(1)} collective-permute-done((bf16[6,32,512]{2,1,0:T(8,128)(2,1)S(1)}, bf16[6,32,512]{2,1,0:T(8,128)(2,1)S(1)}, u32[]{:S(2)}, u32[]{:S(2)}) %collective-permute-start.43) | collective-permute-done | bytes 196640 | tf_op jit(solution)/shard_map/ppermute | solution.py:445
  89.8 4.8 %collective-permute-done.44.refs_7_ = bf16[6,32,512]{2,1,0:T(8,128)(2,1)S(1)} collective-permute-done((bf16[6,32,512]{2,1,0:T(8,128)(2,1)S(1)}, bf16[6,32,512]{2,1,0:T(8,128)(2,1)S(1)}, u32[]{:S(2)}, u32[]{:S(2)}) %collective-permute-start.44) | collective-permute-done | bytes 196640 | tf_op jit(solution)/shard_map/ppermute | solution.py:445
  94.6 2.3 %shard_map.101 = (bf16[22,64,512]{2,1,0:T(8,128)(2,1)}, f32[8,128]{1,0:T(8,128)S(1)}) custom-call(bf16[22,64,512]{2,1,0:T(8,128)(2,1)} %get-tuple-element.125.refs_0_, f32[8,128]{1,0:T(8,128)S(1)} %get-tuple-element.126.refs_1_, s32[32]{0:T(128)S(1)} %copy-done.5, bf16[256,512]{1,0:T(8,128)(2,1)S(1)} %copy-done.4, ...), custom_call_target="tpu_custom_call", output_to_operand_aliasing={{0}: (0, {}), {1}: (1, {})} | custom-call | flops 1 | bytes 1 | tf_op jit(solution)/shard_map/pallas_call | solution.py:340
  (65 shorter events, 2.4 us)
Async XLA Ops:
  1.7 7.2 %collective-permute-start = (bf16[32,4096]{1,0:T(8,128)(2,1)S(1)}, bf16[32,4096]{1,0:T(8,128)(2,1)S(1)}, u32[]{:S(2)}, u32[]{:S(2)}) collective-permute-start(bf16[32,4096]{1,0:T(8,128)(2,1)S(1)} %get-tuple-element.133.refs_1_), channel_id=1, source_target_pairs={{0,2},{2,0},{1,3},{3,1},{4,6},{6,4},{5,7},{7,5},{8,10},{10,8},{9,1... | collective-permute-start | bytes 786440 | tf_op jit(solution)/shard_map/ppermute | solution.py:373
  3.0 8.7 %collective-permute-start.1 = (bf16[32,4096]{1,0:T(8,128)(2,1)S(1)}, bf16[32,4096]{1,0:T(8,128)(2,1)S(1)}, u32[]{:S(2)}, u32[]{:S(2)}) collective-permute-start(bf16[32,4096]{1,0:T(8,128)(2,1)S(1)} %get-tuple-element.133.refs_1_), channel_id=1, source_target_pairs={{0,1},{1,0},{2,3},{3,2},{4,5},{5,4},{6,7},{7,6},{8,9},{9,8},{10,11... | collective-permute-start | bytes 786440 | tf_op jit(solution)/shard_map/ppermute | solution.py:374
  8.9 2.8 %collective-permute-start.2 = (bf16[32,4096]{1,0:T(8,128)(2,1)S(1)}, bf16[32,4096]{1,0:T(8,128)(2,1)S(1)}, u32[]{:S(2)}, u32[]{:S(2)}) collective-permute-start(bf16[32,4096]{1,0:T(8,128)(2,1)S(1)} %collective-permute-done.refs_2_), channel_id=1, source_target_pairs={{0,1},{1,0},{2,3},{3,2},{4,5},{5,4},{6,7},{7,6},{8,9},{9,8},{10,11... | collective-permute-start | bytes 786440 | tf_op jit(solution)/shard_map/ppermute | solution.py:375
  10.5 7.9 %collective-permute-start.4 = (bf16[32,4096]{1,0:T(8,128)(2,1)S(1)}, bf16[32,4096]{1,0:T(8,128)(2,1)S(1)}, u32[]{:S(2)}, u32[]{:S(2)}) collective-permute-start(bf16[32,4096]{1,0:T(8,128)(2,1)S(1)} %get-tuple-element.132.refs_1_.refs_2_), channel_id=1, source_target_pairs={{0,2},{2,0},{1,3},{3,1},{4,6},{6,4},{5,7},{7,5},{8,10},{10,8},{9,1... | collective-permute-start | bytes 786440 | tf_op jit(solution)/shard_map/ppermute | solution.py:373
  11.7 2.2 %copy-start = (bf16[512,4096]{1,0:T(8,128)(2,1)S(1)}, bf16[512,4096]{1,0:T(8,128)(2,1)}, u32[]{:S(2)}) copy-start(bf16[512,4096]{1,0:T(8,128)(2,1)} %refs_11_.1) | copy-start | bytes 12582916
  13.9 7.7 %copy-start.6 = (f32[64]{0:T(128)S(1)}, f32[64]{0:T(128)}, u32[]{:S(2)}) copy-start(f32[64]{0:T(128)} %param.10) | copy-start | bytes 772
  13.9 7.7 %copy-start.7 = (f32[64]{0:T(128)S(1)}, f32[64]{0:T(128)}, u32[]{:S(2)}) copy-start(f32[64]{0:T(128)} %param.12) | copy-start | bytes 772
  13.9 7.7 %copy-start.8 = (f32[64]{0:T(128)S(1)}, f32[64]{0:T(128)}, u32[]{:S(2)}) copy-start(f32[64]{0:T(128)} %param.11) | copy-start | bytes 772
  13.9 7.7 %copy-start.1 = (bf16[512,4096]{1,0:T(8,128)(2,1)S(1)}, bf16[512,4096]{1,0:T(8,128)(2,1)}, u32[]{:S(2)}) copy-start(bf16[512,4096]{1,0:T(8,128)(2,1)} %refs_11_.1) | copy-start | bytes 12582916
  15.5 3.7 %collective-permute-start.3 = (bf16[64,512]{1,0:T(8,128)(2,1)S(1)}, bf16[64,512]{1,0:T(8,128)(2,1)S(1)}, u32[]{:S(2)}, u32[]{:S(2)}) collective-permute-start(bf16[64,512]{1,0:T(8,128)(2,1)S(1)} %get-tuple-element.69), channel_id=1, source_target_pairs={{0,4},{4,0},{8,12},{12,8},{1,5},{5,1},{9,13},{13,9},{2,6},{6,2},{1... | collective-permute-start | bytes 196616 | tf_op jit(solution)/shard_map/ppermute | solution.py:401
  15.7 5.9 %collective-permute-start.5 = (bf16[32,4096]{1,0:T(8,128)(2,1)S(1)}, bf16[32,4096]{1,0:T(8,128)(2,1)S(1)}, u32[]{:S(2)}, u32[]{:S(2)}) collective-permute-start(bf16[32,4096]{1,0:T(8,128)(2,1)S(1)} %get-tuple-element.132.refs_1_.refs_2_), channel_id=1, source_target_pairs={{0,1},{1,0},{2,3},{3,2},{4,5},{5,4},{6,7},{7,6},{8,9},{9,8},{10,11... | collective-permute-start | bytes 786440 | tf_op jit(solution)/shard_map/ppermute | solution.py:374
  18.4 3.2 %collective-permute-start.6 = (bf16[32,4096]{1,0:T(8,128)(2,1)S(1)}, bf16[32,4096]{1,0:T(8,128)(2,1)S(1)}, u32[]{:S(2)}, u32[]{:S(2)}) collective-permute-start(bf16[32,4096]{1,0:T(8,128)(2,1)S(1)} %collective-permute-done.4.refs_2_.refs_3_), channel_id=1, source_target_pairs={{0,1},{1,0},{2,3},{3,2},{4,5},{5,4},{6,7},{7,6},{8,9},{9,8},{10,11... | collective-permute-start | bytes 786440 | tf_op jit(solution)/shard_map/ppermute | solution.py:375
  19.2 4.2 %collective-permute-start.7 = (bf16[64,512]{1,0:T(8,128)(2,1)S(1)}, bf16[64,512]{1,0:T(8,128)(2,1)S(1)}, u32[]{:S(2)}, u32[]{:S(2)}) collective-permute-start(bf16[64,512]{1,0:T(8,128)(2,1)S(1)} %get-tuple-element.72.refs_2_), channel_id=1, source_target_pairs={{0,8},{4,12},{8,0},{12,4},{1,9},{5,13},{9,1},{13,5},{2,10},{6,14},... | collective-permute-start | bytes 196616 | tf_op jit(solution)/shard_map/ppermute | solution.py:404
  21.7 1.8 %copy-start.4 = (bf16[256,512]{1,0:T(8,128)(2,1)S(1)}, bf16[256,512]{1,0:T(8,128)(2,1)}, u32[]{:S(2)}) copy-start(bf16[256,512]{1,0:T(8,128)(2,1)} %refs_3_.1) | copy-start | bytes 786436
  23.2 3.2 %collective-permute-start.8 = (bf16[64,512]{1,0:T(8,128)(2,1)S(1)}, bf16[64,512]{1,0:T(8,128)(2,1)S(1)}, u32[]{:S(2)}, u32[]{:S(2)}) collective-permute-start(bf16[64,512]{1,0:T(8,128)(2,1)S(1)} %get-tuple-element.75), channel_id=1, source_target_pairs={{0,4},{4,0},{8,12},{12,8},{1,5},{5,1},{9,13},{13,9},{2,6},{6,2},{1... | collective-permute-start | bytes 196616 | tf_op jit(solution)/shard_map/ppermute | solution.py:401
  23.5 5.3 %collective-permute-start.10 = (bf16[64,512]{1,0:T(8,128)(2,1)S(1)}, bf16[64,512]{1,0:T(8,128)(2,1)S(1)}, u32[]{:S(2)}, u32[]{:S(2)}) collective-permute-start(bf16[64,512]{1,0:T(8,128)(2,1)S(1)} %get-tuple-element.77.refs_2_), channel_id=1, source_target_pairs={{0,4},{4,0},{8,12},{12,8},{1,5},{5,1},{9,13},{13,9},{2,6},{6,2},{1... | collective-permute-start | bytes 196616 | tf_op jit(solution)/shard_map/ppermute | solution.py:408
  25.0 3.9 %collective-permute-start.9 = (f32[64,3]{1,0:T(8,128)S(1)}, f32[64,3]{1,0:T(8,128)S(1)}, u32[]{:S(2)}, u32[]{:S(2)}) collective-permute-start(f32[64,3]{1,0:T(8,128)S(1)} %copy.30.refs_5_.refs_6_), channel_id=1, source_target_pairs={{0,2},{2,0},{1,3},{3,1},{4,6},{6,4},{5,7},{7,5},{8,10},{10,8},{9,1... | collective-permute-start | bytes 2312 | tf_op jit(solution)/shard_map/ppermute | solution.py:381
  26.4 7.8 %collective-permute-start.11 = (bf16[64,512]{1,0:T(8,128)(2,1)S(1)}, bf16[64,512]{1,0:T(8,128)(2,1)S(1)}, u32[]{:S(2)}, u32[]{:S(2)}) collective-permute-start(bf16[64,512]{1,0:T(8,128)(2,1)S(1)} %get-tuple-element.79.refs_2_), channel_id=1, source_target_pairs={{0,8},{4,12},{8,0},{12,4},{1,9},{5,13},{9,1},{13,5},{2,10},{6,14},... | collective-permute-start | bytes 196616 | tf_op jit(solution)/shard_map/ppermute | solution.py:404
  28.8 2.2 %copy-start.2 = (bf16[512,4096]{1,0:T(8,128)(2,1)S(1)}, bf16[512,4096]{1,0:T(8,128)(2,1)}, u32[]{:S(2)}) copy-start(bf16[512,4096]{1,0:T(8,128)(2,1)} %refs_11_.1) | copy-start | bytes 12582916
  31.0 8.2 %copy-start.3 = (bf16[512,4096]{1,0:T(8,128)(2,1)S(1)}, bf16[512,4096]{1,0:T(8,128)(2,1)}, u32[]{:S(2)}) copy-start(bf16[512,4096]{1,0:T(8,128)(2,1)} %refs_11_.1) | copy-start | bytes 12582916
  31.8 2.9 %collective-permute-start.12 = (bf16[64,512]{1,0:T(8,128)(2,1)S(1)}, bf16[64,512]{1,0:T(8,128)(2,1)S(1)}, u32[]{:S(2)}, u32[]{:S(2)}) collective-permute-start(bf16[64,512]{1,0:T(8,128)(2,1)S(1)} %get-tuple-element.82), channel_id=1, source_target_pairs={{0,1},{1,0},{2,3},{3,2},{4,5},{5,4},{6,7},{7,6},{8,9},{9,8},{10,11... | collective-permute-start | bytes 196616 | tf_op jit(solution)/shard_map/ppermute | solution.py:417
  33.6 1.3 %collective-permute-start.13 = (bf16[64,512]{1,0:T(8,128)(2,1)S(1)}, bf16[64,512]{1,0:T(8,128)(2,1)S(1)}, u32[]{:S(2)}, u32[]{:S(2)}) collective-permute-start(bf16[64,512]{1,0:T(8,128)(2,1)S(1)} %get-tuple-element.83), channel_id=1, source_target_pairs={{0,1},{1,0},{2,3},{3,2},{4,5},{5,4},{6,7},{7,6},{8,9},{9,8},{10,11... | collective-permute-start | bytes 196616 | tf_op jit(solution)/shard_map/ppermute | solution.py:417
  33.7 1.5 %collective-permute-start.14 = (bf16[64,512]{1,0:T(8,128)(2,1)S(1)}, bf16[64,512]{1,0:T(8,128)(2,1)S(1)}, u32[]{:S(2)}, u32[]{:S(2)}) collective-permute-start(bf16[64,512]{1,0:T(8,128)(2,1)S(1)} %get-tuple-element.84), channel_id=1, source_target_pairs={{0,1},{1,0},{2,3},{3,2},{4,5},{5,4},{6,7},{7,6},{8,9},{9,8},{10,11... | collective-permute-start | bytes 196616 | tf_op jit(solution)/shard_map/ppermute | solution.py:417
  34.1 1.3 %collective-permute-start.15 = (bf16[64,512]{1,0:T(8,128)(2,1)S(1)}, bf16[64,512]{1,0:T(8,128)(2,1)S(1)}, u32[]{:S(2)}, u32[]{:S(2)}) collective-permute-start(bf16[64,512]{1,0:T(8,128)(2,1)S(1)} %get-tuple-element.85), channel_id=1, source_target_pairs={{0,1},{1,0},{2,3},{3,2},{4,5},{5,4},{6,7},{7,6},{8,9},{9,8},{10,11... | collective-permute-start | bytes 196616 | tf_op jit(solution)/shard_map/ppermute | solution.py:417
  34.2 2.9 %collective-permute-start.16 = (bf16[64,512]{1,0:T(8,128)(2,1)S(1)}, bf16[64,512]{1,0:T(8,128)(2,1)S(1)}, u32[]{:S(2)}, u32[]{:S(2)}) collective-permute-start(bf16[64,512]{1,0:T(8,128)(2,1)S(1)} %get-tuple-element.86), channel_id=1, source_target_pairs={{0,1},{1,0},{2,3},{3,2},{4,5},{5,4},{6,7},{7,6},{8,9},{9,8},{10,11... | collective-permute-start | bytes 196616 | tf_op jit(solution)/shard_map/ppermute | solution.py:417
  34.7 2.5 %collective-permute-start.17 = (bf16[64,512]{1,0:T(8,128)(2,1)S(1)}, bf16[64,512]{1,0:T(8,128)(2,1)S(1)}, u32[]{:S(2)}, u32[]{:S(2)}) collective-permute-start(bf16[64,512]{1,0:T(8,128)(2,1)S(1)} %get-tuple-element.87), channel_id=1, source_target_pairs={{0,1},{1,0},{2,3},{3,2},{4,5},{5,4},{6,7},{7,6},{8,9},{9,8},{10,11... | collective-permute-start | bytes 196616 | tf_op jit(solution)/shard_map/ppermute | solution.py:417
  34.9 2.2 %collective-permute-start.18 = (bf16[64,512]{1,0:T(8,128)(2,1)S(1)}, bf16[64,512]{1,0:T(8,128)(2,1)S(1)}, u32[]{:S(2)}, u32[]{:S(2)}) collective-permute-start(bf16[64,512]{1,0:T(8,128)(2,1)S(1)} %get-tuple-element.88), channel_id=1, source_target_pairs={{0,1},{1,0},{2,3},{3,2},{4,5},{5,4},{6,7},{7,6},{8,9},{9,8},{10,11... | collective-permute-start | bytes 196616 | tf_op jit(solution)/shard_map/ppermute | solution.py:417
  35.2 2.0 %collective-permute-start.19 = (bf16[64,512]{1,0:T(8,128)(2,1)S(1)}, bf16[64,512]{1,0:T(8,128)(2,1)S(1)}, u32[]{:S(2)}, u32[]{:S(2)}) collective-permute-start(bf16[64,512]{1,0:T(8,128)(2,1)S(1)} %get-tuple-element.89), channel_id=1, source_target_pairs={{0,1},{1,0},{2,3},{3,2},{4,5},{5,4},{6,7},{7,6},{8,9},{9,8},{10,11... | collective-permute-start | bytes 196616 | tf_op jit(solution)/shard_map/ppermute | solution.py:417
  35.5 3.8 %collective-permute-start.20 = (bf16[64,512]{1,0:T(8,128)(2,1)S(1)}, bf16[64,512]{1,0:T(8,128)(2,1)S(1)}, u32[]{:S(2)}, u32[]{:S(2)}) collective-permute-start(bf16[64,512]{1,0:T(8,128)(2,1)S(1)} %get-tuple-element.91.refs_2_), channel_id=1, source_target_pairs={{0,4},{4,0},{8,12},{12,8},{1,5},{5,1},{9,13},{13,9},{2,6},{6,2},{1... | collective-permute-start | bytes 196616 | tf_op jit(solution)/shard_map/ppermute | solution.py:408
  37.3 13.0 %collective-permute-start.29 = (bf16[64,4096]{1,0:T(8,128)(2,1)S(1)}, bf16[64,4096]{1,0:T(8,128)(2,1)S(1)}, u32[]{:S(2)}, u32[]{:S(2)}) collective-permute-start(bf16[64,4096]{1,0:T(8,128)(2,1)S(1)} %get-tuple-element.104), channel_id=1, source_target_pairs={{0,2},{2,0},{1,3},{3,1},{4,6},{6,4},{5,7},{7,5},{8,10},{10,8},{9,1... | collective-permute-start | bytes 1572872 | tf_op jit(solution)/shard_map/ppermute | solution.py:420
  40.0 1.9 %collective-permute-start.21 = (bf16[64,512]{1,0:T(8,128)(2,1)S(1)}, bf16[64,512]{1,0:T(8,128)(2,1)S(1)}, u32[]{:S(2)}, u32[]{:S(2)}) collective-permute-start(bf16[64,512]{1,0:T(8,128)(2,1)S(1)} %get-tuple-element.94), channel_id=1, source_target_pairs={{0,1},{1,0},{2,3},{3,2},{4,5},{5,4},{6,7},{7,6},{8,9},{9,8},{10,11... | collective-permute-start | bytes 196616 | tf_op jit(solution)/shard_map/ppermute | solution.py:417
  41.0 1.3 %collective-permute-start.22 = (bf16[64,512]{1,0:T(8,128)(2,1)S(1)}, bf16[64,512]{1,0:T(8,128)(2,1)S(1)}, u32[]{:S(2)}, u32[]{:S(2)}) collective-permute-start(bf16[64,512]{1,0:T(8,128)(2,1)S(1)} %get-tuple-element.95), channel_id=1, source_target_pairs={{0,1},{1,0},{2,3},{3,2},{4,5},{5,4},{6,7},{7,6},{8,9},{9,8},{10,11... | collective-permute-start | bytes 196616 | tf_op jit(solution)/shard_map/ppermute | solution.py:417
  41.0 1.3 %collective-permute-start.23 = (bf16[64,512]{1,0:T(8,128)(2,1)S(1)}, bf16[64,512]{1,0:T(8,128)(2,1)S(1)}, u32[]{:S(2)}, u32[]{:S(2)}) collective-permute-start(bf16[64,512]{1,0:T(8,128)(2,1)S(1)} %get-tuple-element.96), channel_id=1, source_target_pairs={{0,1},{1,0},{2,3},{3,2},{4,5},{5,4},{6,7},{7,6},{8,9},{9,8},{10,11... | collective-permute-start | bytes 196616 | tf_op jit(solution)/shard_map/ppermute | solution.py:417
  41.5 1.3 %collective-permute-start.24 = (bf16[64,512]{1,0:T(8,128)(2,1)S(1)}, bf16[64,512]{1,0:T(8,128)(2,1)S(1)}, u32[]{:S(2)}, u32[]{:S(2)}) collective-permute-start(bf16[64,512]{1,0:T(8,128)(2,1)S(1)} %get-tuple-element.97), channel_id=1, source_target_pairs={{0,1},{1,0},{2,3},{3,2},{4,5},{5,4},{6,7},{7,6},{8,9},{9,8},{10,11... | collective-permute-start | bytes 196616 | tf_op jit(solution)/shard_map/ppermute | solution.py:417
  41.9 1.3 %collective-permute-start.25 = (bf16[64,512]{1,0:T(8,128)(2,1)S(1)}, bf16[64,512]{1,0:T(8,128)(2,1)S(1)}, u32[]{:S(2)}, u32[]{:S(2)}) collective-permute-start(bf16[64,512]{1,0:T(8,128)(2,1)S(1)} %get-tuple-element.98), channel_id=1, source_target_pairs={{0,1},{1,0},{2,3},{3,2},{4,5},{5,4},{6,7},{7,6},{8,9},{9,8},{10,11... | collective-permute-start | bytes 196616 | tf_op jit(solution)/shard_map/ppermute | solution.py:417
  42.2 1.3 %collective-permute-start.26 = (bf16[64,512]{1,0:T(8,128)(2,1)S(1)}, bf16[64,512]{1,0:T(8,128)(2,1)S(1)}, u32[]{:S(2)}, u32[]{:S(2)}) collective-permute-start(bf16[64,512]{1,0:T(8,128)(2,1)S(1)} %get-tuple-element.99), channel_id=1, source_target_pairs={{0,1},{1,0},{2,3},{3,2},{4,5},{5,4},{6,7},{7,6},{8,9},{9,8},{10,11... | collective-permute-start | bytes 196616 | tf_op jit(solution)/shard_map/ppermute | solution.py:417
  42.4 1.3 %collective-permute-start.27 = (bf16[64,512]{1,0:T(8,128)(2,1)S(1)}, bf16[64,512]{1,0:T(8,128)(2,1)S(1)}, u32[]{:S(2)}, u32[]{:S(2)}) collective-permute-start(bf16[64,512]{1,0:T(8,128)(2,1)S(1)} %get-tuple-element.100), channel_id=1, source_target_pairs={{0,1},{1,0},{2,3},{3,2},{4,5},{5,4},{6,7},{7,6},{8,9},{9,8},{10,11... | collective-permute-start | bytes 196616 | tf_op jit(solution)/shard_map/ppermute | solution.py:417
  42.7 1.3 %collective-permute-start.28 = (bf16[64,512]{1,0:T(8,128)(2,1)S(1)}, bf16[64,512]{1,0:T(8,128)(2,1)S(1)}, u32[]{:S(2)}, u32[]{:S(2)}) collective-permute-start(bf16[64,512]{1,0:T(8,128)(2,1)S(1)} %get-tuple-element.101), channel_id=1, source_target_pairs={{0,1},{1,0},{2,3},{3,2},{4,5},{5,4},{6,7},{7,6},{8,9},{9,8},{10,11... | collective-permute-start | bytes 196616 | tf_op jit(solution)/shard_map/ppermute | solution.py:417
  44.1 11.7 %copy-start.5 = (s32[32]{0:T(128)S(1)}, s32[32]{0:T(128)}, u32[]{:S(2)}) copy-start(s32[32]{0:T(128)} %refs_2_.5) | copy-start | bytes 388
  44.1 17.4 %collective-permute-start.34 = (bf16[64,4096]{1,0:T(8,128)(2,1)S(1)}, bf16[64,4096]{1,0:T(8,128)(2,1)S(1)}, u32[]{:S(2)}, u32[]{:S(2)}) collective-permute-start(bf16[64,4096]{1,0:T(8,128)(2,1)S(1)} %get-tuple-element.113), channel_id=1, source_target_pairs={{0,2},{2,0},{1,3},{3,1},{4,6},{6,4},{5,7},{7,5},{8,10},{10,8},{9,1... | collective-permute-start | bytes 1572872 | tf_op jit(solution)/shard_map/ppermute | solution.py:420
  51.5 3.5 %collective-permute-start.30 = (bf16[64,1024]{1,0:T(8,128)(2,1)S(1)}, bf16[64,1024]{1,0:T(8,128)(2,1)S(1)}, u32[]{:S(2)}, u32[]{:S(2)}) collective-permute-start(bf16[64,1024]{1,0:T(8,128)(2,1)S(1)} %get-tuple-element.106.refs_2_), channel_id=1, source_target_pairs={{0,1},{1,0},{2,3},{3,2},{4,5},{5,4},{6,7},{7,6},{8,9},{9,8},{10,11... | collective-permute-start | bytes 393224 | tf_op jit(solution)/shard_map/ppermute | solution.py:430
  54.0 1.3 %collective-permute-start.31 = (bf16[64,1024]{1,0:T(8,128)(2,1)S(1)}, bf16[64,1024]{1,0:T(8,128)(2,1)S(1)}, u32[]{:S(2)}, u32[]{:S(2)}) collective-permute-start(bf16[64,1024]{1,0:T(8,128)(2,1)S(1)} %get-tuple-element.107.refs_3_), channel_id=1, source_target_pairs={{0,1},{1,0},{2,3},{3,2},{4,5},{5,4},{6,7},{7,6},{8,9},{9,8},{10,11... | collective-permute-start | bytes 393224 | tf_op jit(solution)/shard_map/ppermute | solution.py:430
  54.1 1.5 %collective-permute-start.32 = (bf16[64,1024]{1,0:T(8,128)(2,1)S(1)}, bf16[64,1024]{1,0:T(8,128)(2,1)S(1)}, u32[]{:S(2)}, u32[]{:S(2)}) collective-permute-start(bf16[64,1024]{1,0:T(8,128)(2,1)S(1)} %get-tuple-element.108.refs_4_), channel_id=1, source_target_pairs={{0,1},{1,0},{2,3},{3,2},{4,5},{5,4},{6,7},{7,6},{8,9},{9,8},{10,11... | collective-permute-start | bytes 393224 | tf_op jit(solution)/shard_map/ppermute | solution.py:430
  54.5 1.3 %collective-permute-start.33 = (bf16[64,1024]{1,0:T(8,128)(2,1)S(1)}, bf16[64,1024]{1,0:T(8,128)(2,1)S(1)}, u32[]{:S(2)}, u32[]{:S(2)}) collective-permute-start(bf16[64,1024]{1,0:T(8,128)(2,1)S(1)} %get-tuple-element.109.refs_5_), channel_id=1, source_target_pairs={{0,1},{1,0},{2,3},{3,2},{4,5},{5,4},{6,7},{7,6},{8,9},{9,8},{10,11... | collective-permute-start | bytes 393224 | tf_op jit(solution)/shard_map/ppermute | solution.py:430
  57.9 10.8 %collective-permute-start.35 = (bf16[6,32,512]{2,1,0:T(8,128)(2,1)S(1)}, bf16[6,32,512]{2,1,0:T(8,128)(2,1)S(1)}, u32[]{:S(2)}, u32[]{:S(2)}) collective-permute-start(bf16[6,32,512]{2,1,0:T(8,128)(2,1)S(1)} %get-tuple-element.116), channel_id=1, source_target_pairs={{0,8},{4,12},{8,0},{12,4},{1,9},{5,13},{9,1},{13,5},{2,10},{6,14},... | collective-permute-start | bytes 589832 | tf_op jit(solution)/shard_map/ppermute | solution.py:445
  62.7 2.5 %collective-permute-start.36 = (bf16[64,1024]{1,0:T(8,128)(2,1)S(1)}, bf16[64,1024]{1,0:T(8,128)(2,1)S(1)}, u32[]{:S(2)}, u32[]{:S(2)}) collective-permute-start(bf16[64,1024]{1,0:T(8,128)(2,1)S(1)} %get-tuple-element.117.refs_3_), channel_id=1, source_target_pairs={{0,1},{1,0},{2,3},{3,2},{4,5},{5,4},{6,7},{7,6},{8,9},{9,8},{10,11... | collective-permute-start | bytes 393224 | tf_op jit(solution)/shard_map/ppermute | solution.py:430
  64.2 1.9 %collective-permute-start.37 = (bf16[64,1024]{1,0:T(8,128)(2,1)S(1)}, bf16[64,1024]{1,0:T(8,128)(2,1)S(1)}, u32[]{:S(2)}, u32[]{:S(2)}) collective-permute-start(bf16[64,1024]{1,0:T(8,128)(2,1)S(1)} %get-tuple-element.118.refs_4_), channel_id=1, source_target_pairs={{0,1},{1,0},{2,3},{3,2},{4,5},{5,4},{6,7},{7,6},{8,9},{9,8},{10,11... | collective-permute-start | bytes 393224 | tf_op jit(solution)/shard_map/ppermute | solution.py:430
  64.3 3.2 %collective-permute-start.38 = (bf16[64,1024]{1,0:T(8,128)(2,1)S(1)}, bf16[64,1024]{1,0:T(8,128)(2,1)S(1)}, u32[]{:S(2)}, u32[]{:S(2)}) collective-permute-start(bf16[64,1024]{1,0:T(8,128)(2,1)S(1)} %get-tuple-element.119.refs_5_), channel_id=1, source_target_pairs={{0,1},{1,0},{2,3},{3,2},{4,5},{5,4},{6,7},{7,6},{8,9},{9,8},{10,11... | collective-permute-start | bytes 393224 | tf_op jit(solution)/shard_map/ppermute | solution.py:430
  64.7 2.8 %collective-permute-start.39 = (bf16[64,1024]{1,0:T(8,128)(2,1)S(1)}, bf16[64,1024]{1,0:T(8,128)(2,1)S(1)}, u32[]{:S(2)}, u32[]{:S(2)}) collective-permute-start(bf16[64,1024]{1,0:T(8,128)(2,1)S(1)} %get-tuple-element.120.refs_6_), channel_id=1, source_target_pairs={{0,1},{1,0},{2,3},{3,2},{4,5},{5,4},{6,7},{7,6},{8,9},{9,8},{10,11... | collective-permute-start | bytes 393224 | tf_op jit(solution)/shard_map/ppermute | solution.py:430
  65.2 9.0 %collective-permute-start.40 = (bf16[6,32,512]{2,1,0:T(8,128)(2,1)S(1)}, bf16[6,32,512]{2,1,0:T(8,128)(2,1)S(1)}, u32[]{:S(2)}, u32[]{:S(2)}) collective-permute-start(bf16[6,32,512]{2,1,0:T(8,128)(2,1)S(1)} %get-tuple-element.123), channel_id=1, source_target_pairs={{0,4},{4,0},{8,12},{12,8},{1,5},{5,1},{9,13},{13,9},{2,6},{6,2},{1... | collective-permute-start | bytes 589832 | tf_op jit(solution)/shard_map/ppermute | solution.py:445
  66.1 11.0 %collective-permute-start.41 = (bf16[6,32,512]{2,1,0:T(8,128)(2,1)S(1)}, bf16[6,32,512]{2,1,0:T(8,128)(2,1)S(1)}, u32[]{:S(2)}, u32[]{:S(2)}) collective-permute-start(bf16[6,32,512]{2,1,0:T(8,128)(2,1)S(1)} %get-tuple-element.124), channel_id=1, source_target_pairs={{0,12},{4,8},{8,4},{12,0},{1,13},{5,9},{9,5},{13,1},{2,14},{6,10},... | collective-permute-start | bytes 589832 | tf_op jit(solution)/shard_map/ppermute | solution.py:445
  70.8 14.2 %collective-permute-start.42 = (bf16[6,32,512]{2,1,0:T(8,128)(2,1)S(1)}, bf16[6,32,512]{2,1,0:T(8,128)(2,1)S(1)}, u32[]{:S(2)}, u32[]{:S(2)}) collective-permute-start(bf16[6,32,512]{2,1,0:T(8,128)(2,1)S(1)} %get-tuple-element.128), channel_id=1, source_target_pairs={{0,4},{4,0},{8,12},{12,8},{1,5},{5,1},{9,13},{13,9},{2,6},{6,2},{1... | collective-permute-start | bytes 589832 | tf_op jit(solution)/shard_map/ppermute | solution.py:445
  72.1 17.7 %collective-permute-start.43 = (bf16[6,32,512]{2,1,0:T(8,128)(2,1)S(1)}, bf16[6,32,512]{2,1,0:T(8,128)(2,1)S(1)}, u32[]{:S(2)}, u32[]{:S(2)}) collective-permute-start(bf16[6,32,512]{2,1,0:T(8,128)(2,1)S(1)} %get-tuple-element.129), channel_id=1, source_target_pairs={{0,8},{4,12},{8,0},{12,4},{1,9},{5,13},{9,1},{13,5},{2,10},{6,14},... | collective-permute-start | bytes 589832 | tf_op jit(solution)/shard_map/ppermute | solution.py:445
  74.0 20.6 %collective-permute-start.44 = (bf16[6,32,512]{2,1,0:T(8,128)(2,1)S(1)}, bf16[6,32,512]{2,1,0:T(8,128)(2,1)S(1)}, u32[]{:S(2)}, u32[]{:S(2)}) collective-permute-start(bf16[6,32,512]{2,1,0:T(8,128)(2,1)S(1)} %get-tuple-element.130), channel_id=1, source_target_pairs={{0,12},{4,8},{8,4},{12,0},{1,13},{5,9},{9,5},{13,1},{2,14},{6,10},... | collective-permute-start | bytes 589832 | tf_op jit(solution)/shard_map/ppermute | solution.py:445

commit v5 on v4

--- a/solution.py
+++ b/solution.py
@@ -18,10 +18,19 @@
 CHAIN = True
 RESIDENT = True
 TOUCH = False
+OPEN = True
+REUSE = True
+STAGGER = False
+TOUCHED = ()
+CROSS = (2, 2)
+TRAVEL = (1, 1)
+DENOISE = ((1, 2), (2, 2))
+LIMIT = 4
 HOLD = True
+HOLD_CHIP = False
 FIRST = (1, 1)
 SECOND = ((0, 0, 1, 1), (1, 0, 1, 1))
-ORDER = (('pred', 0), ('two', 0), ('pred', 1), ('res', 0), ('two', 1), ('score', 0), ('res', 1), ('chip', 0), ('score', 1), ('chip', 1), ('den', 0), ('chrom', 0), ('den', 1), ('chrom', 1), ('leave', 0), ('leave', 1))
+ORDER = (('pred', 0), ('two', 0), ('pass', 1), ('pred', 1), ('res', 0), ('two', 1), ('score', 0), ('res', 1), ('chip', 0), ('score', 1), ('chip', 1), ('den', 0), ('chrom', 0), ('den', 1), ('chrom', 1), ('leave', 0), ('leave', 1))
 
 
 def denoise(estimate, scores, prior_logit, slab_var, noise_var, marker_root, people_root):
@@ -101,10 +110,10 @@
         self.genotypes = genotypes
         self.token = jnp.zeros((8, 128), jnp.float32)
 
-    def call(self, body, outs, scalars=(), args=(), streamed=False, scratch=(), after=(), into=None, fresh=None):
+    def call(self, body, outs, scalars=(), args=(), streamed=False, scratch=(), after=(), into=None, fresh=None, touch=False, reuse=False):
         geno = self.genotypes
         tiles = geno.shape[1] // TILE
-        given = streamed or TOUCH
+        given = streamed or TOUCH or touch
         after = list(after) + [into] * (into is not None)
         skip = 1 + len(after)
         filled = [fresh] * (fresh is not None) + [jax.ShapeDtypeStruct(one.shape, one.dtype) for one in [into] * (into is not None)]
@@ -145,9 +154,11 @@
             + [pl.BlockSpec(memory_space=VMEM) if RESIDENT else anywhere] * given,
             out_specs=[anywhere] + [pl.BlockSpec(memory_space=VMEM)] * len(outs) + [anywhere] * len(filled),
             scratch_shapes=stream_scratch + list(scratch),
-            input_output_aliases={0: 0} if into is None else {0: 0, skip - 1: 1 + len(outs)},
+            input_output_aliases={0: 0}
+            | ({} if into is None else {skip - 1: 1 + len(outs)})
+            | ({skip + len(scalars): 1} if reuse else {}),
             cost_estimate=pl.CostEstimate(flops=1, bytes_accessed=1, transcendentals=0),
-            compiler_params=pltpu.CompilerParams(vmem_limit_bytes=12 * 2**20),
+            compiler_params=pltpu.CompilerParams(vmem_limit_bytes=LIMIT * 2**20),
         )(self.token, *after, *scalars, *[pltpu.with_memory_space_constraint(a, VMEM) for a in args], *[pltpu.with_memory_space_constraint(geno, VMEM if RESIDENT else pltpu.MemorySpace.HBM)] * given)
         if CHAIN:
             self.token = token
@@ -167,16 +178,41 @@
 
 
 def piece_of(refs, tile):
-    each = refs[0].shape[1] // TILE
-    return refs[tile // each], columns_of(tile % each)
-
-
-def predict_body(own, across, beside, corner, geno, need, keep, send, product):
+    for ref in refs:
+        if tile < ref.shape[1] // TILE:
+            return ref, columns_of(tile)
+        tile -= ref.shape[1] // TILE
+
+
+def copy_body(*refs):
+    count = len(refs) // 2
+    for source, target in zip(refs[:count], refs[count:]):
+        target[...] = source[...]
+
+
+def open_body(source, prior_logit, slab_var, noise_var, target, coefs):
+    target[...] = source[...]
+    slab, noise = slab_var[...], noise_var[...]
+    spread = slab + noise
+    base = prior_logit[...] + 0.5 * jnp.log(noise / spread)
+    curve = 0.5 * (1.0 / noise - 1.0 / spread)
+    shard = slab.shape[1]
+    here = lax.broadcasted_iota(jnp.int32, (shard, shard), 0) == lax.broadcasted_iota(jnp.int32, (shard, shard), 1)
+    lane = lax.broadcasted_iota(jnp.int32, coefs.shape, 1)
+    value = jnp.zeros(coefs.shape, jnp.float32)
+    for at, row in enumerate((base, curve, slab / spread)):
+        column = jnp.sum(jnp.where(here, jnp.broadcast_to(row, here.shape), 0.0), axis=1, keepdims=True)
+        value = jnp.where(lane == at, column, value)
+    coefs[...] = value
+
+
+def predict_body(parts, *refs):
+    blocks, (geno, need, keep, send, product) = refs[: 4 * parts], refs[4 * parts :]
     odd = place()[1] % 2
-    half = 2 * own.shape[0]
+    half = keep.shape[0]
     for tile in range(geno.shape[1] // TILE):
         part = columns_of(tile)
-        rows = jnp.concatenate([own[:, part], across[:, part], beside[:, part], corner[:, part]], axis=0)
+        rows = jnp.concatenate([ref[:, part] for ref in blocks], axis=0)
         need(tile)
         term = lax.dot_general(rows, geno[:, part], NT, preferred_element_type=jnp.float32)
         product[...] = term if tile == 0 else product[...] + term
@@ -220,35 +256,40 @@
 
 
 def chip_body(keep, *refs):
-    *came, chip, send = refs
+    came, chip, sends = refs[:SCORE_SPLIT], refs[SCORE_SPLIT], refs[SCORE_SPLIT + 1 :]
     height = keep.shape[0] // 2
     for tile in range(keep.shape[1] // TILE):
         part = columns_of(tile)
         ref, inner = piece_of(came, tile)
         total = keep[:, part] + ref[:, inner].astype(jnp.float32)
         chip[:, part] = total
-        send[:height, part] = total[height:].astype(send.dtype)
-        send[height:, part] = total[:height].astype(send.dtype)
-
-
-def denoise_body(marker_root, people_root, low, first, own, across, chip, came, coefs, coefs_across, *refs):
-    *updated, whole, stored = refs
+        send, inner = piece_of(sends, tile)
+        send[:height, inner] = total[height:].astype(send.dtype)
+        send[height:, inner] = total[:height].astype(send.dtype)
+
+
+def denoise_body(marker_root, people_root, low, first, begin, parts, pieces, *refs):
+    own, across, (coefs, coefs_across, chip, *refs) = refs[:pieces], refs[pieces : 2 * pieces], refs[2 * pieces :]
+    came, updated, (whole, stored) = refs[:parts], refs[parts:-2], refs[-2:]
     height = updated[0].shape[0] // 2
     at = slice(low, low + height)
     coef = jnp.concatenate([coefs[first : first + height], coefs_across[first : first + height]], axis=0)
     base, curve, gain = coef[:, 0:1], coef[:, 1:2], coef[:, 2:3]
-    for tile in range(own.shape[1] // TILE):
-        part = columns_of(tile)
-        scores = chip[:, part] + came[:, part].astype(jnp.float32)
-        estimate = jnp.concatenate([own[at, part], across[at, part]], axis=0).astype(jnp.float32)
+    width = updated[0].shape[1]
+    for tile in range(len(updated) * width // TILE):
+        part = columns_of(begin + tile)
+        other, inner = piece_of(came, tile)
+        scores = chip[:, part] + other[:, inner].astype(jnp.float32)
+        blocks = [jnp.concatenate([ref[:, part] for ref in block], axis=0)[at] for block in (own, across)]
+        estimate = jnp.concatenate(blocks, axis=0).astype(jnp.float32)
         observed = marker_root * estimate + scores * (1.0 / people_root)
         log_odds = base + curve * observed * observed
         posterior = jax.nn.sigmoid(log_odds) * gain * observed
         ref, inner = piece_of(updated, tile)
         ref[:, inner] = (posterior * (1.0 / marker_root)).astype(ref.dtype)
-    copies, width = [], updated[0].shape[1]
+    copies = []
     for at, ref in enumerate(updated):
-        target = whole.at[pl.ds(first, height), pl.ds(at * width, width)]
+        target = whole.at[pl.ds(first, height), pl.ds(begin * TILE + at * width, width)]
         copies.append(pltpu.make_async_copy(ref.at[pl.ds(0, height)], target, stored.at[at]))
     for copy in copies:
         copy.start()
@@ -256,8 +297,8 @@
         copy.wait()
 
 
-def chrom_body(together, labels, *refs):
-    own, beside, (geno, need, *outs, acc) = refs[:SPLIT], refs[SPLIT : 2 * SPLIT], refs[2 * SPLIT :]
+def chrom_body(together, pieces, labels, *refs):
+    own, beside, (geno, need, *outs, acc) = refs[:pieces], refs[pieces : 2 * pieces], refs[2 * pieces :]
     if together:
         outs = [outs[0].at[to] for to in range(outs[0].shape[0])]
     me, depth = place()
@@ -286,7 +327,7 @@
 
 
 def loco_body(row, shard, tiles, count, labels, phen, *refs):
-    *sums, out, base, acc, stage, done = refs
+    *sums, out, base, stage, done = refs
     height = base.shape[0]
     _, depth = place()
     if len(sums) == 1:
@@ -302,20 +343,14 @@
     def copy(chrom):
         return pltpu.make_async_copy(stage.at[chrom], out.at[chrom, pl.ds(row, height)], done.at[chrom])
 
-    def step(chrom, carry):
-        acc[...] = base[...]
+    for chrom in range(CHROMS):
+        value = base[...]
         for first, part in zip(firsts, sums):
             slot = chrom - first
-
-            @pl.when((slot >= 0) & (slot < SPAN))
-            def _():
-                acc[...] += part[slot].astype(jnp.float32)
-
-        stage[chrom] = acc[...].astype(stage.dtype)
+            inside = ((slot >= 0) & (slot < SPAN)).astype(jnp.float32)
+            value = value + inside * part[jnp.clip(slot, 0, SPAN - 1)].astype(jnp.float32)
+        stage[chrom] = value.astype(stage.dtype)
         copy(chrom).start()
-        return carry
-
-    lax.fori_loop(0, CHROMS, step, 0)
 
     def finish(chrom, carry):
         copy(chrom).wait()
@@ -342,7 +377,7 @@
         out_shape=[jax.ShapeDtypeStruct(shape, jnp.bfloat16), jax.ShapeDtypeStruct(token.shape, token.dtype)],
         in_specs=specs,
         out_specs=[anywhere, anywhere],
-        scratch_shapes=[pltpu.VMEM((height, people), jnp.float32)] * 2
+        scratch_shapes=[pltpu.VMEM((height, people), jnp.float32)]
         + [pltpu.VMEM((shape[0], height, people), jnp.bfloat16), pltpu.SemaphoreType.DMA((shape[0],))],
         input_output_aliases=aliases,
         cost_estimate=pl.CostEstimate(flops=1, bytes_accessed=1, transcendentals=0),
@@ -369,32 +404,44 @@
         row += firsts[-1][1]
     seconds = [(of, firsts[of][1] * a // n, firsts[of][1] * b // n - firsts[of][1] * a // n) for of, a, b, n in SECOND]
 
-    own = [estimate[row : row + height] for row, height in firsts]
-    across = [lax.ppermute(one, "pp", swap) for one in own]
-    beside = [lax.ppermute(one, "sub", swap) for one in own]
-    corner = [lax.ppermute(one, "sub", swap) for one in across]
-    spread = slab_var + noise_var
-    coefs = jnp.stack(
-        [prior_logit + 0.5 * jnp.log(noise_var / spread), 0.5 * (1.0 / noise_var - 1.0 / spread), slab_var / spread],
-        axis=1,
+    own = []
+    for (row, height), count in zip(firsts, TRAVEL):
+        each = height // count
+        own.append([estimate[row + at * each : row + at * each + each] for at in range(count)])
+    steps, whole, loco = Steps(genotypes), None, None
+    across = [[lax.ppermute(one, "pp", swap) for one in own[0]]]
+    mirror = [list(ones) for ones in own]
+    mirror[0][0], coefs = steps.call(
+        open_body,
+        [pltpu.VMEM(own[0][0].shape, estimate.dtype), pltpu.VMEM((shard, 128), jnp.float32)],
+        args=[own[0][0], *[one.reshape(1, shard) for one in (prior_logit, slab_var, noise_var)]],
+        touch=True,
     )
     coefs_across = lax.ppermute(coefs, "pp", swap)
-    steps, whole, loco = Steps(genotypes), None, None
+    for ones in own[1:]:
+        if STAGGER:
+            ones[0] = steps.call(copy_body, [pltpu.VMEM(ones[0].shape, estimate.dtype)], args=ones[:1], after=across[0])[0]
+        across.append([lax.ppermute(one, "pp", swap) for one in ones])
+    beside = [[lax.ppermute(one, "sub", swap) for one in ones] for ones in mirror]
+    corner = [[lax.ppermute(one, "sub", swap) for one in across[0]]] + [None] * (len(across) - 1)
     before, after = [{} for _ in firsts], [{} for _ in seconds]
     f32, bf16 = jnp.float32, jnp.bfloat16
     for stage, at in ORDER:
+        if stage == "pass":
+            shapes = [pltpu.VMEM(one.shape, one.dtype) for one in across[at]]
+            corner[at] = [lax.ppermute(one, "sub", swap) for one in steps.call(copy_body, shapes, args=across[at], after=[coefs_across])]
+            continue
         if stage in ("pred", "two", "res"):
             now, (row, height) = before[at], firsts[at]
         else:
             now, (of, low, height) = after[at], seconds[at]
             row = firsts[of][0] + low
         half, wide = (2 * height, people_dev), (2 * height, mark_dev)
-        narrow = pltpu.VMEM((2 * height, mark_dev // SPLIT), bf16)
         if stage == "pred":
             keep, send = steps.call(
-                predict_body,
+                functools.partial(predict_body, len(own[at])),
                 [pltpu.VMEM(half, f32), pltpu.VMEM(half, bf16)],
-                args=[own[at], across[at], beside[at], corner[at]],
+                args=own[at] + across[at] + beside[at] + corner[at],
                 streamed=True,
                 scratch=[pltpu.VMEM((4 * height, people_dev), f32)],
             )
@@ -404,7 +451,7 @@
             now["two"] = two, lax.ppermute(two, "mk", along(2))
         elif stage == "res":
             body = functools.partial(residual_body, shard, row)
-            (residual,) = steps.call(body, [pltpu.VMEM(half, bf16)], args=[phenotypes, *now["two"]])
+            (residual,) = steps.call(body, [pltpu.VMEM(half, bf16)], args=[phenotypes, *now["two"]], touch=at in TOUCHED)
             now["res"] = residual, lax.ppermute(residual, "mk", along(1))
         elif stage == "score":
             keep, *sends = steps.call(
@@ -412,26 +459,34 @@
                 [pltpu.VMEM(wide, f32)] + [pltpu.VMEM((2 * height, mark_dev // SCORE_SPLIT), bf16)] * SCORE_SPLIT,
                 args=before[of]["res"],
                 streamed=True,
-                after=[coefs_across],
             )
             now["score"] = [keep] + [lax.ppermute(send, "sub", swap) for send in sends]
         elif stage == "chip":
-            chip, send = steps.call(chip_body, [pltpu.VMEM(wide, f32), pltpu.VMEM(wide, bf16)], args=now["score"])
-            now["chip"] = chip, lax.ppermute(send, "pp", swap)
+            held = [after[at - 1]["chip"][1]] if at and CROSS[at - 1] > 1 and HOLD_CHIP else []
+            parts = [pltpu.VMEM((2 * height, mark_dev // CROSS[at]), bf16)] * CROSS[at]
+            chip, *sends = steps.call(chip_body, [pltpu.VMEM(wide, f32), *parts], args=now["score"], after=held, reuse=REUSE)
+            now["chip"] = [chip] + [lax.ppermute(send, "pp", swap) for send in sends]
         elif stage == "den":
-            *updated, whole = steps.call(
-                functools.partial(denoise_body, marker_root, people_root, low, row),
-                [narrow] * SPLIT,
-                args=[own[of], across[of], *now["chip"], coefs, coefs_across],
-                scratch=[pltpu.SemaphoreType.DMA((SPLIT,))],
-                into=whole,
-                fresh=None if whole is not None else jax.ShapeDtypeStruct(estimate.shape, estimate.dtype),
-            )
-            now["den"] = updated + [lax.ppermute(one, "sub", swap) for one in updated]
+            chip, *came = now["chip"]
+            shares = DENOISE[at] if len(came) > 1 else (SPLIT,)
+            per, tiles = len(came) // len(shares), tile_dev // len(shares)
+            ours, theirs = [], []
+            for share, pieces in enumerate(shares):
+                *updated, whole = steps.call(
+                    functools.partial(denoise_body, marker_root, people_root, low, row, share * tiles, per, len(own[of])),
+                    [pltpu.VMEM((2 * height, tiles * TILE // pieces), bf16)] * pieces,
+                    args=[*own[of], *across[of], coefs, coefs_across, chip, *came[share * per : (share + 1) * per]],
+                    scratch=[pltpu.SemaphoreType.DMA((pieces,))],
+                    into=whole,
+                    fresh=None if whole is not None else jax.ShapeDtypeStruct(estimate.shape, estimate.dtype),
+                )
+                ours += updated
+                theirs += [lax.ppermute(one, "sub", swap) for one in updated]
+            now["den"] = ours + theirs
         elif stage == "chrom":
             block, together = (SPAN, height, people_dev), at in TOGETHER
             sums = steps.call(
-                functools.partial(chrom_body, together),
+                functools.partial(chrom_body, together, len(now["den"]) // 2),
                 [pltpu.VMEM((mk_count, *block), bf16)] if together else [pltpu.VMEM(block, bf16)] * mk_count,
                 [tile_chrom],
                 now["den"],

time: 97.5 us -> 95.5 us (0.979)
  waiting for transfers between devices: 37.5 us -> 34.7 us
  Pallas kernels: 16 us -> 17.2 us
    ppermute x16 -> x17, waiting for transfers between devices: 15.2 us -> 6.11 us  [the longest x4 3.75 us: piece_steps(): now['chip'] = [chip] + [lax.ppermute(send, 'pp', swap) for send in sends]]
    ppermute x2, waiting for transfers between devices: 0.2 us -> 2.64 us  [piece_steps(): now['pred'] = (keep, lax.ppermute(send, 'mk', along(1)))]
    ppermute x2, starting transfers between devices: 3.03 us -> 0.63 us  [piece_steps(): now['res'] = (residual, lax.ppermute(residual, 'mk', along(1)))]
    ppermute x1, waiting for transfers between devices: 0.01 us -> 2.36 us  [piece_steps(): coefs_across = lax.ppermute(coefs, 'pp', swap)]
    ppermute x2, waiting for transfers between devices: 0.01 us -> 1.98 us  [piece_steps(): now['two'] = (two, lax.ppermute(two, 'mk', along(2)))]
    pallas_call x14 -> x18, Pallas kernels: 11.4 us -> 13.1 us  [call(): pl.pallas_call(kernel, out_shape=[jax.ShapeDtypeStruct(self.token.shape,...]
    ppermute x6, starting transfers between devices: 7.9 us -> 9.45 us  [piece_steps(): lax.ppermute(sums[step], 'mk', along(step))]
    ppermute x16 -> x17, starting transfers between devices: 13.3 us -> 13.9 us  [the longest x4 4.35 us: piece_steps(): lax.ppermute(one, 'sub', swap)]
  transfers between devices with their start and end apart: 45 -> 46, of which waited for: 21 -> 23; matrix products, arithmetic and copies ran while one was open for 0% -> 0% of each run, Pallas kernels for 14% -> 16%
where the time goes in v5:
time: 95.5 us; the launch traced here: 95.3 us
  starting transfers between devices  37.4 us (39%)
  waiting for transfers between devices  34.7 us (36%)
  Pallas kernels  17.2 us (18%)
  local copies, waits for them, and re-layouts  5.23 us (5%)
    ppermute x6, waiting for transfers between devices, piece_steps(): lax.ppermute(sums[step], 'mk', along(step))  19.2 us
    pallas_call x18, Pallas kernels, call(): pl.pallas_call(kernel, out_shape=[jax.ShapeDtypeStruct(self.token.shape,...  13.1 us
    ppermute x6, starting transfers between devices, piece_steps(): lax.ppermute(sums[step], 'mk', along(step))  9.45 us
    ppermute x16, starting transfers between devices, piece_steps(): now['score'] = [keep] + [lax.ppermute(send, 'sub', swap) for send in sends]  6.57 us
    ppermute x2, starting transfers between devices, piece_steps(): now['two'] = (two, lax.ppermute(two, 'mk', along(2)))  5.26 us
    ppermute x4, starting transfers between devices, piece_steps(): lax.ppermute(one, 'sub', swap)  4.35 us
    unnamed x14, local copies, waits for them, and re-layouts  4.17 us
    pallas_call x2, Pallas kernels, leave_out(): pl.pallas_call(body, out_shape=[jax.ShapeDtypeStruct(shape, jnp.bfloat16)...  4.1 us
  transfers between devices with their start and end apart: 46, of which 23 were waited for; matrix products, arithmetic and copies ran while one was open for 0% of the time, Pallas kernels for 16%

profile of v5, /device:TPU:13, one launch (start us, length us, event | category | flops | bytes accessed | tf_op | source)
XLA Modules:
  0.0 95.3 jit_solution(8735985725999921146)
XLA Ops:
  0.6 1.1 %fusion = (bf16[32,4096]{1,0:T(8,128)(2,1)S(1)}, bf16[32,4096]{1,0:T(8,128)(2,1)S(1)}) fusion(bf16[64,4096]{1,0:T(8,128)(2,1)} %param.8), kind=kLoop, calls=%fused_computation | loop fusion | bytes 1048576 | tf_op jit(solution)/shard_map/slice | solution.py:410
  1.7 1.3 %collective-permute-start = (bf16[32,4096]{1,0:T(8,128)(2,1)S(1)}, bf16[32,4096]{1,0:T(8,128)(2,1)S(1)}, u32[]{:S(2)}, u32[]{:S(2)}) collective-permute-start(bf16[32,4096]{1,0:T(8,128)(2,1)S(1)} %get-tuple-element.153.refs_1_.refs_2_), channel_id=1, source_target_pairs={{0,2},{2,0},{1,3},{3,1},{4,6},{6,4},{5,7},{7,5},{8,10},{10,8},{9,1... | collective-permute-start | bytes 786440 | tf_op jit(solution)/shard_map/ppermute | solution.py:412
  3.0 2.2 %copy-done = bf16[512,4096]{1,0:T(8,128)(2,1)S(1)} copy-done((bf16[512,4096]{1,0:T(8,128)(2,1)S(1)}, bf16[512,4096]{1,0:T(8,128)(2,1)}, u32[]{:S(2)}) %copy-start) | copy-done | bytes 4194328
  5.2 0.7 copy-done.4
  5.8 0.7 copy-done.5
  6.5 0.7 copy-done.6
  7.2 1.0 %collective-permute-start.1 = (bf16[32,4096]{1,0:T(8,128)(2,1)S(1)}, bf16[32,4096]{1,0:T(8,128)(2,1)S(1)}, u32[]{:S(2)}, u32[]{:S(2)}) collective-permute-start(bf16[32,4096]{1,0:T(8,128)(2,1)S(1)} %get-tuple-element.78), channel_id=1, source_target_pairs={{0,1},{1,0},{2,3},{3,2},{4,5},{5,4},{6,7},{7,6},{8,9},{9,8},{10,11... | collective-permute-start | bytes 786440 | tf_op jit(solution)/shard_map/ppermute | solution.py:425
  8.3 0.7 collective-permute-done.refs_2_.refs_3_
  8.9 1.5 %collective-permute-start.2 = (bf16[32,4096]{1,0:T(8,128)(2,1)S(1)}, bf16[32,4096]{1,0:T(8,128)(2,1)S(1)}, u32[]{:S(2)}, u32[]{:S(2)}) collective-permute-start(bf16[32,4096]{1,0:T(8,128)(2,1)S(1)} %collective-permute-done.refs_2_.refs_3_), channel_id=1, source_target_pairs={{0,1},{1,0},{2,3},{3,2},{4,5},{5,4},{6,7},{7,6},{8,9},{9,8},{10,11... | collective-permute-start | bytes 786440 | tf_op jit(solution)/shard_map/ppermute | solution.py:426
  10.5 1.2 %collective-permute-start.5 = (bf16[32,4096]{1,0:T(8,128)(2,1)S(1)}, bf16[32,4096]{1,0:T(8,128)(2,1)S(1)}, u32[]{:S(2)}, u32[]{:S(2)}) collective-permute-start(bf16[32,4096]{1,0:T(8,128)(2,1)S(1)} %get-tuple-element.152.refs_1_.refs_2_), channel_id=1, source_target_pairs={{0,2},{2,0},{1,3},{3,1},{4,6},{6,4},{5,7},{7,5},{8,10},{10,8},{9,1... | collective-permute-start | bytes 786440 | tf_op jit(solution)/shard_map/ppermute | solution.py:424
  11.7 1.6 %shard_map.87 = (f32[8,128]{1,0:T(8,128)S(1)}, f32[64,512]{1,0:T(8,128)S(1)}, bf16[64,512]{1,0:T(8,128)(2,1)S(1)}) custom-call(f32[8,128]{1,0:T(8,128)S(1)} %get-tuple-element.77.refs_0_, bf16[32,4096]{1,0:T(8,128)(2,1)S(1)} %get-tuple-element.153.refs_1_.refs_2_, ...), custom_call_target="tpu_custom_call", output_to_operand_aliasing={{0}: (0, {})} | custom-call | flops 1 | bytes 1 | tf_op jit(solution)/shard_map/pallas_call | solution.py:148
  13.5 1.1 %collective-permute-start.4 = (f32[64,128]{1,0:T(8,128)S(1)}, f32[64,128]{1,0:T(8,128)S(1)}, u32[]{:S(2)}, u32[]{:S(2)}) collective-permute-start(f32[64,128]{1,0:T(8,128)S(1)} %get-tuple-element.83.refs_3_.refs_4_), channel_id=1, source_target_pairs={{0,2},{2,0},{1,3},{3,1},{4,6},{6,4},{5,7},{7,5},{8,10},{10,8},{9,1... | collective-permute-start | bytes 98312 | tf_op jit(solution)/shard_map/ppermute | solution.py:420
  14.7 0.9 collective-permute-start.6
  15.6 1.2 %collective-permute-done.3.refs_2_ = bf16[64,512]{1,0:T(8,128)(2,1)S(1)} collective-permute-done((bf16[64,512]{1,0:T(8,128)(2,1)S(1)}, bf16[64,512]{1,0:T(8,128)(2,1)S(1)}, u32[]{:S(2)}, u32[]{:S(2)}) %collective-permute-start.3) | collective-permute-done | bytes 65568 | tf_op jit(solution)/shard_map/ppermute | solution.py:448
  16.8 2.4 %collective-permute-done.4.refs_1_.refs_4_.refs_5_ = f32[64,128]{1,0:T(8,128)S(1)} collective-permute-done((f32[64,128]{1,0:T(8,128)S(1)}, f32[64,128]{1,0:T(8,128)S(1)}, u32[]{:S(2)}, u32[]{:S(2)}) %collective-permute-start.4) | collective-permute-done | bytes 32800 | tf_op jit(solution)/shard_map/ppermute | solution.py:420
  19.2 0.8 collective-permute-start.7
  20.0 2.3 %collective-permute-start.8 = (bf16[64,512]{1,0:T(8,128)(2,1)S(1)}, bf16[64,512]{1,0:T(8,128)(2,1)S(1)}, u32[]{:S(2)}, u32[]{:S(2)}) collective-permute-start(bf16[64,512]{1,0:T(8,128)(2,1)S(1)} %get-tuple-element.87.refs_2_), channel_id=1, source_target_pairs={{0,8},{4,12},{8,0},{12,4},{1,9},{5,13},{9,1},{13,5},{2,10},{6,14},... | collective-permute-start | bytes 196616 | tf_op jit(solution)/shard_map/ppermute | solution.py:451
  22.3 1.6 %shard_map.90 = (f32[8,128]{1,0:T(8,128)S(1)}, f32[64,512]{1,0:T(8,128)S(1)}, bf16[64,512]{1,0:T(8,128)(2,1)S(1)}) custom-call(f32[8,128]{1,0:T(8,128)S(1)} %get-tuple-element.84.refs_0_, bf16[32,4096]{1,0:T(8,128)(2,1)S(1)} %get-tuple-element.152.refs_1_.refs_2_, ...), custom_call_target="tpu_custom_call", output_to_operand_aliasing={{0}: (0, {})} | custom-call | flops 1 | bytes 1 | tf_op jit(solution)/shard_map/pallas_call | solution.py:148
  24.1 1.3 %collective-permute-done.8.refs_3_ = bf16[64,512]{1,0:T(8,128)(2,1)S(1)} collective-permute-done((bf16[64,512]{1,0:T(8,128)(2,1)S(1)}, bf16[64,512]{1,0:T(8,128)(2,1)S(1)}, u32[]{:S(2)}, u32[]{:S(2)}) %collective-permute-start.8) | collective-permute-done | bytes 65568 | tf_op jit(solution)/shard_map/ppermute | solution.py:451
  25.6 1.5 %collective-permute-done.9.refs_2_ = bf16[64,512]{1,0:T(8,128)(2,1)S(1)} collective-permute-done((bf16[64,512]{1,0:T(8,128)(2,1)S(1)}, bf16[64,512]{1,0:T(8,128)(2,1)S(1)}, u32[]{:S(2)}, u32[]{:S(2)}) %collective-permute-start.9) | collective-permute-done | bytes 65568 | tf_op jit(solution)/shard_map/ppermute | solution.py:448
  27.1 2.9 %collective-permute-start.11 = (bf16[64,512]{1,0:T(8,128)(2,1)S(1)}, bf16[64,512]{1,0:T(8,128)(2,1)S(1)}, u32[]{:S(2)}, u32[]{:S(2)}) collective-permute-start(bf16[64,512]{1,0:T(8,128)(2,1)S(1)} %get-tuple-element.94.refs_2_), channel_id=1, source_target_pairs={{0,8},{4,12},{8,0},{12,4},{1,9},{5,13},{9,1},{13,5},{2,10},{6,14},... | collective-permute-start | bytes 196616 | tf_op jit(solution)/shard_map/ppermute | solution.py:451
  30.0 0.7 shard_map.93
  30.8 0.8 collective-permute-start.12
  31.7 0.4 collective-permute-start.14
  32.2 0.6 collective-permute-done.11.refs_3_
  32.8 1.0 %collective-permute-start.16 = (bf16[64,512]{1,0:T(8,128)(2,1)S(1)}, bf16[64,512]{1,0:T(8,128)(2,1)S(1)}, u32[]{:S(2)}, u32[]{:S(2)}) collective-permute-start(bf16[64,512]{1,0:T(8,128)(2,1)S(1)} %get-tuple-element.101), channel_id=1, source_target_pairs={{0,1},{1,0},{2,3},{3,2},{4,5},{5,4},{6,7},{7,6},{8,9},{9,8},{10,11... | collective-permute-start | bytes 196616 | tf_op jit(solution)/shard_map/ppermute | solution.py:463
  33.9 0.5 collective-permute-start.18
  34.5 0.6 collective-permute-start.20
  35.8 1.3 %collective-permute-start.29 = (bf16[64,2048]{1,0:T(8,128)(2,1)S(1)}, bf16[64,2048]{1,0:T(8,128)(2,1)S(1)}, u32[]{:S(2)}, u32[]{:S(2)}) collective-permute-start(bf16[64,2048]{1,0:T(8,128)(2,1)S(1)} %get-tuple-element.119), channel_id=1, source_target_pairs={{0,2},{2,0},{1,3},{3,1},{4,6},{6,4},{5,7},{7,5},{8,10},{10,8},{9,1... | collective-permute-start | bytes 786440 | tf_op jit(solution)/shard_map/ppermute | solution.py:468
  37.1 0.6 collective-permute-done.20.refs_2_
  37.7 0.7 shard_map.96
  38.4 1.6 %collective-permute-start.21 = (bf16[64,512]{1,0:T(8,128)(2,1)S(1)}, bf16[64,512]{1,0:T(8,128)(2,1)S(1)}, u32[]{:S(2)}, u32[]{:S(2)}) collective-permute-start(bf16[64,512]{1,0:T(8,128)(2,1)S(1)} %get-tuple-element.109), channel_id=1, source_target_pairs={{0,1},{1,0},{2,3},{3,2},{4,5},{5,4},{6,7},{7,6},{8,9},{9,8},{10,11... | collective-permute-start | bytes 196616 | tf_op jit(solution)/shard_map/ppermute | solution.py:463
  40.1 0.4 collective-permute-start.23
  41.3 1.2 %collective-permute-start.30 = (bf16[64,2048]{1,0:T(8,128)(2,1)S(1)}, bf16[64,2048]{1,0:T(8,128)(2,1)S(1)}, u32[]{:S(2)}, u32[]{:S(2)}) collective-permute-start(bf16[64,2048]{1,0:T(8,128)(2,1)S(1)} %get-tuple-element.122), channel_id=1, source_target_pairs={{0,2},{2,0},{1,3},{3,1},{4,6},{6,4},{5,7},{7,5},{8,10},{10,8},{9,1... | collective-permute-start | bytes 786440 | tf_op jit(solution)/shard_map/ppermute | solution.py:468
  42.5 0.4 collective-permute-start.26
  43.0 0.4 collective-permute-start.28
  43.5 0.4 collective-permute-done.26.refs_7_
  44.6 1.0 shard_map.98
  45.6 0.4 collective-permute-start.31
  46.0 1.0 %collective-permute-start.34 = (bf16[64,2048]{1,0:T(8,128)(2,1)S(1)}, bf16[64,2048]{1,0:T(8,128)(2,1)S(1)}, u32[]{:S(2)}, u32[]{:S(2)}) collective-permute-start(bf16[64,2048]{1,0:T(8,128)(2,1)S(1)} %get-tuple-element.130), channel_id=1, source_target_pairs={{0,2},{2,0},{1,3},{3,1},{4,6},{6,4},{5,7},{7,5},{8,10},{10,8},{9,1... | collective-permute-start | bytes 786440 | tf_op jit(solution)/shard_map/ppermute | solution.py:468
  47.0 0.5 collective-permute-start.35
  47.5 2.0 %collective-permute-done.30.refs_7_ = bf16[64,2048]{1,0:T(8,128)(2,1)S(1)} collective-permute-done((bf16[64,2048]{1,0:T(8,128)(2,1)S(1)}, bf16[64,2048]{1,0:T(8,128)(2,1)S(1)}, u32[]{:S(2)}, u32[]{:S(2)}) %collective-permute-start.30) | collective-permute-done | bytes 262176 | tf_op jit(solution)/shard_map/ppermute | solution.py:468
  49.5 0.9 shard_map.99
  50.4 1.2 %collective-permute-start.32 = (bf16[64,1024]{1,0:T(8,128)(2,1)S(1)}, bf16[64,1024]{1,0:T(8,128)(2,1)S(1)}, u32[]{:S(2)}, u32[]{:S(2)}) collective-permute-start(bf16[64,1024]{1,0:T(8,128)(2,1)S(1)} %get-tuple-element.125.refs_3_), channel_id=1, source_target_pairs={{0,1},{1,0},{2,3},{3,2},{4,5},{5,4},{6,7},{7,6},{8,9},{9,8},{10,11... | collective-permute-start | bytes 393224 | tf_op jit(solution)/shard_map/ppermute | solution.py:484
  51.7 0.9 collective-permute-done.32.refs_6_
  53.0 2.1 %shard_map.100 = (f32[8,128]{1,0:T(8,128)S(1)}, bf16[6,32,512]{2,1,0:T(8,128)(2,1)S(1)}, bf16[6,32,512]{2,1,0:T(8,128)(2,1)S(1)}, bf16[6,32,512]{2,1,0:T(8,128)(2,1)S(1)}, bf16[6,32,512]{2,1,0:T(8,128)(2,1)S(1)}) custom-call(f32[8,128]{1,0:T(8,128)S(1)} %get-tuple-element.123.refs_0_, s32[32]{0:T(128)S(1)} %copy-done.3, ...), custom_call_target="tpu_custom_call", output_to_operand_aliasing={{0}: (0, {})} | custom-call | flops 1 | bytes 1 | tf_op jit(solution)/shard_map/pallas_call | solution.py:148
  55.0 3.0 %collective-permute-start.36 = (bf16[6,32,512]{2,1,0:T(8,128)(2,1)S(1)}, bf16[6,32,512]{2,1,0:T(8,128)(2,1)S(1)}, u32[]{:S(2)}, u32[]{:S(2)}) collective-permute-start(bf16[6,32,512]{2,1,0:T(8,128)(2,1)S(1)} %get-tuple-element.136), channel_id=1, source_target_pairs={{0,8},{4,12},{8,0},{12,4},{1,9},{5,13},{9,1},{13,5},{2,10},{6,14},... | collective-permute-start | bytes 589832 | tf_op jit(solution)/shard_map/ppermute | solution.py:500
  58.0 0.9 shard_map.101
  59.0 1.7 %collective-permute-done.35.refs_7_ = bf16[64,2048]{1,0:T(8,128)(2,1)S(1)} collective-permute-done((bf16[64,2048]{1,0:T(8,128)(2,1)S(1)}, bf16[64,2048]{1,0:T(8,128)(2,1)S(1)}, u32[]{:S(2)}, u32[]{:S(2)}) %collective-permute-start.35) | collective-permute-done | bytes 262176 | tf_op jit(solution)/shard_map/ppermute | solution.py:468
  60.7 0.9 shard_map.102
  61.7 0.8 collective-permute-start.39
  62.6 0.4 collective-permute-start.37
  63.1 0.4 collective-permute-done.39.refs_9_
  63.5 0.5 collective-permute-start.41
  64.0 2.7 %collective-permute-start.42 = (bf16[6,32,512]{2,1,0:T(8,128)(2,1)S(1)}, bf16[6,32,512]{2,1,0:T(8,128)(2,1)S(1)}, u32[]{:S(2)}, u32[]{:S(2)}) collective-permute-start(bf16[6,32,512]{2,1,0:T(8,128)(2,1)S(1)} %get-tuple-element.144), channel_id=1, source_target_pairs={{0,12},{4,8},{8,4},{12,0},{1,13},{5,9},{9,5},{13,1},{2,14},{6,10},... | collective-permute-start | bytes 589832 | tf_op jit(solution)/shard_map/ppermute | solution.py:500
  66.7 2.1 %shard_map.103 = (f32[8,128]{1,0:T(8,128)S(1)}, bf16[6,32,512]{2,1,0:T(8,128)(2,1)S(1)}, bf16[6,32,512]{2,1,0:T(8,128)(2,1)S(1)}, bf16[6,32,512]{2,1,0:T(8,128)(2,1)S(1)}, bf16[6,32,512]{2,1,0:T(8,128)(2,1)S(1)}) custom-call(f32[8,128]{1,0:T(8,128)S(1)} %get-tuple-element.135.refs_0_, ...), custom_call_target="tpu_custom_call", output_to_operand_aliasing={{0}: (0, {})} | custom-call | flops 1 | bytes 1 | tf_op jit(solution)/shard_map/pallas_call | solution.py:148
  68.8 1.5 %collective-permute-start.43 = (bf16[6,32,512]{2,1,0:T(8,128)(2,1)S(1)}, bf16[6,32,512]{2,1,0:T(8,128)(2,1)S(1)}, u32[]{:S(2)}, u32[]{:S(2)}) collective-permute-start(bf16[6,32,512]{2,1,0:T(8,128)(2,1)S(1)} %get-tuple-element.148), channel_id=1, source_target_pairs={{0,4},{4,0},{8,12},{12,8},{1,5},{5,1},{9,13},{13,9},{2,6},{6,2},{1... | collective-permute-start | bytes 589832 | tf_op jit(solution)/shard_map/ppermute | solution.py:500
  70.3 1.5 %collective-permute-start.44 = (bf16[6,32,512]{2,1,0:T(8,128)(2,1)S(1)}, bf16[6,32,512]{2,1,0:T(8,128)(2,1)S(1)}, u32[]{:S(2)}, u32[]{:S(2)}) collective-permute-start(bf16[6,32,512]{2,1,0:T(8,128)(2,1)S(1)} %get-tuple-element.149), channel_id=1, source_target_pairs={{0,8},{4,12},{8,0},{12,4},{1,9},{5,13},{9,1},{13,5},{2,10},{6,14},... | collective-permute-start | bytes 589832 | tf_op jit(solution)/shard_map/ppermute | solution.py:500
  72.0 2.0 %collective-permute-done.42.refs_6_ = bf16[6,32,512]{2,1,0:T(8,128)(2,1)S(1)} collective-permute-done((bf16[6,32,512]{2,1,0:T(8,128)(2,1)S(1)}, bf16[6,32,512]{2,1,0:T(8,128)(2,1)S(1)}, u32[]{:S(2)}, u32[]{:S(2)}) %collective-permute-start.42) | collective-permute-done | bytes 196640 | tf_op jit(solution)/shard_map/ppermute | solution.py:500
  74.1 2.1 %shard_map.104 = (bf16[22,64,512]{2,1,0:T(8,128)(2,1)}, f32[8,128]{1,0:T(8,128)S(1)}) custom-call(f32[8,128]{1,0:T(8,128)S(1)} %get-tuple-element.141.refs_0_, s32[32]{0:T(128)S(1)} %copy-done.3, bf16[256,512]{1,0:T(8,128)(2,1)S(1)} %copy-done.2, bf16[6,32,512]{2,1,0:T(8,128)(2,1)S(1)} %get-tuple-element.142.refs_3_, ...), custom_call_target="tpu_custom_call", output_to_operand_aliasing={{1}: (0, {})} | custom-call | flops 1 | bytes 1 | tf_op jit(solution)/shard_map/pallas_call | solution.py:375
  76.1 6.5 %collective-permute-done.43.refs_5_ = bf16[6,32,512]{2,1,0:T(8,128)(2,1)S(1)} collective-permute-done((bf16[6,32,512]{2,1,0:T(8,128)(2,1)S(1)}, bf16[6,32,512]{2,1,0:T(8,128)(2,1)S(1)}, u32[]{:S(2)}, u32[]{:S(2)}) %collective-permute-start.43) | collective-permute-done | bytes 196640 | tf_op jit(solution)/shard_map/ppermute | solution.py:500
  82.6 4.4 %collective-permute-done.44.refs_6_ = bf16[6,32,512]{2,1,0:T(8,128)(2,1)S(1)} collective-permute-done((bf16[6,32,512]{2,1,0:T(8,128)(2,1)S(1)}, bf16[6,32,512]{2,1,0:T(8,128)(2,1)S(1)}, u32[]{:S(2)}, u32[]{:S(2)}) %collective-permute-start.44) | collective-permute-done | bytes 196640 | tf_op jit(solution)/shard_map/ppermute | solution.py:500
  87.0 6.3 %collective-permute-done.45.refs_7_ = bf16[6,32,512]{2,1,0:T(8,128)(2,1)S(1)} collective-permute-done((bf16[6,32,512]{2,1,0:T(8,128)(2,1)S(1)}, bf16[6,32,512]{2,1,0:T(8,128)(2,1)S(1)}, u32[]{:S(2)}, u32[]{:S(2)}) %collective-permute-start.45) | collective-permute-done | bytes 196640 | tf_op jit(solution)/shard_map/ppermute | solution.py:500
  93.3 2.1 %shard_map.105 = (bf16[22,64,512]{2,1,0:T(8,128)(2,1)}, f32[8,128]{1,0:T(8,128)S(1)}) custom-call(bf16[22,64,512]{2,1,0:T(8,128)(2,1)} %get-tuple-element.145.refs_0_, f32[8,128]{1,0:T(8,128)S(1)} %get-tuple-element.146.refs_1_, s32[32]{0:T(128)S(1)} %copy-done.3, bf16[256,512]{1,0:T(8,128)(2,1)S(1)} %copy-done.2, ...), custom_call_target="tpu_custom_call", output_to_operand_aliasing={{0}: (0, {}), {1}: (1, {})} | custom-call | flops 1 | bytes 1 | tf_op jit(solution)/shard_map/pallas_call | solution.py:375
  (64 shorter events, 4.3 us)
Async XLA Ops:
  1.7 7.2 %collective-permute-start = (bf16[32,4096]{1,0:T(8,128)(2,1)S(1)}, bf16[32,4096]{1,0:T(8,128)(2,1)S(1)}, u32[]{:S(2)}, u32[]{:S(2)}) collective-permute-start(bf16[32,4096]{1,0:T(8,128)(2,1)S(1)} %get-tuple-element.153.refs_1_.refs_2_), channel_id=1, source_target_pairs={{0,2},{2,0},{1,3},{3,1},{4,6},{6,4},{5,7},{7,5},{8,10},{10,8},{9,1... | collective-permute-start | bytes 786440 | tf_op jit(solution)/shard_map/ppermute | solution.py:412
  3.0 2.2 %copy-start = (bf16[512,4096]{1,0:T(8,128)(2,1)S(1)}, bf16[512,4096]{1,0:T(8,128)(2,1)}, u32[]{:S(2)}) copy-start(bf16[512,4096]{1,0:T(8,128)(2,1)} %refs_11_.1) | copy-start | bytes 12582916
  5.2 0.7 copy-start.4
  5.8 0.7 copy-start.5
  6.5 0.7 copy-start.6
  7.1 4.6 %copy-start.1 = (bf16[512,4096]{1,0:T(8,128)(2,1)S(1)}, bf16[512,4096]{1,0:T(8,128)(2,1)}, u32[]{:S(2)}) copy-start(bf16[512,4096]{1,0:T(8,128)(2,1)} %refs_11_.1) | copy-start | bytes 12582916
  7.2 4.5 %collective-permute-start.1 = (bf16[32,4096]{1,0:T(8,128)(2,1)S(1)}, bf16[32,4096]{1,0:T(8,128)(2,1)S(1)}, u32[]{:S(2)}, u32[]{:S(2)}) collective-permute-start(bf16[32,4096]{1,0:T(8,128)(2,1)S(1)} %get-tuple-element.78), channel_id=1, source_target_pairs={{0,1},{1,0},{2,3},{3,2},{4,5},{5,4},{6,7},{7,6},{8,9},{9,8},{10,11... | collective-permute-start | bytes 786440 | tf_op jit(solution)/shard_map/ppermute | solution.py:425
  8.9 2.8 %collective-permute-start.2 = (bf16[32,4096]{1,0:T(8,128)(2,1)S(1)}, bf16[32,4096]{1,0:T(8,128)(2,1)S(1)}, u32[]{:S(2)}, u32[]{:S(2)}) collective-permute-start(bf16[32,4096]{1,0:T(8,128)(2,1)S(1)} %collective-permute-done.refs_2_.refs_3_), channel_id=1, source_target_pairs={{0,1},{1,0},{2,3},{3,2},{4,5},{5,4},{6,7},{7,6},{8,9},{9,8},{10,11... | collective-permute-start | bytes 786440 | tf_op jit(solution)/shard_map/ppermute | solution.py:426
  10.5 8.6 %collective-permute-start.5 = (bf16[32,4096]{1,0:T(8,128)(2,1)S(1)}, bf16[32,4096]{1,0:T(8,128)(2,1)S(1)}, u32[]{:S(2)}, u32[]{:S(2)}) collective-permute-start(bf16[32,4096]{1,0:T(8,128)(2,1)S(1)} %get-tuple-element.152.refs_1_.refs_2_), channel_id=1, source_target_pairs={{0,2},{2,0},{1,3},{3,1},{4,6},{6,4},{5,7},{7,5},{8,10},{10,8},{9,1... | collective-permute-start | bytes 786440 | tf_op jit(solution)/shard_map/ppermute | solution.py:424
  13.3 3.5 %collective-permute-start.3 = (bf16[64,512]{1,0:T(8,128)(2,1)S(1)}, bf16[64,512]{1,0:T(8,128)(2,1)S(1)}, u32[]{:S(2)}, u32[]{:S(2)}) collective-permute-start(bf16[64,512]{1,0:T(8,128)(2,1)S(1)} %get-tuple-element.81), channel_id=1, source_target_pairs={{0,4},{4,0},{8,12},{12,8},{1,5},{5,1},{9,13},{13,9},{2,6},{6,2},{1... | collective-permute-start | bytes 196616 | tf_op jit(solution)/shard_map/ppermute | solution.py:448
  13.5 5.6 %collective-permute-start.4 = (f32[64,128]{1,0:T(8,128)S(1)}, f32[64,128]{1,0:T(8,128)S(1)}, u32[]{:S(2)}, u32[]{:S(2)}) collective-permute-start(f32[64,128]{1,0:T(8,128)S(1)} %get-tuple-element.83.refs_3_.refs_4_), channel_id=1, source_target_pairs={{0,2},{2,0},{1,3},{3,1},{4,6},{6,4},{5,7},{7,5},{8,10},{10,8},{9,1... | collective-permute-start | bytes 98312 | tf_op jit(solution)/shard_map/ppermute | solution.py:420
  14.7 7.7 %collective-permute-start.6 = (bf16[32,4096]{1,0:T(8,128)(2,1)S(1)}, bf16[32,4096]{1,0:T(8,128)(2,1)S(1)}, u32[]{:S(2)}, u32[]{:S(2)}) collective-permute-start(bf16[32,4096]{1,0:T(8,128)(2,1)S(1)} %get-tuple-element.152.refs_1_.refs_2_), channel_id=1, source_target_pairs={{0,1},{1,0},{2,3},{3,2},{4,5},{5,4},{6,7},{7,6},{8,9},{9,8},{10,11... | collective-permute-start | bytes 786440 | tf_op jit(solution)/shard_map/ppermute | solution.py:425
  19.2 3.2 %collective-permute-start.7 = (bf16[32,4096]{1,0:T(8,128)(2,1)S(1)}, bf16[32,4096]{1,0:T(8,128)(2,1)S(1)}, u32[]{:S(2)}, u32[]{:S(2)}) collective-permute-start(bf16[32,4096]{1,0:T(8,128)(2,1)S(1)} %get-tuple-element.85), channel_id=1, source_target_pairs={{0,1},{1,0},{2,3},{3,2},{4,5},{5,4},{6,7},{7,6},{8,9},{9,8},{10,11... | collective-permute-start | bytes 786440 | tf_op jit(solution)/shard_map/ppermute | solution.py:432
  20.0 5.5 %collective-permute-start.8 = (bf16[64,512]{1,0:T(8,128)(2,1)S(1)}, bf16[64,512]{1,0:T(8,128)(2,1)S(1)}, u32[]{:S(2)}, u32[]{:S(2)}) collective-permute-start(bf16[64,512]{1,0:T(8,128)(2,1)S(1)} %get-tuple-element.87.refs_2_), channel_id=1, source_target_pairs={{0,8},{4,12},{8,0},{12,4},{1,9},{5,13},{9,1},{13,5},{2,10},{6,14},... | collective-permute-start | bytes 196616 | tf_op jit(solution)/shard_map/ppermute | solution.py:451
  22.3 3.1 %copy-start.2 = (bf16[256,512]{1,0:T(8,128)(2,1)S(1)}, bf16[256,512]{1,0:T(8,128)(2,1)}, u32[]{:S(2)}) copy-start(bf16[256,512]{1,0:T(8,128)(2,1)} %refs_3_.5) | copy-start | bytes 786436
  23.9 3.2 %collective-permute-start.9 = (bf16[64,512]{1,0:T(8,128)(2,1)S(1)}, bf16[64,512]{1,0:T(8,128)(2,1)S(1)}, u32[]{:S(2)}, u32[]{:S(2)}) collective-permute-start(bf16[64,512]{1,0:T(8,128)(2,1)S(1)} %get-tuple-element.90), channel_id=1, source_target_pairs={{0,4},{4,0},{8,12},{12,8},{1,5},{5,1},{9,13},{13,9},{2,6},{6,2},{1... | collective-permute-start | bytes 196616 | tf_op jit(solution)/shard_map/ppermute | solution.py:448
  25.5 4.5 %collective-permute-start.10 = (bf16[64,512]{1,0:T(8,128)(2,1)S(1)}, bf16[64,512]{1,0:T(8,128)(2,1)S(1)}, u32[]{:S(2)}, u32[]{:S(2)}) collective-permute-start(bf16[64,512]{1,0:T(8,128)(2,1)S(1)} %get-tuple-element.92.refs_1_), channel_id=1, source_target_pairs={{0,4},{4,0},{8,12},{12,8},{1,5},{5,1},{9,13},{13,9},{2,6},{6,2},{1... | collective-permute-start | bytes 196616 | tf_op jit(solution)/shard_map/ppermute | solution.py:455
  27.1 5.7 %collective-permute-start.11 = (bf16[64,512]{1,0:T(8,128)(2,1)S(1)}, bf16[64,512]{1,0:T(8,128)(2,1)S(1)}, u32[]{:S(2)}, u32[]{:S(2)}) collective-permute-start(bf16[64,512]{1,0:T(8,128)(2,1)S(1)} %get-tuple-element.94.refs_2_), channel_id=1, source_target_pairs={{0,8},{4,12},{8,0},{12,4},{1,9},{5,13},{9,1},{13,5},{2,10},{6,14},... | collective-permute-start | bytes 196616 | tf_op jit(solution)/shard_map/ppermute | solution.py:451
  30.8 3.1 %collective-permute-start.12 = (bf16[64,512]{1,0:T(8,128)(2,1)S(1)}, bf16[64,512]{1,0:T(8,128)(2,1)S(1)}, u32[]{:S(2)}, u32[]{:S(2)}) collective-permute-start(bf16[64,512]{1,0:T(8,128)(2,1)S(1)} %get-tuple-element.97), channel_id=1, source_target_pairs={{0,1},{1,0},{2,3},{3,2},{4,5},{5,4},{6,7},{7,6},{8,9},{9,8},{10,11... | collective-permute-start | bytes 196616 | tf_op jit(solution)/shard_map/ppermute | solution.py:463
  31.6 2.3 %collective-permute-start.13 = (bf16[64,512]{1,0:T(8,128)(2,1)S(1)}, bf16[64,512]{1,0:T(8,128)(2,1)S(1)}, u32[]{:S(2)}, u32[]{:S(2)}) collective-permute-start(bf16[64,512]{1,0:T(8,128)(2,1)S(1)} %get-tuple-element.98), channel_id=1, source_target_pairs={{0,1},{1,0},{2,3},{3,2},{4,5},{5,4},{6,7},{7,6},{8,9},{9,8},{10,11... | collective-permute-start | bytes 196616 | tf_op jit(solution)/shard_map/ppermute | solution.py:463
  31.7 2.7 %collective-permute-start.14 = (bf16[64,512]{1,0:T(8,128)(2,1)S(1)}, bf16[64,512]{1,0:T(8,128)(2,1)S(1)}, u32[]{:S(2)}, u32[]{:S(2)}) collective-permute-start(bf16[64,512]{1,0:T(8,128)(2,1)S(1)} %get-tuple-element.99), channel_id=1, source_target_pairs={{0,1},{1,0},{2,3},{3,2},{4,5},{5,4},{6,7},{7,6},{8,9},{9,8},{10,11... | collective-permute-start | bytes 196616 | tf_op jit(solution)/shard_map/ppermute | solution.py:463
  32.1 2.4 %collective-permute-start.15 = (bf16[64,512]{1,0:T(8,128)(2,1)S(1)}, bf16[64,512]{1,0:T(8,128)(2,1)S(1)}, u32[]{:S(2)}, u32[]{:S(2)}) collective-permute-start(bf16[64,512]{1,0:T(8,128)(2,1)S(1)} %get-tuple-element.100), channel_id=1, source_target_pairs={{0,1},{1,0},{2,3},{3,2},{4,5},{5,4},{6,7},{7,6},{8,9},{9,8},{10,11... | collective-permute-start | bytes 196616 | tf_op jit(solution)/shard_map/ppermute | solution.py:463
  32.8 2.2 %collective-permute-start.16 = (bf16[64,512]{1,0:T(8,128)(2,1)S(1)}, bf16[64,512]{1,0:T(8,128)(2,1)S(1)}, u32[]{:S(2)}, u32[]{:S(2)}) collective-permute-start(bf16[64,512]{1,0:T(8,128)(2,1)S(1)} %get-tuple-element.101), channel_id=1, source_target_pairs={{0,1},{1,0},{2,3},{3,2},{4,5},{5,4},{6,7},{7,6},{8,9},{9,8},{10,11... | collective-permute-start | bytes 196616 | tf_op jit(solution)/shard_map/ppermute | solution.py:463
  33.9 1.3 %collective-permute-start.17 = (bf16[64,512]{1,0:T(8,128)(2,1)S(1)}, bf16[64,512]{1,0:T(8,128)(2,1)S(1)}, u32[]{:S(2)}, u32[]{:S(2)}) collective-permute-start(bf16[64,512]{1,0:T(8,128)(2,1)S(1)} %get-tuple-element.102), channel_id=1, source_target_pairs={{0,1},{1,0},{2,3},{3,2},{4,5},{5,4},{6,7},{7,6},{8,9},{9,8},{10,11... | collective-permute-start | bytes 196616 | tf_op jit(solution)/shard_map/ppermute | solution.py:463
  33.9 1.4 %collective-permute-start.18 = (bf16[64,512]{1,0:T(8,128)(2,1)S(1)}, bf16[64,512]{1,0:T(8,128)(2,1)S(1)}, u32[]{:S(2)}, u32[]{:S(2)}) collective-permute-start(bf16[64,512]{1,0:T(8,128)(2,1)S(1)} %get-tuple-element.103), channel_id=1, source_target_pairs={{0,1},{1,0},{2,3},{3,2},{4,5},{5,4},{6,7},{7,6},{8,9},{9,8},{10,11... | collective-permute-start | bytes 196616 | tf_op jit(solution)/shard_map/ppermute | solution.py:463
  34.4 1.3 %collective-permute-start.19 = (bf16[64,512]{1,0:T(8,128)(2,1)S(1)}, bf16[64,512]{1,0:T(8,128)(2,1)S(1)}, u32[]{:S(2)}, u32[]{:S(2)}) collective-permute-start(bf16[64,512]{1,0:T(8,128)(2,1)S(1)} %get-tuple-element.104), channel_id=1, source_target_pairs={{0,1},{1,0},{2,3},{3,2},{4,5},{5,4},{6,7},{7,6},{8,9},{9,8},{10,11... | collective-permute-start | bytes 196616 | tf_op jit(solution)/shard_map/ppermute | solution.py:463
  34.5 3.2 %collective-permute-start.20 = (bf16[64,512]{1,0:T(8,128)(2,1)S(1)}, bf16[64,512]{1,0:T(8,128)(2,1)S(1)}, u32[]{:S(2)}, u32[]{:S(2)}) collective-permute-start(bf16[64,512]{1,0:T(8,128)(2,1)S(1)} %get-tuple-element.106.refs_1_), channel_id=1, source_target_pairs={{0,4},{4,0},{8,12},{12,8},{1,5},{5,1},{9,13},{13,9},{2,6},{6,2},{1... | collective-permute-start | bytes 196616 | tf_op jit(solution)/shard_map/ppermute | solution.py:455
  35.8 8.8 %collective-permute-start.29 = (bf16[64,2048]{1,0:T(8,128)(2,1)S(1)}, bf16[64,2048]{1,0:T(8,128)(2,1)S(1)}, u32[]{:S(2)}, u32[]{:S(2)}) collective-permute-start(bf16[64,2048]{1,0:T(8,128)(2,1)S(1)} %get-tuple-element.119), channel_id=1, source_target_pairs={{0,2},{2,0},{1,3},{3,1},{4,6},{6,4},{5,7},{7,5},{8,10},{10,8},{9,1... | collective-permute-start | bytes 786440 | tf_op jit(solution)/shard_map/ppermute | solution.py:468
  38.4 2.6 %collective-permute-start.21 = (bf16[64,512]{1,0:T(8,128)(2,1)S(1)}, bf16[64,512]{1,0:T(8,128)(2,1)S(1)}, u32[]{:S(2)}, u32[]{:S(2)}) collective-permute-start(bf16[64,512]{1,0:T(8,128)(2,1)S(1)} %get-tuple-element.109), channel_id=1, source_target_pairs={{0,1},{1,0},{2,3},{3,2},{4,5},{5,4},{6,7},{7,6},{8,9},{9,8},{10,11... | collective-permute-start | bytes 196616 | tf_op jit(solution)/shard_map/ppermute | solution.py:463
  40.0 1.3 %collective-permute-start.22 = (bf16[64,512]{1,0:T(8,128)(2,1)S(1)}, bf16[64,512]{1,0:T(8,128)(2,1)S(1)}, u32[]{:S(2)}, u32[]{:S(2)}) collective-permute-start(bf16[64,512]{1,0:T(8,128)(2,1)S(1)} %get-tuple-element.110), channel_id=1, source_target_pairs={{0,1},{1,0},{2,3},{3,2},{4,5},{5,4},{6,7},{7,6},{8,9},{9,8},{10,11... | collective-permute-start | bytes 196616 | tf_op jit(solution)/shard_map/ppermute | solution.py:463
  40.1 2.4 %collective-permute-start.23 = (bf16[64,512]{1,0:T(8,128)(2,1)S(1)}, bf16[64,512]{1,0:T(8,128)(2,1)S(1)}, u32[]{:S(2)}, u32[]{:S(2)}) collective-permute-start(bf16[64,512]{1,0:T(8,128)(2,1)S(1)} %get-tuple-element.111), channel_id=1, source_target_pairs={{0,1},{1,0},{2,3},{3,2},{4,5},{5,4},{6,7},{7,6},{8,9},{9,8},{10,11... | collective-permute-start | bytes 196616 | tf_op jit(solution)/shard_map/ppermute | solution.py:463
  40.6 2.4 %collective-permute-start.24 = (bf16[64,512]{1,0:T(8,128)(2,1)S(1)}, bf16[64,512]{1,0:T(8,128)(2,1)S(1)}, u32[]{:S(2)}, u32[]{:S(2)}) collective-permute-start(bf16[64,512]{1,0:T(8,128)(2,1)S(1)} %get-tuple-element.112), channel_id=1, source_target_pairs={{0,1},{1,0},{2,3},{3,2},{4,5},{5,4},{6,7},{7,6},{8,9},{9,8},{10,11... | collective-permute-start | bytes 196616 | tf_op jit(solution)/shard_map/ppermute | solution.py:463
  40.9 2.1 %collective-permute-start.25 = (bf16[64,512]{1,0:T(8,128)(2,1)S(1)}, bf16[64,512]{1,0:T(8,128)(2,1)S(1)}, u32[]{:S(2)}, u32[]{:S(2)}) collective-permute-start(bf16[64,512]{1,0:T(8,128)(2,1)S(1)} %get-tuple-element.113), channel_id=1, source_target_pairs={{0,1},{1,0},{2,3},{3,2},{4,5},{5,4},{6,7},{7,6},{8,9},{9,8},{10,11... | collective-permute-start | bytes 196616 | tf_op jit(solution)/shard_map/ppermute | solution.py:463
  41.3 8.2 %collective-permute-start.30 = (bf16[64,2048]{1,0:T(8,128)(2,1)S(1)}, bf16[64,2048]{1,0:T(8,128)(2,1)S(1)}, u32[]{:S(2)}, u32[]{:S(2)}) collective-permute-start(bf16[64,2048]{1,0:T(8,128)(2,1)S(1)} %get-tuple-element.122), channel_id=1, source_target_pairs={{0,2},{2,0},{1,3},{3,1},{4,6},{6,4},{5,7},{7,5},{8,10},{10,8},{9,1... | collective-permute-start | bytes 786440 | tf_op jit(solution)/shard_map/ppermute | solution.py:468
  42.5 1.3 %collective-permute-start.26 = (bf16[64,512]{1,0:T(8,128)(2,1)S(1)}, bf16[64,512]{1,0:T(8,128)(2,1)S(1)}, u32[]{:S(2)}, u32[]{:S(2)}) collective-permute-start(bf16[64,512]{1,0:T(8,128)(2,1)S(1)} %get-tuple-element.114), channel_id=1, source_target_pairs={{0,1},{1,0},{2,3},{3,2},{4,5},{5,4},{6,7},{7,6},{8,9},{9,8},{10,11... | collective-permute-start | bytes 196616 | tf_op jit(solution)/shard_map/ppermute | solution.py:463
  43.0 1.3 %collective-permute-start.27 = (bf16[64,512]{1,0:T(8,128)(2,1)S(1)}, bf16[64,512]{1,0:T(8,128)(2,1)S(1)}, u32[]{:S(2)}, u32[]{:S(2)}) collective-permute-start(bf16[64,512]{1,0:T(8,128)(2,1)S(1)} %get-tuple-element.115), channel_id=1, source_target_pairs={{0,1},{1,0},{2,3},{3,2},{4,5},{5,4},{6,7},{7,6},{8,9},{9,8},{10,11... | collective-permute-start | bytes 196616 | tf_op jit(solution)/shard_map/ppermute | solution.py:463
  43.0 1.3 %collective-permute-start.28 = (bf16[64,512]{1,0:T(8,128)(2,1)S(1)}, bf16[64,512]{1,0:T(8,128)(2,1)S(1)}, u32[]{:S(2)}, u32[]{:S(2)}) collective-permute-start(bf16[64,512]{1,0:T(8,128)(2,1)S(1)} %get-tuple-element.116), channel_id=1, source_target_pairs={{0,1},{1,0},{2,3},{3,2},{4,5},{5,4},{6,7},{7,6},{8,9},{9,8},{10,11... | collective-permute-start | bytes 196616 | tf_op jit(solution)/shard_map/ppermute | solution.py:463
  45.6 7.4 %copy-start.3 = (s32[32]{0:T(128)S(1)}, s32[32]{0:T(128)}, u32[]{:S(2)}) copy-start(s32[32]{0:T(128)} %refs_2_.5) | copy-start | bytes 388
  45.6 7.4 %collective-permute-start.31 = (bf16[64,2048]{1,0:T(8,128)(2,1)S(1)}, bf16[64,2048]{1,0:T(8,128)(2,1)S(1)}, u32[]{:S(2)}, u32[]{:S(2)}) collective-permute-start(bf16[64,2048]{1,0:T(8,128)(2,1)S(1)} %get-tuple-element.124.refs_2_), channel_id=1, source_target_pairs={{0,1},{1,0},{2,3},{3,2},{4,5},{5,4},{6,7},{7,6},{8,9},{9,8},{10,11... | collective-permute-start | bytes 786440 | tf_op jit(solution)/shard_map/ppermute | solution.py:484
  46.0 12.0 %collective-permute-start.34 = (bf16[64,2048]{1,0:T(8,128)(2,1)S(1)}, bf16[64,2048]{1,0:T(8,128)(2,1)S(1)}, u32[]{:S(2)}, u32[]{:S(2)}) collective-permute-start(bf16[64,2048]{1,0:T(8,128)(2,1)S(1)} %get-tuple-element.130), channel_id=1, source_target_pairs={{0,2},{2,0},{1,3},{3,1},{4,6},{6,4},{5,7},{7,5},{8,10},{10,8},{9,1... | collective-permute-start | bytes 786440 | tf_op jit(solution)/shard_map/ppermute | solution.py:468
  47.0 13.7 %collective-permute-start.35 = (bf16[64,2048]{1,0:T(8,128)(2,1)S(1)}, bf16[64,2048]{1,0:T(8,128)(2,1)S(1)}, u32[]{:S(2)}, u32[]{:S(2)}) collective-permute-start(bf16[64,2048]{1,0:T(8,128)(2,1)S(1)} %get-tuple-element.133), channel_id=1, source_target_pairs={{0,2},{2,0},{1,3},{3,1},{4,6},{6,4},{5,7},{7,5},{8,10},{10,8},{9,1... | collective-permute-start | bytes 786440 | tf_op jit(solution)/shard_map/ppermute | solution.py:468
  50.4 2.2 %collective-permute-start.32 = (bf16[64,1024]{1,0:T(8,128)(2,1)S(1)}, bf16[64,1024]{1,0:T(8,128)(2,1)S(1)}, u32[]{:S(2)}, u32[]{:S(2)}) collective-permute-start(bf16[64,1024]{1,0:T(8,128)(2,1)S(1)} %get-tuple-element.125.refs_3_), channel_id=1, source_target_pairs={{0,1},{1,0},{2,3},{3,2},{4,5},{5,4},{6,7},{7,6},{8,9},{9,8},{10,11... | collective-permute-start | bytes 393224 | tf_op jit(solution)/shard_map/ppermute | solution.py:484
  51.6 1.3 %collective-permute-start.33 = (bf16[64,1024]{1,0:T(8,128)(2,1)S(1)}, bf16[64,1024]{1,0:T(8,128)(2,1)S(1)}, u32[]{:S(2)}, u32[]{:S(2)}) collective-permute-start(bf16[64,1024]{1,0:T(8,128)(2,1)S(1)} %get-tuple-element.126.refs_4_), channel_id=1, source_target_pairs={{0,1},{1,0},{2,3},{3,2},{4,5},{5,4},{6,7},{7,6},{8,9},{9,8},{10,11... | collective-permute-start | bytes 393224 | tf_op jit(solution)/shard_map/ppermute | solution.py:484
  55.0 11.6 %collective-permute-start.36 = (bf16[6,32,512]{2,1,0:T(8,128)(2,1)S(1)}, bf16[6,32,512]{2,1,0:T(8,128)(2,1)S(1)}, u32[]{:S(2)}, u32[]{:S(2)}) collective-permute-start(bf16[6,32,512]{2,1,0:T(8,128)(2,1)S(1)} %get-tuple-element.136), channel_id=1, source_target_pairs={{0,8},{4,12},{8,0},{12,4},{1,9},{5,13},{9,1},{13,5},{2,10},{6,14},... | collective-permute-start | bytes 589832 | tf_op jit(solution)/shard_map/ppermute | solution.py:500
  61.7 1.8 %collective-permute-start.39 = (bf16[64,1024]{1,0:T(8,128)(2,1)S(1)}, bf16[64,1024]{1,0:T(8,128)(2,1)S(1)}, u32[]{:S(2)}, u32[]{:S(2)}) collective-permute-start(bf16[64,1024]{1,0:T(8,128)(2,1)S(1)} %get-tuple-element.139.refs_5_), channel_id=1, source_target_pairs={{0,1},{1,0},{2,3},{3,2},{4,5},{5,4},{6,7},{7,6},{8,9},{9,8},{10,11... | collective-permute-start | bytes 393224 | tf_op jit(solution)/shard_map/ppermute | solution.py:484
  62.5 1.5 %collective-permute-start.40 = (bf16[64,1024]{1,0:T(8,128)(2,1)S(1)}, bf16[64,1024]{1,0:T(8,128)(2,1)S(1)}, u32[]{:S(2)}, u32[]{:S(2)}) collective-permute-start(bf16[64,1024]{1,0:T(8,128)(2,1)S(1)} %get-tuple-element.140.refs_6_), channel_id=1, source_target_pairs={{0,1},{1,0},{2,3},{3,2},{4,5},{5,4},{6,7},{7,6},{8,9},{9,8},{10,11... | collective-permute-start | bytes 393224 | tf_op jit(solution)/shard_map/ppermute | solution.py:484
  62.6 4.1 %collective-permute-start.37 = (bf16[64,1024]{1,0:T(8,128)(2,1)S(1)}, bf16[64,1024]{1,0:T(8,128)(2,1)S(1)}, u32[]{:S(2)}, u32[]{:S(2)}) collective-permute-start(bf16[64,1024]{1,0:T(8,128)(2,1)S(1)} %get-tuple-element.137.refs_3_), channel_id=1, source_target_pairs={{0,1},{1,0},{2,3},{3,2},{4,5},{5,4},{6,7},{7,6},{8,9},{9,8},{10,11... | collective-permute-start | bytes 393224 | tf_op jit(solution)/shard_map/ppermute | solution.py:484
  63.0 3.7 %collective-permute-start.38 = (bf16[64,1024]{1,0:T(8,128)(2,1)S(1)}, bf16[64,1024]{1,0:T(8,128)(2,1)S(1)}, u32[]{:S(2)}, u32[]{:S(2)}) collective-permute-start(bf16[64,1024]{1,0:T(8,128)(2,1)S(1)} %get-tuple-element.138.refs_4_), channel_id=1, source_target_pairs={{0,1},{1,0},{2,3},{3,2},{4,5},{5,4},{6,7},{7,6},{8,9},{9,8},{10,11... | collective-permute-start | bytes 393224 | tf_op jit(solution)/shard_map/ppermute | solution.py:484
  63.5 8.6 %collective-permute-start.41 = (bf16[6,32,512]{2,1,0:T(8,128)(2,1)S(1)}, bf16[6,32,512]{2,1,0:T(8,128)(2,1)S(1)}, u32[]{:S(2)}, u32[]{:S(2)}) collective-permute-start(bf16[6,32,512]{2,1,0:T(8,128)(2,1)S(1)} %get-tuple-element.143), channel_id=1, source_target_pairs={{0,4},{4,0},{8,12},{12,8},{1,5},{5,1},{9,13},{13,9},{2,6},{6,2},{1... | collective-permute-start | bytes 589832 | tf_op jit(solution)/shard_map/ppermute | solution.py:500
  64.0 10.1 %collective-permute-start.42 = (bf16[6,32,512]{2,1,0:T(8,128)(2,1)S(1)}, bf16[6,32,512]{2,1,0:T(8,128)(2,1)S(1)}, u32[]{:S(2)}, u32[]{:S(2)}) collective-permute-start(bf16[6,32,512]{2,1,0:T(8,128)(2,1)S(1)} %get-tuple-element.144), channel_id=1, source_target_pairs={{0,12},{4,8},{8,4},{12,0},{1,13},{5,9},{9,5},{13,1},{2,14},{6,10},... | collective-permute-start | bytes 589832 | tf_op jit(solution)/shard_map/ppermute | solution.py:500
  68.8 13.8 %collective-permute-start.43 = (bf16[6,32,512]{2,1,0:T(8,128)(2,1)S(1)}, bf16[6,32,512]{2,1,0:T(8,128)(2,1)S(1)}, u32[]{:S(2)}, u32[]{:S(2)}) collective-permute-start(bf16[6,32,512]{2,1,0:T(8,128)(2,1)S(1)} %get-tuple-element.148), channel_id=1, source_target_pairs={{0,4},{4,0},{8,12},{12,8},{1,5},{5,1},{9,13},{13,9},{2,6},{6,2},{1... | collective-permute-start | bytes 589832 | tf_op jit(solution)/shard_map/ppermute | solution.py:500
  70.3 16.7 %collective-permute-start.44 = (bf16[6,32,512]{2,1,0:T(8,128)(2,1)S(1)}, bf16[6,32,512]{2,1,0:T(8,128)(2,1)S(1)}, u32[]{:S(2)}, u32[]{:S(2)}) collective-permute-start(bf16[6,32,512]{2,1,0:T(8,128)(2,1)S(1)} %get-tuple-element.149), channel_id=1, source_target_pairs={{0,8},{4,12},{8,0},{12,4},{1,9},{5,13},{9,1},{13,5},{2,10},{6,14},... | collective-permute-start | bytes 589832 | tf_op jit(solution)/shard_map/ppermute | solution.py:500
  71.8 21.5 %collective-permute-start.45 = (bf16[6,32,512]{2,1,0:T(8,128)(2,1)S(1)}, bf16[6,32,512]{2,1,0:T(8,128)(2,1)S(1)}, u32[]{:S(2)}, u32[]{:S(2)}) collective-permute-start(bf16[6,32,512]{2,1,0:T(8,128)(2,1)S(1)} %get-tuple-element.150), channel_id=1, source_target_pairs={{0,12},{4,8},{8,4},{12,0},{1,13},{5,9},{9,5},{13,1},{2,14},{6,10},... | collective-permute-start | bytes 589832 | tf_op jit(solution)/shard_map/ppermute | solution.py:500

commit v6 on v5

--- a/solution.py
+++ b/solution.py
@@ -30,7 +30,7 @@
 HOLD_CHIP = False
 FIRST = (1, 1)
 SECOND = ((0, 0, 1, 1), (1, 0, 1, 1))
-ORDER = (('pred', 0), ('two', 0), ('pass', 1), ('pred', 1), ('res', 0), ('two', 1), ('score', 0), ('res', 1), ('chip', 0), ('score', 1), ('chip', 1), ('den', 0), ('chrom', 0), ('den', 1), ('chrom', 1), ('leave', 0), ('leave', 1))
+ORDER = (('pred', 0), ('two', 0), ('pass', 1), ('pred', 1), ('res', 0), ('two', 1), ('score', 0), ('res', 1), ('chip', 0), ('score', 1), ('chip', 1), ('den', 0), ('chrom', 0), ('den', 1), ('chrom', 1), ('leave', 0), ('store', 0), ('store', 1), ('leave', 1))
 
 
 def denoise(estimate, scores, prior_logit, slab_var, noise_var, marker_root, people_root):
@@ -270,7 +270,7 @@
 
 def denoise_body(marker_root, people_root, low, first, begin, parts, pieces, *refs):
     own, across, (coefs, coefs_across, chip, *refs) = refs[:pieces], refs[pieces : 2 * pieces], refs[2 * pieces :]
-    came, updated, (whole, stored) = refs[:parts], refs[parts:-2], refs[-2:]
+    came, updated = refs[:parts], refs[parts:]
     height = updated[0].shape[0] // 2
     at = slice(low, low + height)
     coef = jnp.concatenate([coefs[first : first + height], coefs_across[first : first + height]], axis=0)
@@ -287,12 +287,16 @@
         posterior = jax.nn.sigmoid(log_odds) * gain * observed
         ref, inner = piece_of(updated, tile)
         ref[:, inner] = (posterior * (1.0 / marker_root)).astype(ref.dtype)
-    copies = []
-    for at, ref in enumerate(updated):
-        target = whole.at[pl.ds(first, height), pl.ds(begin * TILE + at * width, width)]
+
+
+def store_body(first, *refs):
+    *parts, whole, stored = refs
+    copies, begin, height = [], 0, parts[0].shape[0] // 2
+    for at, ref in enumerate(parts):
+        target = whole.at[pl.ds(first, height), pl.ds(begin, ref.shape[1])]
         copies.append(pltpu.make_async_copy(ref.at[pl.ds(0, height)], target, stored.at[at]))
-    for copy in copies:
-        copy.start()
+        copies[-1].start()
+        begin += ref.shape[1]
     for copy in copies:
         copy.wait()
 
@@ -340,9 +344,8 @@
             total = total + part[slot].astype(jnp.float32)
     base[...] = phen[row_at(depth * shard + row, height), :].astype(jnp.float32) - total
 
-    def copy(chrom):
-        return pltpu.make_async_copy(stage.at[chrom], out.at[chrom, pl.ds(row, height)], done.at[chrom])
-
+    group = -(-CHROMS // done.shape[0])
+    copies = []
     for chrom in range(CHROMS):
         value = base[...]
         for first, part in zip(firsts, sums):
@@ -350,13 +353,13 @@
             inside = ((slot >= 0) & (slot < SPAN)).astype(jnp.float32)
             value = value + inside * part[jnp.clip(slot, 0, SPAN - 1)].astype(jnp.float32)
         stage[chrom] = value.astype(stage.dtype)
-        copy(chrom).start()
-
-    def finish(chrom, carry):
-        copy(chrom).wait()
-        return carry
-
-    lax.fori_loop(0, CHROMS, finish, 0)
+        if (chrom + 1) % group == 0 or chrom + 1 == CHROMS:
+            begin = chrom // group * group
+            some = pl.ds(begin, chrom + 1 - begin)
+            copies.append(pltpu.make_async_copy(stage.at[some], out.at[some, pl.ds(row, height)], done.at[len(copies)]))
+            copies[-1].start()
+    for copy in copies:
+        copy.wait()
 
 
 def leave_out(loco, token, shape, row, height, tiles, count, labels, phen, sums):
@@ -378,7 +381,7 @@
         in_specs=specs,
         out_specs=[anywhere, anywhere],
         scratch_shapes=[pltpu.VMEM((height, people), jnp.float32)]
-        + [pltpu.VMEM((shape[0], height, people), jnp.bfloat16), pltpu.SemaphoreType.DMA((shape[0],))],
+        + [pltpu.VMEM((shape[0], height, people), jnp.bfloat16), pltpu.SemaphoreType.DMA((3,))],
         input_output_aliases=aliases,
         cost_estimate=pl.CostEstimate(flops=1, bytes_accessed=1, transcendentals=0),
         compiler_params=pltpu.CompilerParams(vmem_limit_bytes=8 * 2**20),
@@ -472,21 +475,29 @@
             per, tiles = len(came) // len(shares), tile_dev // len(shares)
             ours, theirs = [], []
             for share, pieces in enumerate(shares):
-                *updated, whole = steps.call(
+                updated = steps.call(
                     functools.partial(denoise_body, marker_root, people_root, low, row, share * tiles, per, len(own[of])),
                     [pltpu.VMEM((2 * height, tiles * TILE // pieces), bf16)] * pieces,
                     args=[*own[of], *across[of], coefs, coefs_across, chip, *came[share * per : (share + 1) * per]],
-                    scratch=[pltpu.SemaphoreType.DMA((pieces,))],
-                    into=whole,
-                    fresh=None if whole is not None else jax.ShapeDtypeStruct(estimate.shape, estimate.dtype),
                 )
                 ours += updated
                 theirs += [lax.ppermute(one, "sub", swap) for one in updated]
             now["den"] = ours + theirs
+        elif stage == "store":
+            mine = now["den"][: len(now["den"]) // 2]
+            (whole,) = steps.call(
+                functools.partial(store_body, row),
+                [],
+                args=mine,
+                scratch=[pltpu.SemaphoreType.DMA((len(mine),))],
+                into=whole,
+                fresh=None if whole is not None else jax.ShapeDtypeStruct(estimate.shape, estimate.dtype),
+            )
         elif stage == "chrom":
             block, together = (SPAN, height, people_dev), at in TOGETHER
+            pieces = len(now["den"]) // 2
             sums = steps.call(
-                functools.partial(chrom_body, together, len(now["den"]) // 2),
+                functools.partial(chrom_body, together, pieces),
                 [pltpu.VMEM((mk_count, *block), bf16)] if together else [pltpu.VMEM(block, bf16)] * mk_count,
                 [tile_chrom],
                 now["den"],

time: 95.5 us -> 94.4 us (0.988)
  Pallas kernels: 17.2 us -> 15.8 us
    ppermute x4, waiting for transfers between devices: 3.75 us -> 5.09 us  [piece_steps(): now['chip'] = [chip] + [lax.ppermute(send, 'pp', swap) for send in sends]]
    ppermute x6, waiting for transfers between devices: 19.2 us -> 17.8 us  [piece_steps(): lax.ppermute(sums[step], 'mk', along(step))]
    pallas_call x18 -> x20, Pallas kernels: 13.1 us -> 11.9 us  [call(): pl.pallas_call(kernel, out_shape=[jax.ShapeDtypeStruct(self.token.shape,...]
  transfers between devices with their start and end apart: 46 -> 46, of which waited for: 23 -> 23; matrix products, arithmetic and copies ran while one was open for 0% -> 0% of each run, Pallas kernels for 16% -> 15%
where the time goes in v6:
time: 94.4 us; the launch traced here: 93.9 us
  starting transfers between devices  37.7 us (40%)
  waiting for transfers between devices  34.3 us (36%)
  Pallas kernels  15.8 us (17%)
  local copies, waits for them, and re-layouts  5.23 us (6%)
    ppermute x6, waiting for transfers between devices, piece_steps(): lax.ppermute(sums[step], 'mk', along(step))  17.8 us
    pallas_call x20, Pallas kernels, call(): pl.pallas_call(kernel, out_shape=[jax.ShapeDtypeStruct(self.token.shape,...  11.9 us
    ppermute x6, starting transfers between devices, piece_steps(): lax.ppermute(sums[step], 'mk', along(step))  9.63 us
    ppermute x16, starting transfers between devices, piece_steps(): now['score'] = [keep] + [lax.ppermute(send, 'sub', swap) for send in sends]  6.58 us
    ppermute x2, starting transfers between devices, piece_steps(): now['two'] = (two, lax.ppermute(two, 'mk', along(2)))  5.26 us
    ppermute x4, waiting for transfers between devices, piece_steps(): now['chip'] = [chip] + [lax.ppermute(send, 'pp', swap) for send in sends]  5.09 us
    ppermute x4, starting transfers between devices, piece_steps(): lax.ppermute(one, 'sub', swap)  4.35 us
    unnamed x14, local copies, waits for them, and re-layouts  4.17 us
  transfers between devices with their start and end apart: 46, of which 23 were waited for; matrix products, arithmetic and copies ran while one was open for 0% of the time, Pallas kernels for 15%

profile of v6, /device:TPU:13, one launch (start us, length us, event | category | flops | bytes accessed | tf_op | source)
XLA Modules:
  0.0 93.9 jit_solution(4175606363269923228)
XLA Ops:
  0.6 1.1 %fusion = (bf16[32,4096]{1,0:T(8,128)(2,1)S(1)}, bf16[32,4096]{1,0:T(8,128)(2,1)S(1)}) fusion(bf16[64,4096]{1,0:T(8,128)(2,1)} %param.8), kind=kLoop, calls=%fused_computation | loop fusion | bytes 1048576 | tf_op jit(solution)/shard_map/slice | solution.py:413
  1.7 1.3 %collective-permute-start = (bf16[32,4096]{1,0:T(8,128)(2,1)S(1)}, bf16[32,4096]{1,0:T(8,128)(2,1)S(1)}, u32[]{:S(2)}, u32[]{:S(2)}) collective-permute-start(bf16[32,4096]{1,0:T(8,128)(2,1)S(1)} %get-tuple-element.153.refs_1_), channel_id=1, source_target_pairs={{0,2},{2,0},{1,3},{3,1},{4,6},{6,4},{5,7},{7,5},{8,10},{10,8},{9,1... | collective-permute-start | bytes 786440 | tf_op jit(solution)/shard_map/ppermute | solution.py:415
  3.0 2.2 %copy-done = bf16[512,4096]{1,0:T(8,128)(2,1)S(1)} copy-done((bf16[512,4096]{1,0:T(8,128)(2,1)S(1)}, bf16[512,4096]{1,0:T(8,128)(2,1)}, u32[]{:S(2)}) %copy-start) | copy-done | bytes 4194328
  5.2 0.7 copy-done.4
  5.8 0.7 copy-done.5
  6.5 0.7 copy-done.6
  7.2 1.0 %collective-permute-start.1 = (bf16[32,4096]{1,0:T(8,128)(2,1)S(1)}, bf16[32,4096]{1,0:T(8,128)(2,1)S(1)}, u32[]{:S(2)}, u32[]{:S(2)}) collective-permute-start(bf16[32,4096]{1,0:T(8,128)(2,1)S(1)} %get-tuple-element.78), channel_id=1, source_target_pairs={{0,1},{1,0},{2,3},{3,2},{4,5},{5,4},{6,7},{7,6},{8,9},{9,8},{10,11... | collective-permute-start | bytes 786440 | tf_op jit(solution)/shard_map/ppermute | solution.py:428
  8.3 0.7 collective-permute-done.refs_2_
  8.9 1.5 %collective-permute-start.2 = (bf16[32,4096]{1,0:T(8,128)(2,1)S(1)}, bf16[32,4096]{1,0:T(8,128)(2,1)S(1)}, u32[]{:S(2)}, u32[]{:S(2)}) collective-permute-start(bf16[32,4096]{1,0:T(8,128)(2,1)S(1)} %collective-permute-done.refs_2_), channel_id=1, source_target_pairs={{0,1},{1,0},{2,3},{3,2},{4,5},{5,4},{6,7},{7,6},{8,9},{9,8},{10,11... | collective-permute-start | bytes 786440 | tf_op jit(solution)/shard_map/ppermute | solution.py:429
  10.5 1.2 %collective-permute-start.5 = (bf16[32,4096]{1,0:T(8,128)(2,1)S(1)}, bf16[32,4096]{1,0:T(8,128)(2,1)S(1)}, u32[]{:S(2)}, u32[]{:S(2)}) collective-permute-start(bf16[32,4096]{1,0:T(8,128)(2,1)S(1)} %get-tuple-element.152.refs_1_), channel_id=1, source_target_pairs={{0,2},{2,0},{1,3},{3,1},{4,6},{6,4},{5,7},{7,5},{8,10},{10,8},{9,1... | collective-permute-start | bytes 786440 | tf_op jit(solution)/shard_map/ppermute | solution.py:427
  11.7 1.6 %shard_map.87 = (f32[8,128]{1,0:T(8,128)S(1)}, f32[64,512]{1,0:T(8,128)S(1)}, bf16[64,512]{1,0:T(8,128)(2,1)S(1)}) custom-call(f32[8,128]{1,0:T(8,128)S(1)} %get-tuple-element.77.refs_0_, bf16[32,4096]{1,0:T(8,128)(2,1)S(1)} %get-tuple-element.153.refs_1_, bf16[32,4096]{1,0:T(8,128)(2,1)S(1)} %collective-permute-done.refs_2_, ...), custom_call_target="tpu_custom_call", output_to_operand_aliasing={{0}: (0, {})} | custom-call | flops 1 | bytes 1 | tf_op jit(solution)/shard_map/pallas_call | solution.py:148
  13.5 1.1 %collective-permute-start.4 = (f32[64,128]{1,0:T(8,128)S(1)}, f32[64,128]{1,0:T(8,128)S(1)}, u32[]{:S(2)}, u32[]{:S(2)}) collective-permute-start(f32[64,128]{1,0:T(8,128)S(1)} %get-tuple-element.83.refs_3_), channel_id=1, source_target_pairs={{0,2},{2,0},{1,3},{3,1},{4,6},{6,4},{5,7},{7,5},{8,10},{10,8},{9,1... | collective-permute-start | bytes 98312 | tf_op jit(solution)/shard_map/ppermute | solution.py:423
  14.7 0.9 collective-permute-start.6
  15.6 1.2 %collective-permute-done.3.refs_2_ = bf16[64,512]{1,0:T(8,128)(2,1)S(1)} collective-permute-done((bf16[64,512]{1,0:T(8,128)(2,1)S(1)}, bf16[64,512]{1,0:T(8,128)(2,1)S(1)}, u32[]{:S(2)}, u32[]{:S(2)}) %collective-permute-start.3) | collective-permute-done | bytes 65568 | tf_op jit(solution)/shard_map/ppermute | solution.py:451
  16.8 2.4 %collective-permute-done.4.refs_1_.refs_4_ = f32[64,128]{1,0:T(8,128)S(1)} collective-permute-done((f32[64,128]{1,0:T(8,128)S(1)}, f32[64,128]{1,0:T(8,128)S(1)}, u32[]{:S(2)}, u32[]{:S(2)}) %collective-permute-start.4) | collective-permute-done | bytes 32800 | tf_op jit(solution)/shard_map/ppermute | solution.py:423
  19.2 0.8 collective-permute-start.7
  20.0 2.3 %collective-permute-start.8 = (bf16[64,512]{1,0:T(8,128)(2,1)S(1)}, bf16[64,512]{1,0:T(8,128)(2,1)S(1)}, u32[]{:S(2)}, u32[]{:S(2)}) collective-permute-start(bf16[64,512]{1,0:T(8,128)(2,1)S(1)} %get-tuple-element.87.refs_2_), channel_id=1, source_target_pairs={{0,8},{4,12},{8,0},{12,4},{1,9},{5,13},{9,1},{13,5},{2,10},{6,14},... | collective-permute-start | bytes 196616 | tf_op jit(solution)/shard_map/ppermute | solution.py:454
  22.3 1.6 %shard_map.90 = (f32[8,128]{1,0:T(8,128)S(1)}, f32[64,512]{1,0:T(8,128)S(1)}, bf16[64,512]{1,0:T(8,128)(2,1)S(1)}) custom-call(f32[8,128]{1,0:T(8,128)S(1)} %get-tuple-element.84.refs_0_, bf16[32,4096]{1,0:T(8,128)(2,1)S(1)} %get-tuple-element.152.refs_1_, bf16[32,4096]{1,0:T(8,128)(2,1)S(1)} %collective-permute-done.5.refs_2_, ...), custom_call_target="tpu_custom_call", output_to_operand_aliasing={{0}: (0, {})} | custom-call | flops 1 | bytes 1 | tf_op jit(solution)/shard_map/pallas_call | solution.py:148
  24.1 1.3 %collective-permute-done.8.refs_3_ = bf16[64,512]{1,0:T(8,128)(2,1)S(1)} collective-permute-done((bf16[64,512]{1,0:T(8,128)(2,1)S(1)}, bf16[64,512]{1,0:T(8,128)(2,1)S(1)}, u32[]{:S(2)}, u32[]{:S(2)}) %collective-permute-start.8) | collective-permute-done | bytes 65568 | tf_op jit(solution)/shard_map/ppermute | solution.py:454
  25.6 1.5 %collective-permute-done.9.refs_2_ = bf16[64,512]{1,0:T(8,128)(2,1)S(1)} collective-permute-done((bf16[64,512]{1,0:T(8,128)(2,1)S(1)}, bf16[64,512]{1,0:T(8,128)(2,1)S(1)}, u32[]{:S(2)}, u32[]{:S(2)}) %collective-permute-start.9) | collective-permute-done | bytes 65568 | tf_op jit(solution)/shard_map/ppermute | solution.py:451
  27.1 2.9 %collective-permute-start.11 = (bf16[64,512]{1,0:T(8,128)(2,1)S(1)}, bf16[64,512]{1,0:T(8,128)(2,1)S(1)}, u32[]{:S(2)}, u32[]{:S(2)}) collective-permute-start(bf16[64,512]{1,0:T(8,128)(2,1)S(1)} %get-tuple-element.94.refs_2_), channel_id=1, source_target_pairs={{0,8},{4,12},{8,0},{12,4},{1,9},{5,13},{9,1},{13,5},{2,10},{6,14},... | collective-permute-start | bytes 196616 | tf_op jit(solution)/shard_map/ppermute | solution.py:454
  30.0 0.7 shard_map.93
  30.8 0.8 collective-permute-start.12
  31.7 0.4 collective-permute-start.14
  32.2 0.6 collective-permute-done.11.refs_3_
  32.8 1.0 %collective-permute-start.16 = (bf16[64,512]{1,0:T(8,128)(2,1)S(1)}, bf16[64,512]{1,0:T(8,128)(2,1)S(1)}, u32[]{:S(2)}, u32[]{:S(2)}) collective-permute-start(bf16[64,512]{1,0:T(8,128)(2,1)S(1)} %get-tuple-element.101), channel_id=1, source_target_pairs={{0,1},{1,0},{2,3},{3,2},{4,5},{5,4},{6,7},{7,6},{8,9},{9,8},{10,11... | collective-permute-start | bytes 196616 | tf_op jit(solution)/shard_map/ppermute | solution.py:466
  33.9 0.5 collective-permute-start.18
  34.5 0.6 collective-permute-start.20
  35.8 1.3 %collective-permute-start.29 = (bf16[64,2048]{1,0:T(8,128)(2,1)S(1)}, bf16[64,2048]{1,0:T(8,128)(2,1)S(1)}, u32[]{:S(2)}, u32[]{:S(2)}) collective-permute-start(bf16[64,2048]{1,0:T(8,128)(2,1)S(1)} %get-tuple-element.119), channel_id=1, source_target_pairs={{0,2},{2,0},{1,3},{3,1},{4,6},{6,4},{5,7},{7,5},{8,10},{10,8},{9,1... | collective-permute-start | bytes 786440 | tf_op jit(solution)/shard_map/ppermute | solution.py:471
  37.1 0.6 collective-permute-done.20.refs_2_
  37.7 0.7 shard_map.96
  38.4 1.7 %collective-permute-start.21 = (bf16[64,512]{1,0:T(8,128)(2,1)S(1)}, bf16[64,512]{1,0:T(8,128)(2,1)S(1)}, u32[]{:S(2)}, u32[]{:S(2)}) collective-permute-start(bf16[64,512]{1,0:T(8,128)(2,1)S(1)} %get-tuple-element.109), channel_id=1, source_target_pairs={{0,1},{1,0},{2,3},{3,2},{4,5},{5,4},{6,7},{7,6},{8,9},{9,8},{10,11... | collective-permute-start | bytes 196616 | tf_op jit(solution)/shard_map/ppermute | solution.py:466
  40.1 0.4 collective-permute-start.23
  41.3 1.2 %collective-permute-start.30 = (bf16[64,2048]{1,0:T(8,128)(2,1)S(1)}, bf16[64,2048]{1,0:T(8,128)(2,1)S(1)}, u32[]{:S(2)}, u32[]{:S(2)}) collective-permute-start(bf16[64,2048]{1,0:T(8,128)(2,1)S(1)} %get-tuple-element.121), channel_id=1, source_target_pairs={{0,2},{2,0},{1,3},{3,1},{4,6},{6,4},{5,7},{7,5},{8,10},{10,8},{9,1... | collective-permute-start | bytes 786440 | tf_op jit(solution)/shard_map/ppermute | solution.py:471
  42.5 0.4 collective-permute-start.26
  43.0 0.4 collective-permute-start.28
  43.5 0.4 collective-permute-done.26.refs_7_
  43.9 0.4 collective-permute-done.27.refs_8_
  44.9 0.4 collective-permute-start.31
  45.3 1.0 %collective-permute-start.34 = (bf16[64,2048]{1,0:T(8,128)(2,1)S(1)}, bf16[64,2048]{1,0:T(8,128)(2,1)S(1)}, u32[]{:S(2)}, u32[]{:S(2)}) collective-permute-start(bf16[64,2048]{1,0:T(8,128)(2,1)S(1)} %get-tuple-element.128), channel_id=1, source_target_pairs={{0,2},{2,0},{1,3},{3,1},{4,6},{6,4},{5,7},{7,5},{8,10},{10,8},{9,1... | collective-permute-start | bytes 786440 | tf_op jit(solution)/shard_map/ppermute | solution.py:471
  46.3 0.5 collective-permute-start.35
  46.8 2.7 %collective-permute-done.30.refs_6_ = bf16[64,2048]{1,0:T(8,128)(2,1)S(1)} collective-permute-done((bf16[64,2048]{1,0:T(8,128)(2,1)S(1)}, bf16[64,2048]{1,0:T(8,128)(2,1)S(1)}, u32[]{:S(2)}, u32[]{:S(2)}) %collective-permute-start.30) | collective-permute-done | bytes 262176 | tf_op jit(solution)/shard_map/ppermute | solution.py:471
  49.8 1.2 %collective-permute-start.32 = (bf16[64,1024]{1,0:T(8,128)(2,1)S(1)}, bf16[64,1024]{1,0:T(8,128)(2,1)S(1)}, u32[]{:S(2)}, u32[]{:S(2)}) collective-permute-start(bf16[64,1024]{1,0:T(8,128)(2,1)S(1)} %get-tuple-element.124.refs_3_.refs_2_), channel_id=1, source_target_pairs={{0,1},{1,0},{2,3},{3,2},{4,5},{5,4},{6,7},{7,6},{8,9},{9,8},{10,11... | collective-permute-start | bytes 393224 | tf_op jit(solution)/shard_map/ppermute | solution.py:484
  51.0 0.9 collective-permute-done.32.refs_6_
  51.9 0.4 collective-permute-done.33.refs_7_
  52.3 2.1 %shard_map.100 = (f32[8,128]{1,0:T(8,128)S(1)}, bf16[6,32,512]{2,1,0:T(8,128)(2,1)S(1)}, bf16[6,32,512]{2,1,0:T(8,128)(2,1)S(1)}, bf16[6,32,512]{2,1,0:T(8,128)(2,1)S(1)}, bf16[6,32,512]{2,1,0:T(8,128)(2,1)S(1)}) custom-call(f32[8,128]{1,0:T(8,128)S(1)} %get-tuple-element.122.refs_0_, s32[32]{0:T(128)S(1)} %copy-done.3, ...), custom_call_target="tpu_custom_call", output_to_operand_aliasing={{0}: (0, {})} | custom-call | flops 1 | bytes 1 | tf_op jit(solution)/shard_map/pallas_call | solution.py:148
  54.4 3.0 %collective-permute-start.36 = (bf16[6,32,512]{2,1,0:T(8,128)(2,1)S(1)}, bf16[6,32,512]{2,1,0:T(8,128)(2,1)S(1)}, u32[]{:S(2)}, u32[]{:S(2)}) collective-permute-start(bf16[6,32,512]{2,1,0:T(8,128)(2,1)S(1)} %get-tuple-element.132), channel_id=1, source_target_pairs={{0,8},{4,12},{8,0},{12,4},{1,9},{5,13},{9,1},{13,5},{2,10},{6,14},... | collective-permute-start | bytes 589832 | tf_op jit(solution)/shard_map/ppermute | solution.py:511
  57.7 0.5 collective-permute-start.37
  58.3 2.4 %collective-permute-done.35.refs_6_ = bf16[64,2048]{1,0:T(8,128)(2,1)S(1)} collective-permute-done((bf16[64,2048]{1,0:T(8,128)(2,1)S(1)}, bf16[64,2048]{1,0:T(8,128)(2,1)S(1)}, u32[]{:S(2)}, u32[]{:S(2)}) %collective-permute-start.35) | collective-permute-done | bytes 262176 | tf_op jit(solution)/shard_map/ppermute | solution.py:471
  61.0 0.8 collective-permute-start.39
  61.9 0.5 collective-permute-start.41
  62.4 2.7 %collective-permute-start.42 = (bf16[6,32,512]{2,1,0:T(8,128)(2,1)S(1)}, bf16[6,32,512]{2,1,0:T(8,128)(2,1)S(1)}, u32[]{:S(2)}, u32[]{:S(2)}) collective-permute-start(bf16[6,32,512]{2,1,0:T(8,128)(2,1)S(1)} %get-tuple-element.140), channel_id=1, source_target_pairs={{0,12},{4,8},{8,4},{12,0},{1,13},{5,9},{9,5},{13,1},{2,14},{6,10},... | collective-permute-start | bytes 589832 | tf_op jit(solution)/shard_map/ppermute | solution.py:511
  65.1 0.6 collective-permute-done.36.refs_1_.refs_5_
  65.7 2.1 %shard_map.103 = (f32[8,128]{1,0:T(8,128)S(1)}, bf16[6,32,512]{2,1,0:T(8,128)(2,1)S(1)}, bf16[6,32,512]{2,1,0:T(8,128)(2,1)S(1)}, bf16[6,32,512]{2,1,0:T(8,128)(2,1)S(1)}, bf16[6,32,512]{2,1,0:T(8,128)(2,1)S(1)}) custom-call(f32[8,128]{1,0:T(8,128)S(1)} %get-tuple-element.131.refs_0_, ...), custom_call_target="tpu_custom_call", output_to_operand_aliasing={{0}: (0, {})} | custom-call | flops 1 | bytes 1 | tf_op jit(solution)/shard_map/pallas_call | solution.py:148
  67.8 2.0 %collective-permute-start.43 = (bf16[6,32,512]{2,1,0:T(8,128)(2,1)S(1)}, bf16[6,32,512]{2,1,0:T(8,128)(2,1)S(1)}, u32[]{:S(2)}, u32[]{:S(2)}) collective-permute-start(bf16[6,32,512]{2,1,0:T(8,128)(2,1)S(1)} %get-tuple-element.148), channel_id=1, source_target_pairs={{0,4},{4,0},{8,12},{12,8},{1,5},{5,1},{9,13},{13,9},{2,6},{6,2},{1... | collective-permute-start | bytes 589832 | tf_op jit(solution)/shard_map/ppermute | solution.py:511
  69.8 1.3 %collective-permute-start.44 = (bf16[6,32,512]{2,1,0:T(8,128)(2,1)S(1)}, bf16[6,32,512]{2,1,0:T(8,128)(2,1)S(1)}, u32[]{:S(2)}, u32[]{:S(2)}) collective-permute-start(bf16[6,32,512]{2,1,0:T(8,128)(2,1)S(1)} %get-tuple-element.149), channel_id=1, source_target_pairs={{0,8},{4,12},{8,0},{12,4},{1,9},{5,13},{9,1},{13,5},{2,10},{6,14},... | collective-permute-start | bytes 589832 | tf_op jit(solution)/shard_map/ppermute | solution.py:511
  71.3 2.9 %collective-permute-done.42.refs_6_ = bf16[6,32,512]{2,1,0:T(8,128)(2,1)S(1)} collective-permute-done((bf16[6,32,512]{2,1,0:T(8,128)(2,1)S(1)}, bf16[6,32,512]{2,1,0:T(8,128)(2,1)S(1)}, u32[]{:S(2)}, u32[]{:S(2)}) %collective-permute-start.42) | collective-permute-done | bytes 196640 | tf_op jit(solution)/shard_map/ppermute | solution.py:511
  74.2 1.9 %shard_map.104 = (bf16[22,64,512]{2,1,0:T(8,128)(2,1)}, f32[8,128]{1,0:T(8,128)S(1)}) custom-call(f32[8,128]{1,0:T(8,128)S(1)} %get-tuple-element.137.refs_0_, s32[32]{0:T(128)S(1)} %copy-done.3, bf16[256,512]{1,0:T(8,128)(2,1)S(1)} %copy-done.2, bf16[6,32,512]{2,1,0:T(8,128)(2,1)S(1)} %get-tuple-element.138.refs_3_, ...), custom_call_target="tpu_custom_call", output_to_operand_aliasing={{1}: (0, {})} | custom-call | flops 1 | bytes 1 | tf_op jit(solution)/shard_map/pallas_call | solution.py:378
  76.1 0.7 shard_map.105
  76.8 0.7 shard_map.106
  77.6 5.0 %collective-permute-done.43.refs_5_ = bf16[6,32,512]{2,1,0:T(8,128)(2,1)S(1)} collective-permute-done((bf16[6,32,512]{2,1,0:T(8,128)(2,1)S(1)}, bf16[6,32,512]{2,1,0:T(8,128)(2,1)S(1)}, u32[]{:S(2)}, u32[]{:S(2)}) %collective-permute-start.43) | collective-permute-done | bytes 196640 | tf_op jit(solution)/shard_map/ppermute | solution.py:511
  82.6 4.2 %collective-permute-done.44.refs_6_ = bf16[6,32,512]{2,1,0:T(8,128)(2,1)S(1)} collective-permute-done((bf16[6,32,512]{2,1,0:T(8,128)(2,1)S(1)}, bf16[6,32,512]{2,1,0:T(8,128)(2,1)S(1)}, u32[]{:S(2)}, u32[]{:S(2)}) %collective-permute-start.44) | collective-permute-done | bytes 196640 | tf_op jit(solution)/shard_map/ppermute | solution.py:511
  86.8 5.1 %collective-permute-done.45.refs_7_ = bf16[6,32,512]{2,1,0:T(8,128)(2,1)S(1)} collective-permute-done((bf16[6,32,512]{2,1,0:T(8,128)(2,1)S(1)}, bf16[6,32,512]{2,1,0:T(8,128)(2,1)S(1)}, u32[]{:S(2)}, u32[]{:S(2)}) %collective-permute-start.45) | collective-permute-done | bytes 196640 | tf_op jit(solution)/shard_map/ppermute | solution.py:511
  91.9 1.9 %shard_map.107 = (bf16[22,64,512]{2,1,0:T(8,128)(2,1)}, f32[8,128]{1,0:T(8,128)S(1)}) custom-call(bf16[22,64,512]{2,1,0:T(8,128)(2,1)} %get-tuple-element.145.refs_0_, f32[8,128]{1,0:T(8,128)S(1)} %get-tuple-element.146.refs_1_, s32[32]{0:T(128)S(1)} %copy-done.3, bf16[256,512]{1,0:T(8,128)(2,1)S(1)} %copy-done.2, ...), custom_call_target="tpu_custom_call", output_to_operand_aliasing={{0}: (0, {}), {1}: (1, {})} | custom-call | flops 1 | bytes 1 | tf_op jit(solution)/shard_map/pallas_call | solution.py:378
  (66 shorter events, 4.7 us)
Async XLA Ops:
  1.7 7.2 %collective-permute-start = (bf16[32,4096]{1,0:T(8,128)(2,1)S(1)}, bf16[32,4096]{1,0:T(8,128)(2,1)S(1)}, u32[]{:S(2)}, u32[]{:S(2)}) collective-permute-start(bf16[32,4096]{1,0:T(8,128)(2,1)S(1)} %get-tuple-element.153.refs_1_), channel_id=1, source_target_pairs={{0,2},{2,0},{1,3},{3,1},{4,6},{6,4},{5,7},{7,5},{8,10},{10,8},{9,1... | collective-permute-start | bytes 786440 | tf_op jit(solution)/shard_map/ppermute | solution.py:415
  3.0 2.2 %copy-start = (bf16[512,4096]{1,0:T(8,128)(2,1)S(1)}, bf16[512,4096]{1,0:T(8,128)(2,1)}, u32[]{:S(2)}) copy-start(bf16[512,4096]{1,0:T(8,128)(2,1)} %refs_11_.1) | copy-start | bytes 12582916
  5.2 0.7 copy-start.4
  5.8 0.7 copy-start.5
  6.5 0.7 copy-start.6
  7.1 4.6 %copy-start.1 = (bf16[512,4096]{1,0:T(8,128)(2,1)S(1)}, bf16[512,4096]{1,0:T(8,128)(2,1)}, u32[]{:S(2)}) copy-start(bf16[512,4096]{1,0:T(8,128)(2,1)} %refs_11_.1) | copy-start | bytes 12582916
  7.2 4.5 %collective-permute-start.1 = (bf16[32,4096]{1,0:T(8,128)(2,1)S(1)}, bf16[32,4096]{1,0:T(8,128)(2,1)S(1)}, u32[]{:S(2)}, u32[]{:S(2)}) collective-permute-start(bf16[32,4096]{1,0:T(8,128)(2,1)S(1)} %get-tuple-element.78), channel_id=1, source_target_pairs={{0,1},{1,0},{2,3},{3,2},{4,5},{5,4},{6,7},{7,6},{8,9},{9,8},{10,11... | collective-permute-start | bytes 786440 | tf_op jit(solution)/shard_map/ppermute | solution.py:428
  8.9 2.8 %collective-permute-start.2 = (bf16[32,4096]{1,0:T(8,128)(2,1)S(1)}, bf16[32,4096]{1,0:T(8,128)(2,1)S(1)}, u32[]{:S(2)}, u32[]{:S(2)}) collective-permute-start(bf16[32,4096]{1,0:T(8,128)(2,1)S(1)} %collective-permute-done.refs_2_), channel_id=1, source_target_pairs={{0,1},{1,0},{2,3},{3,2},{4,5},{5,4},{6,7},{7,6},{8,9},{9,8},{10,11... | collective-permute-start | bytes 786440 | tf_op jit(solution)/shard_map/ppermute | solution.py:429
  10.5 8.6 %collective-permute-start.5 = (bf16[32,4096]{1,0:T(8,128)(2,1)S(1)}, bf16[32,4096]{1,0:T(8,128)(2,1)S(1)}, u32[]{:S(2)}, u32[]{:S(2)}) collective-permute-start(bf16[32,4096]{1,0:T(8,128)(2,1)S(1)} %get-tuple-element.152.refs_1_), channel_id=1, source_target_pairs={{0,2},{2,0},{1,3},{3,1},{4,6},{6,4},{5,7},{7,5},{8,10},{10,8},{9,1... | collective-permute-start | bytes 786440 | tf_op jit(solution)/shard_map/ppermute | solution.py:427
  13.3 3.5 %collective-permute-start.3 = (bf16[64,512]{1,0:T(8,128)(2,1)S(1)}, bf16[64,512]{1,0:T(8,128)(2,1)S(1)}, u32[]{:S(2)}, u32[]{:S(2)}) collective-permute-start(bf16[64,512]{1,0:T(8,128)(2,1)S(1)} %get-tuple-element.81), channel_id=1, source_target_pairs={{0,4},{4,0},{8,12},{12,8},{1,5},{5,1},{9,13},{13,9},{2,6},{6,2},{1... | collective-permute-start | bytes 196616 | tf_op jit(solution)/shard_map/ppermute | solution.py:451
  13.5 5.6 %collective-permute-start.4 = (f32[64,128]{1,0:T(8,128)S(1)}, f32[64,128]{1,0:T(8,128)S(1)}, u32[]{:S(2)}, u32[]{:S(2)}) collective-permute-start(f32[64,128]{1,0:T(8,128)S(1)} %get-tuple-element.83.refs_3_), channel_id=1, source_target_pairs={{0,2},{2,0},{1,3},{3,1},{4,6},{6,4},{5,7},{7,5},{8,10},{10,8},{9,1... | collective-permute-start | bytes 98312 | tf_op jit(solution)/shard_map/ppermute | solution.py:423
  14.7 7.7 %collective-permute-start.6 = (bf16[32,4096]{1,0:T(8,128)(2,1)S(1)}, bf16[32,4096]{1,0:T(8,128)(2,1)S(1)}, u32[]{:S(2)}, u32[]{:S(2)}) collective-permute-start(bf16[32,4096]{1,0:T(8,128)(2,1)S(1)} %get-tuple-element.152.refs_1_), channel_id=1, source_target_pairs={{0,1},{1,0},{2,3},{3,2},{4,5},{5,4},{6,7},{7,6},{8,9},{9,8},{10,11... | collective-permute-start | bytes 786440 | tf_op jit(solution)/shard_map/ppermute | solution.py:428
  19.2 3.2 %collective-permute-start.7 = (bf16[32,4096]{1,0:T(8,128)(2,1)S(1)}, bf16[32,4096]{1,0:T(8,128)(2,1)S(1)}, u32[]{:S(2)}, u32[]{:S(2)}) collective-permute-start(bf16[32,4096]{1,0:T(8,128)(2,1)S(1)} %get-tuple-element.85), channel_id=1, source_target_pairs={{0,1},{1,0},{2,3},{3,2},{4,5},{5,4},{6,7},{7,6},{8,9},{9,8},{10,11... | collective-permute-start | bytes 786440 | tf_op jit(solution)/shard_map/ppermute | solution.py:435
  20.0 5.5 %collective-permute-start.8 = (bf16[64,512]{1,0:T(8,128)(2,1)S(1)}, bf16[64,512]{1,0:T(8,128)(2,1)S(1)}, u32[]{:S(2)}, u32[]{:S(2)}) collective-permute-start(bf16[64,512]{1,0:T(8,128)(2,1)S(1)} %get-tuple-element.87.refs_2_), channel_id=1, source_target_pairs={{0,8},{4,12},{8,0},{12,4},{1,9},{5,13},{9,1},{13,5},{2,10},{6,14},... | collective-permute-start | bytes 196616 | tf_op jit(solution)/shard_map/ppermute | solution.py:454
  22.3 3.1 %copy-start.2 = (bf16[256,512]{1,0:T(8,128)(2,1)S(1)}, bf16[256,512]{1,0:T(8,128)(2,1)}, u32[]{:S(2)}) copy-start(bf16[256,512]{1,0:T(8,128)(2,1)} %refs_3_.5) | copy-start | bytes 786436
  23.9 3.2 %collective-permute-start.9 = (bf16[64,512]{1,0:T(8,128)(2,1)S(1)}, bf16[64,512]{1,0:T(8,128)(2,1)S(1)}, u32[]{:S(2)}, u32[]{:S(2)}) collective-permute-start(bf16[64,512]{1,0:T(8,128)(2,1)S(1)} %get-tuple-element.90), channel_id=1, source_target_pairs={{0,4},{4,0},{8,12},{12,8},{1,5},{5,1},{9,13},{13,9},{2,6},{6,2},{1... | collective-permute-start | bytes 196616 | tf_op jit(solution)/shard_map/ppermute | solution.py:451
  25.5 4.5 %collective-permute-start.10 = (bf16[64,512]{1,0:T(8,128)(2,1)S(1)}, bf16[64,512]{1,0:T(8,128)(2,1)S(1)}, u32[]{:S(2)}, u32[]{:S(2)}) collective-permute-start(bf16[64,512]{1,0:T(8,128)(2,1)S(1)} %get-tuple-element.92.refs_1_), channel_id=1, source_target_pairs={{0,4},{4,0},{8,12},{12,8},{1,5},{5,1},{9,13},{13,9},{2,6},{6,2},{1... | collective-permute-start | bytes 196616 | tf_op jit(solution)/shard_map/ppermute | solution.py:458
  27.1 5.7 %collective-permute-start.11 = (bf16[64,512]{1,0:T(8,128)(2,1)S(1)}, bf16[64,512]{1,0:T(8,128)(2,1)S(1)}, u32[]{:S(2)}, u32[]{:S(2)}) collective-permute-start(bf16[64,512]{1,0:T(8,128)(2,1)S(1)} %get-tuple-element.94.refs_2_), channel_id=1, source_target_pairs={{0,8},{4,12},{8,0},{12,4},{1,9},{5,13},{9,1},{13,5},{2,10},{6,14},... | collective-permute-start | bytes 196616 | tf_op jit(solution)/shard_map/ppermute | solution.py:454
  30.8 3.1 %collective-permute-start.12 = (bf16[64,512]{1,0:T(8,128)(2,1)S(1)}, bf16[64,512]{1,0:T(8,128)(2,1)S(1)}, u32[]{:S(2)}, u32[]{:S(2)}) collective-permute-start(bf16[64,512]{1,0:T(8,128)(2,1)S(1)} %get-tuple-element.97), channel_id=1, source_target_pairs={{0,1},{1,0},{2,3},{3,2},{4,5},{5,4},{6,7},{7,6},{8,9},{9,8},{10,11... | collective-permute-start | bytes 196616 | tf_op jit(solution)/shard_map/ppermute | solution.py:466
  31.6 2.3 %collective-permute-start.13 = (bf16[64,512]{1,0:T(8,128)(2,1)S(1)}, bf16[64,512]{1,0:T(8,128)(2,1)S(1)}, u32[]{:S(2)}, u32[]{:S(2)}) collective-permute-start(bf16[64,512]{1,0:T(8,128)(2,1)S(1)} %get-tuple-element.98), channel_id=1, source_target_pairs={{0,1},{1,0},{2,3},{3,2},{4,5},{5,4},{6,7},{7,6},{8,9},{9,8},{10,11... | collective-permute-start | bytes 196616 | tf_op jit(solution)/shard_map/ppermute | solution.py:466
  31.7 2.7 %collective-permute-start.14 = (bf16[64,512]{1,0:T(8,128)(2,1)S(1)}, bf16[64,512]{1,0:T(8,128)(2,1)S(1)}, u32[]{:S(2)}, u32[]{:S(2)}) collective-permute-start(bf16[64,512]{1,0:T(8,128)(2,1)S(1)} %get-tuple-element.99), channel_id=1, source_target_pairs={{0,1},{1,0},{2,3},{3,2},{4,5},{5,4},{6,7},{7,6},{8,9},{9,8},{10,11... | collective-permute-start | bytes 196616 | tf_op jit(solution)/shard_map/ppermute | solution.py:466
  32.1 2.4 %collective-permute-start.15 = (bf16[64,512]{1,0:T(8,128)(2,1)S(1)}, bf16[64,512]{1,0:T(8,128)(2,1)S(1)}, u32[]{:S(2)}, u32[]{:S(2)}) collective-permute-start(bf16[64,512]{1,0:T(8,128)(2,1)S(1)} %get-tuple-element.100), channel_id=1, source_target_pairs={{0,1},{1,0},{2,3},{3,2},{4,5},{5,4},{6,7},{7,6},{8,9},{9,8},{10,11... | collective-permute-start | bytes 196616 | tf_op jit(solution)/shard_map/ppermute | solution.py:466
  32.8 2.2 %collective-permute-start.16 = (bf16[64,512]{1,0:T(8,128)(2,1)S(1)}, bf16[64,512]{1,0:T(8,128)(2,1)S(1)}, u32[]{:S(2)}, u32[]{:S(2)}) collective-permute-start(bf16[64,512]{1,0:T(8,128)(2,1)S(1)} %get-tuple-element.101), channel_id=1, source_target_pairs={{0,1},{1,0},{2,3},{3,2},{4,5},{5,4},{6,7},{7,6},{8,9},{9,8},{10,11... | collective-permute-start | bytes 196616 | tf_op jit(solution)/shard_map/ppermute | solution.py:466
  33.9 1.3 %collective-permute-start.17 = (bf16[64,512]{1,0:T(8,128)(2,1)S(1)}, bf16[64,512]{1,0:T(8,128)(2,1)S(1)}, u32[]{:S(2)}, u32[]{:S(2)}) collective-permute-start(bf16[64,512]{1,0:T(8,128)(2,1)S(1)} %get-tuple-element.102), channel_id=1, source_target_pairs={{0,1},{1,0},{2,3},{3,2},{4,5},{5,4},{6,7},{7,6},{8,9},{9,8},{10,11... | collective-permute-start | bytes 196616 | tf_op jit(solution)/shard_map/ppermute | solution.py:466
  33.9 1.4 %collective-permute-start.18 = (bf16[64,512]{1,0:T(8,128)(2,1)S(1)}, bf16[64,512]{1,0:T(8,128)(2,1)S(1)}, u32[]{:S(2)}, u32[]{:S(2)}) collective-permute-start(bf16[64,512]{1,0:T(8,128)(2,1)S(1)} %get-tuple-element.103), channel_id=1, source_target_pairs={{0,1},{1,0},{2,3},{3,2},{4,5},{5,4},{6,7},{7,6},{8,9},{9,8},{10,11... | collective-permute-start | bytes 196616 | tf_op jit(solution)/shard_map/ppermute | solution.py:466
  34.4 1.3 %collective-permute-start.19 = (bf16[64,512]{1,0:T(8,128)(2,1)S(1)}, bf16[64,512]{1,0:T(8,128)(2,1)S(1)}, u32[]{:S(2)}, u32[]{:S(2)}) collective-permute-start(bf16[64,512]{1,0:T(8,128)(2,1)S(1)} %get-tuple-element.104), channel_id=1, source_target_pairs={{0,1},{1,0},{2,3},{3,2},{4,5},{5,4},{6,7},{7,6},{8,9},{9,8},{10,11... | collective-permute-start | bytes 196616 | tf_op jit(solution)/shard_map/ppermute | solution.py:466
  34.5 3.2 %collective-permute-start.20 = (bf16[64,512]{1,0:T(8,128)(2,1)S(1)}, bf16[64,512]{1,0:T(8,128)(2,1)S(1)}, u32[]{:S(2)}, u32[]{:S(2)}) collective-permute-start(bf16[64,512]{1,0:T(8,128)(2,1)S(1)} %get-tuple-element.106.refs_1_), channel_id=1, source_target_pairs={{0,4},{4,0},{8,12},{12,8},{1,5},{5,1},{9,13},{13,9},{2,6},{6,2},{1... | collective-permute-start | bytes 196616 | tf_op jit(solution)/shard_map/ppermute | solution.py:458
  35.8 8.8 %collective-permute-start.29 = (bf16[64,2048]{1,0:T(8,128)(2,1)S(1)}, bf16[64,2048]{1,0:T(8,128)(2,1)S(1)}, u32[]{:S(2)}, u32[]{:S(2)}) collective-permute-start(bf16[64,2048]{1,0:T(8,128)(2,1)S(1)} %get-tuple-element.119), channel_id=1, source_target_pairs={{0,2},{2,0},{1,3},{3,1},{4,6},{6,4},{5,7},{7,5},{8,10},{10,8},{9,1... | collective-permute-start | bytes 786440 | tf_op jit(solution)/shard_map/ppermute | solution.py:471
  38.4 2.6 %collective-permute-start.21 = (bf16[64,512]{1,0:T(8,128)(2,1)S(1)}, bf16[64,512]{1,0:T(8,128)(2,1)S(1)}, u32[]{:S(2)}, u32[]{:S(2)}) collective-permute-start(bf16[64,512]{1,0:T(8,128)(2,1)S(1)} %get-tuple-element.109), channel_id=1, source_target_pairs={{0,1},{1,0},{2,3},{3,2},{4,5},{5,4},{6,7},{7,6},{8,9},{9,8},{10,11... | collective-permute-start | bytes 196616 | tf_op jit(solution)/shard_map/ppermute | solution.py:466
  40.1 1.3 %collective-permute-start.22 = (bf16[64,512]{1,0:T(8,128)(2,1)S(1)}, bf16[64,512]{1,0:T(8,128)(2,1)S(1)}, u32[]{:S(2)}, u32[]{:S(2)}) collective-permute-start(bf16[64,512]{1,0:T(8,128)(2,1)S(1)} %get-tuple-element.110), channel_id=1, source_target_pairs={{0,1},{1,0},{2,3},{3,2},{4,5},{5,4},{6,7},{7,6},{8,9},{9,8},{10,11... | collective-permute-start | bytes 196616 | tf_op jit(solution)/shard_map/ppermute | solution.py:466
  40.1 2.4 %collective-permute-start.23 = (bf16[64,512]{1,0:T(8,128)(2,1)S(1)}, bf16[64,512]{1,0:T(8,128)(2,1)S(1)}, u32[]{:S(2)}, u32[]{:S(2)}) collective-permute-start(bf16[64,512]{1,0:T(8,128)(2,1)S(1)} %get-tuple-element.111), channel_id=1, source_target_pairs={{0,1},{1,0},{2,3},{3,2},{4,5},{5,4},{6,7},{7,6},{8,9},{9,8},{10,11... | collective-permute-start | bytes 196616 | tf_op jit(solution)/shard_map/ppermute | solution.py:466
  40.6 2.4 %collective-permute-start.24 = (bf16[64,512]{1,0:T(8,128)(2,1)S(1)}, bf16[64,512]{1,0:T(8,128)(2,1)S(1)}, u32[]{:S(2)}, u32[]{:S(2)}) collective-permute-start(bf16[64,512]{1,0:T(8,128)(2,1)S(1)} %get-tuple-element.112), channel_id=1, source_target_pairs={{0,1},{1,0},{2,3},{3,2},{4,5},{5,4},{6,7},{7,6},{8,9},{9,8},{10,11... | collective-permute-start | bytes 196616 | tf_op jit(solution)/shard_map/ppermute | solution.py:466
  41.0 2.1 %collective-permute-start.25 = (bf16[64,512]{1,0:T(8,128)(2,1)S(1)}, bf16[64,512]{1,0:T(8,128)(2,1)S(1)}, u32[]{:S(2)}, u32[]{:S(2)}) collective-permute-start(bf16[64,512]{1,0:T(8,128)(2,1)S(1)} %get-tuple-element.113), channel_id=1, source_target_pairs={{0,1},{1,0},{2,3},{3,2},{4,5},{5,4},{6,7},{7,6},{8,9},{9,8},{10,11... | collective-permute-start | bytes 196616 | tf_op jit(solution)/shard_map/ppermute | solution.py:466
  41.3 8.2 %collective-permute-start.30 = (bf16[64,2048]{1,0:T(8,128)(2,1)S(1)}, bf16[64,2048]{1,0:T(8,128)(2,1)S(1)}, u32[]{:S(2)}, u32[]{:S(2)}) collective-permute-start(bf16[64,2048]{1,0:T(8,128)(2,1)S(1)} %get-tuple-element.121), channel_id=1, source_target_pairs={{0,2},{2,0},{1,3},{3,1},{4,6},{6,4},{5,7},{7,5},{8,10},{10,8},{9,1... | collective-permute-start | bytes 786440 | tf_op jit(solution)/shard_map/ppermute | solution.py:471
  42.5 1.3 %collective-permute-start.26 = (bf16[64,512]{1,0:T(8,128)(2,1)S(1)}, bf16[64,512]{1,0:T(8,128)(2,1)S(1)}, u32[]{:S(2)}, u32[]{:S(2)}) collective-permute-start(bf16[64,512]{1,0:T(8,128)(2,1)S(1)} %get-tuple-element.114), channel_id=1, source_target_pairs={{0,1},{1,0},{2,3},{3,2},{4,5},{5,4},{6,7},{7,6},{8,9},{9,8},{10,11... | collective-permute-start | bytes 196616 | tf_op jit(solution)/shard_map/ppermute | solution.py:466
  43.0 1.3 %collective-permute-start.27 = (bf16[64,512]{1,0:T(8,128)(2,1)S(1)}, bf16[64,512]{1,0:T(8,128)(2,1)S(1)}, u32[]{:S(2)}, u32[]{:S(2)}) collective-permute-start(bf16[64,512]{1,0:T(8,128)(2,1)S(1)} %get-tuple-element.115), channel_id=1, source_target_pairs={{0,1},{1,0},{2,3},{3,2},{4,5},{5,4},{6,7},{7,6},{8,9},{9,8},{10,11... | collective-permute-start | bytes 196616 | tf_op jit(solution)/shard_map/ppermute | solution.py:466
  43.0 1.3 %collective-permute-start.28 = (bf16[64,512]{1,0:T(8,128)(2,1)S(1)}, bf16[64,512]{1,0:T(8,128)(2,1)S(1)}, u32[]{:S(2)}, u32[]{:S(2)}) collective-permute-start(bf16[64,512]{1,0:T(8,128)(2,1)S(1)} %get-tuple-element.116), channel_id=1, source_target_pairs={{0,1},{1,0},{2,3},{3,2},{4,5},{5,4},{6,7},{7,6},{8,9},{9,8},{10,11... | collective-permute-start | bytes 196616 | tf_op jit(solution)/shard_map/ppermute | solution.py:466
  44.6 7.7 %copy-start.3 = (s32[32]{0:T(128)S(1)}, s32[32]{0:T(128)}, u32[]{:S(2)}) copy-start(s32[32]{0:T(128)} %refs_2_.5) | copy-start | bytes 388
  44.9 7.4 %collective-permute-start.31 = (bf16[64,2048]{1,0:T(8,128)(2,1)S(1)}, bf16[64,2048]{1,0:T(8,128)(2,1)S(1)}, u32[]{:S(2)}, u32[]{:S(2)}) collective-permute-start(bf16[64,2048]{1,0:T(8,128)(2,1)S(1)} %get-tuple-element.123.refs_2_.refs_1_), channel_id=1, source_target_pairs={{0,1},{1,0},{2,3},{3,2},{4,5},{5,4},{6,7},{7,6},{8,9},{9,8},{10,11... | collective-permute-start | bytes 786440 | tf_op jit(solution)/shard_map/ppermute | solution.py:484
  45.3 12.1 %collective-permute-start.34 = (bf16[64,2048]{1,0:T(8,128)(2,1)S(1)}, bf16[64,2048]{1,0:T(8,128)(2,1)S(1)}, u32[]{:S(2)}, u32[]{:S(2)}) collective-permute-start(bf16[64,2048]{1,0:T(8,128)(2,1)S(1)} %get-tuple-element.128), channel_id=1, source_target_pairs={{0,2},{2,0},{1,3},{3,1},{4,6},{6,4},{5,7},{7,5},{8,10},{10,8},{9,1... | collective-permute-start | bytes 786440 | tf_op jit(solution)/shard_map/ppermute | solution.py:471
  46.3 14.4 %collective-permute-start.35 = (bf16[64,2048]{1,0:T(8,128)(2,1)S(1)}, bf16[64,2048]{1,0:T(8,128)(2,1)S(1)}, u32[]{:S(2)}, u32[]{:S(2)}) collective-permute-start(bf16[64,2048]{1,0:T(8,128)(2,1)S(1)} %get-tuple-element.130), channel_id=1, source_target_pairs={{0,2},{2,0},{1,3},{3,1},{4,6},{6,4},{5,7},{7,5},{8,10},{10,8},{9,1... | collective-permute-start | bytes 786440 | tf_op jit(solution)/shard_map/ppermute | solution.py:471
  49.8 2.2 %collective-permute-start.32 = (bf16[64,1024]{1,0:T(8,128)(2,1)S(1)}, bf16[64,1024]{1,0:T(8,128)(2,1)S(1)}, u32[]{:S(2)}, u32[]{:S(2)}) collective-permute-start(bf16[64,1024]{1,0:T(8,128)(2,1)S(1)} %get-tuple-element.124.refs_3_.refs_2_), channel_id=1, source_target_pairs={{0,1},{1,0},{2,3},{3,2},{4,5},{5,4},{6,7},{7,6},{8,9},{9,8},{10,11... | collective-permute-start | bytes 393224 | tf_op jit(solution)/shard_map/ppermute | solution.py:484
  50.9 1.3 %collective-permute-start.33 = (bf16[64,1024]{1,0:T(8,128)(2,1)S(1)}, bf16[64,1024]{1,0:T(8,128)(2,1)S(1)}, u32[]{:S(2)}, u32[]{:S(2)}) collective-permute-start(bf16[64,1024]{1,0:T(8,128)(2,1)S(1)} %get-tuple-element.125.refs_4_.refs_3_), channel_id=1, source_target_pairs={{0,1},{1,0},{2,3},{3,2},{4,5},{5,4},{6,7},{7,6},{8,9},{9,8},{10,11... | collective-permute-start | bytes 393224 | tf_op jit(solution)/shard_map/ppermute | solution.py:484
  54.4 11.3 %collective-permute-start.36 = (bf16[6,32,512]{2,1,0:T(8,128)(2,1)S(1)}, bf16[6,32,512]{2,1,0:T(8,128)(2,1)S(1)}, u32[]{:S(2)}, u32[]{:S(2)}) collective-permute-start(bf16[6,32,512]{2,1,0:T(8,128)(2,1)S(1)} %get-tuple-element.132), channel_id=1, source_target_pairs={{0,8},{4,12},{8,0},{12,4},{1,9},{5,13},{9,1},{13,5},{2,10},{6,14},... | collective-permute-start | bytes 589832 | tf_op jit(solution)/shard_map/ppermute | solution.py:511
  57.7 4.2 %collective-permute-start.37 = (bf16[64,1024]{1,0:T(8,128)(2,1)S(1)}, bf16[64,1024]{1,0:T(8,128)(2,1)S(1)}, u32[]{:S(2)}, u32[]{:S(2)}) collective-permute-start(bf16[64,1024]{1,0:T(8,128)(2,1)S(1)} %get-tuple-element.133.refs_3_.refs_2_), channel_id=1, source_target_pairs={{0,1},{1,0},{2,3},{3,2},{4,5},{5,4},{6,7},{7,6},{8,9},{9,8},{10,11... | collective-permute-start | bytes 393224 | tf_op jit(solution)/shard_map/ppermute | solution.py:484
  58.2 4.2 %collective-permute-start.38 = (bf16[64,1024]{1,0:T(8,128)(2,1)S(1)}, bf16[64,1024]{1,0:T(8,128)(2,1)S(1)}, u32[]{:S(2)}, u32[]{:S(2)}) collective-permute-start(bf16[64,1024]{1,0:T(8,128)(2,1)S(1)} %get-tuple-element.134.refs_4_.refs_3_), channel_id=1, source_target_pairs={{0,1},{1,0},{2,3},{3,2},{4,5},{5,4},{6,7},{7,6},{8,9},{9,8},{10,11... | collective-permute-start | bytes 393224 | tf_op jit(solution)/shard_map/ppermute | solution.py:484
  61.0 4.1 %collective-permute-start.39 = (bf16[64,1024]{1,0:T(8,128)(2,1)S(1)}, bf16[64,1024]{1,0:T(8,128)(2,1)S(1)}, u32[]{:S(2)}, u32[]{:S(2)}) collective-permute-start(bf16[64,1024]{1,0:T(8,128)(2,1)S(1)} %get-tuple-element.135.refs_5_.refs_4_), channel_id=1, source_target_pairs={{0,1},{1,0},{2,3},{3,2},{4,5},{5,4},{6,7},{7,6},{8,9},{9,8},{10,11... | collective-permute-start | bytes 393224 | tf_op jit(solution)/shard_map/ppermute | solution.py:484
  61.8 3.3 %collective-permute-start.40 = (bf16[64,1024]{1,0:T(8,128)(2,1)S(1)}, bf16[64,1024]{1,0:T(8,128)(2,1)S(1)}, u32[]{:S(2)}, u32[]{:S(2)}) collective-permute-start(bf16[64,1024]{1,0:T(8,128)(2,1)S(1)} %get-tuple-element.136.refs_6_.refs_5_), channel_id=1, source_target_pairs={{0,1},{1,0},{2,3},{3,2},{4,5},{5,4},{6,7},{7,6},{8,9},{9,8},{10,11... | collective-permute-start | bytes 393224 | tf_op jit(solution)/shard_map/ppermute | solution.py:484
  61.9 9.4 %collective-permute-start.41 = (bf16[6,32,512]{2,1,0:T(8,128)(2,1)S(1)}, bf16[6,32,512]{2,1,0:T(8,128)(2,1)S(1)}, u32[]{:S(2)}, u32[]{:S(2)}) collective-permute-start(bf16[6,32,512]{2,1,0:T(8,128)(2,1)S(1)} %get-tuple-element.139), channel_id=1, source_target_pairs={{0,4},{4,0},{8,12},{12,8},{1,5},{5,1},{9,13},{13,9},{2,6},{6,2},{1... | collective-permute-start | bytes 589832 | tf_op jit(solution)/shard_map/ppermute | solution.py:511
  62.4 11.8 %collective-permute-start.42 = (bf16[6,32,512]{2,1,0:T(8,128)(2,1)S(1)}, bf16[6,32,512]{2,1,0:T(8,128)(2,1)S(1)}, u32[]{:S(2)}, u32[]{:S(2)}) collective-permute-start(bf16[6,32,512]{2,1,0:T(8,128)(2,1)S(1)} %get-tuple-element.140), channel_id=1, source_target_pairs={{0,12},{4,8},{8,4},{12,0},{1,13},{5,9},{9,5},{13,1},{2,14},{6,10},... | collective-permute-start | bytes 589832 | tf_op jit(solution)/shard_map/ppermute | solution.py:511
  67.8 14.8 %collective-permute-start.43 = (bf16[6,32,512]{2,1,0:T(8,128)(2,1)S(1)}, bf16[6,32,512]{2,1,0:T(8,128)(2,1)S(1)}, u32[]{:S(2)}, u32[]{:S(2)}) collective-permute-start(bf16[6,32,512]{2,1,0:T(8,128)(2,1)S(1)} %get-tuple-element.148), channel_id=1, source_target_pairs={{0,4},{4,0},{8,12},{12,8},{1,5},{5,1},{9,13},{13,9},{2,6},{6,2},{1... | collective-permute-start | bytes 589832 | tf_op jit(solution)/shard_map/ppermute | solution.py:511
  69.8 17.0 %collective-permute-start.44 = (bf16[6,32,512]{2,1,0:T(8,128)(2,1)S(1)}, bf16[6,32,512]{2,1,0:T(8,128)(2,1)S(1)}, u32[]{:S(2)}, u32[]{:S(2)}) collective-permute-start(bf16[6,32,512]{2,1,0:T(8,128)(2,1)S(1)} %get-tuple-element.149), channel_id=1, source_target_pairs={{0,8},{4,12},{8,0},{12,4},{1,9},{5,13},{9,1},{13,5},{2,10},{6,14},... | collective-permute-start | bytes 589832 | tf_op jit(solution)/shard_map/ppermute | solution.py:511
  71.1 20.9 %collective-permute-start.45 = (bf16[6,32,512]{2,1,0:T(8,128)(2,1)S(1)}, bf16[6,32,512]{2,1,0:T(8,128)(2,1)S(1)}, u32[]{:S(2)}, u32[]{:S(2)}) collective-permute-start(bf16[6,32,512]{2,1,0:T(8,128)(2,1)S(1)} %get-tuple-element.150), channel_id=1, source_target_pairs={{0,12},{4,8},{8,4},{12,0},{1,13},{5,9},{9,5},{13,1},{2,14},{6,10},... | collective-permute-start | bytes 589832 | tf_op jit(solution)/shard_map/ppermute | solution.py:511

commit v7 on v6

--- a/solution.py
+++ b/solution.py
@@ -331,7 +331,7 @@
 
 
 def loco_body(row, shard, tiles, count, labels, phen, *refs):
-    *sums, out, base, stage, done = refs
+    *sums, out, base, acc, stage, done = refs
     height = base.shape[0]
     _, depth = place()
     if len(sums) == 1:
@@ -344,15 +344,16 @@
             total = total + part[slot].astype(jnp.float32)
     base[...] = phen[row_at(depth * shard + row, height), :].astype(jnp.float32) - total
 
+    for chrom in range(CHROMS):
+        acc[chrom] = base[...]
+    for first, part in zip(firsts, sums):
+        for slot in range(SPAN):
+            chrom = jnp.minimum(first + slot, CHROMS - 1)
+            acc[chrom] = acc[chrom] + part[slot].astype(jnp.float32)
     group = -(-CHROMS // done.shape[0])
     copies = []
     for chrom in range(CHROMS):
-        value = base[...]
-        for first, part in zip(firsts, sums):
-            slot = chrom - first
-            inside = ((slot >= 0) & (slot < SPAN)).astype(jnp.float32)
-            value = value + inside * part[jnp.clip(slot, 0, SPAN - 1)].astype(jnp.float32)
-        stage[chrom] = value.astype(stage.dtype)
+        stage[chrom] = acc[chrom].astype(stage.dtype)
         if (chrom + 1) % group == 0 or chrom + 1 == CHROMS:
             begin = chrom // group * group
             some = pl.ds(begin, chrom + 1 - begin)
@@ -380,7 +381,7 @@
         out_shape=[jax.ShapeDtypeStruct(shape, jnp.bfloat16), jax.ShapeDtypeStruct(token.shape, token.dtype)],
         in_specs=specs,
         out_specs=[anywhere, anywhere],
-        scratch_shapes=[pltpu.VMEM((height, people), jnp.float32)]
+        scratch_shapes=[pltpu.VMEM((height, people), jnp.float32), pltpu.VMEM((shape[0], height, people), jnp.float32)]
         + [pltpu.VMEM((shape[0], height, people), jnp.bfloat16), pltpu.SemaphoreType.DMA((3,))],
         input_output_aliases=aliases,
         cost_estimate=pl.CostEstimate(flops=1, bytes_accessed=1, transcendentals=0),
@@ -503,7 +504,7 @@
                 now["den"],
                 streamed=True,
                 scratch=[pltpu.VMEM((4 * height, people_dev), f32)],
-                after=[after[at - 1]["chrom"][2]] if at and HOLD else [],
+                after=[after[at - 1]["chrom"][3]] if at and HOLD else [],
             )
             if together:
                 now["chrom"] = [lax.all_to_all(sums[0], "mk", 0, 0, tiled=True)]

time: 94.4 us -> 94 us (level)
  waiting for transfers between devices: 34.3 us -> 35.4 us
  starting transfers between devices: 37.7 us -> 36.7 us
    ppermute x6, starting transfers between devices: 9.63 us -> 8.66 us  [piece_steps(): lax.ppermute(sums[step], 'mk', along(step))]
where the time goes in v7:
time: 94 us; the launch traced here: 93.8 us
  starting transfers between devices  36.7 us (39%)
  waiting for transfers between devices  35.4 us (38%)
  Pallas kernels  15.5 us (16%)
  local copies, waits for them, and re-layouts  5.23 us (6%)
    ppermute x6, waiting for transfers between devices, piece_steps(): lax.ppermute(sums[step], 'mk', along(step))  18.6 us
    pallas_call x20, Pallas kernels, call(): pl.pallas_call(kernel, out_shape=[jax.ShapeDtypeStruct(self.token.shape,...  11.9 us
    ppermute x6, starting transfers between devices, piece_steps(): lax.ppermute(sums[step], 'mk', along(step))  8.66 us
    ppermute x16, starting transfers between devices, piece_steps(): now['score'] = [keep] + [lax.ppermute(send, 'sub', swap) for send in sends]  6.58 us
    ppermute x4, waiting for transfers between devices, piece_steps(): now['chip'] = [chip] + [lax.ppermute(send, 'pp', swap) for send in sends]  5.48 us
    ppermute x2, starting transfers between devices, piece_steps(): now['two'] = (two, lax.ppermute(two, 'mk', along(2)))  5.26 us
    ppermute x4, starting transfers between devices, piece_steps(): lax.ppermute(one, 'sub', swap)  4.35 us
    unnamed x14, local copies, waits for them, and re-layouts  4.17 us
  transfers between devices with their start and end apart: 46, of which 23 were waited for; matrix products, arithmetic and copies ran while one was open for 0% of the time, Pallas kernels for 15%

profile of v7, /device:TPU:13, one launch (start us, length us, event | category | flops | bytes accessed | tf_op | source)
XLA Modules:
  0.0 93.8 jit_solution(10462159165554325159)
XLA Ops:
  0.6 1.1 %fusion = (bf16[32,4096]{1,0:T(8,128)(2,1)S(1)}, bf16[32,4096]{1,0:T(8,128)(2,1)S(1)}) fusion(bf16[64,4096]{1,0:T(8,128)(2,1)} %param.8), kind=kLoop, calls=%fused_computation | loop fusion | bytes 1048576 | tf_op jit(solution)/shard_map/slice | solution.py:414
  1.7 1.3 %collective-permute-start = (bf16[32,4096]{1,0:T(8,128)(2,1)S(1)}, bf16[32,4096]{1,0:T(8,128)(2,1)S(1)}, u32[]{:S(2)}, u32[]{:S(2)}) collective-permute-start(bf16[32,4096]{1,0:T(8,128)(2,1)S(1)} %get-tuple-element.153.refs_1_), channel_id=1, source_target_pairs={{0,2},{2,0},{1,3},{3,1},{4,6},{6,4},{5,7},{7,5},{8,10},{10,8},{9,1... | collective-permute-start | bytes 786440 | tf_op jit(solution)/shard_map/ppermute | solution.py:416
  3.0 2.2 %copy-done = bf16[512,4096]{1,0:T(8,128)(2,1)S(1)} copy-done((bf16[512,4096]{1,0:T(8,128)(2,1)S(1)}, bf16[512,4096]{1,0:T(8,128)(2,1)}, u32[]{:S(2)}) %copy-start) | copy-done | bytes 4194328
  5.2 0.7 copy-done.4
  5.8 0.7 copy-done.5
  6.5 0.7 copy-done.6
  7.2 1.0 %collective-permute-start.1 = (bf16[32,4096]{1,0:T(8,128)(2,1)S(1)}, bf16[32,4096]{1,0:T(8,128)(2,1)S(1)}, u32[]{:S(2)}, u32[]{:S(2)}) collective-permute-start(bf16[32,4096]{1,0:T(8,128)(2,1)S(1)} %get-tuple-element.78), channel_id=1, source_target_pairs={{0,1},{1,0},{2,3},{3,2},{4,5},{5,4},{6,7},{7,6},{8,9},{9,8},{10,11... | collective-permute-start | bytes 786440 | tf_op jit(solution)/shard_map/ppermute | solution.py:429
  8.3 0.7 collective-permute-done.refs_2_
  8.9 1.5 %collective-permute-start.2 = (bf16[32,4096]{1,0:T(8,128)(2,1)S(1)}, bf16[32,4096]{1,0:T(8,128)(2,1)S(1)}, u32[]{:S(2)}, u32[]{:S(2)}) collective-permute-start(bf16[32,4096]{1,0:T(8,128)(2,1)S(1)} %collective-permute-done.refs_2_), channel_id=1, source_target_pairs={{0,1},{1,0},{2,3},{3,2},{4,5},{5,4},{6,7},{7,6},{8,9},{9,8},{10,11... | collective-permute-start | bytes 786440 | tf_op jit(solution)/shard_map/ppermute | solution.py:430
  10.5 1.2 %collective-permute-start.5 = (bf16[32,4096]{1,0:T(8,128)(2,1)S(1)}, bf16[32,4096]{1,0:T(8,128)(2,1)S(1)}, u32[]{:S(2)}, u32[]{:S(2)}) collective-permute-start(bf16[32,4096]{1,0:T(8,128)(2,1)S(1)} %get-tuple-element.152.refs_1_), channel_id=1, source_target_pairs={{0,2},{2,0},{1,3},{3,1},{4,6},{6,4},{5,7},{7,5},{8,10},{10,8},{9,1... | collective-permute-start | bytes 786440 | tf_op jit(solution)/shard_map/ppermute | solution.py:428
  11.7 1.6 %shard_map.87 = (f32[8,128]{1,0:T(8,128)S(1)}, f32[64,512]{1,0:T(8,128)S(1)}, bf16[64,512]{1,0:T(8,128)(2,1)S(1)}) custom-call(f32[8,128]{1,0:T(8,128)S(1)} %get-tuple-element.77.refs_0_, bf16[32,4096]{1,0:T(8,128)(2,1)S(1)} %get-tuple-element.153.refs_1_, bf16[32,4096]{1,0:T(8,128)(2,1)S(1)} %collective-permute-done.refs_2_, ...), custom_call_target="tpu_custom_call", output_to_operand_aliasing={{0}: (0, {})} | custom-call | flops 1 | bytes 1 | tf_op jit(solution)/shard_map/pallas_call | solution.py:148
  13.5 1.1 %collective-permute-start.4 = (f32[64,128]{1,0:T(8,128)S(1)}, f32[64,128]{1,0:T(8,128)S(1)}, u32[]{:S(2)}, u32[]{:S(2)}) collective-permute-start(f32[64,128]{1,0:T(8,128)S(1)} %get-tuple-element.83.refs_3_), channel_id=1, source_target_pairs={{0,2},{2,0},{1,3},{3,1},{4,6},{6,4},{5,7},{7,5},{8,10},{10,8},{9,1... | collective-permute-start | bytes 98312 | tf_op jit(solution)/shard_map/ppermute | solution.py:424
  14.7 0.9 collective-permute-start.6
  15.6 1.2 %collective-permute-done.3.refs_2_ = bf16[64,512]{1,0:T(8,128)(2,1)S(1)} collective-permute-done((bf16[64,512]{1,0:T(8,128)(2,1)S(1)}, bf16[64,512]{1,0:T(8,128)(2,1)S(1)}, u32[]{:S(2)}, u32[]{:S(2)}) %collective-permute-start.3) | collective-permute-done | bytes 65568 | tf_op jit(solution)/shard_map/ppermute | solution.py:452
  16.8 2.4 %collective-permute-done.4.refs_1_.refs_4_ = f32[64,128]{1,0:T(8,128)S(1)} collective-permute-done((f32[64,128]{1,0:T(8,128)S(1)}, f32[64,128]{1,0:T(8,128)S(1)}, u32[]{:S(2)}, u32[]{:S(2)}) %collective-permute-start.4) | collective-permute-done | bytes 32800 | tf_op jit(solution)/shard_map/ppermute | solution.py:424
  19.2 0.8 collective-permute-start.7
  20.0 2.3 %collective-permute-start.8 = (bf16[64,512]{1,0:T(8,128)(2,1)S(1)}, bf16[64,512]{1,0:T(8,128)(2,1)S(1)}, u32[]{:S(2)}, u32[]{:S(2)}) collective-permute-start(bf16[64,512]{1,0:T(8,128)(2,1)S(1)} %get-tuple-element.87.refs_2_), channel_id=1, source_target_pairs={{0,8},{4,12},{8,0},{12,4},{1,9},{5,13},{9,1},{13,5},{2,10},{6,14},... | collective-permute-start | bytes 196616 | tf_op jit(solution)/shard_map/ppermute | solution.py:455
  22.3 1.6 %shard_map.90 = (f32[8,128]{1,0:T(8,128)S(1)}, f32[64,512]{1,0:T(8,128)S(1)}, bf16[64,512]{1,0:T(8,128)(2,1)S(1)}) custom-call(f32[8,128]{1,0:T(8,128)S(1)} %get-tuple-element.84.refs_0_, bf16[32,4096]{1,0:T(8,128)(2,1)S(1)} %get-tuple-element.152.refs_1_, bf16[32,4096]{1,0:T(8,128)(2,1)S(1)} %collective-permute-done.5.refs_2_, ...), custom_call_target="tpu_custom_call", output_to_operand_aliasing={{0}: (0, {})} | custom-call | flops 1 | bytes 1 | tf_op jit(solution)/shard_map/pallas_call | solution.py:148
  24.1 1.3 %collective-permute-done.8.refs_3_ = bf16[64,512]{1,0:T(8,128)(2,1)S(1)} collective-permute-done((bf16[64,512]{1,0:T(8,128)(2,1)S(1)}, bf16[64,512]{1,0:T(8,128)(2,1)S(1)}, u32[]{:S(2)}, u32[]{:S(2)}) %collective-permute-start.8) | collective-permute-done | bytes 65568 | tf_op jit(solution)/shard_map/ppermute | solution.py:455
  25.6 1.5 %collective-permute-done.9.refs_2_ = bf16[64,512]{1,0:T(8,128)(2,1)S(1)} collective-permute-done((bf16[64,512]{1,0:T(8,128)(2,1)S(1)}, bf16[64,512]{1,0:T(8,128)(2,1)S(1)}, u32[]{:S(2)}, u32[]{:S(2)}) %collective-permute-start.9) | collective-permute-done | bytes 65568 | tf_op jit(solution)/shard_map/ppermute | solution.py:452
  27.1 2.9 %collective-permute-start.11 = (bf16[64,512]{1,0:T(8,128)(2,1)S(1)}, bf16[64,512]{1,0:T(8,128)(2,1)S(1)}, u32[]{:S(2)}, u32[]{:S(2)}) collective-permute-start(bf16[64,512]{1,0:T(8,128)(2,1)S(1)} %get-tuple-element.94.refs_2_), channel_id=1, source_target_pairs={{0,8},{4,12},{8,0},{12,4},{1,9},{5,13},{9,1},{13,5},{2,10},{6,14},... | collective-permute-start | bytes 196616 | tf_op jit(solution)/shard_map/ppermute | solution.py:455
  30.0 0.7 shard_map.93
  30.8 0.8 collective-permute-start.12
  31.7 0.4 collective-permute-start.14
  32.2 0.6 collective-permute-done.11.refs_3_
  32.8 1.0 %collective-permute-start.16 = (bf16[64,512]{1,0:T(8,128)(2,1)S(1)}, bf16[64,512]{1,0:T(8,128)(2,1)S(1)}, u32[]{:S(2)}, u32[]{:S(2)}) collective-permute-start(bf16[64,512]{1,0:T(8,128)(2,1)S(1)} %get-tuple-element.101), channel_id=1, source_target_pairs={{0,1},{1,0},{2,3},{3,2},{4,5},{5,4},{6,7},{7,6},{8,9},{9,8},{10,11... | collective-permute-start | bytes 196616 | tf_op jit(solution)/shard_map/ppermute | solution.py:467
  33.9 0.5 collective-permute-start.18
  34.5 0.6 collective-permute-start.20
  35.3 0.4 collective-permute-done.19.refs_9_
  35.8 1.3 %collective-permute-start.29 = (bf16[64,2048]{1,0:T(8,128)(2,1)S(1)}, bf16[64,2048]{1,0:T(8,128)(2,1)S(1)}, u32[]{:S(2)}, u32[]{:S(2)}) collective-permute-start(bf16[64,2048]{1,0:T(8,128)(2,1)S(1)} %get-tuple-element.119), channel_id=1, source_target_pairs={{0,2},{2,0},{1,3},{3,1},{4,6},{6,4},{5,7},{7,5},{8,10},{10,8},{9,1... | collective-permute-start | bytes 786440 | tf_op jit(solution)/shard_map/ppermute | solution.py:472
  37.1 0.6 collective-permute-done.20.refs_2_
  37.7 0.7 shard_map.96
  38.4 1.7 %collective-permute-start.21 = (bf16[64,512]{1,0:T(8,128)(2,1)S(1)}, bf16[64,512]{1,0:T(8,128)(2,1)S(1)}, u32[]{:S(2)}, u32[]{:S(2)}) collective-permute-start(bf16[64,512]{1,0:T(8,128)(2,1)S(1)} %get-tuple-element.109), channel_id=1, source_target_pairs={{0,1},{1,0},{2,3},{3,2},{4,5},{5,4},{6,7},{7,6},{8,9},{9,8},{10,11... | collective-permute-start | bytes 196616 | tf_op jit(solution)/shard_map/ppermute | solution.py:467
  40.1 0.4 collective-permute-start.23
  41.3 1.2 %collective-permute-start.30 = (bf16[64,2048]{1,0:T(8,128)(2,1)S(1)}, bf16[64,2048]{1,0:T(8,128)(2,1)S(1)}, u32[]{:S(2)}, u32[]{:S(2)}) collective-permute-start(bf16[64,2048]{1,0:T(8,128)(2,1)S(1)} %get-tuple-element.121), channel_id=1, source_target_pairs={{0,2},{2,0},{1,3},{3,1},{4,6},{6,4},{5,7},{7,5},{8,10},{10,8},{9,1... | collective-permute-start | bytes 786440 | tf_op jit(solution)/shard_map/ppermute | solution.py:472
  42.5 0.4 collective-permute-start.26
  43.0 0.4 collective-permute-start.28
  43.5 0.4 collective-permute-done.26.refs_7_
  43.9 0.4 collective-permute-done.27.refs_8_
  44.9 0.4 collective-permute-start.31
  45.3 1.0 %collective-permute-start.34 = (bf16[64,2048]{1,0:T(8,128)(2,1)S(1)}, bf16[64,2048]{1,0:T(8,128)(2,1)S(1)}, u32[]{:S(2)}, u32[]{:S(2)}) collective-permute-start(bf16[64,2048]{1,0:T(8,128)(2,1)S(1)} %get-tuple-element.128), channel_id=1, source_target_pairs={{0,2},{2,0},{1,3},{3,1},{4,6},{6,4},{5,7},{7,5},{8,10},{10,8},{9,1... | collective-permute-start | bytes 786440 | tf_op jit(solution)/shard_map/ppermute | solution.py:472
  46.3 0.5 collective-permute-start.35
  46.8 2.7 %collective-permute-done.30.refs_6_ = bf16[64,2048]{1,0:T(8,128)(2,1)S(1)} collective-permute-done((bf16[64,2048]{1,0:T(8,128)(2,1)S(1)}, bf16[64,2048]{1,0:T(8,128)(2,1)S(1)}, u32[]{:S(2)}, u32[]{:S(2)}) %collective-permute-start.30) | collective-permute-done | bytes 262176 | tf_op jit(solution)/shard_map/ppermute | solution.py:472
  49.8 1.2 %collective-permute-start.32 = (bf16[64,1024]{1,0:T(8,128)(2,1)S(1)}, bf16[64,1024]{1,0:T(8,128)(2,1)S(1)}, u32[]{:S(2)}, u32[]{:S(2)}) collective-permute-start(bf16[64,1024]{1,0:T(8,128)(2,1)S(1)} %get-tuple-element.124.refs_3_.refs_2_), channel_id=1, source_target_pairs={{0,1},{1,0},{2,3},{3,2},{4,5},{5,4},{6,7},{7,6},{8,9},{9,8},{10,11... | collective-permute-start | bytes 393224 | tf_op jit(solution)/shard_map/ppermute | solution.py:485
  51.0 0.9 collective-permute-done.32.refs_6_
  51.9 0.4 collective-permute-done.33.refs_7_
  52.3 2.1 %shard_map.100 = (f32[8,128]{1,0:T(8,128)S(1)}, bf16[6,32,512]{2,1,0:T(8,128)(2,1)S(1)}, bf16[6,32,512]{2,1,0:T(8,128)(2,1)S(1)}, bf16[6,32,512]{2,1,0:T(8,128)(2,1)S(1)}, bf16[6,32,512]{2,1,0:T(8,128)(2,1)S(1)}) custom-call(f32[8,128]{1,0:T(8,128)S(1)} %get-tuple-element.122.refs_0_, s32[32]{0:T(128)S(1)} %copy-done.3, ...), custom_call_target="tpu_custom_call", output_to_operand_aliasing={{0}: (0, {})} | custom-call | flops 1 | bytes 1 | tf_op jit(solution)/shard_map/pallas_call | solution.py:148
  54.4 2.6 %collective-permute-start.36 = (bf16[6,32,512]{2,1,0:T(8,128)(2,1)S(1)}, bf16[6,32,512]{2,1,0:T(8,128)(2,1)S(1)}, u32[]{:S(2)}, u32[]{:S(2)}) collective-permute-start(bf16[6,32,512]{2,1,0:T(8,128)(2,1)S(1)} %get-tuple-element.132), channel_id=1, source_target_pairs={{0,12},{4,8},{8,4},{12,0},{1,13},{5,9},{9,5},{13,1},{2,14},{6,10},... | collective-permute-start | bytes 589832 | tf_op jit(solution)/shard_map/ppermute | solution.py:512
  57.3 0.5 collective-permute-start.37
  57.9 2.8 %collective-permute-done.35.refs_6_ = bf16[64,2048]{1,0:T(8,128)(2,1)S(1)} collective-permute-done((bf16[64,2048]{1,0:T(8,128)(2,1)S(1)}, bf16[64,2048]{1,0:T(8,128)(2,1)S(1)}, u32[]{:S(2)}, u32[]{:S(2)}) %collective-permute-start.35) | collective-permute-done | bytes 262176 | tf_op jit(solution)/shard_map/ppermute | solution.py:472
  61.0 0.8 collective-permute-start.39
  61.9 0.5 collective-permute-start.41
  62.4 2.8 %collective-permute-start.42 = (bf16[6,32,512]{2,1,0:T(8,128)(2,1)S(1)}, bf16[6,32,512]{2,1,0:T(8,128)(2,1)S(1)}, u32[]{:S(2)}, u32[]{:S(2)}) collective-permute-start(bf16[6,32,512]{2,1,0:T(8,128)(2,1)S(1)} %get-tuple-element.140), channel_id=1, source_target_pairs={{0,8},{4,12},{8,0},{12,4},{1,9},{5,13},{9,1},{13,5},{2,10},{6,14},... | collective-permute-start | bytes 589832 | tf_op jit(solution)/shard_map/ppermute | solution.py:512
  65.2 1.2 %collective-permute-done.36.refs_1_.refs_6_ = bf16[6,32,512]{2,1,0:T(8,128)(2,1)S(1)} collective-permute-done((bf16[6,32,512]{2,1,0:T(8,128)(2,1)S(1)}, bf16[6,32,512]{2,1,0:T(8,128)(2,1)S(1)}, u32[]{:S(2)}, u32[]{:S(2)}) %collective-permute-start.36) | collective-permute-done | bytes 196640 | tf_op jit(solution)/shard_map/ppermute | solution.py:512
  66.4 2.1 %shard_map.103 = (f32[8,128]{1,0:T(8,128)S(1)}, bf16[6,32,512]{2,1,0:T(8,128)(2,1)S(1)}, bf16[6,32,512]{2,1,0:T(8,128)(2,1)S(1)}, bf16[6,32,512]{2,1,0:T(8,128)(2,1)S(1)}, bf16[6,32,512]{2,1,0:T(8,128)(2,1)S(1)}) custom-call(f32[8,128]{1,0:T(8,128)S(1)} %get-tuple-element.131.refs_0_, ...), custom_call_target="tpu_custom_call", output_to_operand_aliasing={{0}: (0, {})} | custom-call | flops 1 | bytes 1 | tf_op jit(solution)/shard_map/pallas_call | solution.py:148
  68.6 2.3 %collective-permute-start.44 = (bf16[6,32,512]{2,1,0:T(8,128)(2,1)S(1)}, bf16[6,32,512]{2,1,0:T(8,128)(2,1)S(1)}, u32[]{:S(2)}, u32[]{:S(2)}) collective-permute-start(bf16[6,32,512]{2,1,0:T(8,128)(2,1)S(1)} %get-tuple-element.149), channel_id=1, source_target_pairs={{0,8},{4,12},{8,0},{12,4},{1,9},{5,13},{9,1},{13,5},{2,10},{6,14},... | collective-permute-start | bytes 589832 | tf_op jit(solution)/shard_map/ppermute | solution.py:512
  71.2 2.8 %collective-permute-done.42.refs_5_ = bf16[6,32,512]{2,1,0:T(8,128)(2,1)S(1)} collective-permute-done((bf16[6,32,512]{2,1,0:T(8,128)(2,1)S(1)}, bf16[6,32,512]{2,1,0:T(8,128)(2,1)S(1)}, u32[]{:S(2)}, u32[]{:S(2)}) %collective-permute-start.42) | collective-permute-done | bytes 196640 | tf_op jit(solution)/shard_map/ppermute | solution.py:512
  74.1 1.8 %shard_map.104 = (bf16[22,64,512]{2,1,0:T(8,128)(2,1)}, f32[8,128]{1,0:T(8,128)S(1)}) custom-call(f32[8,128]{1,0:T(8,128)S(1)} %get-tuple-element.137.refs_0_, s32[32]{0:T(128)S(1)} %copy-done.3, bf16[256,512]{1,0:T(8,128)(2,1)S(1)} %copy-done.2, bf16[6,32,512]{2,1,0:T(8,128)(2,1)S(1)} %get-tuple-element.138.refs_3_, ...), custom_call_target="tpu_custom_call", output_to_operand_aliasing={{1}: (0, {})} | custom-call | flops 1 | bytes 1 | tf_op jit(solution)/shard_map/pallas_call | solution.py:379
  75.9 0.7 shard_map.105
  76.6 0.7 shard_map.106
  77.4 0.4 collective-permute-done.43.refs_5_
  77.7 8.3 %collective-permute-done.44.refs_6_ = bf16[6,32,512]{2,1,0:T(8,128)(2,1)S(1)} collective-permute-done((bf16[6,32,512]{2,1,0:T(8,128)(2,1)S(1)}, bf16[6,32,512]{2,1,0:T(8,128)(2,1)S(1)}, u32[]{:S(2)}, u32[]{:S(2)}) %collective-permute-start.44) | collective-permute-done | bytes 196640 | tf_op jit(solution)/shard_map/ppermute | solution.py:512
  86.1 5.9 %collective-permute-done.45.refs_7_ = bf16[6,32,512]{2,1,0:T(8,128)(2,1)S(1)} collective-permute-done((bf16[6,32,512]{2,1,0:T(8,128)(2,1)S(1)}, bf16[6,32,512]{2,1,0:T(8,128)(2,1)S(1)}, u32[]{:S(2)}, u32[]{:S(2)}) %collective-permute-start.45) | collective-permute-done | bytes 196640 | tf_op jit(solution)/shard_map/ppermute | solution.py:512
  92.0 1.8 %shard_map.107 = (bf16[22,64,512]{2,1,0:T(8,128)(2,1)}, f32[8,128]{1,0:T(8,128)S(1)}) custom-call(bf16[22,64,512]{2,1,0:T(8,128)(2,1)} %get-tuple-element.145.refs_0_, f32[8,128]{1,0:T(8,128)S(1)} %get-tuple-element.146.refs_1_, s32[32]{0:T(128)S(1)} %copy-done.3, bf16[256,512]{1,0:T(8,128)(2,1)S(1)} %copy-done.2, ...), custom_call_target="tpu_custom_call", output_to_operand_aliasing={{0}: (0, {}), {1}: (1, {})} | custom-call | flops 1 | bytes 1 | tf_op jit(solution)/shard_map/pallas_call | solution.py:379
  (66 shorter events, 4.5 us)
Async XLA Ops:
  1.7 7.2 %collective-permute-start = (bf16[32,4096]{1,0:T(8,128)(2,1)S(1)}, bf16[32,4096]{1,0:T(8,128)(2,1)S(1)}, u32[]{:S(2)}, u32[]{:S(2)}) collective-permute-start(bf16[32,4096]{1,0:T(8,128)(2,1)S(1)} %get-tuple-element.153.refs_1_), channel_id=1, source_target_pairs={{0,2},{2,0},{1,3},{3,1},{4,6},{6,4},{5,7},{7,5},{8,10},{10,8},{9,1... | collective-permute-start | bytes 786440 | tf_op jit(solution)/shard_map/ppermute | solution.py:416
  3.0 2.2 %copy-start = (bf16[512,4096]{1,0:T(8,128)(2,1)S(1)}, bf16[512,4096]{1,0:T(8,128)(2,1)}, u32[]{:S(2)}) copy-start(bf16[512,4096]{1,0:T(8,128)(2,1)} %refs_11_.1) | copy-start | bytes 12582916
  5.2 0.7 copy-start.4
  5.8 0.7 copy-start.5
  6.5 0.7 copy-start.6
  7.1 4.6 %copy-start.1 = (bf16[512,4096]{1,0:T(8,128)(2,1)S(1)}, bf16[512,4096]{1,0:T(8,128)(2,1)}, u32[]{:S(2)}) copy-start(bf16[512,4096]{1,0:T(8,128)(2,1)} %refs_11_.1) | copy-start | bytes 12582916
  7.2 4.5 %collective-permute-start.1 = (bf16[32,4096]{1,0:T(8,128)(2,1)S(1)}, bf16[32,4096]{1,0:T(8,128)(2,1)S(1)}, u32[]{:S(2)}, u32[]{:S(2)}) collective-permute-start(bf16[32,4096]{1,0:T(8,128)(2,1)S(1)} %get-tuple-element.78), channel_id=1, source_target_pairs={{0,1},{1,0},{2,3},{3,2},{4,5},{5,4},{6,7},{7,6},{8,9},{9,8},{10,11... | collective-permute-start | bytes 786440 | tf_op jit(solution)/shard_map/ppermute | solution.py:429
  8.9 2.8 %collective-permute-start.2 = (bf16[32,4096]{1,0:T(8,128)(2,1)S(1)}, bf16[32,4096]{1,0:T(8,128)(2,1)S(1)}, u32[]{:S(2)}, u32[]{:S(2)}) collective-permute-start(bf16[32,4096]{1,0:T(8,128)(2,1)S(1)} %collective-permute-done.refs_2_), channel_id=1, source_target_pairs={{0,1},{1,0},{2,3},{3,2},{4,5},{5,4},{6,7},{7,6},{8,9},{9,8},{10,11... | collective-permute-start | bytes 786440 | tf_op jit(solution)/shard_map/ppermute | solution.py:430
  10.5 8.6 %collective-permute-start.5 = (bf16[32,4096]{1,0:T(8,128)(2,1)S(1)}, bf16[32,4096]{1,0:T(8,128)(2,1)S(1)}, u32[]{:S(2)}, u32[]{:S(2)}) collective-permute-start(bf16[32,4096]{1,0:T(8,128)(2,1)S(1)} %get-tuple-element.152.refs_1_), channel_id=1, source_target_pairs={{0,2},{2,0},{1,3},{3,1},{4,6},{6,4},{5,7},{7,5},{8,10},{10,8},{9,1... | collective-permute-start | bytes 786440 | tf_op jit(solution)/shard_map/ppermute | solution.py:428
  13.3 3.5 %collective-permute-start.3 = (bf16[64,512]{1,0:T(8,128)(2,1)S(1)}, bf16[64,512]{1,0:T(8,128)(2,1)S(1)}, u32[]{:S(2)}, u32[]{:S(2)}) collective-permute-start(bf16[64,512]{1,0:T(8,128)(2,1)S(1)} %get-tuple-element.81), channel_id=1, source_target_pairs={{0,4},{4,0},{8,12},{12,8},{1,5},{5,1},{9,13},{13,9},{2,6},{6,2},{1... | collective-permute-start | bytes 196616 | tf_op jit(solution)/shard_map/ppermute | solution.py:452
  13.5 5.6 %collective-permute-start.4 = (f32[64,128]{1,0:T(8,128)S(1)}, f32[64,128]{1,0:T(8,128)S(1)}, u32[]{:S(2)}, u32[]{:S(2)}) collective-permute-start(f32[64,128]{1,0:T(8,128)S(1)} %get-tuple-element.83.refs_3_), channel_id=1, source_target_pairs={{0,2},{2,0},{1,3},{3,1},{4,6},{6,4},{5,7},{7,5},{8,10},{10,8},{9,1... | collective-permute-start | bytes 98312 | tf_op jit(solution)/shard_map/ppermute | solution.py:424
  14.7 7.7 %collective-permute-start.6 = (bf16[32,4096]{1,0:T(8,128)(2,1)S(1)}, bf16[32,4096]{1,0:T(8,128)(2,1)S(1)}, u32[]{:S(2)}, u32[]{:S(2)}) collective-permute-start(bf16[32,4096]{1,0:T(8,128)(2,1)S(1)} %get-tuple-element.152.refs_1_), channel_id=1, source_target_pairs={{0,1},{1,0},{2,3},{3,2},{4,5},{5,4},{6,7},{7,6},{8,9},{9,8},{10,11... | collective-permute-start | bytes 786440 | tf_op jit(solution)/shard_map/ppermute | solution.py:429
  19.2 3.2 %collective-permute-start.7 = (bf16[32,4096]{1,0:T(8,128)(2,1)S(1)}, bf16[32,4096]{1,0:T(8,128)(2,1)S(1)}, u32[]{:S(2)}, u32[]{:S(2)}) collective-permute-start(bf16[32,4096]{1,0:T(8,128)(2,1)S(1)} %get-tuple-element.85), channel_id=1, source_target_pairs={{0,1},{1,0},{2,3},{3,2},{4,5},{5,4},{6,7},{7,6},{8,9},{9,8},{10,11... | collective-permute-start | bytes 786440 | tf_op jit(solution)/shard_map/ppermute | solution.py:436
  20.0 5.5 %collective-permute-start.8 = (bf16[64,512]{1,0:T(8,128)(2,1)S(1)}, bf16[64,512]{1,0:T(8,128)(2,1)S(1)}, u32[]{:S(2)}, u32[]{:S(2)}) collective-permute-start(bf16[64,512]{1,0:T(8,128)(2,1)S(1)} %get-tuple-element.87.refs_2_), channel_id=1, source_target_pairs={{0,8},{4,12},{8,0},{12,4},{1,9},{5,13},{9,1},{13,5},{2,10},{6,14},... | collective-permute-start | bytes 196616 | tf_op jit(solution)/shard_map/ppermute | solution.py:455
  22.3 3.1 %copy-start.2 = (bf16[256,512]{1,0:T(8,128)(2,1)S(1)}, bf16[256,512]{1,0:T(8,128)(2,1)}, u32[]{:S(2)}) copy-start(bf16[256,512]{1,0:T(8,128)(2,1)} %refs_3_.5) | copy-start | bytes 786436
  23.9 3.2 %collective-permute-start.9 = (bf16[64,512]{1,0:T(8,128)(2,1)S(1)}, bf16[64,512]{1,0:T(8,128)(2,1)S(1)}, u32[]{:S(2)}, u32[]{:S(2)}) collective-permute-start(bf16[64,512]{1,0:T(8,128)(2,1)S(1)} %get-tuple-element.90), channel_id=1, source_target_pairs={{0,4},{4,0},{8,12},{12,8},{1,5},{5,1},{9,13},{13,9},{2,6},{6,2},{1... | collective-permute-start | bytes 196616 | tf_op jit(solution)/shard_map/ppermute | solution.py:452
  25.5 4.5 %collective-permute-start.10 = (bf16[64,512]{1,0:T(8,128)(2,1)S(1)}, bf16[64,512]{1,0:T(8,128)(2,1)S(1)}, u32[]{:S(2)}, u32[]{:S(2)}) collective-permute-start(bf16[64,512]{1,0:T(8,128)(2,1)S(1)} %get-tuple-element.92.refs_1_), channel_id=1, source_target_pairs={{0,4},{4,0},{8,12},{12,8},{1,5},{5,1},{9,13},{13,9},{2,6},{6,2},{1... | collective-permute-start | bytes 196616 | tf_op jit(solution)/shard_map/ppermute | solution.py:459
  27.1 5.7 %collective-permute-start.11 = (bf16[64,512]{1,0:T(8,128)(2,1)S(1)}, bf16[64,512]{1,0:T(8,128)(2,1)S(1)}, u32[]{:S(2)}, u32[]{:S(2)}) collective-permute-start(bf16[64,512]{1,0:T(8,128)(2,1)S(1)} %get-tuple-element.94.refs_2_), channel_id=1, source_target_pairs={{0,8},{4,12},{8,0},{12,4},{1,9},{5,13},{9,1},{13,5},{2,10},{6,14},... | collective-permute-start | bytes 196616 | tf_op jit(solution)/shard_map/ppermute | solution.py:455
  30.8 3.1 %collective-permute-start.12 = (bf16[64,512]{1,0:T(8,128)(2,1)S(1)}, bf16[64,512]{1,0:T(8,128)(2,1)S(1)}, u32[]{:S(2)}, u32[]{:S(2)}) collective-permute-start(bf16[64,512]{1,0:T(8,128)(2,1)S(1)} %get-tuple-element.97), channel_id=1, source_target_pairs={{0,1},{1,0},{2,3},{3,2},{4,5},{5,4},{6,7},{7,6},{8,9},{9,8},{10,11... | collective-permute-start | bytes 196616 | tf_op jit(solution)/shard_map/ppermute | solution.py:467
  31.6 2.3 %collective-permute-start.13 = (bf16[64,512]{1,0:T(8,128)(2,1)S(1)}, bf16[64,512]{1,0:T(8,128)(2,1)S(1)}, u32[]{:S(2)}, u32[]{:S(2)}) collective-permute-start(bf16[64,512]{1,0:T(8,128)(2,1)S(1)} %get-tuple-element.98), channel_id=1, source_target_pairs={{0,1},{1,0},{2,3},{3,2},{4,5},{5,4},{6,7},{7,6},{8,9},{9,8},{10,11... | collective-permute-start | bytes 196616 | tf_op jit(solution)/shard_map/ppermute | solution.py:467
  31.7 2.7 %collective-permute-start.14 = (bf16[64,512]{1,0:T(8,128)(2,1)S(1)}, bf16[64,512]{1,0:T(8,128)(2,1)S(1)}, u32[]{:S(2)}, u32[]{:S(2)}) collective-permute-start(bf16[64,512]{1,0:T(8,128)(2,1)S(1)} %get-tuple-element.99), channel_id=1, source_target_pairs={{0,1},{1,0},{2,3},{3,2},{4,5},{5,4},{6,7},{7,6},{8,9},{9,8},{10,11... | collective-permute-start | bytes 196616 | tf_op jit(solution)/shard_map/ppermute | solution.py:467
  32.1 2.4 %collective-permute-start.15 = (bf16[64,512]{1,0:T(8,128)(2,1)S(1)}, bf16[64,512]{1,0:T(8,128)(2,1)S(1)}, u32[]{:S(2)}, u32[]{:S(2)}) collective-permute-start(bf16[64,512]{1,0:T(8,128)(2,1)S(1)} %get-tuple-element.100), channel_id=1, source_target_pairs={{0,1},{1,0},{2,3},{3,2},{4,5},{5,4},{6,7},{7,6},{8,9},{9,8},{10,11... | collective-permute-start | bytes 196616 | tf_op jit(solution)/shard_map/ppermute | solution.py:467
  32.8 2.2 %collective-permute-start.16 = (bf16[64,512]{1,0:T(8,128)(2,1)S(1)}, bf16[64,512]{1,0:T(8,128)(2,1)S(1)}, u32[]{:S(2)}, u32[]{:S(2)}) collective-permute-start(bf16[64,512]{1,0:T(8,128)(2,1)S(1)} %get-tuple-element.101), channel_id=1, source_target_pairs={{0,1},{1,0},{2,3},{3,2},{4,5},{5,4},{6,7},{7,6},{8,9},{9,8},{10,11... | collective-permute-start | bytes 196616 | tf_op jit(solution)/shard_map/ppermute | solution.py:467
  33.9 1.3 %collective-permute-start.17 = (bf16[64,512]{1,0:T(8,128)(2,1)S(1)}, bf16[64,512]{1,0:T(8,128)(2,1)S(1)}, u32[]{:S(2)}, u32[]{:S(2)}) collective-permute-start(bf16[64,512]{1,0:T(8,128)(2,1)S(1)} %get-tuple-element.102), channel_id=1, source_target_pairs={{0,1},{1,0},{2,3},{3,2},{4,5},{5,4},{6,7},{7,6},{8,9},{9,8},{10,11... | collective-permute-start | bytes 196616 | tf_op jit(solution)/shard_map/ppermute | solution.py:467
  33.9 1.4 %collective-permute-start.18 = (bf16[64,512]{1,0:T(8,128)(2,1)S(1)}, bf16[64,512]{1,0:T(8,128)(2,1)S(1)}, u32[]{:S(2)}, u32[]{:S(2)}) collective-permute-start(bf16[64,512]{1,0:T(8,128)(2,1)S(1)} %get-tuple-element.103), channel_id=1, source_target_pairs={{0,1},{1,0},{2,3},{3,2},{4,5},{5,4},{6,7},{7,6},{8,9},{9,8},{10,11... | collective-permute-start | bytes 196616 | tf_op jit(solution)/shard_map/ppermute | solution.py:467
  34.4 1.3 %collective-permute-start.19 = (bf16[64,512]{1,0:T(8,128)(2,1)S(1)}, bf16[64,512]{1,0:T(8,128)(2,1)S(1)}, u32[]{:S(2)}, u32[]{:S(2)}) collective-permute-start(bf16[64,512]{1,0:T(8,128)(2,1)S(1)} %get-tuple-element.104), channel_id=1, source_target_pairs={{0,1},{1,0},{2,3},{3,2},{4,5},{5,4},{6,7},{7,6},{8,9},{9,8},{10,11... | collective-permute-start | bytes 196616 | tf_op jit(solution)/shard_map/ppermute | solution.py:467
  34.5 3.2 %collective-permute-start.20 = (bf16[64,512]{1,0:T(8,128)(2,1)S(1)}, bf16[64,512]{1,0:T(8,128)(2,1)S(1)}, u32[]{:S(2)}, u32[]{:S(2)}) collective-permute-start(bf16[64,512]{1,0:T(8,128)(2,1)S(1)} %get-tuple-element.106.refs_1_), channel_id=1, source_target_pairs={{0,4},{4,0},{8,12},{12,8},{1,5},{5,1},{9,13},{13,9},{2,6},{6,2},{1... | collective-permute-start | bytes 196616 | tf_op jit(solution)/shard_map/ppermute | solution.py:459
  35.8 8.8 %collective-permute-start.29 = (bf16[64,2048]{1,0:T(8,128)(2,1)S(1)}, bf16[64,2048]{1,0:T(8,128)(2,1)S(1)}, u32[]{:S(2)}, u32[]{:S(2)}) collective-permute-start(bf16[64,2048]{1,0:T(8,128)(2,1)S(1)} %get-tuple-element.119), channel_id=1, source_target_pairs={{0,2},{2,0},{1,3},{3,1},{4,6},{6,4},{5,7},{7,5},{8,10},{10,8},{9,1... | collective-permute-start | bytes 786440 | tf_op jit(solution)/shard_map/ppermute | solution.py:472
  38.4 2.6 %collective-permute-start.21 = (bf16[64,512]{1,0:T(8,128)(2,1)S(1)}, bf16[64,512]{1,0:T(8,128)(2,1)S(1)}, u32[]{:S(2)}, u32[]{:S(2)}) collective-permute-start(bf16[64,512]{1,0:T(8,128)(2,1)S(1)} %get-tuple-element.109), channel_id=1, source_target_pairs={{0,1},{1,0},{2,3},{3,2},{4,5},{5,4},{6,7},{7,6},{8,9},{9,8},{10,11... | collective-permute-start | bytes 196616 | tf_op jit(solution)/shard_map/ppermute | solution.py:467
  40.1 1.3 %collective-permute-start.22 = (bf16[64,512]{1,0:T(8,128)(2,1)S(1)}, bf16[64,512]{1,0:T(8,128)(2,1)S(1)}, u32[]{:S(2)}, u32[]{:S(2)}) collective-permute-start(bf16[64,512]{1,0:T(8,128)(2,1)S(1)} %get-tuple-element.110), channel_id=1, source_target_pairs={{0,1},{1,0},{2,3},{3,2},{4,5},{5,4},{6,7},{7,6},{8,9},{9,8},{10,11... | collective-permute-start | bytes 196616 | tf_op jit(solution)/shard_map/ppermute | solution.py:467
  40.1 2.4 %collective-permute-start.23 = (bf16[64,512]{1,0:T(8,128)(2,1)S(1)}, bf16[64,512]{1,0:T(8,128)(2,1)S(1)}, u32[]{:S(2)}, u32[]{:S(2)}) collective-permute-start(bf16[64,512]{1,0:T(8,128)(2,1)S(1)} %get-tuple-element.111), channel_id=1, source_target_pairs={{0,1},{1,0},{2,3},{3,2},{4,5},{5,4},{6,7},{7,6},{8,9},{9,8},{10,11... | collective-permute-start | bytes 196616 | tf_op jit(solution)/shard_map/ppermute | solution.py:467
  40.6 2.4 %collective-permute-start.24 = (bf16[64,512]{1,0:T(8,128)(2,1)S(1)}, bf16[64,512]{1,0:T(8,128)(2,1)S(1)}, u32[]{:S(2)}, u32[]{:S(2)}) collective-permute-start(bf16[64,512]{1,0:T(8,128)(2,1)S(1)} %get-tuple-element.112), channel_id=1, source_target_pairs={{0,1},{1,0},{2,3},{3,2},{4,5},{5,4},{6,7},{7,6},{8,9},{9,8},{10,11... | collective-permute-start | bytes 196616 | tf_op jit(solution)/shard_map/ppermute | solution.py:467
  41.0 2.1 %collective-permute-start.25 = (bf16[64,512]{1,0:T(8,128)(2,1)S(1)}, bf16[64,512]{1,0:T(8,128)(2,1)S(1)}, u32[]{:S(2)}, u32[]{:S(2)}) collective-permute-start(bf16[64,512]{1,0:T(8,128)(2,1)S(1)} %get-tuple-element.113), channel_id=1, source_target_pairs={{0,1},{1,0},{2,3},{3,2},{4,5},{5,4},{6,7},{7,6},{8,9},{9,8},{10,11... | collective-permute-start | bytes 196616 | tf_op jit(solution)/shard_map/ppermute | solution.py:467
  41.3 8.2 %collective-permute-start.30 = (bf16[64,2048]{1,0:T(8,128)(2,1)S(1)}, bf16[64,2048]{1,0:T(8,128)(2,1)S(1)}, u32[]{:S(2)}, u32[]{:S(2)}) collective-permute-start(bf16[64,2048]{1,0:T(8,128)(2,1)S(1)} %get-tuple-element.121), channel_id=1, source_target_pairs={{0,2},{2,0},{1,3},{3,1},{4,6},{6,4},{5,7},{7,5},{8,10},{10,8},{9,1... | collective-permute-start | bytes 786440 | tf_op jit(solution)/shard_map/ppermute | solution.py:472
  42.5 1.3 %collective-permute-start.26 = (bf16[64,512]{1,0:T(8,128)(2,1)S(1)}, bf16[64,512]{1,0:T(8,128)(2,1)S(1)}, u32[]{:S(2)}, u32[]{:S(2)}) collective-permute-start(bf16[64,512]{1,0:T(8,128)(2,1)S(1)} %get-tuple-element.114), channel_id=1, source_target_pairs={{0,1},{1,0},{2,3},{3,2},{4,5},{5,4},{6,7},{7,6},{8,9},{9,8},{10,11... | collective-permute-start | bytes 196616 | tf_op jit(solution)/shard_map/ppermute | solution.py:467
  43.0 1.3 %collective-permute-start.27 = (bf16[64,512]{1,0:T(8,128)(2,1)S(1)}, bf16[64,512]{1,0:T(8,128)(2,1)S(1)}, u32[]{:S(2)}, u32[]{:S(2)}) collective-permute-start(bf16[64,512]{1,0:T(8,128)(2,1)S(1)} %get-tuple-element.115), channel_id=1, source_target_pairs={{0,1},{1,0},{2,3},{3,2},{4,5},{5,4},{6,7},{7,6},{8,9},{9,8},{10,11... | collective-permute-start | bytes 196616 | tf_op jit(solution)/shard_map/ppermute | solution.py:467
  43.0 1.3 %collective-permute-start.28 = (bf16[64,512]{1,0:T(8,128)(2,1)S(1)}, bf16[64,512]{1,0:T(8,128)(2,1)S(1)}, u32[]{:S(2)}, u32[]{:S(2)}) collective-permute-start(bf16[64,512]{1,0:T(8,128)(2,1)S(1)} %get-tuple-element.116), channel_id=1, source_target_pairs={{0,1},{1,0},{2,3},{3,2},{4,5},{5,4},{6,7},{7,6},{8,9},{9,8},{10,11... | collective-permute-start | bytes 196616 | tf_op jit(solution)/shard_map/ppermute | solution.py:467
  44.6 7.7 %copy-start.3 = (s32[32]{0:T(128)S(1)}, s32[32]{0:T(128)}, u32[]{:S(2)}) copy-start(s32[32]{0:T(128)} %refs_2_.5) | copy-start | bytes 388
  44.9 7.4 %collective-permute-start.31 = (bf16[64,2048]{1,0:T(8,128)(2,1)S(1)}, bf16[64,2048]{1,0:T(8,128)(2,1)S(1)}, u32[]{:S(2)}, u32[]{:S(2)}) collective-permute-start(bf16[64,2048]{1,0:T(8,128)(2,1)S(1)} %get-tuple-element.123.refs_2_.refs_1_), channel_id=1, source_target_pairs={{0,1},{1,0},{2,3},{3,2},{4,5},{5,4},{6,7},{7,6},{8,9},{9,8},{10,11... | collective-permute-start | bytes 786440 | tf_op jit(solution)/shard_map/ppermute | solution.py:485
  45.3 11.7 %collective-permute-start.34 = (bf16[64,2048]{1,0:T(8,128)(2,1)S(1)}, bf16[64,2048]{1,0:T(8,128)(2,1)S(1)}, u32[]{:S(2)}, u32[]{:S(2)}) collective-permute-start(bf16[64,2048]{1,0:T(8,128)(2,1)S(1)} %get-tuple-element.128), channel_id=1, source_target_pairs={{0,2},{2,0},{1,3},{3,1},{4,6},{6,4},{5,7},{7,5},{8,10},{10,8},{9,1... | collective-permute-start | bytes 786440 | tf_op jit(solution)/shard_map/ppermute | solution.py:472
  46.3 14.4 %collective-permute-start.35 = (bf16[64,2048]{1,0:T(8,128)(2,1)S(1)}, bf16[64,2048]{1,0:T(8,128)(2,1)S(1)}, u32[]{:S(2)}, u32[]{:S(2)}) collective-permute-start(bf16[64,2048]{1,0:T(8,128)(2,1)S(1)} %get-tuple-element.130), channel_id=1, source_target_pairs={{0,2},{2,0},{1,3},{3,1},{4,6},{6,4},{5,7},{7,5},{8,10},{10,8},{9,1... | collective-permute-start | bytes 786440 | tf_op jit(solution)/shard_map/ppermute | solution.py:472
  49.8 2.2 %collective-permute-start.32 = (bf16[64,1024]{1,0:T(8,128)(2,1)S(1)}, bf16[64,1024]{1,0:T(8,128)(2,1)S(1)}, u32[]{:S(2)}, u32[]{:S(2)}) collective-permute-start(bf16[64,1024]{1,0:T(8,128)(2,1)S(1)} %get-tuple-element.124.refs_3_.refs_2_), channel_id=1, source_target_pairs={{0,1},{1,0},{2,3},{3,2},{4,5},{5,4},{6,7},{7,6},{8,9},{9,8},{10,11... | collective-permute-start | bytes 393224 | tf_op jit(solution)/shard_map/ppermute | solution.py:485
  50.9 1.3 %collective-permute-start.33 = (bf16[64,1024]{1,0:T(8,128)(2,1)S(1)}, bf16[64,1024]{1,0:T(8,128)(2,1)S(1)}, u32[]{:S(2)}, u32[]{:S(2)}) collective-permute-start(bf16[64,1024]{1,0:T(8,128)(2,1)S(1)} %get-tuple-element.125.refs_4_.refs_3_), channel_id=1, source_target_pairs={{0,1},{1,0},{2,3},{3,2},{4,5},{5,4},{6,7},{7,6},{8,9},{9,8},{10,11... | collective-permute-start | bytes 393224 | tf_op jit(solution)/shard_map/ppermute | solution.py:485
  54.4 12.0 %collective-permute-start.36 = (bf16[6,32,512]{2,1,0:T(8,128)(2,1)S(1)}, bf16[6,32,512]{2,1,0:T(8,128)(2,1)S(1)}, u32[]{:S(2)}, u32[]{:S(2)}) collective-permute-start(bf16[6,32,512]{2,1,0:T(8,128)(2,1)S(1)} %get-tuple-element.132), channel_id=1, source_target_pairs={{0,12},{4,8},{8,4},{12,0},{1,13},{5,9},{9,5},{13,1},{2,14},{6,10},... | collective-permute-start | bytes 589832 | tf_op jit(solution)/shard_map/ppermute | solution.py:512
  57.3 4.6 %collective-permute-start.37 = (bf16[64,1024]{1,0:T(8,128)(2,1)S(1)}, bf16[64,1024]{1,0:T(8,128)(2,1)S(1)}, u32[]{:S(2)}, u32[]{:S(2)}) collective-permute-start(bf16[64,1024]{1,0:T(8,128)(2,1)S(1)} %get-tuple-element.133.refs_3_.refs_2_), channel_id=1, source_target_pairs={{0,1},{1,0},{2,3},{3,2},{4,5},{5,4},{6,7},{7,6},{8,9},{9,8},{10,11... | collective-permute-start | bytes 393224 | tf_op jit(solution)/shard_map/ppermute | solution.py:485
  57.8 4.6 %collective-permute-start.38 = (bf16[64,1024]{1,0:T(8,128)(2,1)S(1)}, bf16[64,1024]{1,0:T(8,128)(2,1)S(1)}, u32[]{:S(2)}, u32[]{:S(2)}) collective-permute-start(bf16[64,1024]{1,0:T(8,128)(2,1)S(1)} %get-tuple-element.134.refs_4_.refs_3_), channel_id=1, source_target_pairs={{0,1},{1,0},{2,3},{3,2},{4,5},{5,4},{6,7},{7,6},{8,9},{9,8},{10,11... | collective-permute-start | bytes 393224 | tf_op jit(solution)/shard_map/ppermute | solution.py:485
  61.0 4.3 %collective-permute-start.39 = (bf16[64,1024]{1,0:T(8,128)(2,1)S(1)}, bf16[64,1024]{1,0:T(8,128)(2,1)S(1)}, u32[]{:S(2)}, u32[]{:S(2)}) collective-permute-start(bf16[64,1024]{1,0:T(8,128)(2,1)S(1)} %get-tuple-element.135.refs_5_.refs_4_), channel_id=1, source_target_pairs={{0,1},{1,0},{2,3},{3,2},{4,5},{5,4},{6,7},{7,6},{8,9},{9,8},{10,11... | collective-permute-start | bytes 393224 | tf_op jit(solution)/shard_map/ppermute | solution.py:485
  61.8 3.4 %collective-permute-start.40 = (bf16[64,1024]{1,0:T(8,128)(2,1)S(1)}, bf16[64,1024]{1,0:T(8,128)(2,1)S(1)}, u32[]{:S(2)}, u32[]{:S(2)}) collective-permute-start(bf16[64,1024]{1,0:T(8,128)(2,1)S(1)} %get-tuple-element.136.refs_6_.refs_5_), channel_id=1, source_target_pairs={{0,1},{1,0},{2,3},{3,2},{4,5},{5,4},{6,7},{7,6},{8,9},{9,8},{10,11... | collective-permute-start | bytes 393224 | tf_op jit(solution)/shard_map/ppermute | solution.py:485
  61.9 9.3 %collective-permute-start.41 = (bf16[6,32,512]{2,1,0:T(8,128)(2,1)S(1)}, bf16[6,32,512]{2,1,0:T(8,128)(2,1)S(1)}, u32[]{:S(2)}, u32[]{:S(2)}) collective-permute-start(bf16[6,32,512]{2,1,0:T(8,128)(2,1)S(1)} %get-tuple-element.139), channel_id=1, source_target_pairs={{0,4},{4,0},{8,12},{12,8},{1,5},{5,1},{9,13},{13,9},{2,6},{6,2},{1... | collective-permute-start | bytes 589832 | tf_op jit(solution)/shard_map/ppermute | solution.py:512
  62.4 11.7 %collective-permute-start.42 = (bf16[6,32,512]{2,1,0:T(8,128)(2,1)S(1)}, bf16[6,32,512]{2,1,0:T(8,128)(2,1)S(1)}, u32[]{:S(2)}, u32[]{:S(2)}) collective-permute-start(bf16[6,32,512]{2,1,0:T(8,128)(2,1)S(1)} %get-tuple-element.140), channel_id=1, source_target_pairs={{0,8},{4,12},{8,0},{12,4},{1,9},{5,13},{9,1},{13,5},{2,10},{6,14},... | collective-permute-start | bytes 589832 | tf_op jit(solution)/shard_map/ppermute | solution.py:512
  68.5 9.2 %collective-permute-start.43 = (bf16[6,32,512]{2,1,0:T(8,128)(2,1)S(1)}, bf16[6,32,512]{2,1,0:T(8,128)(2,1)S(1)}, u32[]{:S(2)}, u32[]{:S(2)}) collective-permute-start(bf16[6,32,512]{2,1,0:T(8,128)(2,1)S(1)} %get-tuple-element.148), channel_id=1, source_target_pairs={{0,4},{4,0},{8,12},{12,8},{1,5},{5,1},{9,13},{13,9},{2,6},{6,2},{1... | collective-permute-start | bytes 589832 | tf_op jit(solution)/shard_map/ppermute | solution.py:512
  68.6 17.5 %collective-permute-start.44 = (bf16[6,32,512]{2,1,0:T(8,128)(2,1)S(1)}, bf16[6,32,512]{2,1,0:T(8,128)(2,1)S(1)}, u32[]{:S(2)}, u32[]{:S(2)}) collective-permute-start(bf16[6,32,512]{2,1,0:T(8,128)(2,1)S(1)} %get-tuple-element.149), channel_id=1, source_target_pairs={{0,8},{4,12},{8,0},{12,4},{1,9},{5,13},{9,1},{13,5},{2,10},{6,14},... | collective-permute-start | bytes 589832 | tf_op jit(solution)/shard_map/ppermute | solution.py:512
  70.9 21.1 %collective-permute-start.45 = (bf16[6,32,512]{2,1,0:T(8,128)(2,1)S(1)}, bf16[6,32,512]{2,1,0:T(8,128)(2,1)S(1)}, u32[]{:S(2)}, u32[]{:S(2)}) collective-permute-start(bf16[6,32,512]{2,1,0:T(8,128)(2,1)S(1)} %get-tuple-element.150), channel_id=1, source_target_pairs={{0,12},{4,8},{8,4},{12,0},{1,13},{5,9},{9,5},{13,1},{2,14},{6,10},... | collective-permute-start | bytes 589832 | tf_op jit(solution)/shard_map/ppermute | solution.py:512

commit v8 on v7

--- a/solution.py
+++ b/solution.py
@@ -325,9 +325,15 @@
         else:
             same = (labels[base + tile] == labels[base + tile - 1]).astype(jnp.float32)
             acc[...] = acc[...] * same + product
-        slot = labels[base + tile] - labels[base]
-        for start, out in zip(starts, outs):
-            out[slot] = acc[row_at(start, height), :].astype(out.dtype)
+
+        def put(slot=labels[base + tile] - labels[base]):
+            for start, out in zip(starts, outs):
+                out[slot] = acc[row_at(start, height), :].astype(out.dtype)
+
+        if tile + 1 == geno.shape[1] // TILE:
+            put()
+        else:
+            pl.when(labels[base + tile + 1] != labels[base + tile])(put)
 
 
 def loco_body(row, shard, tiles, count, labels, phen, *refs):

time: 94 us -> 95 us (1.011)
  Pallas kernels: 15.5 us -> 17.6 us
  waiting for transfers between devices: 35.4 us -> 34.2 us
    pallas_call x20, Pallas kernels: 11.9 us -> 14 us  [call(): pl.pallas_call(kernel, out_shape=[jax.ShapeDtypeStruct(self.token.shape,...]
    ppermute x4, waiting for transfers between devices: 5.48 us -> 4.41 us  [piece_steps(): now['chip'] = [chip] + [lax.ppermute(send, 'pp', swap) for send in sends]]
  transfers between devices with their start and end apart: 46 -> 46, of which waited for: 23 -> 22; matrix products, arithmetic and copies ran while one was open for 0% -> 0% of each run, Pallas kernels for 15% -> 17%
where the time goes in v8:
time: 95 us; the launch traced here: 94.7 us
  starting transfers between devices  36.7 us (39%)
  waiting for transfers between devices  34.2 us (36%)
  Pallas kernels  17.6 us (19%)
  local copies, waits for them, and re-layouts  5.23 us (6%)
    ppermute x6, waiting for transfers between devices, piece_steps(): lax.ppermute(sums[step], 'mk', along(step))  18.5 us
    pallas_call x20, Pallas kernels, call(): pl.pallas_call(kernel, out_shape=[jax.ShapeDtypeStruct(self.token.shape,...  14 us
    ppermute x6, starting transfers between devices, piece_steps(): lax.ppermute(sums[step], 'mk', along(step))  8.68 us
    ppermute x16, starting transfers between devices, piece_steps(): now['score'] = [keep] + [lax.ppermute(send, 'sub', swap) for send in sends]  6.58 us
    ppermute x2, starting transfers between devices, piece_steps(): now['two'] = (two, lax.ppermute(two, 'mk', along(2)))  5.26 us
    ppermute x4, waiting for transfers between devices, piece_steps(): now['chip'] = [chip] + [lax.ppermute(send, 'pp', swap) for send in sends]  4.41 us
    ppermute x4, starting transfers between devices, piece_steps(): lax.ppermute(one, 'sub', swap)  4.35 us
    unnamed x14, local copies, waits for them, and re-layouts  4.17 us
  transfers between devices with their start and end apart: 46, of which 22 were waited for; matrix products, arithmetic and copies ran while one was open for 0% of the time, Pallas kernels for 17%

profile of v8, /device:TPU:13, one launch (start us, length us, event | category | flops | bytes accessed | tf_op | source)
XLA Modules:
  0.0 94.7 jit_solution(4970900653384472373)
XLA Ops:
  0.6 1.1 %fusion = (bf16[32,4096]{1,0:T(8,128)(2,1)S(1)}, bf16[32,4096]{1,0:T(8,128)(2,1)S(1)}) fusion(bf16[64,4096]{1,0:T(8,128)(2,1)} %param.8), kind=kLoop, calls=%fused_computation | loop fusion | bytes 1048576 | tf_op jit(solution)/shard_map/slice | solution.py:420
  1.7 1.3 %collective-permute-start = (bf16[32,4096]{1,0:T(8,128)(2,1)S(1)}, bf16[32,4096]{1,0:T(8,128)(2,1)S(1)}, u32[]{:S(2)}, u32[]{:S(2)}) collective-permute-start(bf16[32,4096]{1,0:T(8,128)(2,1)S(1)} %get-tuple-element.153.refs_1_), channel_id=1, source_target_pairs={{0,2},{2,0},{1,3},{3,1},{4,6},{6,4},{5,7},{7,5},{8,10},{10,8},{9,1... | collective-permute-start | bytes 786440 | tf_op jit(solution)/shard_map/ppermute | solution.py:422
  3.0 2.2 %copy-done = bf16[512,4096]{1,0:T(8,128)(2,1)S(1)} copy-done((bf16[512,4096]{1,0:T(8,128)(2,1)S(1)}, bf16[512,4096]{1,0:T(8,128)(2,1)}, u32[]{:S(2)}) %copy-start) | copy-done | bytes 4194328
  5.2 0.7 copy-done.4
  5.8 0.7 copy-done.5
  6.5 0.7 copy-done.6
  7.2 1.0 %collective-permute-start.1 = (bf16[32,4096]{1,0:T(8,128)(2,1)S(1)}, bf16[32,4096]{1,0:T(8,128)(2,1)S(1)}, u32[]{:S(2)}, u32[]{:S(2)}) collective-permute-start(bf16[32,4096]{1,0:T(8,128)(2,1)S(1)} %get-tuple-element.78), channel_id=1, source_target_pairs={{0,1},{1,0},{2,3},{3,2},{4,5},{5,4},{6,7},{7,6},{8,9},{9,8},{10,11... | collective-permute-start | bytes 786440 | tf_op jit(solution)/shard_map/ppermute | solution.py:435
  8.3 0.7 collective-permute-done.refs_2_
  8.9 1.5 %collective-permute-start.2 = (bf16[32,4096]{1,0:T(8,128)(2,1)S(1)}, bf16[32,4096]{1,0:T(8,128)(2,1)S(1)}, u32[]{:S(2)}, u32[]{:S(2)}) collective-permute-start(bf16[32,4096]{1,0:T(8,128)(2,1)S(1)} %collective-permute-done.refs_2_), channel_id=1, source_target_pairs={{0,1},{1,0},{2,3},{3,2},{4,5},{5,4},{6,7},{7,6},{8,9},{9,8},{10,11... | collective-permute-start | bytes 786440 | tf_op jit(solution)/shard_map/ppermute | solution.py:436
  10.5 1.2 %collective-permute-start.5 = (bf16[32,4096]{1,0:T(8,128)(2,1)S(1)}, bf16[32,4096]{1,0:T(8,128)(2,1)S(1)}, u32[]{:S(2)}, u32[]{:S(2)}) collective-permute-start(bf16[32,4096]{1,0:T(8,128)(2,1)S(1)} %get-tuple-element.152.refs_1_), channel_id=1, source_target_pairs={{0,2},{2,0},{1,3},{3,1},{4,6},{6,4},{5,7},{7,5},{8,10},{10,8},{9,1... | collective-permute-start | bytes 786440 | tf_op jit(solution)/shard_map/ppermute | solution.py:434
  11.7 1.6 %shard_map.87 = (f32[8,128]{1,0:T(8,128)S(1)}, f32[64,512]{1,0:T(8,128)S(1)}, bf16[64,512]{1,0:T(8,128)(2,1)S(1)}) custom-call(f32[8,128]{1,0:T(8,128)S(1)} %get-tuple-element.77.refs_0_, bf16[32,4096]{1,0:T(8,128)(2,1)S(1)} %get-tuple-element.153.refs_1_, bf16[32,4096]{1,0:T(8,128)(2,1)S(1)} %collective-permute-done.refs_2_, ...), custom_call_target="tpu_custom_call", output_to_operand_aliasing={{0}: (0, {})} | custom-call | flops 1 | bytes 1 | tf_op jit(solution)/shard_map/pallas_call | solution.py:148
  13.5 1.1 %collective-permute-start.4 = (f32[64,128]{1,0:T(8,128)S(1)}, f32[64,128]{1,0:T(8,128)S(1)}, u32[]{:S(2)}, u32[]{:S(2)}) collective-permute-start(f32[64,128]{1,0:T(8,128)S(1)} %get-tuple-element.83.refs_3_), channel_id=1, source_target_pairs={{0,2},{2,0},{1,3},{3,1},{4,6},{6,4},{5,7},{7,5},{8,10},{10,8},{9,1... | collective-permute-start | bytes 98312 | tf_op jit(solution)/shard_map/ppermute | solution.py:430
  14.7 0.9 collective-permute-start.6
  15.6 1.2 %collective-permute-done.3.refs_2_ = bf16[64,512]{1,0:T(8,128)(2,1)S(1)} collective-permute-done((bf16[64,512]{1,0:T(8,128)(2,1)S(1)}, bf16[64,512]{1,0:T(8,128)(2,1)S(1)}, u32[]{:S(2)}, u32[]{:S(2)}) %collective-permute-start.3) | collective-permute-done | bytes 65568 | tf_op jit(solution)/shard_map/ppermute | solution.py:458
  16.8 2.4 %collective-permute-done.4.refs_1_.refs_4_ = f32[64,128]{1,0:T(8,128)S(1)} collective-permute-done((f32[64,128]{1,0:T(8,128)S(1)}, f32[64,128]{1,0:T(8,128)S(1)}, u32[]{:S(2)}, u32[]{:S(2)}) %collective-permute-start.4) | collective-permute-done | bytes 32800 | tf_op jit(solution)/shard_map/ppermute | solution.py:430
  19.2 0.8 collective-permute-start.7
  20.0 2.3 %collective-permute-start.8 = (bf16[64,512]{1,0:T(8,128)(2,1)S(1)}, bf16[64,512]{1,0:T(8,128)(2,1)S(1)}, u32[]{:S(2)}, u32[]{:S(2)}) collective-permute-start(bf16[64,512]{1,0:T(8,128)(2,1)S(1)} %get-tuple-element.87.refs_2_), channel_id=1, source_target_pairs={{0,8},{4,12},{8,0},{12,4},{1,9},{5,13},{9,1},{13,5},{2,10},{6,14},... | collective-permute-start | bytes 196616 | tf_op jit(solution)/shard_map/ppermute | solution.py:461
  22.3 1.6 %shard_map.90 = (f32[8,128]{1,0:T(8,128)S(1)}, f32[64,512]{1,0:T(8,128)S(1)}, bf16[64,512]{1,0:T(8,128)(2,1)S(1)}) custom-call(f32[8,128]{1,0:T(8,128)S(1)} %get-tuple-element.84.refs_0_, bf16[32,4096]{1,0:T(8,128)(2,1)S(1)} %get-tuple-element.152.refs_1_, bf16[32,4096]{1,0:T(8,128)(2,1)S(1)} %collective-permute-done.5.refs_2_, ...), custom_call_target="tpu_custom_call", output_to_operand_aliasing={{0}: (0, {})} | custom-call | flops 1 | bytes 1 | tf_op jit(solution)/shard_map/pallas_call | solution.py:148
  24.1 1.3 %collective-permute-done.8.refs_3_ = bf16[64,512]{1,0:T(8,128)(2,1)S(1)} collective-permute-done((bf16[64,512]{1,0:T(8,128)(2,1)S(1)}, bf16[64,512]{1,0:T(8,128)(2,1)S(1)}, u32[]{:S(2)}, u32[]{:S(2)}) %collective-permute-start.8) | collective-permute-done | bytes 65568 | tf_op jit(solution)/shard_map/ppermute | solution.py:461
  25.6 1.5 %collective-permute-done.9.refs_2_ = bf16[64,512]{1,0:T(8,128)(2,1)S(1)} collective-permute-done((bf16[64,512]{1,0:T(8,128)(2,1)S(1)}, bf16[64,512]{1,0:T(8,128)(2,1)S(1)}, u32[]{:S(2)}, u32[]{:S(2)}) %collective-permute-start.9) | collective-permute-done | bytes 65568 | tf_op jit(solution)/shard_map/ppermute | solution.py:458
  27.1 2.9 %collective-permute-start.11 = (bf16[64,512]{1,0:T(8,128)(2,1)S(1)}, bf16[64,512]{1,0:T(8,128)(2,1)S(1)}, u32[]{:S(2)}, u32[]{:S(2)}) collective-permute-start(bf16[64,512]{1,0:T(8,128)(2,1)S(1)} %get-tuple-element.94.refs_2_), channel_id=1, source_target_pairs={{0,8},{4,12},{8,0},{12,4},{1,9},{5,13},{9,1},{13,5},{2,10},{6,14},... | collective-permute-start | bytes 196616 | tf_op jit(solution)/shard_map/ppermute | solution.py:461
  30.0 0.7 shard_map.93
  30.8 0.8 collective-permute-start.12
  31.7 0.4 collective-permute-start.14
  32.2 0.6 collective-permute-done.11.refs_3_
  32.8 1.0 %collective-permute-start.16 = (bf16[64,512]{1,0:T(8,128)(2,1)S(1)}, bf16[64,512]{1,0:T(8,128)(2,1)S(1)}, u32[]{:S(2)}, u32[]{:S(2)}) collective-permute-start(bf16[64,512]{1,0:T(8,128)(2,1)S(1)} %get-tuple-element.101), channel_id=1, source_target_pairs={{0,1},{1,0},{2,3},{3,2},{4,5},{5,4},{6,7},{7,6},{8,9},{9,8},{10,11... | collective-permute-start | bytes 196616 | tf_op jit(solution)/shard_map/ppermute | solution.py:473
  33.9 0.5 collective-permute-start.18
  34.5 0.6 collective-permute-start.20
  35.3 0.4 collective-permute-done.19.refs_9_
  35.8 1.3 %collective-permute-start.29 = (bf16[64,2048]{1,0:T(8,128)(2,1)S(1)}, bf16[64,2048]{1,0:T(8,128)(2,1)S(1)}, u32[]{:S(2)}, u32[]{:S(2)}) collective-permute-start(bf16[64,2048]{1,0:T(8,128)(2,1)S(1)} %get-tuple-element.119), channel_id=1, source_target_pairs={{0,2},{2,0},{1,3},{3,1},{4,6},{6,4},{5,7},{7,5},{8,10},{10,8},{9,1... | collective-permute-start | bytes 786440 | tf_op jit(solution)/shard_map/ppermute | solution.py:478
  37.1 0.6 collective-permute-done.20.refs_2_
  37.7 0.7 shard_map.96
  38.4 1.7 %collective-permute-start.21 = (bf16[64,512]{1,0:T(8,128)(2,1)S(1)}, bf16[64,512]{1,0:T(8,128)(2,1)S(1)}, u32[]{:S(2)}, u32[]{:S(2)}) collective-permute-start(bf16[64,512]{1,0:T(8,128)(2,1)S(1)} %get-tuple-element.109), channel_id=1, source_target_pairs={{0,1},{1,0},{2,3},{3,2},{4,5},{5,4},{6,7},{7,6},{8,9},{9,8},{10,11... | collective-permute-start | bytes 196616 | tf_op jit(solution)/shard_map/ppermute | solution.py:473
  40.1 0.4 collective-permute-start.23
  41.0 0.4 collective-permute-start.25
  41.3 1.2 %collective-permute-start.30 = (bf16[64,2048]{1,0:T(8,128)(2,1)S(1)}, bf16[64,2048]{1,0:T(8,128)(2,1)S(1)}, u32[]{:S(2)}, u32[]{:S(2)}) collective-permute-start(bf16[64,2048]{1,0:T(8,128)(2,1)S(1)} %get-tuple-element.121), channel_id=1, source_target_pairs={{0,2},{2,0},{1,3},{3,1},{4,6},{6,4},{5,7},{7,5},{8,10},{10,8},{9,1... | collective-permute-start | bytes 786440 | tf_op jit(solution)/shard_map/ppermute | solution.py:478
  42.5 0.4 collective-permute-start.26
  43.0 0.4 collective-permute-start.28
  43.5 0.4 collective-permute-done.26.refs_7_
  43.9 0.4 collective-permute-done.27.refs_8_
  44.9 0.4 collective-permute-start.31
  45.3 1.0 %collective-permute-start.34 = (bf16[64,2048]{1,0:T(8,128)(2,1)S(1)}, bf16[64,2048]{1,0:T(8,128)(2,1)S(1)}, u32[]{:S(2)}, u32[]{:S(2)}) collective-permute-start(bf16[64,2048]{1,0:T(8,128)(2,1)S(1)} %get-tuple-element.128), channel_id=1, source_target_pairs={{0,2},{2,0},{1,3},{3,1},{4,6},{6,4},{5,7},{7,5},{8,10},{10,8},{9,1... | collective-permute-start | bytes 786440 | tf_op jit(solution)/shard_map/ppermute | solution.py:478
  46.3 0.5 collective-permute-start.35
  46.8 2.7 %collective-permute-done.30.refs_6_ = bf16[64,2048]{1,0:T(8,128)(2,1)S(1)} collective-permute-done((bf16[64,2048]{1,0:T(8,128)(2,1)S(1)}, bf16[64,2048]{1,0:T(8,128)(2,1)S(1)}, u32[]{:S(2)}, u32[]{:S(2)}) %collective-permute-start.30) | collective-permute-done | bytes 262176 | tf_op jit(solution)/shard_map/ppermute | solution.py:478
  49.8 1.2 %collective-permute-start.32 = (bf16[64,1024]{1,0:T(8,128)(2,1)S(1)}, bf16[64,1024]{1,0:T(8,128)(2,1)S(1)}, u32[]{:S(2)}, u32[]{:S(2)}) collective-permute-start(bf16[64,1024]{1,0:T(8,128)(2,1)S(1)} %get-tuple-element.124.refs_3_.refs_2_), channel_id=1, source_target_pairs={{0,1},{1,0},{2,3},{3,2},{4,5},{5,4},{6,7},{7,6},{8,9},{9,8},{10,11... | collective-permute-start | bytes 393224 | tf_op jit(solution)/shard_map/ppermute | solution.py:491
  51.0 0.9 collective-permute-done.32.refs_6_
  51.9 0.4 collective-permute-done.33.refs_7_
  52.3 3.1 %shard_map.100 = (f32[8,128]{1,0:T(8,128)S(1)}, bf16[6,32,512]{2,1,0:T(8,128)(2,1)S(1)}, bf16[6,32,512]{2,1,0:T(8,128)(2,1)S(1)}, bf16[6,32,512]{2,1,0:T(8,128)(2,1)S(1)}, bf16[6,32,512]{2,1,0:T(8,128)(2,1)S(1)}) custom-call(f32[8,128]{1,0:T(8,128)S(1)} %get-tuple-element.122.refs_0_, s32[32]{0:T(128)S(1)} %copy-done.3, ...), custom_call_target="tpu_custom_call", output_to_operand_aliasing={{0}: (0, {})} | custom-call | flops 1 | bytes 1 | tf_op jit(solution)/shard_map/pallas_call | solution.py:148
  55.5 2.6 %collective-permute-start.36 = (bf16[6,32,512]{2,1,0:T(8,128)(2,1)S(1)}, bf16[6,32,512]{2,1,0:T(8,128)(2,1)S(1)}, u32[]{:S(2)}, u32[]{:S(2)}) collective-permute-start(bf16[6,32,512]{2,1,0:T(8,128)(2,1)S(1)} %get-tuple-element.132), channel_id=1, source_target_pairs={{0,12},{4,8},{8,4},{12,0},{1,13},{5,9},{9,5},{13,1},{2,14},{6,10},... | collective-permute-start | bytes 589832 | tf_op jit(solution)/shard_map/ppermute | solution.py:518
  58.4 0.5 collective-permute-start.37
  59.0 1.7 %collective-permute-done.35.refs_6_ = bf16[64,2048]{1,0:T(8,128)(2,1)S(1)} collective-permute-done((bf16[64,2048]{1,0:T(8,128)(2,1)S(1)}, bf16[64,2048]{1,0:T(8,128)(2,1)S(1)}, u32[]{:S(2)}, u32[]{:S(2)}) %collective-permute-start.35) | collective-permute-done | bytes 262176 | tf_op jit(solution)/shard_map/ppermute | solution.py:478
  61.0 0.8 collective-permute-start.39
  61.9 0.5 collective-permute-start.41
  62.4 2.8 %collective-permute-start.42 = (bf16[6,32,512]{2,1,0:T(8,128)(2,1)S(1)}, bf16[6,32,512]{2,1,0:T(8,128)(2,1)S(1)}, u32[]{:S(2)}, u32[]{:S(2)}) collective-permute-start(bf16[6,32,512]{2,1,0:T(8,128)(2,1)S(1)} %get-tuple-element.140), channel_id=1, source_target_pairs={{0,8},{4,12},{8,0},{12,4},{1,9},{5,13},{9,1},{13,5},{2,10},{6,14},... | collective-permute-start | bytes 589832 | tf_op jit(solution)/shard_map/ppermute | solution.py:518
  65.2 2.3 %collective-permute-done.36.refs_1_.refs_6_ = bf16[6,32,512]{2,1,0:T(8,128)(2,1)S(1)} collective-permute-done((bf16[6,32,512]{2,1,0:T(8,128)(2,1)S(1)}, bf16[6,32,512]{2,1,0:T(8,128)(2,1)S(1)}, u32[]{:S(2)}, u32[]{:S(2)}) %collective-permute-start.36) | collective-permute-done | bytes 196640 | tf_op jit(solution)/shard_map/ppermute | solution.py:518
  67.5 3.1 %shard_map.103 = (f32[8,128]{1,0:T(8,128)S(1)}, bf16[6,32,512]{2,1,0:T(8,128)(2,1)S(1)}, bf16[6,32,512]{2,1,0:T(8,128)(2,1)S(1)}, bf16[6,32,512]{2,1,0:T(8,128)(2,1)S(1)}, bf16[6,32,512]{2,1,0:T(8,128)(2,1)S(1)}) custom-call(f32[8,128]{1,0:T(8,128)S(1)} %get-tuple-element.131.refs_0_, ...), custom_call_target="tpu_custom_call", output_to_operand_aliasing={{0}: (0, {})} | custom-call | flops 1 | bytes 1 | tf_op jit(solution)/shard_map/pallas_call | solution.py:148
  70.7 2.3 %collective-permute-start.44 = (bf16[6,32,512]{2,1,0:T(8,128)(2,1)S(1)}, bf16[6,32,512]{2,1,0:T(8,128)(2,1)S(1)}, u32[]{:S(2)}, u32[]{:S(2)}) collective-permute-start(bf16[6,32,512]{2,1,0:T(8,128)(2,1)S(1)} %get-tuple-element.149), channel_id=1, source_target_pairs={{0,8},{4,12},{8,0},{12,4},{1,9},{5,13},{9,1},{13,5},{2,10},{6,14},... | collective-permute-start | bytes 589832 | tf_op jit(solution)/shard_map/ppermute | solution.py:518
  73.4 1.6 %collective-permute-done.42.refs_5_ = bf16[6,32,512]{2,1,0:T(8,128)(2,1)S(1)} collective-permute-done((bf16[6,32,512]{2,1,0:T(8,128)(2,1)S(1)}, bf16[6,32,512]{2,1,0:T(8,128)(2,1)S(1)}, u32[]{:S(2)}, u32[]{:S(2)}) %collective-permute-start.42) | collective-permute-done | bytes 196640 | tf_op jit(solution)/shard_map/ppermute | solution.py:518
  74.9 1.8 %shard_map.104 = (bf16[22,64,512]{2,1,0:T(8,128)(2,1)}, f32[8,128]{1,0:T(8,128)S(1)}) custom-call(f32[8,128]{1,0:T(8,128)S(1)} %get-tuple-element.137.refs_0_, s32[32]{0:T(128)S(1)} %copy-done.3, bf16[256,512]{1,0:T(8,128)(2,1)S(1)} %copy-done.2, bf16[6,32,512]{2,1,0:T(8,128)(2,1)S(1)} %get-tuple-element.138.refs_3_, ...), custom_call_target="tpu_custom_call", output_to_operand_aliasing={{1}: (0, {})} | custom-call | flops 1 | bytes 1 | tf_op jit(solution)/shard_map/pallas_call | solution.py:385
  76.7 0.7 shard_map.105
  77.5 0.7 shard_map.106
  78.2 9.3 %collective-permute-done.44.refs_6_ = bf16[6,32,512]{2,1,0:T(8,128)(2,1)S(1)} collective-permute-done((bf16[6,32,512]{2,1,0:T(8,128)(2,1)S(1)}, bf16[6,32,512]{2,1,0:T(8,128)(2,1)S(1)}, u32[]{:S(2)}, u32[]{:S(2)}) %collective-permute-start.44) | collective-permute-done | bytes 196640 | tf_op jit(solution)/shard_map/ppermute | solution.py:518
  87.6 5.3 %collective-permute-done.45.refs_7_ = bf16[6,32,512]{2,1,0:T(8,128)(2,1)S(1)} collective-permute-done((bf16[6,32,512]{2,1,0:T(8,128)(2,1)S(1)}, bf16[6,32,512]{2,1,0:T(8,128)(2,1)S(1)}, u32[]{:S(2)}, u32[]{:S(2)}) %collective-permute-start.45) | collective-permute-done | bytes 196640 | tf_op jit(solution)/shard_map/ppermute | solution.py:518
  92.9 1.8 %shard_map.107 = (bf16[22,64,512]{2,1,0:T(8,128)(2,1)}, f32[8,128]{1,0:T(8,128)S(1)}) custom-call(bf16[22,64,512]{2,1,0:T(8,128)(2,1)} %get-tuple-element.145.refs_0_, f32[8,128]{1,0:T(8,128)S(1)} %get-tuple-element.146.refs_1_, s32[32]{0:T(128)S(1)} %copy-done.3, bf16[256,512]{1,0:T(8,128)(2,1)S(1)} %copy-done.2, ...), custom_call_target="tpu_custom_call", output_to_operand_aliasing={{0}: (0, {}), {1}: (1, {})} | custom-call | flops 1 | bytes 1 | tf_op jit(solution)/shard_map/pallas_call | solution.py:385
  (66 shorter events, 4.2 us)
Async XLA Ops:
  1.7 7.2 %collective-permute-start = (bf16[32,4096]{1,0:T(8,128)(2,1)S(1)}, bf16[32,4096]{1,0:T(8,128)(2,1)S(1)}, u32[]{:S(2)}, u32[]{:S(2)}) collective-permute-start(bf16[32,4096]{1,0:T(8,128)(2,1)S(1)} %get-tuple-element.153.refs_1_), channel_id=1, source_target_pairs={{0,2},{2,0},{1,3},{3,1},{4,6},{6,4},{5,7},{7,5},{8,10},{10,8},{9,1... | collective-permute-start | bytes 786440 | tf_op jit(solution)/shard_map/ppermute | solution.py:422
  3.0 2.2 %copy-start = (bf16[512,4096]{1,0:T(8,128)(2,1)S(1)}, bf16[512,4096]{1,0:T(8,128)(2,1)}, u32[]{:S(2)}) copy-start(bf16[512,4096]{1,0:T(8,128)(2,1)} %refs_11_.1) | copy-start | bytes 12582916
  5.2 0.7 copy-start.4
  5.8 0.7 copy-start.5
  6.5 0.7 copy-start.6
  7.1 4.6 %copy-start.1 = (bf16[512,4096]{1,0:T(8,128)(2,1)S(1)}, bf16[512,4096]{1,0:T(8,128)(2,1)}, u32[]{:S(2)}) copy-start(bf16[512,4096]{1,0:T(8,128)(2,1)} %refs_11_.1) | copy-start | bytes 12582916
  7.2 4.5 %collective-permute-start.1 = (bf16[32,4096]{1,0:T(8,128)(2,1)S(1)}, bf16[32,4096]{1,0:T(8,128)(2,1)S(1)}, u32[]{:S(2)}, u32[]{:S(2)}) collective-permute-start(bf16[32,4096]{1,0:T(8,128)(2,1)S(1)} %get-tuple-element.78), channel_id=1, source_target_pairs={{0,1},{1,0},{2,3},{3,2},{4,5},{5,4},{6,7},{7,6},{8,9},{9,8},{10,11... | collective-permute-start | bytes 786440 | tf_op jit(solution)/shard_map/ppermute | solution.py:435
  8.9 2.8 %collective-permute-start.2 = (bf16[32,4096]{1,0:T(8,128)(2,1)S(1)}, bf16[32,4096]{1,0:T(8,128)(2,1)S(1)}, u32[]{:S(2)}, u32[]{:S(2)}) collective-permute-start(bf16[32,4096]{1,0:T(8,128)(2,1)S(1)} %collective-permute-done.refs_2_), channel_id=1, source_target_pairs={{0,1},{1,0},{2,3},{3,2},{4,5},{5,4},{6,7},{7,6},{8,9},{9,8},{10,11... | collective-permute-start | bytes 786440 | tf_op jit(solution)/shard_map/ppermute | solution.py:436
  10.5 8.6 %collective-permute-start.5 = (bf16[32,4096]{1,0:T(8,128)(2,1)S(1)}, bf16[32,4096]{1,0:T(8,128)(2,1)S(1)}, u32[]{:S(2)}, u32[]{:S(2)}) collective-permute-start(bf16[32,4096]{1,0:T(8,128)(2,1)S(1)} %get-tuple-element.152.refs_1_), channel_id=1, source_target_pairs={{0,2},{2,0},{1,3},{3,1},{4,6},{6,4},{5,7},{7,5},{8,10},{10,8},{9,1... | collective-permute-start | bytes 786440 | tf_op jit(solution)/shard_map/ppermute | solution.py:434
  13.3 3.5 %collective-permute-start.3 = (bf16[64,512]{1,0:T(8,128)(2,1)S(1)}, bf16[64,512]{1,0:T(8,128)(2,1)S(1)}, u32[]{:S(2)}, u32[]{:S(2)}) collective-permute-start(bf16[64,512]{1,0:T(8,128)(2,1)S(1)} %get-tuple-element.81), channel_id=1, source_target_pairs={{0,4},{4,0},{8,12},{12,8},{1,5},{5,1},{9,13},{13,9},{2,6},{6,2},{1... | collective-permute-start | bytes 196616 | tf_op jit(solution)/shard_map/ppermute | solution.py:458
  13.5 5.6 %collective-permute-start.4 = (f32[64,128]{1,0:T(8,128)S(1)}, f32[64,128]{1,0:T(8,128)S(1)}, u32[]{:S(2)}, u32[]{:S(2)}) collective-permute-start(f32[64,128]{1,0:T(8,128)S(1)} %get-tuple-element.83.refs_3_), channel_id=1, source_target_pairs={{0,2},{2,0},{1,3},{3,1},{4,6},{6,4},{5,7},{7,5},{8,10},{10,8},{9,1... | collective-permute-start | bytes 98312 | tf_op jit(solution)/shard_map/ppermute | solution.py:430
  14.7 7.7 %collective-permute-start.6 = (bf16[32,4096]{1,0:T(8,128)(2,1)S(1)}, bf16[32,4096]{1,0:T(8,128)(2,1)S(1)}, u32[]{:S(2)}, u32[]{:S(2)}) collective-permute-start(bf16[32,4096]{1,0:T(8,128)(2,1)S(1)} %get-tuple-element.152.refs_1_), channel_id=1, source_target_pairs={{0,1},{1,0},{2,3},{3,2},{4,5},{5,4},{6,7},{7,6},{8,9},{9,8},{10,11... | collective-permute-start | bytes 786440 | tf_op jit(solution)/shard_map/ppermute | solution.py:435
  19.2 3.2 %collective-permute-start.7 = (bf16[32,4096]{1,0:T(8,128)(2,1)S(1)}, bf16[32,4096]{1,0:T(8,128)(2,1)S(1)}, u32[]{:S(2)}, u32[]{:S(2)}) collective-permute-start(bf16[32,4096]{1,0:T(8,128)(2,1)S(1)} %get-tuple-element.85), channel_id=1, source_target_pairs={{0,1},{1,0},{2,3},{3,2},{4,5},{5,4},{6,7},{7,6},{8,9},{9,8},{10,11... | collective-permute-start | bytes 786440 | tf_op jit(solution)/shard_map/ppermute | solution.py:442
  20.0 5.5 %collective-permute-start.8 = (bf16[64,512]{1,0:T(8,128)(2,1)S(1)}, bf16[64,512]{1,0:T(8,128)(2,1)S(1)}, u32[]{:S(2)}, u32[]{:S(2)}) collective-permute-start(bf16[64,512]{1,0:T(8,128)(2,1)S(1)} %get-tuple-element.87.refs_2_), channel_id=1, source_target_pairs={{0,8},{4,12},{8,0},{12,4},{1,9},{5,13},{9,1},{13,5},{2,10},{6,14},... | collective-permute-start | bytes 196616 | tf_op jit(solution)/shard_map/ppermute | solution.py:461
  22.3 3.1 %copy-start.2 = (bf16[256,512]{1,0:T(8,128)(2,1)S(1)}, bf16[256,512]{1,0:T(8,128)(2,1)}, u32[]{:S(2)}) copy-start(bf16[256,512]{1,0:T(8,128)(2,1)} %refs_3_.5) | copy-start | bytes 786436
  23.9 3.2 %collective-permute-start.9 = (bf16[64,512]{1,0:T(8,128)(2,1)S(1)}, bf16[64,512]{1,0:T(8,128)(2,1)S(1)}, u32[]{:S(2)}, u32[]{:S(2)}) collective-permute-start(bf16[64,512]{1,0:T(8,128)(2,1)S(1)} %get-tuple-element.90), channel_id=1, source_target_pairs={{0,4},{4,0},{8,12},{12,8},{1,5},{5,1},{9,13},{13,9},{2,6},{6,2},{1... | collective-permute-start | bytes 196616 | tf_op jit(solution)/shard_map/ppermute | solution.py:458
  25.5 4.5 %collective-permute-start.10 = (bf16[64,512]{1,0:T(8,128)(2,1)S(1)}, bf16[64,512]{1,0:T(8,128)(2,1)S(1)}, u32[]{:S(2)}, u32[]{:S(2)}) collective-permute-start(bf16[64,512]{1,0:T(8,128)(2,1)S(1)} %get-tuple-element.92.refs_1_), channel_id=1, source_target_pairs={{0,4},{4,0},{8,12},{12,8},{1,5},{5,1},{9,13},{13,9},{2,6},{6,2},{1... | collective-permute-start | bytes 196616 | tf_op jit(solution)/shard_map/ppermute | solution.py:465
  27.1 5.7 %collective-permute-start.11 = (bf16[64,512]{1,0:T(8,128)(2,1)S(1)}, bf16[64,512]{1,0:T(8,128)(2,1)S(1)}, u32[]{:S(2)}, u32[]{:S(2)}) collective-permute-start(bf16[64,512]{1,0:T(8,128)(2,1)S(1)} %get-tuple-element.94.refs_2_), channel_id=1, source_target_pairs={{0,8},{4,12},{8,0},{12,4},{1,9},{5,13},{9,1},{13,5},{2,10},{6,14},... | collective-permute-start | bytes 196616 | tf_op jit(solution)/shard_map/ppermute | solution.py:461
  30.8 3.1 %collective-permute-start.12 = (bf16[64,512]{1,0:T(8,128)(2,1)S(1)}, bf16[64,512]{1,0:T(8,128)(2,1)S(1)}, u32[]{:S(2)}, u32[]{:S(2)}) collective-permute-start(bf16[64,512]{1,0:T(8,128)(2,1)S(1)} %get-tuple-element.97), channel_id=1, source_target_pairs={{0,1},{1,0},{2,3},{3,2},{4,5},{5,4},{6,7},{7,6},{8,9},{9,8},{10,11... | collective-permute-start | bytes 196616 | tf_op jit(solution)/shard_map/ppermute | solution.py:473
  31.6 2.3 %collective-permute-start.13 = (bf16[64,512]{1,0:T(8,128)(2,1)S(1)}, bf16[64,512]{1,0:T(8,128)(2,1)S(1)}, u32[]{:S(2)}, u32[]{:S(2)}) collective-permute-start(bf16[64,512]{1,0:T(8,128)(2,1)S(1)} %get-tuple-element.98), channel_id=1, source_target_pairs={{0,1},{1,0},{2,3},{3,2},{4,5},{5,4},{6,7},{7,6},{8,9},{9,8},{10,11... | collective-permute-start | bytes 196616 | tf_op jit(solution)/shard_map/ppermute | solution.py:473
  31.7 2.7 %collective-permute-start.14 = (bf16[64,512]{1,0:T(8,128)(2,1)S(1)}, bf16[64,512]{1,0:T(8,128)(2,1)S(1)}, u32[]{:S(2)}, u32[]{:S(2)}) collective-permute-start(bf16[64,512]{1,0:T(8,128)(2,1)S(1)} %get-tuple-element.99), channel_id=1, source_target_pairs={{0,1},{1,0},{2,3},{3,2},{4,5},{5,4},{6,7},{7,6},{8,9},{9,8},{10,11... | collective-permute-start | bytes 196616 | tf_op jit(solution)/shard_map/ppermute | solution.py:473
  32.1 2.4 %collective-permute-start.15 = (bf16[64,512]{1,0:T(8,128)(2,1)S(1)}, bf16[64,512]{1,0:T(8,128)(2,1)S(1)}, u32[]{:S(2)}, u32[]{:S(2)}) collective-permute-start(bf16[64,512]{1,0:T(8,128)(2,1)S(1)} %get-tuple-element.100), channel_id=1, source_target_pairs={{0,1},{1,0},{2,3},{3,2},{4,5},{5,4},{6,7},{7,6},{8,9},{9,8},{10,11... | collective-permute-start | bytes 196616 | tf_op jit(solution)/shard_map/ppermute | solution.py:473
  32.8 2.2 %collective-permute-start.16 = (bf16[64,512]{1,0:T(8,128)(2,1)S(1)}, bf16[64,512]{1,0:T(8,128)(2,1)S(1)}, u32[]{:S(2)}, u32[]{:S(2)}) collective-permute-start(bf16[64,512]{1,0:T(8,128)(2,1)S(1)} %get-tuple-element.101), channel_id=1, source_target_pairs={{0,1},{1,0},{2,3},{3,2},{4,5},{5,4},{6,7},{7,6},{8,9},{9,8},{10,11... | collective-permute-start | bytes 196616 | tf_op jit(solution)/shard_map/ppermute | solution.py:473
  33.9 1.3 %collective-permute-start.17 = (bf16[64,512]{1,0:T(8,128)(2,1)S(1)}, bf16[64,512]{1,0:T(8,128)(2,1)S(1)}, u32[]{:S(2)}, u32[]{:S(2)}) collective-permute-start(bf16[64,512]{1,0:T(8,128)(2,1)S(1)} %get-tuple-element.102), channel_id=1, source_target_pairs={{0,1},{1,0},{2,3},{3,2},{4,5},{5,4},{6,7},{7,6},{8,9},{9,8},{10,11... | collective-permute-start | bytes 196616 | tf_op jit(solution)/shard_map/ppermute | solution.py:473
  33.9 1.4 %collective-permute-start.18 = (bf16[64,512]{1,0:T(8,128)(2,1)S(1)}, bf16[64,512]{1,0:T(8,128)(2,1)S(1)}, u32[]{:S(2)}, u32[]{:S(2)}) collective-permute-start(bf16[64,512]{1,0:T(8,128)(2,1)S(1)} %get-tuple-element.103), channel_id=1, source_target_pairs={{0,1},{1,0},{2,3},{3,2},{4,5},{5,4},{6,7},{7,6},{8,9},{9,8},{10,11... | collective-permute-start | bytes 196616 | tf_op jit(solution)/shard_map/ppermute | solution.py:473
  34.4 1.3 %collective-permute-start.19 = (bf16[64,512]{1,0:T(8,128)(2,1)S(1)}, bf16[64,512]{1,0:T(8,128)(2,1)S(1)}, u32[]{:S(2)}, u32[]{:S(2)}) collective-permute-start(bf16[64,512]{1,0:T(8,128)(2,1)S(1)} %get-tuple-element.104), channel_id=1, source_target_pairs={{0,1},{1,0},{2,3},{3,2},{4,5},{5,4},{6,7},{7,6},{8,9},{9,8},{10,11... | collective-permute-start | bytes 196616 | tf_op jit(solution)/shard_map/ppermute | solution.py:473
  34.5 3.2 %collective-permute-start.20 = (bf16[64,512]{1,0:T(8,128)(2,1)S(1)}, bf16[64,512]{1,0:T(8,128)(2,1)S(1)}, u32[]{:S(2)}, u32[]{:S(2)}) collective-permute-start(bf16[64,512]{1,0:T(8,128)(2,1)S(1)} %get-tuple-element.106.refs_1_), channel_id=1, source_target_pairs={{0,4},{4,0},{8,12},{12,8},{1,5},{5,1},{9,13},{13,9},{2,6},{6,2},{1... | collective-permute-start | bytes 196616 | tf_op jit(solution)/shard_map/ppermute | solution.py:465
  35.8 8.8 %collective-permute-start.29 = (bf16[64,2048]{1,0:T(8,128)(2,1)S(1)}, bf16[64,2048]{1,0:T(8,128)(2,1)S(1)}, u32[]{:S(2)}, u32[]{:S(2)}) collective-permute-start(bf16[64,2048]{1,0:T(8,128)(2,1)S(1)} %get-tuple-element.119), channel_id=1, source_target_pairs={{0,2},{2,0},{1,3},{3,1},{4,6},{6,4},{5,7},{7,5},{8,10},{10,8},{9,1... | collective-permute-start | bytes 786440 | tf_op jit(solution)/shard_map/ppermute | solution.py:478
  38.4 2.6 %collective-permute-start.21 = (bf16[64,512]{1,0:T(8,128)(2,1)S(1)}, bf16[64,512]{1,0:T(8,128)(2,1)S(1)}, u32[]{:S(2)}, u32[]{:S(2)}) collective-permute-start(bf16[64,512]{1,0:T(8,128)(2,1)S(1)} %get-tuple-element.109), channel_id=1, source_target_pairs={{0,1},{1,0},{2,3},{3,2},{4,5},{5,4},{6,7},{7,6},{8,9},{9,8},{10,11... | collective-permute-start | bytes 196616 | tf_op jit(solution)/shard_map/ppermute | solution.py:473
  40.1 1.3 %collective-permute-start.22 = (bf16[64,512]{1,0:T(8,128)(2,1)S(1)}, bf16[64,512]{1,0:T(8,128)(2,1)S(1)}, u32[]{:S(2)}, u32[]{:S(2)}) collective-permute-start(bf16[64,512]{1,0:T(8,128)(2,1)S(1)} %get-tuple-element.110), channel_id=1, source_target_pairs={{0,1},{1,0},{2,3},{3,2},{4,5},{5,4},{6,7},{7,6},{8,9},{9,8},{10,11... | collective-permute-start | bytes 196616 | tf_op jit(solution)/shard_map/ppermute | solution.py:473
  40.1 2.4 %collective-permute-start.23 = (bf16[64,512]{1,0:T(8,128)(2,1)S(1)}, bf16[64,512]{1,0:T(8,128)(2,1)S(1)}, u32[]{:S(2)}, u32[]{:S(2)}) collective-permute-start(bf16[64,512]{1,0:T(8,128)(2,1)S(1)} %get-tuple-element.111), channel_id=1, source_target_pairs={{0,1},{1,0},{2,3},{3,2},{4,5},{5,4},{6,7},{7,6},{8,9},{9,8},{10,11... | collective-permute-start | bytes 196616 | tf_op jit(solution)/shard_map/ppermute | solution.py:473
  40.6 2.4 %collective-permute-start.24 = (bf16[64,512]{1,0:T(8,128)(2,1)S(1)}, bf16[64,512]{1,0:T(8,128)(2,1)S(1)}, u32[]{:S(2)}, u32[]{:S(2)}) collective-permute-start(bf16[64,512]{1,0:T(8,128)(2,1)S(1)} %get-tuple-element.112), channel_id=1, source_target_pairs={{0,1},{1,0},{2,3},{3,2},{4,5},{5,4},{6,7},{7,6},{8,9},{9,8},{10,11... | collective-permute-start | bytes 196616 | tf_op jit(solution)/shard_map/ppermute | solution.py:473
  41.0 2.1 %collective-permute-start.25 = (bf16[64,512]{1,0:T(8,128)(2,1)S(1)}, bf16[64,512]{1,0:T(8,128)(2,1)S(1)}, u32[]{:S(2)}, u32[]{:S(2)}) collective-permute-start(bf16[64,512]{1,0:T(8,128)(2,1)S(1)} %get-tuple-element.113), channel_id=1, source_target_pairs={{0,1},{1,0},{2,3},{3,2},{4,5},{5,4},{6,7},{7,6},{8,9},{9,8},{10,11... | collective-permute-start | bytes 196616 | tf_op jit(solution)/shard_map/ppermute | solution.py:473
  41.3 8.2 %collective-permute-start.30 = (bf16[64,2048]{1,0:T(8,128)(2,1)S(1)}, bf16[64,2048]{1,0:T(8,128)(2,1)S(1)}, u32[]{:S(2)}, u32[]{:S(2)}) collective-permute-start(bf16[64,2048]{1,0:T(8,128)(2,1)S(1)} %get-tuple-element.121), channel_id=1, source_target_pairs={{0,2},{2,0},{1,3},{3,1},{4,6},{6,4},{5,7},{7,5},{8,10},{10,8},{9,1... | collective-permute-start | bytes 786440 | tf_op jit(solution)/shard_map/ppermute | solution.py:478
  42.5 1.3 %collective-permute-start.26 = (bf16[64,512]{1,0:T(8,128)(2,1)S(1)}, bf16[64,512]{1,0:T(8,128)(2,1)S(1)}, u32[]{:S(2)}, u32[]{:S(2)}) collective-permute-start(bf16[64,512]{1,0:T(8,128)(2,1)S(1)} %get-tuple-element.114), channel_id=1, source_target_pairs={{0,1},{1,0},{2,3},{3,2},{4,5},{5,4},{6,7},{7,6},{8,9},{9,8},{10,11... | collective-permute-start | bytes 196616 | tf_op jit(solution)/shard_map/ppermute | solution.py:473
  43.0 1.3 %collective-permute-start.27 = (bf16[64,512]{1,0:T(8,128)(2,1)S(1)}, bf16[64,512]{1,0:T(8,128)(2,1)S(1)}, u32[]{:S(2)}, u32[]{:S(2)}) collective-permute-start(bf16[64,512]{1,0:T(8,128)(2,1)S(1)} %get-tuple-element.115), channel_id=1, source_target_pairs={{0,1},{1,0},{2,3},{3,2},{4,5},{5,4},{6,7},{7,6},{8,9},{9,8},{10,11... | collective-permute-start | bytes 196616 | tf_op jit(solution)/shard_map/ppermute | solution.py:473
  43.0 1.3 %collective-permute-start.28 = (bf16[64,512]{1,0:T(8,128)(2,1)S(1)}, bf16[64,512]{1,0:T(8,128)(2,1)S(1)}, u32[]{:S(2)}, u32[]{:S(2)}) collective-permute-start(bf16[64,512]{1,0:T(8,128)(2,1)S(1)} %get-tuple-element.116), channel_id=1, source_target_pairs={{0,1},{1,0},{2,3},{3,2},{4,5},{5,4},{6,7},{7,6},{8,9},{9,8},{10,11... | collective-permute-start | bytes 196616 | tf_op jit(solution)/shard_map/ppermute | solution.py:473
  44.6 7.7 %copy-start.3 = (s32[32]{0:T(128)S(1)}, s32[32]{0:T(128)}, u32[]{:S(2)}) copy-start(s32[32]{0:T(128)} %refs_2_.5) | copy-start | bytes 388
  44.9 7.4 %collective-permute-start.31 = (bf16[64,2048]{1,0:T(8,128)(2,1)S(1)}, bf16[64,2048]{1,0:T(8,128)(2,1)S(1)}, u32[]{:S(2)}, u32[]{:S(2)}) collective-permute-start(bf16[64,2048]{1,0:T(8,128)(2,1)S(1)} %get-tuple-element.123.refs_2_.refs_1_), channel_id=1, source_target_pairs={{0,1},{1,0},{2,3},{3,2},{4,5},{5,4},{6,7},{7,6},{8,9},{9,8},{10,11... | collective-permute-start | bytes 786440 | tf_op jit(solution)/shard_map/ppermute | solution.py:491
  45.3 12.8 %collective-permute-start.34 = (bf16[64,2048]{1,0:T(8,128)(2,1)S(1)}, bf16[64,2048]{1,0:T(8,128)(2,1)S(1)}, u32[]{:S(2)}, u32[]{:S(2)}) collective-permute-start(bf16[64,2048]{1,0:T(8,128)(2,1)S(1)} %get-tuple-element.128), channel_id=1, source_target_pairs={{0,2},{2,0},{1,3},{3,1},{4,6},{6,4},{5,7},{7,5},{8,10},{10,8},{9,1... | collective-permute-start | bytes 786440 | tf_op jit(solution)/shard_map/ppermute | solution.py:478
  46.3 14.4 %collective-permute-start.35 = (bf16[64,2048]{1,0:T(8,128)(2,1)S(1)}, bf16[64,2048]{1,0:T(8,128)(2,1)S(1)}, u32[]{:S(2)}, u32[]{:S(2)}) collective-permute-start(bf16[64,2048]{1,0:T(8,128)(2,1)S(1)} %get-tuple-element.130), channel_id=1, source_target_pairs={{0,2},{2,0},{1,3},{3,1},{4,6},{6,4},{5,7},{7,5},{8,10},{10,8},{9,1... | collective-permute-start | bytes 786440 | tf_op jit(solution)/shard_map/ppermute | solution.py:478
  49.8 2.2 %collective-permute-start.32 = (bf16[64,1024]{1,0:T(8,128)(2,1)S(1)}, bf16[64,1024]{1,0:T(8,128)(2,1)S(1)}, u32[]{:S(2)}, u32[]{:S(2)}) collective-permute-start(bf16[64,1024]{1,0:T(8,128)(2,1)S(1)} %get-tuple-element.124.refs_3_.refs_2_), channel_id=1, source_target_pairs={{0,1},{1,0},{2,3},{3,2},{4,5},{5,4},{6,7},{7,6},{8,9},{9,8},{10,11... | collective-permute-start | bytes 393224 | tf_op jit(solution)/shard_map/ppermute | solution.py:491
  50.9 1.3 %collective-permute-start.33 = (bf16[64,1024]{1,0:T(8,128)(2,1)S(1)}, bf16[64,1024]{1,0:T(8,128)(2,1)S(1)}, u32[]{:S(2)}, u32[]{:S(2)}) collective-permute-start(bf16[64,1024]{1,0:T(8,128)(2,1)S(1)} %get-tuple-element.125.refs_4_.refs_3_), channel_id=1, source_target_pairs={{0,1},{1,0},{2,3},{3,2},{4,5},{5,4},{6,7},{7,6},{8,9},{9,8},{10,11... | collective-permute-start | bytes 393224 | tf_op jit(solution)/shard_map/ppermute | solution.py:491
  55.5 12.1 %collective-permute-start.36 = (bf16[6,32,512]{2,1,0:T(8,128)(2,1)S(1)}, bf16[6,32,512]{2,1,0:T(8,128)(2,1)S(1)}, u32[]{:S(2)}, u32[]{:S(2)}) collective-permute-start(bf16[6,32,512]{2,1,0:T(8,128)(2,1)S(1)} %get-tuple-element.132), channel_id=1, source_target_pairs={{0,12},{4,8},{8,4},{12,0},{1,13},{5,9},{9,5},{13,1},{2,14},{6,10},... | collective-permute-start | bytes 589832 | tf_op jit(solution)/shard_map/ppermute | solution.py:518
  58.4 3.5 %collective-permute-start.37 = (bf16[64,1024]{1,0:T(8,128)(2,1)S(1)}, bf16[64,1024]{1,0:T(8,128)(2,1)S(1)}, u32[]{:S(2)}, u32[]{:S(2)}) collective-permute-start(bf16[64,1024]{1,0:T(8,128)(2,1)S(1)} %get-tuple-element.133.refs_3_.refs_2_), channel_id=1, source_target_pairs={{0,1},{1,0},{2,3},{3,2},{4,5},{5,4},{6,7},{7,6},{8,9},{9,8},{10,11... | collective-permute-start | bytes 393224 | tf_op jit(solution)/shard_map/ppermute | solution.py:491
  58.9 3.5 %collective-permute-start.38 = (bf16[64,1024]{1,0:T(8,128)(2,1)S(1)}, bf16[64,1024]{1,0:T(8,128)(2,1)S(1)}, u32[]{:S(2)}, u32[]{:S(2)}) collective-permute-start(bf16[64,1024]{1,0:T(8,128)(2,1)S(1)} %get-tuple-element.134.refs_4_.refs_3_), channel_id=1, source_target_pairs={{0,1},{1,0},{2,3},{3,2},{4,5},{5,4},{6,7},{7,6},{8,9},{9,8},{10,11... | collective-permute-start | bytes 393224 | tf_op jit(solution)/shard_map/ppermute | solution.py:491
  61.0 4.3 %collective-permute-start.39 = (bf16[64,1024]{1,0:T(8,128)(2,1)S(1)}, bf16[64,1024]{1,0:T(8,128)(2,1)S(1)}, u32[]{:S(2)}, u32[]{:S(2)}) collective-permute-start(bf16[64,1024]{1,0:T(8,128)(2,1)S(1)} %get-tuple-element.135.refs_5_.refs_4_), channel_id=1, source_target_pairs={{0,1},{1,0},{2,3},{3,2},{4,5},{5,4},{6,7},{7,6},{8,9},{9,8},{10,11... | collective-permute-start | bytes 393224 | tf_op jit(solution)/shard_map/ppermute | solution.py:491
  61.8 3.4 %collective-permute-start.40 = (bf16[64,1024]{1,0:T(8,128)(2,1)S(1)}, bf16[64,1024]{1,0:T(8,128)(2,1)S(1)}, u32[]{:S(2)}, u32[]{:S(2)}) collective-permute-start(bf16[64,1024]{1,0:T(8,128)(2,1)S(1)} %get-tuple-element.136.refs_6_.refs_5_), channel_id=1, source_target_pairs={{0,1},{1,0},{2,3},{3,2},{4,5},{5,4},{6,7},{7,6},{8,9},{9,8},{10,11... | collective-permute-start | bytes 393224 | tf_op jit(solution)/shard_map/ppermute | solution.py:491
  61.9 11.5 %collective-permute-start.41 = (bf16[6,32,512]{2,1,0:T(8,128)(2,1)S(1)}, bf16[6,32,512]{2,1,0:T(8,128)(2,1)S(1)}, u32[]{:S(2)}, u32[]{:S(2)}) collective-permute-start(bf16[6,32,512]{2,1,0:T(8,128)(2,1)S(1)} %get-tuple-element.139), channel_id=1, source_target_pairs={{0,4},{4,0},{8,12},{12,8},{1,5},{5,1},{9,13},{13,9},{2,6},{6,2},{1... | collective-permute-start | bytes 589832 | tf_op jit(solution)/shard_map/ppermute | solution.py:518
  62.4 12.5 %collective-permute-start.42 = (bf16[6,32,512]{2,1,0:T(8,128)(2,1)S(1)}, bf16[6,32,512]{2,1,0:T(8,128)(2,1)S(1)}, u32[]{:S(2)}, u32[]{:S(2)}) collective-permute-start(bf16[6,32,512]{2,1,0:T(8,128)(2,1)S(1)} %get-tuple-element.140), channel_id=1, source_target_pairs={{0,8},{4,12},{8,0},{12,4},{1,9},{5,13},{9,1},{13,5},{2,10},{6,14},... | collective-permute-start | bytes 589832 | tf_op jit(solution)/shard_map/ppermute | solution.py:518
  70.6 7.6 %collective-permute-start.43 = (bf16[6,32,512]{2,1,0:T(8,128)(2,1)S(1)}, bf16[6,32,512]{2,1,0:T(8,128)(2,1)S(1)}, u32[]{:S(2)}, u32[]{:S(2)}) collective-permute-start(bf16[6,32,512]{2,1,0:T(8,128)(2,1)S(1)} %get-tuple-element.148), channel_id=1, source_target_pairs={{0,4},{4,0},{8,12},{12,8},{1,5},{5,1},{9,13},{13,9},{2,6},{6,2},{1... | collective-permute-start | bytes 589832 | tf_op jit(solution)/shard_map/ppermute | solution.py:518
  70.7 16.8 %collective-permute-start.44 = (bf16[6,32,512]{2,1,0:T(8,128)(2,1)S(1)}, bf16[6,32,512]{2,1,0:T(8,128)(2,1)S(1)}, u32[]{:S(2)}, u32[]{:S(2)}) collective-permute-start(bf16[6,32,512]{2,1,0:T(8,128)(2,1)S(1)} %get-tuple-element.149), channel_id=1, source_target_pairs={{0,8},{4,12},{8,0},{12,4},{1,9},{5,13},{9,1},{13,5},{2,10},{6,14},... | collective-permute-start | bytes 589832 | tf_op jit(solution)/shard_map/ppermute | solution.py:518
  73.0 19.8 %collective-permute-start.45 = (bf16[6,32,512]{2,1,0:T(8,128)(2,1)S(1)}, bf16[6,32,512]{2,1,0:T(8,128)(2,1)S(1)}, u32[]{:S(2)}, u32[]{:S(2)}) collective-permute-start(bf16[6,32,512]{2,1,0:T(8,128)(2,1)S(1)} %get-tuple-element.150), channel_id=1, source_target_pairs={{0,12},{4,8},{8,4},{12,0},{1,13},{5,9},{9,5},{13,1},{2,14},{6,10},... | collective-permute-start | bytes 589832 | tf_op jit(solution)/shard_map/ppermute | solution.py:518
